TPU v7x, 32 devices: a whole 2x2x4 slice. The times are simulated.
32 devices in a mesh: seq: 8 (over z, y), rows: 4 (over x, core).
Axes of the slice: x: 2, y: 2, z: 4, core: 2. Of those that a mesh axis runs over, the one named last changes fastest.
Arguments:
- inputs: bfloat16 [16, 2048, 1280], P('rows', 'seq'), may hold values from -6 to 6
- cell_ids: int32 [16, 2048], P('rows'), may hold values from 0 to 6, as said below
- valid_counts: int32 [16], P('rows'), may hold values from 1920 to 2048, as said below
- cotangent: bfloat16 [16, 2048, 1280], P('rows', 'seq'), may hold values from -6 to 6
- attention_gain: float32 [1280], replicated, may hold values from 0.5 to 1.5
- qkv_weight: bfloat16 [1280, 3840], replicated, may hold values from -0.15625 to 0.15625
- out_weight: bfloat16 [1280, 1280], replicated, may hold values from -2 to 2
- feed_gain: float32 [1280], replicated, may hold values from 0.5 to 1.5
- up_weight: bfloat16 [1280, 5120], replicated, may hold values from -0.15625 to 0.15625
- down_weight: bfloat16 [5120, 1280], replicated, may hold values from -0.078125 to 0.078125
Outputs:
- outputs: bfloat16 [16, 2048, 1280], P('rows', 'seq')
- input_grad: bfloat16 [16, 2048, 1280], P('rows', 'seq')
- attention_gain_grad: float32 [1280], P('seq')
- qkv_weight_grad: float32 [1280, 3840], P('seq')
- out_weight_grad: float32 [1280, 1280], P('seq')
- feed_gain_grad: float32 [1280], P('seq')
- up_weight_grad: float32 [1280, 5120], P('seq')
- down_weight_grad: float32 [5120, 1280], P('seq')
Inputs may be any that keep to these rules, and one draw needn't show every extreme that they name: `cell_ids`: along each row the ids start at 0 and never fall. In each group of 4 rows held at one index of rows, one row, drawn from the seed, is a single cell without padding; every other row holds at most 7 cells (ids 0 to 6); a cell may lie wholly in padding. `valid_counts`: positions from this count on are padding.
All inputs are finite; a program needn't handle non-finite values.
Results may differ from a plain program's by a relative error of at most 0.019.
Values may be sent and summed in bfloat16 or wider, within the bound.
A program may use at most 512 MiB of HBM per device.

v0:
```python
from functools import partial

import jax
import jax.numpy as jnp
from jax import lax
from jax.sharding import PartitionSpec as P

HDIM = 64


epsilon = 1e-05
group_heads = 4
masked_score = -1e30


def norm_rows(values, gain_vector):
    center = values - jnp.mean(values, axis=-1, keepdims=True)
    spread = jnp.mean(center * center, axis=-1, keepdims=True)
    return center * lax.rsqrt(spread + epsilon) * gain_vector


def head_slice(source, column, set_lanes):
    piece = lax.dynamic_slice_in_dim(source, column, set_lanes, 2)
    return piece.reshape(piece.shape[0], piece.shape[1], group_heads, set_lanes // group_heads)


def per_device(
    inputs,
    cell_ids,
    valid_counts,
    cotangent,
    attention_gain,
    qkv_weight,
    out_weight,
    feed_gain,
    up_weight,
    down_weight,
):
    row_count, block_len, model_width = inputs.shape
    seq_len = cell_ids.shape[1]
    set_lanes = group_heads * HDIM
    head_sets = model_width // set_lanes
    score_scale = HDIM ** (-0.5)
    offset = lax.axis_index("seq") * block_len
    places = jnp.arange(seq_len, dtype=jnp.int32)
    token_tags = jnp.where(places[None, :] < valid_counts[:, None], cell_ids, -1)
    query_tags = lax.dynamic_slice_in_dim(token_tags, offset, block_len, 1)
    query_places = offset + jnp.arange(block_len, dtype=jnp.int32)
    allowed = (query_tags[:, :, None] == token_tags[:, None, :]) & (token_tags[:, None, :] >= 0)
    allowed = allowed | (query_places[:, None] == places[None, :])[None]

    def scores_of(query_part, key_part):
        raw = jnp.einsum(
            "rihe,rjhe->rhij", query_part, key_part, preferred_element_type=jnp.float32
        )
        return jnp.where(allowed[:, None], raw * score_scale, masked_score)

    start_values = inputs.astype(jnp.float32)
    first_norm, first_back = jax.vjp(norm_rows, start_values, attention_gain)
    first_low = first_norm.astype(jnp.bfloat16)
    projected = jnp.einsum(
        "rbd,de->rbe", first_low, qkv_weight, preferred_element_type=jnp.float32
    ).astype(jnp.bfloat16)
    queries = projected[..., :model_width]
    key_values = projected[..., model_width:]
    gathered = lax.all_gather(key_values, "seq", axis=1, tiled=True)

    def forward_set(head_set, running):
        outputs, totals = running
        column = head_set * set_lanes
        query_part = head_slice(queries, column, set_lanes)
        key_part = head_slice(gathered, column, set_lanes)
        value_part = head_slice(gathered, model_width + column, set_lanes)
        scores = scores_of(query_part, key_part)
        row_peak = jnp.max(scores, axis=-1, keepdims=True)
        powers = jnp.exp(scores - row_peak)
        divisor = jnp.sum(powers, axis=-1, keepdims=True)
        weights = (powers / divisor).astype(jnp.bfloat16)
        mixture = jnp.einsum(
            "rhij,rjhe->rihe", weights, value_part, preferred_element_type=jnp.float32
        )
        outputs = lax.dynamic_update_slice_in_dim(
            outputs, mixture.reshape(row_count, block_len, set_lanes), column, 2
        )
        log_total = (row_peak + jnp.log(divisor))[..., 0]
        totals = lax.dynamic_update_slice_in_dim(totals, log_total, head_set * group_heads, 1)
        return (outputs, totals)

    mixed_all, log_totals = lax.fori_loop(
        0,
        head_sets,
        forward_set,
        (
            jnp.zeros((row_count, block_len, model_width), jnp.float32),
            jnp.zeros((row_count, model_width // HDIM, block_len), jnp.float32),
        ),
    )
    mixed_low = mixed_all.astype(jnp.bfloat16)
    middle = start_values + jnp.einsum(
        "rbd,de->rbe", mixed_low, out_weight, preferred_element_type=jnp.float32
    )
    second_norm, second_back = jax.vjp(norm_rows, middle, feed_gain)
    second_low = second_norm.astype(jnp.bfloat16)
    hidden_up = jnp.einsum("rbd,df->rbf", second_low, up_weight, preferred_element_type=jnp.float32)
    activated, gelu_back = jax.vjp(partial(jax.nn.gelu, approximate=False), hidden_up)
    activated_low = activated.astype(jnp.bfloat16)
    outputs = (
        middle
        + jnp.einsum("rbf,fd->rbd", activated_low, down_weight, preferred_element_type=jnp.float32)
    ).astype(jnp.bfloat16)
    down_grad = jnp.einsum(
        "rbf,rbd->fd", activated_low, cotangent, preferred_element_type=jnp.float32
    )
    act_grad = jnp.einsum("rbd,fd->rbf", cotangent, down_weight, preferred_element_type=jnp.float32)
    (up_in_grad,) = gelu_back(act_grad)
    up_low = up_in_grad.astype(jnp.bfloat16)
    up_grad = jnp.einsum("rbd,rbf->df", second_low, up_low, preferred_element_type=jnp.float32)
    second_grad = jnp.einsum("rbf,df->rbd", up_low, up_weight, preferred_element_type=jnp.float32)
    middle_part, feed_gain_part = second_back(second_grad)
    middle_grad = cotangent.astype(jnp.float32) + middle_part
    attended_low = middle_grad.astype(jnp.bfloat16)
    out_grad = jnp.einsum(
        "rbd,rbe->de", mixed_low, attended_low, preferred_element_type=jnp.float32
    )
    mixed_grad = jnp.einsum(
        "rbe,de->rbd", attended_low, out_weight, preferred_element_type=jnp.float32
    ).astype(jnp.bfloat16)
    gathered_back = lax.all_gather(key_values, "seq", axis=1, tiled=True)

    def backward_set(head_set, running):
        query_grads, pair_grads = running
        column = head_set * set_lanes
        query_part = head_slice(queries, column, set_lanes)
        key_part = head_slice(gathered_back, column, set_lanes)
        value_part = head_slice(gathered_back, model_width + column, set_lanes)
        mixed_part = head_slice(mixed_grad, column, set_lanes)
        scores = scores_of(query_part, key_part)
        log_total = lax.dynamic_slice_in_dim(log_totals, head_set * group_heads, group_heads, 1)
        chances = jnp.exp(scores - log_total[..., None])
        weights = chances.astype(jnp.bfloat16)
        weight_grad = jnp.einsum(
            "rihe,rjhe->rhij", mixed_part, value_part, preferred_element_type=jnp.float32
        )
        inner = jnp.sum(chances * weight_grad, axis=-1, keepdims=True)
        score_grad = (chances * (weight_grad - inner) * score_scale).astype(jnp.bfloat16)
        query_piece = jnp.einsum(
            "rhij,rjhe->rihe", score_grad, key_part, preferred_element_type=jnp.float32
        )
        key_piece = jnp.einsum(
            "rhij,rihe->rjhe", score_grad, query_part, preferred_element_type=jnp.float32
        )
        value_piece = jnp.einsum(
            "rhij,rihe->rjhe", weights, mixed_part, preferred_element_type=jnp.float32
        )
        query_grads = lax.dynamic_update_slice_in_dim(
            query_grads, query_piece.reshape(row_count, block_len, set_lanes), column, 2
        )
        pair_grads = lax.dynamic_update_slice_in_dim(
            pair_grads, key_piece.reshape(row_count, seq_len, set_lanes), column, 2
        )
        pair_grads = lax.dynamic_update_slice_in_dim(
            pair_grads, value_piece.reshape(row_count, seq_len, set_lanes), model_width + column, 2
        )
        return (query_grads, pair_grads)

    query_grads, pair_grads = lax.fori_loop(
        0,
        head_sets,
        backward_set,
        (
            jnp.zeros((row_count, block_len, model_width), jnp.float32),
            jnp.zeros((row_count, seq_len, 2 * model_width), jnp.float32),
        ),
    )
    pair_sums = lax.psum_scatter(
        pair_grads.astype(jnp.bfloat16), "seq", scatter_dimension=1, tiled=True
    ).astype(jnp.float32)
    projected_grad = jnp.concatenate([query_grads, pair_sums], axis=2).astype(jnp.bfloat16)
    qkv_grad = jnp.einsum(
        "rbd,rbe->de", first_low, projected_grad, preferred_element_type=jnp.float32
    )
    first_grad = jnp.einsum(
        "rbe,de->rbd", projected_grad, qkv_weight, preferred_element_type=jnp.float32
    )
    start_part, attention_gain_part = first_back(first_grad)
    input_grad = (middle_grad + start_part).astype(jnp.bfloat16)
    shares = (
        lax.psum_scatter(
            attention_gain_part.astype(jnp.bfloat16), "seq", scatter_dimension=0, tiled=True
        ).astype(jnp.float32),
        lax.psum_scatter(
            qkv_grad.astype(jnp.bfloat16), "seq", scatter_dimension=0, tiled=True
        ).astype(jnp.float32),
        lax.psum_scatter(
            out_grad.astype(jnp.bfloat16), "seq", scatter_dimension=0, tiled=True
        ).astype(jnp.float32),
        lax.psum_scatter(
            feed_gain_part.astype(jnp.bfloat16), "seq", scatter_dimension=0, tiled=True
        ).astype(jnp.float32),
        lax.psum_scatter(
            up_grad.astype(jnp.bfloat16), "seq", scatter_dimension=0, tiled=True
        ).astype(jnp.float32),
        lax.psum_scatter(
            down_grad.astype(jnp.bfloat16), "seq", scatter_dimension=0, tiled=True
        ).astype(jnp.float32),
    )
    summed = (
        lax.psum(shares[0].astype(jnp.bfloat16), "rows").astype(jnp.float32),
        lax.psum(shares[1].astype(jnp.bfloat16), "rows").astype(jnp.float32),
        lax.psum(shares[2].astype(jnp.bfloat16), "rows").astype(jnp.float32),
        lax.psum(shares[3].astype(jnp.bfloat16), "rows").astype(jnp.float32),
        lax.psum(shares[4].astype(jnp.bfloat16), "rows").astype(jnp.float32),
        lax.psum(shares[5].astype(jnp.bfloat16), "rows").astype(jnp.float32),
    )
    gain_first, qkv_total, out_total, gain_second, up_total, down_total = summed
    return (
        outputs,
        input_grad,
        gain_first,
        qkv_total,
        out_total,
        gain_second,
        up_total,
        down_total,
    )


def solution(mesh):
    placed = (
        P("rows", "seq", None),
        P("rows", None),
        P("rows"),
        P("rows", "seq", None),
        P(),
        P(),
        P(),
        P(),
        P(),
        P(),
    )
    return jax.shard_map(
        per_device,
        mesh=mesh,
        in_specs=placed,
        out_specs=(
            P("rows", "seq", None),
            P("rows", "seq", None),
            P("seq"),
            P("seq", None),
            P("seq", None),
            P("seq"),
            P("seq", None),
            P("seq", None),
        ),
        check_vma=False,
    )
```

profile of v0, /device:TPU:0, one launch (start us, length us, event | category | flops | bytes accessed | tf_op | source)
XLA Modules:
  0.0 3766.4 jit_solution(18186726040079254990)
XLA Ops:
  12.7 14.8 fusion.74
  43.1 788.3 %all-gather.2.cloned.1.call-done = bf16[4,2048,2560]{2,1,0:T(8,128)(2,1)} async-done(((bf16[4,256,2560]{2,1,0:T(8,128)(2,1)}), bf16[4,2048,2560]{2,1,0:T(8,128)(2,1)}) %all-gather.2.cloned.1.call-update) | async-done | bytes 41943056 | tf_op jit(solution)/shard_map/all_gather | solution.py:66
  831.3 51.1 %copy.29 = bf16[4,2048,2560]{1,2,0:T(8,128)(2,1)} copy(bf16[4,2048,2560]{2,1,0:T(8,128)(2,1)} %all-gather.2.cloned.1.call-done) | data formatting | bytes 83886080
  884.1 297.7 %while.36 = (s32[]{:T(128)}, bf16[4,256,1280]{1,2,0:T(8,128)(2,1)}, f32[4,20,256]{2,1,0:T(8,128)S(1)}, bf16[4,2048,2560]{1,2,0:T(8,128)(2,1)}, bf16[4,256,1280]{...) while((s32[]{:T(128)}, bf16[4,256,1280]{1,2,0:T(8,128)(2,1)}, ...), condition=%wide.region_5.6_spmd.clone, body=%wide.region_2.5_spmd.clone.sunk | while | flops 2254434304 | bytes 154841456 | solution.py:89
  896.8 16.3 fusion.150
  913.1 15.4 fusion.151
  956.3 16.3 fusion.150
  972.6 15.4 fusion.151
  988.0 14.3 fusion.152
  1015.8 16.3 fusion.150
  1032.1 15.4 fusion.151
  1075.3 16.3 fusion.150
  1091.6 15.4 fusion.151
  1134.8 16.3 fusion.150
  1151.1 15.4 fusion.151
  1191.8 28.6 fusion.84
  1220.4 69.9 %add_convert_fusion = (bf16[4,256,5120]{2,1,0:T(8,128)(2,1)}, f32[4,256,5120]{2,1,0:T(8,128)}) fusion(f32[4,256,5120]{2,1,0:T(8,128)} %get-tuple-element.526, u8[256,5120]{1,0:T(8,128)(4,1)} %get-tuple-element.459, u8[256,5120]{1,0:T(8,128)(4,1)} %get-tuple-element.458, bf16[4,256,1280]{2,1,0:T(8,128)(2,1)} %param.17, bf16[5120,1280]{1,0:T(8,128)(2,1)} %param.23), kind=kOutput, calls=%fused_computation.60 | convolution fusion | flops 13825474560 | bytes 70778880 | tf_op jit(solution)/shard_map/rbd,fd->rbf/dot_general | solution.py:114
  1290.4 22.9 multiply_reduce_fusion.1
  1339.2 909.0 %while.37 = (s32[]{:T(128)}, bf16[4,256,1280]{2,1,0:T(8,128)(2,1)}, bf16[4,2048,2560]{1,2,0:T(8,128)(2,1)}, bf16[4,2048,2560]{1,2,0:T(8,128)(2,1)}, bf16[4,256,1...) while((s32[]{:T(128)}, bf16[4,256,1280]{2,1,0:T(8,128)(2,1)}, ...), condition=%wide.region_12.13_spmd.clone, body=%wide.region_10.12_spmd.clone.sunk | while | flops 5593116672 | bytes 339866016 | solution.py:166
  1376.3 57.8 %fusion.165 = bf16[4,4,64,256]{3,2,1,0:T(8,128)(2,1)S(1)} fusion(bf16[4,2048,4,64]{1,3,2,0:T(8,128)(2,1)} %bitcast.128, f32[4,4,256,2048]{3,2,1,0:T(8,128)} %fusion.163, f32[4,4,256,2048]{3,2,1,0:T(8,128)} %fusion.164, f32[4,4,256]{2,1,0:T(4,128)S(1)} %constant_dynamic-slice_fusion.20, pred[4,256,2048]{2,1,0:T(8,128)(4,1)} %and_or_fusion.5), kind=kOutput, calls=%fused_computation.23.clone.1 | convolution fusion | flops 1166022656 | bytes 73940992 | tf_op jit(solution)/shard_map/while/body/eval_jaxpr/rhij,rjhe->rihe/dot_general | solution.py:146
  1434.1 61.4 %fusion.166 = bf16[4,4,64,2048]{3,2,1,0:T(8,128)(2,1)} fusion(bf16[4,256,4,64]{1,3,2,0:T(8,128)(2,1)S(1)} %bitcast.136, f32[4,4,256,2048]{3,2,1,0:T(8,128)} %fusion.163, f32[4,4,256,2048]{3,2,1,0:T(8,128)} %fusion.164, f32[4,4,256]{2,1,0:T(4,128)S(1)} %constant_dynamic-slice_fusion.20, pred[4,256,2048]{2,1,0:T(8,128)(4,1)} %and_or_fusion.5), kind=kOutput, calls=%fused_computation.22.clone.1 | convolution fusion | flops 1166022656 | bytes 73940992 | tf_op jit(solution)/shard_map/while/body/eval_jaxpr/rhij,rihe->rjhe/dot_general | solution.py:149
  1495.5 16.9 fusion.167
  1557.9 57.8 %fusion.165 = bf16[4,4,64,256]{3,2,1,0:T(8,128)(2,1)S(1)} fusion(bf16[4,2048,4,64]{1,3,2,0:T(8,128)(2,1)} %bitcast.128, f32[4,4,256,2048]{3,2,1,0:T(8,128)} %fusion.163, f32[4,4,256,2048]{3,2,1,0:T(8,128)} %fusion.164, f32[4,4,256]{2,1,0:T(4,128)S(1)} %constant_dynamic-slice_fusion.20, pred[4,256,2048]{2,1,0:T(8,128)(4,1)} %and_or_fusion.5), kind=kOutput, calls=%fused_computation.23.clone.1 | convolution fusion | flops 1166022656 | bytes 73940992 | tf_op jit(solution)/shard_map/while/body/eval_jaxpr/rhij,rjhe->rihe/dot_general | solution.py:146
  1615.8 61.4 %fusion.166 = bf16[4,4,64,2048]{3,2,1,0:T(8,128)(2,1)} fusion(bf16[4,256,4,64]{1,3,2,0:T(8,128)(2,1)S(1)} %bitcast.136, f32[4,4,256,2048]{3,2,1,0:T(8,128)} %fusion.163, f32[4,4,256,2048]{3,2,1,0:T(8,128)} %fusion.164, f32[4,4,256]{2,1,0:T(4,128)S(1)} %constant_dynamic-slice_fusion.20, pred[4,256,2048]{2,1,0:T(8,128)(4,1)} %and_or_fusion.5), kind=kOutput, calls=%fused_computation.22.clone.1 | convolution fusion | flops 1166022656 | bytes 73940992 | tf_op jit(solution)/shard_map/while/body/eval_jaxpr/rhij,rihe->rjhe/dot_general | solution.py:149
  1677.2 16.9 fusion.167
  1739.7 57.8 %fusion.165 = bf16[4,4,64,256]{3,2,1,0:T(8,128)(2,1)S(1)} fusion(bf16[4,2048,4,64]{1,3,2,0:T(8,128)(2,1)} %bitcast.128, f32[4,4,256,2048]{3,2,1,0:T(8,128)} %fusion.163, f32[4,4,256,2048]{3,2,1,0:T(8,128)} %fusion.164, f32[4,4,256]{2,1,0:T(4,128)S(1)} %constant_dynamic-slice_fusion.20, pred[4,256,2048]{2,1,0:T(8,128)(4,1)} %and_or_fusion.5), kind=kOutput, calls=%fused_computation.23.clone.1 | convolution fusion | flops 1166022656 | bytes 73940992 | tf_op jit(solution)/shard_map/while/body/eval_jaxpr/rhij,rjhe->rihe/dot_general | solution.py:146
  1797.6 61.4 %fusion.166 = bf16[4,4,64,2048]{3,2,1,0:T(8,128)(2,1)} fusion(bf16[4,256,4,64]{1,3,2,0:T(8,128)(2,1)S(1)} %bitcast.136, f32[4,4,256,2048]{3,2,1,0:T(8,128)} %fusion.163, f32[4,4,256,2048]{3,2,1,0:T(8,128)} %fusion.164, f32[4,4,256]{2,1,0:T(4,128)S(1)} %constant_dynamic-slice_fusion.20, pred[4,256,2048]{2,1,0:T(8,128)(4,1)} %and_or_fusion.5), kind=kOutput, calls=%fused_computation.22.clone.1 | convolution fusion | flops 1166022656 | bytes 73940992 | tf_op jit(solution)/shard_map/while/body/eval_jaxpr/rhij,rihe->rjhe/dot_general | solution.py:149
  1859.0 16.9 fusion.167
  1921.4 57.8 %fusion.165 = bf16[4,4,64,256]{3,2,1,0:T(8,128)(2,1)S(1)} fusion(bf16[4,2048,4,64]{1,3,2,0:T(8,128)(2,1)} %bitcast.128, f32[4,4,256,2048]{3,2,1,0:T(8,128)} %fusion.163, f32[4,4,256,2048]{3,2,1,0:T(8,128)} %fusion.164, f32[4,4,256]{2,1,0:T(4,128)S(1)} %constant_dynamic-slice_fusion.20, pred[4,256,2048]{2,1,0:T(8,128)(4,1)} %and_or_fusion.5), kind=kOutput, calls=%fused_computation.23.clone.1 | convolution fusion | flops 1166022656 | bytes 73940992 | tf_op jit(solution)/shard_map/while/body/eval_jaxpr/rhij,rjhe->rihe/dot_general | solution.py:146
  1979.3 61.4 %fusion.166 = bf16[4,4,64,2048]{3,2,1,0:T(8,128)(2,1)} fusion(bf16[4,256,4,64]{1,3,2,0:T(8,128)(2,1)S(1)} %bitcast.136, f32[4,4,256,2048]{3,2,1,0:T(8,128)} %fusion.163, f32[4,4,256,2048]{3,2,1,0:T(8,128)} %fusion.164, f32[4,4,256]{2,1,0:T(4,128)S(1)} %constant_dynamic-slice_fusion.20, pred[4,256,2048]{2,1,0:T(8,128)(4,1)} %and_or_fusion.5), kind=kOutput, calls=%fused_computation.22.clone.1 | convolution fusion | flops 1166022656 | bytes 73940992 | tf_op jit(solution)/shard_map/while/body/eval_jaxpr/rhij,rihe->rjhe/dot_general | solution.py:149
  2040.7 16.9 fusion.167
  2103.1 57.8 %fusion.165 = bf16[4,4,64,256]{3,2,1,0:T(8,128)(2,1)S(1)} fusion(bf16[4,2048,4,64]{1,3,2,0:T(8,128)(2,1)} %bitcast.128, f32[4,4,256,2048]{3,2,1,0:T(8,128)} %fusion.163, f32[4,4,256,2048]{3,2,1,0:T(8,128)} %fusion.164, f32[4,4,256]{2,1,0:T(4,128)S(1)} %constant_dynamic-slice_fusion.20, pred[4,256,2048]{2,1,0:T(8,128)(4,1)} %and_or_fusion.5), kind=kOutput, calls=%fused_computation.23.clone.1 | convolution fusion | flops 1166022656 | bytes 73940992 | tf_op jit(solution)/shard_map/while/body/eval_jaxpr/rhij,rjhe->rihe/dot_general | solution.py:146
  2160.9 61.4 %fusion.166 = bf16[4,4,64,2048]{3,2,1,0:T(8,128)(2,1)} fusion(bf16[4,256,4,64]{1,3,2,0:T(8,128)(2,1)S(1)} %bitcast.136, f32[4,4,256,2048]{3,2,1,0:T(8,128)} %fusion.163, f32[4,4,256,2048]{3,2,1,0:T(8,128)} %fusion.164, f32[4,4,256]{2,1,0:T(4,128)S(1)} %constant_dynamic-slice_fusion.20, pred[4,256,2048]{2,1,0:T(8,128)(4,1)} %and_or_fusion.5), kind=kOutput, calls=%fused_computation.22.clone.1 | convolution fusion | flops 1166022656 | bytes 73940992 | tf_op jit(solution)/shard_map/while/body/eval_jaxpr/rhij,rihe->rjhe/dot_general | solution.py:149
  2222.3 16.9 fusion.167
  2248.2 50.2 %copy.36 = bf16[4,2048,2560]{2,1,0:T(8,128)(2,1)} copy(bf16[4,2048,2560]{1,2,0:T(8,128)(2,1)} %get-tuple-element.365) | data formatting | bytes 83886080 | tf_op jit(solution)/shard_map/while | solution.py:166
  2306.8 14.7 multiply_convert_fusion.1
  2325.5 16.5 bitcast_convert_fusion
  2342.7 21.7 bitcast_convert_fusion.1
  2364.5 599.1 %reduce-scatter.6.cloned.1.call-done = bf16[4,256,2560]{2,1,0:T(8,128)(2,1)} async-done(((bf16[4,2048,2560]{2,1,0:T(8,128)(2,1)}), bf16[4,256,2560]{2,1,0:T(8,128)(2,1)}) %reduce-scatter.6.cloned.1.call-update) | async-done | bytes 5242896 | tf_op jit(solution)/shard_map/reduce_scatter | solution.py:175
  2963.6 16.9 bitcast_convert_fusion.2
  2982.4 21.4 add_convert_fusion.2
  3003.8 17.4 fusion.82
  3021.2 22.4 reduce-scatter.10.cloned.1.call-done
  3043.5 217.0 %reduce-scatter.14.cloned.1.call-done = bf16[640,1280]{1,0:T(8,128)(2,1)} async-done(((bf16[5120,1280]{1,0:T(8,128)(2,1)}), bf16[640,1280]{1,0:T(8,128)(2,1)}) %reduce-scatter.14.cloned.1.call-update) | async-done | bytes 1638416 | tf_op jit(solution)/shard_map/reduce_scatter | solution.py:203
  3260.6 217.1 %reduce-scatter.12.cloned.1.call-done = bf16[160,5120]{1,0:T(8,128)(2,1)} async-done(((bf16[1280,5120]{1,0:T(8,128)(2,1)}), bf16[160,5120]{1,0:T(8,128)(2,1)}) %reduce-scatter.12.cloned.1.call-update) | async-done | bytes 1638416 | tf_op jit(solution)/shard_map/reduce_scatter | solution.py:200
  3477.7 171.6 %reduce-scatter.8.cloned.1.call-done = bf16[160,3840]{1,0:T(8,128)(2,1)} async-done(((bf16[1280,3840]{1,0:T(8,128)(2,1)}), bf16[160,3840]{1,0:T(8,128)(2,1)}) %reduce-scatter.8.cloned.1.call-update) | async-done | bytes 1228816 | tf_op jit(solution)/shard_map/reduce_scatter | solution.py:191
  3653.3 19.7 all-reduce.2
  3689.2 59.7 %all-reduce.7.cloned.1.call-done = (bf16[160,3840]{1,0:T(8,128)(2,1)}, bf16[160,1280]{1,0:T(8,128)(2,1)}, bf16[160,5120]{1,0:T(8,128)(2,1)}, bf16[640,1280]{1,0:T(8,128)(2,1)}) async-done(((bf16[160,3840]{1,0:T(8,128)(2,1)}, bf16[160,1280]{1,0:T(8,128)(2,1)}, bf16[160,5120]{1,0:T(8,128)(2,1)}, bf16[640,1280]{1,0:T(8,128)(2,1)}), (bf16[160,3840]{1,0:T(8,128)(2,1)}, bf16[160,1280]{1,0:T(8,128)(2,1)}, ...) | async-done | bytes 4915216 | tf_op jit(solution)/shard_map/psum | solution.py:209
  (260 shorter events, 456.0 us)
Async XLA Ops:
  7.2 1174.7 %copy-start = (bf16[1280,1280]{1,0:T(8,128)(2,1)S(1)}, bf16[1280,1280]{1,0:T(8,128)(2,1)}, u32[]{:S(2)}) copy-start(bf16[1280,1280]{1,0:T(8,128)(2,1)} %param.20) | copy-start | bytes 9830404
  7.2 824.2 %all-gather.2.cloned.1.call-start = ((), (), s32[]{:S(2)}) async-start(), calls=%async_computation.5 | async-start | bytes 47185920 | tf_op jit(solution)/shard_map/all_gather | solution.py:66
  9.5 18.0 copy-start.23
  12.7 14.8 copy-start.29
  33.4 8.4 copy-start.36
  33.4 8.4 copy-start.45
  33.4 2930.2 %reduce-scatter.6.cloned.1.call-start = ((), (), s32[]{:S(2)}) async-start(), calls=%async_computation.6 | async-start | bytes 47185920 | tf_op jit(solution)/shard_map/reduce_scatter | solution.py:175
  913.1 15.4 copy-start.4
  972.6 15.4 copy-start.4
  1032.1 15.4 copy-start.4
  1091.6 15.4 copy-start.4
  1151.1 15.4 copy-start.4
  1181.8 9.4 copy-start.14
  1181.8 9.4 copy-start.18
  1181.8 9.4 copy-start.20
  1181.8 9.4 copy-start.22
  1181.8 10.0 copy-start.41
  1188.2 32.2 copy-start.33
  1191.8 28.6 copy-start.38
  1220.4 69.9 %copy-start.34 = (f32[4,256]{1,0:T(4,128)S(1)}, f32[4,256]{1,0:T(4,128)}, u32[]{:S(2)}) copy-start(f32[4,256]{1,0:T(4,128)} %copy-done.33) | copy-start | bytes 12292
  1220.4 69.9 %copy-start.39 = (f32[4,256]{1,0:T(4,128)S(1)}, f32[4,256]{1,0:T(4,128)}, u32[]{:S(2)}) copy-start(f32[4,256]{1,0:T(4,128)} %copy-done.38) | copy-start | bytes 12292
  1220.4 69.9 %copy-start.42 = (f32[1280]{0:T(1024)S(1)}, f32[1280]{0:T(1024)}, u32[]{:S(2)}) copy-start(f32[1280]{0:T(1024)} %param.21) | copy-start | bytes 15364
  1290.4 22.9 copy-start.28
  1325.6 13.6 copy-start.6
  1325.6 13.6 copy-start.15
  1325.6 13.6 copy-start.19
  1325.6 13.6 copy-start.21
  1350.0 13.1 copy-start.2
  1531.7 13.1 copy-start.2
  1694.2 6.3 copy-start.3
  1713.5 13.1 copy-start.2
  1895.2 13.1 copy-start.2
  2076.9 13.1 copy-start.2
  2298.4 745.1 %reduce-scatter.10.cloned.1.call-start = ((), (), s32[]{:S(2)}) async-start(), calls=%async_computation.8 | async-start | bytes 3686400 | tf_op jit(solution)/shard_map/reduce_scatter | solution.py:194
  2306.8 953.8 %reduce-scatter.14.cloned.1.call-start = ((), (), s32[]{:S(2)}) async-start(), calls=%async_computation.10 | async-start | bytes 14745600 | tf_op jit(solution)/shard_map/reduce_scatter | solution.py:203
  2306.8 18.7 copy-start.12
  2342.0 1135.6 %reduce-scatter.12.cloned.1.call-start = ((), (), s32[]{:S(2)}) async-start(), calls=%async_computation.9 | async-start | bytes 14745600 | tf_op jit(solution)/shard_map/reduce_scatter | solution.py:200
  2364.4 599.2 %copy-start.5 = (bf16[4,256,1280]{2,1,0:T(8,128)(2,1)S(1)}, bf16[4,256,1280]{2,1,0:T(8,128)(2,1)}, u32[]{:S(2)}) copy-start(bf16[4,256,1280]{2,1,0:T(8,128)(2,1)} %param.14) | copy-start | bytes 7864324
  2364.4 599.2 %copy-start.24 = (f32[4,256]{1,0:T(4,128)S(1)}, f32[4,256]{1,0:T(4,128)}, u32[]{:S(2)}) copy-start(f32[4,256]{1,0:T(4,128)} %copy-done.23) | copy-start | bytes 12292
  2364.4 599.2 %copy-start.30 = (f32[4,256]{1,0:T(4,128)S(1)}, f32[4,256]{1,0:T(4,128)}, u32[]{:S(2)}) copy-start(f32[4,256]{1,0:T(4,128)} %copy-done.29) | copy-start | bytes 12292
  2364.4 599.2 %copy-start.37 = (f32[1280]{0:T(1024)S(1)}, f32[1280]{0:T(1024)}, u32[]{:S(2)}) copy-start(f32[1280]{0:T(1024)} %param.18) | copy-start | bytes 15364
  2364.4 1284.8 %reduce-scatter.8.cloned.1.call-start = ((), (), s32[]{:S(2)}) async-start(), calls=%async_computation.7 | async-start | bytes 11059200 | tf_op jit(solution)/shard_map/reduce_scatter | solution.py:191
  2980.5 768.4 %all-reduce.7.cloned.1.call-start = ((), (), s32[]{:S(2)}) async-start(), calls=%async_computation.11 | async-start | bytes 9830400 | tf_op jit(solution)/shard_map/psum | solution.py:209
  3003.8 645.5 %copy-start.26 = (f32[4,256]{1,0:T(4,128)S(1)}, f32[4,256]{1,0:T(4,128)}, u32[]{:S(2)}) copy-start(f32[4,256]{1,0:T(4,128)} %copy-done.25) | copy-start | bytes 12292
  3021.2 632.1 %copy-start.44 = (bf16[1280]{0:T(1024)(128)(2,1)S(1)}, bf16[1280]{0:T(1024)(128)(2,1)}, u32[]{:S(2)}) copy-start(bf16[1280]{0:T(1024)(128)(2,1)} %get-tuple-element.460) | copy-start | bytes 7684
  3021.2 659.7 %copy-start.32 = (f32[4,256]{1,0:T(4,128)S(1)}, f32[4,256]{1,0:T(4,128)}, u32[]{:S(2)}) copy-start(f32[4,256]{1,0:T(4,128)} %copy-done.31) | copy-start | bytes 12292
  3680.8 78.5 %copy-start.1 = (bf16[1280,1280]{1,0:T(8,128)(2,1)S(1)}, bf16[1280,1280]{1,0:T(8,128)(2,1)}, u32[]{:S(2)}) copy-start(bf16[1280,1280]{1,0:T(8,128)(2,1)} %param.20) | copy-start | bytes 9830404
  3748.9 8.4 copy-start.17
  (18 other events, 60.8 us)
Sparse Core Ops, SparseCore 0:
  33.6 797.7 all-gather.1
  2298.5 665.0 reduce-scatter.5
  2968.2 75.2 reduce-scatter.9
  3047.0 213.4 reduce-scatter.13
  3264.0 213.5 reduce-scatter.11
  3481.2 168.0 reduce-scatter.7
  3651.9 96.9 all-reduce.6
where the time goes:
time: 3780 us; the launch traced here: 3770 us
  waiting for transfers between devices  2080 us (55%)
  matrix products  1210 us (32%)
  local copies, waits for them, and re-layouts  276 us (7%)
  other arithmetic  160 us (4%)
    all_gather x1, waiting for transfers between devices, per_device(): gathered = lax.all_gather(key_values, 'seq', axis=1, tiled=True)  788 us
    reduce_scatter x1, waiting for transfers between devices, per_device(): lax.psum_scatter(pair_grads.astype(jnp.bfloat16), 'seq', scatter_dimensio...  599 us
    dot_general x5, matrix products, backward_set(): jnp.einsum('rhij,rihe->rjhe', score_grad, query_part, preferred_element_t...  307 us
    dot_general x5, matrix products, backward_set(): jnp.einsum('rhij,rjhe->rihe', score_grad, key_part, preferred_element_typ...  289 us
    reduce_scatter x1, waiting for transfers between devices, per_device(): lax.psum_scatter(up_grad.astype(jnp.bfloat16), 'seq', scatter_dimension=0...  217 us
    reduce_scatter x1, waiting for transfers between devices, per_device(): lax.psum_scatter(down_grad.astype(jnp.bfloat16), 'seq', scatter_dimension...  217 us
    reduce_scatter x1, waiting for transfers between devices, per_device(): lax.psum_scatter(qkv_grad.astype(jnp.bfloat16), 'seq', scatter_dimension=...  172 us
    dot_general x10, matrix products, scores_of(): jnp.einsum('rihe,rjhe->rhij', query_part, key_part, preferred_element_typ...  147 us
  transfers between devices with their start and end apart: 7, of which 7 were waited for; matrix products, arithmetic and copies ran while one was open for 4% of the time, Pallas kernels for 0%

commit v1 on v0

v1 whole, which is shorter than its diff:
```python
import functools

import jax
import jax.numpy as jnp
from jax import lax
from jax.experimental import pallas as pl
from jax.experimental.pallas import tpu as pltpu
from jax.sharding import PartitionSpec as P

HDIM = 64
CORES = 2
epsilon = 1e-05
masked_score = -1e30
score_scale = HDIM ** (-0.5)
log2e = 1.4426950408889634
bf16 = jnp.bfloat16
f32 = jnp.float32
AXES = ("seq", "rows")
vmem_bytes = 56 * 2**20


def dot(a, b, ca, cb):
    return lax.dot_general(a, b, (((ca,), (cb,)), ((), ())), preferred_element_type=f32)


def attend_kernel(tile, key_tags, query_tags, q_ref, k_ref, v_ref, o_ref, lse_ref, v_turned):
    tokens = q_ref.shape[0]
    v_turned[...] = v_ref[...].T
    lane = lax.broadcasted_iota(jnp.int32, (tile, 2 * HDIM), 1)

    def body(step, _):
        part = pl.ds(pl.multiple_of(step * tile, tile), tile)
        q = q_ref[part, :]
        allowed = key_tags[...] == query_tags[:, part]
        pieces = []
        for head in range(2):
            own = jnp.where((lane // HDIM) == head, q, bf16(0))
            scores = dot(k_ref[...], own, 1, 1)
            scores = jnp.where(allowed, scores, masked_score)
            peak = jnp.max(scores, axis=0, keepdims=True)
            powers = jnp.exp2((scores - peak) * (score_scale * log2e))
            total = jnp.sum(powers, axis=0, keepdims=True)
            mixed = dot(v_turned[head * HDIM : (head + 1) * HDIM, :], powers.astype(bf16), 1, 0)
            pieces.append(mixed * (1.0 / total))
            lse_ref[head : head + 1, part] = peak * (score_scale * log2e) + jnp.log2(total)
        o_ref[part, :] = jnp.concatenate(pieces, axis=0).T.astype(bf16)
        return 0

    lax.fori_loop(0, tokens // tile, body, 0)


def attend(qkv, key_tags, query_tags):
    tokens, width = qkv.shape
    pairs = width // (6 * HDIM)
    tile = min(512, tokens)
    lanes = 2 * HDIM
    return pl.pallas_call(
        functools.partial(attend_kernel, tile),
        grid=(pairs,),
        in_specs=[
            pl.BlockSpec((tokens, 1), lambda i: (0, 0)),
            pl.BlockSpec((1, tokens), lambda i: (0, 0)),
            pl.BlockSpec((tokens, lanes), lambda i: (0, i)),
            pl.BlockSpec((tokens, lanes), lambda i: (0, pairs + i)),
            pl.BlockSpec((tokens, lanes), lambda i: (0, 2 * pairs + i)),
        ],
        out_specs=[
            pl.BlockSpec((tokens, lanes), lambda i: (0, i)),
            pl.BlockSpec((None, 2, tokens), lambda i: (i, 0, 0)),
        ],
        out_shape=[
            jax.ShapeDtypeStruct((tokens, pairs * lanes), bf16),
            jax.ShapeDtypeStruct((pairs, 2, tokens), f32),
        ],
        scratch_shapes=[pltpu.VMEM((lanes, tokens), bf16)],
        compiler_params=pltpu.CompilerParams(vmem_limit_bytes=vmem_bytes),
        cost_estimate=pl.CostEstimate(
            flops=16 * pairs * tokens * tokens * HDIM,
            bytes_accessed=8 * tokens * pairs * lanes,
            transcendentals=2 * pairs * tokens * tokens,
        ),
        name="attend",
    )(key_tags, query_tags, qkv, qkv, qkv)


def attend_back_kernel(
    tile, key_tags, query_tags, q_ref, k_ref, v_ref, do_ref, lse_ref, delta_ref, dq_ref, dk_ref, dv_ref, k_turned, dq_turned
):
    tokens = q_ref.shape[0]
    k_turned[...] = k_ref[...].T
    dq_turned[...] = jnp.zeros_like(dq_turned)
    first = lax.broadcasted_iota(jnp.int32, (tile, 2 * HDIM), 1) < HDIM

    def body(step, _):
        part = pl.ds(pl.multiple_of(step * tile, tile), tile)
        k, v = k_ref[part, :], v_ref[part, :]
        q, do = q_ref[...], do_ref[...]
        allowed = key_tags[part, :] == query_tags[...]
        dk, dv = [], []
        for head in range(2):
            own = first if head == 0 else jnp.logical_not(first)
            own_rows = slice(head * HDIM, (head + 1) * HDIM)
            scores = dot(jnp.where(own, k, bf16(0)), q, 1, 1)
            scores = jnp.where(allowed, scores, masked_score)
            chances = jnp.exp2(scores * (score_scale * log2e) - lse_ref[head : head + 1, :])
            weight_grad = dot(jnp.where(own, v, bf16(0)), do, 1, 1)
            score_grad = (chances * (weight_grad - delta_ref[head : head + 1, :])).astype(bf16)
            dv.append(dot(chances.astype(bf16), do, 1, 0))
            dk.append(dot(score_grad, q, 1, 0))
            dq_turned[own_rows, :] += dot(k_turned[own_rows, part], score_grad, 1, 0)
        dk_ref[part, :] = (jnp.where(first, dk[0], dk[1]) * score_scale).astype(bf16)
        dv_ref[part, :] = jnp.where(first, dv[0], dv[1]).astype(bf16)
        return 0

    lax.fori_loop(0, tokens // tile, body, 0)
    dq_ref[...] = (dq_turned[...] * score_scale).T.astype(bf16)


def attend_back(qkv, do, lse, delta, key_tags, query_tags, start, count):
    tokens, width = qkv.shape
    pairs = width // (6 * HDIM)
    tile = min(512, tokens)
    lanes = 2 * HDIM

    def columns(place):
        return pl.BlockSpec((tokens, lanes), lambda i: (0, place * pairs + start + i))

    stat = pl.BlockSpec((None, 2, tokens), lambda i: (start + i, 0, 0))
    return pl.pallas_call(
        functools.partial(attend_back_kernel, tile),
        grid=(count,),
        in_specs=[
            pl.BlockSpec((tokens, 1), lambda i: (0, 0)),
            pl.BlockSpec((1, tokens), lambda i: (0, 0)),
            columns(0),
            columns(1),
            columns(2),
            columns(0),
            stat,
            stat,
        ],
        out_specs=[pl.BlockSpec((tokens, lanes), lambda i: (0, i))] * 3,
        out_shape=[jax.ShapeDtypeStruct((tokens, count * lanes), bf16)] * 3,
        scratch_shapes=[pltpu.VMEM((lanes, tokens), bf16), pltpu.VMEM((lanes, tokens), f32)],
        compiler_params=pltpu.CompilerParams(vmem_limit_bytes=vmem_bytes),
        cost_estimate=pl.CostEstimate(
            flops=40 * count * tokens * tokens * HDIM,
            bytes_accessed=14 * tokens * count * lanes,
            transcendentals=2 * count * tokens * tokens,
        ),
        name="attend_back",
    )(key_tags, query_tags, qkv, qkv, qkv, do, lse, delta)


def hidden_kernel(n_ref, cot_ref, up_ref, down_ref, act_ref, d_up_ref):
    up = dot(n_ref[...], up_ref[...], 1, 0)
    d_act = dot(cot_ref[...], down_ref[...], 1, 1)
    half = 0.5 + 0.5 * lax.erf(up * (0.5**0.5))
    density = jnp.exp(-0.5 * up * up) * 0.3989422804014327
    act_ref[...] = (up * half).astype(bf16)
    d_up_ref[...] = (d_act * (half + up * density)).astype(bf16)


def hidden(n2, cotangent, up_weight, down_weight):
    tokens, width = n2.shape
    wide = up_weight.shape[1]
    tile = 256
    return pl.pallas_call(
        hidden_kernel,
        grid=(wide // tile,),
        in_specs=[
            pl.BlockSpec((tokens, width), lambda i: (0, 0)),
            pl.BlockSpec((tokens, width), lambda i: (0, 0)),
            pl.BlockSpec((width, tile), lambda i: (0, i)),
            pl.BlockSpec((tile, width), lambda i: (i, 0)),
        ],
        out_specs=[pl.BlockSpec((tokens, tile), lambda i: (0, i))] * 2,
        out_shape=[jax.ShapeDtypeStruct((tokens, wide), bf16)] * 2,
        compiler_params=pltpu.CompilerParams(vmem_limit_bytes=vmem_bytes),
        cost_estimate=pl.CostEstimate(
            flops=4 * tokens * width * wide,
            bytes_accessed=4 * tokens * (width + wide) + 4 * width * wide,
            transcendentals=2 * tokens * wide,
        ),
        name="hidden",
    )(n2, cotangent, up_weight, down_weight)


def norm_parts(values):
    center = values - jnp.mean(values, axis=-1, keepdims=True)
    spread = jnp.mean(center * center, axis=-1, keepdims=True)
    scale = lax.rsqrt(spread + epsilon)
    return center * scale, scale


def norm_back(grad, gain, unit, scale):
    e = grad * gain
    return scale * (
        e - jnp.mean(e, axis=-1, keepdims=True) - unit * jnp.mean(e * unit, axis=-1, keepdims=True)
    )


def build(n_seq, n_rows):
    devices = n_seq * n_rows
    highs = n_rows // CORES
    seq_bits = n_seq.bit_length() - 1
    high_bits = highs.bit_length() - 1

    def permute(value, target):
        pairs = []
        for s in range(n_seq):
            for r in range(n_rows):
                to_s, to_r = target(s, r)
                pairs.append((s * n_rows + r, to_s * n_rows + to_r))
        return lax.ppermute(value, AXES, pairs)

    def other_core(value):
        return permute(value, lambda s, r: (s, r ^ 1))

    def per_device(
        inputs, cell_ids, valid_counts, cotangent, attention_gain, qkv_weight, out_weight, feed_gain, up_weight, down_weight
    ):
        row_count, block, width = inputs.shape
        seq_len = cell_ids.shape[1]
        heads = width // HDIM
        seq_at, rows_at = lax.axis_index("seq"), lax.axis_index("rows")
        core = rows_at % CORES
        chips = n_seq // (CORES * row_count)
        group = chips * CORES
        sub = block // group
        tokens = n_seq * sub
        member = (seq_at % chips) * CORES + core
        group_heads = heads // group
        padded_heads = group_heads + group_heads % 2
        group_width = group_heads * HDIM
        padded = padded_heads * HDIM - group_width

        def to_member(value, hop):
            def target(s, r):
                place = ((s % chips) * CORES + r % CORES + hop) % group
                return (s // chips * chips + place // CORES, r // CORES * CORES + place % CORES)

            return permute(value, target)

        def pick(value, place, axis):
            return lax.dynamic_index_in_dim(value, place, axis, keepdims=False)

        def ordered(own, received, axis):
            return jnp.where(
                core == 0,
                jnp.concatenate([own, received], axis),
                jnp.concatenate([received, own], axis),
            )

        def to_rows(value):
            halves = value.reshape(row_count, CORES, block // CORES, width)
            received = other_core(pick(halves, 1 - core, 1))
            both = ordered(pick(halves, core, 1), received, 0)
            both = both.reshape(n_seq, sub, width) if chips == 1 else both.reshape(
                CORES * row_count, chips, sub, width
            ).reshape(n_seq, sub, width)
            return lax.all_to_all(both, "seq", 0, 0, tiled=True).reshape(tokens, width)

        def from_rows(value):
            both = lax.all_to_all(value.reshape(n_seq, sub, width), "seq", 0, 0, tiled=True)
            both = both.reshape(CORES, row_count, block // CORES, width)
            received = other_core(pick(both, 1 - core, 0))
            own = pick(both, core, 0)
            return ordered(own[:, None], received[:, None], 1).reshape(row_count, block, width)

        places = jnp.arange(seq_len, dtype=jnp.int32)
        tags = jnp.where(places[None, :] < valid_counts[:, None], cell_ids, -1 - places[None, :])
        tags = ordered(tags, other_core(tags), 0)
        tags = pick(tags, seq_at // chips, 0).reshape(n_seq, CORES, chips, sub)
        tags = tags.transpose(2, 1, 0, 3).reshape(group, tokens)
        order = (member - jnp.arange(group, dtype=jnp.int32)) % group
        tags = jnp.take(tags, order, axis=0).reshape(1, seq_len)
        query_tags, key_tags = tags, tags.reshape(seq_len, 1)

        def pad_heads(value, axis):
            if not padded:
                return value
            fill = [(0, 0)] * value.ndim
            fill[axis] = (0, padded)
            return jnp.pad(value, fill)

        qkv_split = qkv_weight.reshape(width, 3, group, group_width)
        out_split = out_weight.reshape(group, group_width, width)

        def qkv_of(hop):
            piece = pick(qkv_split, (member + hop) % group, 2)
            return pad_heads(piece, 2).reshape(width, -1)

        def out_of(hop):
            return pad_heads(pick(out_split, (member + hop) % group, 0), 0)

        qkv_parts = [qkv_of(hop) for hop in range(group)]
        out_parts = [out_of(hop) for hop in range(group)]

        start = to_rows(inputs).astype(f32)
        cot = to_rows(cotangent)
        unit1, scale1 = norm_parts(start)
        n1 = (unit1 * attention_gain).astype(bf16)
        n1_all = jnp.concatenate([n1] + [to_member(n1, hop) for hop in range(1, group)], 0)
        qkv = dot(n1_all, qkv_parts[0], 1, 0).astype(bf16)
        mixed, lse = attend(qkv, key_tags, query_tags)
        mixed_parts = [mixed[:tokens]] + [
            to_member(mixed[hop * tokens : (hop + 1) * tokens], group - hop) for hop in range(1, group)
        ]
        middle = start
        for part, weight in zip(mixed_parts, out_parts):
            middle = middle + dot(part, weight, 1, 0)
        unit2, scale2 = norm_parts(middle)
        n2 = (unit2 * feed_gain).astype(bf16)
        act, d_up = hidden(n2, cot, up_weight, down_weight)
        outputs = from_rows((middle + dot(act, down_weight, 1, 0)).astype(bf16))

        def halve(value, lead):
            value = value.reshape((2,) * (seq_bits + high_bits) + value.shape[lead:])
            steps = [("rows", b + 1, seq_bits + high_bits - 1 - b) for b in reversed(range(high_bits))]
            steps += [("seq", b, seq_bits - 1 - b) for b in range(seq_bits)]
            gone = []
            for axis_name, bit, axis in steps:
                at = rows_at if axis_name == "rows" else seq_at
                mine = (at >> bit) & 1
                place = axis - sum(1 for g in gone if g < axis)
                gone.append(axis)
                sent = pick(value, 1 - mine, place)
                if axis_name == "rows":
                    received = permute(sent, lambda s, r: (s, r ^ (1 << bit)))
                else:
                    received = permute(sent, lambda s, r: (s ^ (1 << bit), r))
                value = (pick(value, mine, place).astype(f32) + received.astype(f32)).astype(bf16)
            return value

        def gather_rows(value):
            for b in range(high_bits):
                bit = 1 << (b + 1)
                received = permute(value, lambda s, r: (s, r ^ bit))
                mine = (rows_at >> (b + 1)) & 1
                value = jnp.where(
                    mine == 0,
                    jnp.concatenate([value, received], 0),
                    jnp.concatenate([received, value], 0),
                )
            return value

        def reduce_halves(value, rows):
            parts = n_seq * highs
            value = halve(value.reshape(parts, rows // parts, -1), 1)
            return gather_rows(value)

        def weight_total(left, right):
            rows, columns = left.shape[1], right.shape[1]
            right = right.reshape(right.shape[0], CORES, columns // CORES)
            sent = dot(left, pick(right, 1 - core, 1), 0, 0).astype(bf16)
            kept = dot(left, pick(right, core, 1), 0, 0)
            kept = (kept + other_core(sent).astype(f32)).astype(bf16)
            part = reduce_halves(kept, rows)
            return ordered(part, other_core(part), 1).astype(f32)

        down_total = weight_total(act, cot)
        up_total = weight_total(n2, d_up)

        d_n2 = dot(d_up, up_weight, 1, 1)
        d_middle = cot.astype(f32) + norm_back(d_n2, feed_gain, unit2, scale2)
        d_attn = d_middle.astype(bf16)
        d_attn_all = jnp.concatenate([d_attn] + [to_member(d_attn, hop) for hop in range(1, group)], 0)
        d_mixed = dot(d_attn_all, out_parts[0], 1, 1).astype(bf16)
        if group == 2:
            mixed_own = ordered(mixed_parts[0], mixed_parts[1], 1)
        else:
            slots = jnp.stack([part[:, :group_width] for part in mixed_parts])
            back = (jnp.arange(group, dtype=jnp.int32) - member) % group
            mixed_own = jnp.take(slots, back, axis=0).transpose(1, 0, 2).reshape(tokens, width)
        out_total = weight_total(mixed_own, d_attn)
        delta = jnp.sum(
            (d_mixed.astype(f32) * mixed.astype(f32)).reshape(seq_len, padded_heads, HDIM), axis=-1
        )
        delta = delta.T.reshape(padded_heads // 2, 2, seq_len)
        d_qkv = attend_back(qkv, d_mixed, lse, delta, key_tags, query_tags, 0, padded_heads // 2)
        d_qkv = jnp.concatenate(d_qkv, axis=1)
        if group == 2:
            part = reduce_halves(dot(n1_all, d_qkv, 0, 0).astype(bf16), width)
            part = part.reshape(-1, 3, group_width)
            qkv_total = ordered(part[:, :, None], other_core(part)[:, :, None], 2)
            qkv_total = qkv_total.reshape(-1, 3 * width).astype(f32)
        else:
            grad = dot(n1_all, d_qkv, 0, 0).reshape(width, 3, 1, -1)[..., :group_width]
            grad = lax.dynamic_update_slice_in_dim(
                jnp.zeros((width, 3, group, group_width), f32), grad, member, 2
            )
            grad = grad.reshape(width, 3, CORES, width // CORES)
            kept = pick(grad, core, 2) + other_core(pick(grad, 1 - core, 2).astype(bf16)).astype(f32)
            part = reduce_halves(kept.reshape(width, -1).astype(bf16), width)
            part = part.reshape(-1, 3, width // CORES)
            qkv_total = ordered(part[:, :, None], other_core(part)[:, :, None], 2)
            qkv_total = qkv_total.reshape(-1, 3 * width).astype(f32)

        d_parts = [d_qkv[:tokens]] + [
            to_member(d_qkv[hop * tokens : (hop + 1) * tokens], group - hop) for hop in range(1, group)
        ]
        d_n1 = jnp.zeros((tokens, width), f32)
        for part, weight in zip(d_parts, qkv_parts):
            d_n1 = d_n1 + dot(part, weight, 1, 1)
        input_grad = d_middle + norm_back(d_n1, attention_gain, unit1, scale1)
        input_grad = from_rows(input_grad.astype(bf16))

        shard = width // n_seq

        def gain_total(weight, total, gain):
            rows = lax.dynamic_slice_in_dim(weight, seq_at * shard, shard, 0).astype(f32)
            return jnp.sum(rows * total, axis=1) / lax.dynamic_slice_in_dim(gain, seq_at * shard, shard, 0)

        return (
            outputs,
            input_grad,
            gain_total(qkv_weight, qkv_total, attention_gain),
            qkv_total,
            out_total,
            gain_total(up_weight, up_total, feed_gain),
            up_total,
            down_total,
        )

    return per_device


def solution(mesh):
    placed = (
        P("rows", "seq", None),
        P("rows", None),
        P("rows"),
        P("rows", "seq", None),
        P(),
        P(),
        P(),
        P(),
        P(),
        P(),
    )
    return jax.shard_map(
        build(mesh.shape["seq"], mesh.shape["rows"]),
        mesh=mesh,
        in_specs=placed,
        out_specs=(
            P("rows", "seq", None),
            P("rows", "seq", None),
            P("seq"),
            P("seq", None),
            P("seq", None),
            P("seq"),
            P("seq", None),
            P("seq", None),
        ),
        check_vma=False,
    )
```

time: 3780 us -> 981 us (0.26)
  waiting for transfers between devices: 2080 us -> 202 us
  matrix products: 1210 us -> 168 us
  Pallas kernels: 0 us -> 238 us
  local copies, waits for them, and re-layouts: 276 us -> 182 us
  other arithmetic: 160 us -> 75.4 us
  blocking collectives: 26.2 us -> 66.7 us
  starting transfers between devices: 0.81 us -> 38.7 us
    reduce_scatter x5 -> x0, waiting for transfers between devices: 1230 us -> none  [the longest x1 599 us: per_device(): lax.psum_scatter(pair_grads.astype(jnp.bfloat16), 'seq', scatter_dimensio...]
    dot_general x47 -> x15, matrix products: 1210 us -> 168 us  [dot(): lax.dot_general(a, b, (((ca,), (cb,)), ((), ())), preferred_element_type=...]
    all_gather x1 -> x0, waiting for transfers between devices: 788 us -> none  [per_device(): gathered = lax.all_gather(key_values, 'seq', axis=1, tiled=True)]
    pallas_call x0 -> x3, Pallas kernels: none -> 238 us  [the longest x1 117 us: attend_back(): pl.pallas_call(functools.partial(attend_back_kernel, tile), grid=(count,)...]
    ppermute x0 -> x36, waiting for transfers between devices: none -> 202 us  [permute(): return lax.ppermute(value, AXES, pairs)]
    reduce_sum x10 -> x6, other arithmetic: 91.3 us -> 10.2 us  [the longest x2 5.48 us: gain_total(): jnp.sum(rows * total, axis=1)]
    all_to_all x0 -> x1, blocking collectives: none -> 66.7 us  [to_rows(): return lax.all_to_all(both, 'seq', 0, 0, tiled=True).reshape(tokens, width)]
    psum x1 -> x0, waiting for transfers between devices: 59.7 us -> none  [per_device(): lax.psum(shares[1].astype(jnp.bfloat16), 'rows').astype(jnp.float32)]
  transfers between devices with their start and end apart: 7 -> 39, of which waited for: 7 -> 11; matrix products, arithmetic and copies ran while one was open for 4% -> 37% of each run, Pallas kernels for 0% -> 20%
where the time goes in v1:
time: 981 us; the launch traced here: 973 us
  Pallas kernels  238 us (24%)
  waiting for transfers between devices  202 us (21%)
  local copies, waits for them, and re-layouts  182 us (19%)
  matrix products  168 us (17%)
  other arithmetic  75.4 us (8%)
  blocking collectives  66.7 us (7%)
  starting transfers between devices  38.7 us (4%)
    ppermute x36, waiting for transfers between devices, permute(): return lax.ppermute(value, AXES, pairs)  202 us
    dot_general x15, matrix products, dot(): lax.dot_general(a, b, (((ca,), (cb,)), ((), ())), preferred_element_type=...  168 us
    pallas_call x1, Pallas kernels, attend_back(): pl.pallas_call(functools.partial(attend_back_kernel, tile), grid=(count,)...  117 us
    pallas_call x1, Pallas kernels, attend(): pl.pallas_call(functools.partial(attend_kernel, tile), grid=(pairs,), in_...  80.8 us
    all_to_all x1, blocking collectives, to_rows(): return lax.all_to_all(both, 'seq', 0, 0, tiled=True).reshape(tokens, width)  66.7 us
    dynamic_slice x13, local copies, waits for them, and re-layouts, pick(): return lax.dynamic_index_in_dim(value, place, axis, keepdims=False)  53.8 us
    pallas_call x1, Pallas kernels, hidden(): pl.pallas_call(hidden_kernel, grid=(wide // tile,), in_specs=[pl.BlockSpe...  40 us
    unnamed x123, local copies, waits for them, and re-layouts  31.3 us
  transfers between devices with their start and end apart: 39, of which 11 were waited for; matrix products, arithmetic and copies ran while one was open for 37% of the time, Pallas kernels for 20%

profile of v1, /device:TPU:0, one launch (start us, length us, event | category | flops | bytes accessed | tf_op | source)
XLA Modules:
  0.0 972.9 jit_solution(17992715446298655746)
XLA Ops:
  0.7 3.5 constant_dynamic-slice_fusion.17
  12.9 66.7 %all_to_all.20 = bf16[8,128,1280]{1,2,0:T(8,128)(2,1)S(1)} all-to-all(bf16[8,128,1280]{1,2,0:T(8,128)(2,1)S(1)} %maximum_select_fusion), channel_id=1, replica_groups=mesh['seq'=8,'rows'=4] {'seq'}, dimensions={0} | all-to-all | bytes 5242880 | tf_op jit(solution)/shard_map/all_to_all | solution.py:262
  81.8 4.9 copy.109
  86.7 4.9 multiply_convert_fusion.1
  96.4 13.7 %copy.110 = bf16[1280,3840]{0,1:T(8,128)(2,1)} copy(bf16[1280,3840]{1,0:T(8,128)(2,1)} %param.15) | data formatting | bytes 19660800 | tf_op args[5]
  110.1 8.2 constant_dynamic-slice_fusion.12
  122.8 3.8 maximum_select_fusion.1
  126.6 4.6 all-to-all-start.1
  131.2 16.6 %convolution_convert_fusion.3.q_ref.k_ref.v_ref = bf16[2048,1920]{1,0:T(8,128)(2,1)} fusion(bf16[1280,1920]{0,1:T(8,128)(2,1)} %bitcast.238, bf16[1024,1280]{1,0:T(8,128)(2,1)} %collective-permute-done.2, bf16[1024,1280]{1,0:T(8,128)(2,1)} %multiply_convert_fusion.1), kind=kOutput, calls=%fused_computation.6 | convolution fusion | flops 10080747520 | bytes 18022400 | tf_op jit(solution)/shard_map/dot_general | solution.py:23
  147.7 80.8 %attend.1 = (bf16[2048,640]{1,0:T(8,128)(2,1)}, f32[5,2,2048]{2,1,0:T(2,128)}) custom-call(s32[2048,1]{1,0:T(8,128)} %bitcast.250, s32[1,2048]{1,0:T(1,128)} %bitcast.256, bf16[2048,1920]{1,0:T(8,128)(2,1)} %convolution_convert_fusion.3.q_ref.k_ref.v_ref, bf16[2048,1920]{1,0:T(8,128)(2,1)} %convolution_convert_fusion.3.q_ref.k_ref.v_ref, ...), custom_call_target="tpu_custom_call" | custom-call | flops 21474836480 | bytes 10485760 | tf_op jit(solution)/shard_map/attend/pallas_call | solution.py:57
  232.5 9.3 copy.134
  241.9 5.2 reshape_reshape.19
  247.1 4.4 copy.114
  251.5 3.7 fusion.26
  255.2 3.8 fusion.70
  262.2 40.0 %hidden.1 = (bf16[1024,5120]{1,0:T(8,128)(2,1)}, bf16[1024,5120]{1,0:T(8,128)(2,1)}) custom-call(bf16[1024,1280]{1,0:T(8,128)(2,1)} %multiply_convert_fusion.n_ref, bf16[1024,1280]{1,0:T(8,128)(2,1)} %bitcast.227, bf16[1280,5120]{1,0:T(8,128)(2,1)} %up_ref.1, bf16[5120,1280]{1,0:T(8,128)(2,1)} %down_ref.1), custom_call_target="tpu_custom_call" | custom-call | flops 26843545600 | bytes 52428800 | tf_op jit(solution)/shard_map/hidden/pallas_call | solution.py:168
  302.2 22.3 %fusion.66 = (f32[1024]{0:T(1024)S(1)}, f32[1024]{0:T(1024)S(1)}, f32[1024,1280]{1,0:T(8,128)}) fusion(f32[1024]{0:T(1024)S(1)} %add_rsqrt_fusion, f32[1024,1280]{1,0:T(8,128)} %copy-done.2, f32[1024]{0:T(1024)S(1)} %broadcast_multiply_fusion.4, f32[1280]{0:T(1024)S(1)} %copy-done.36, bf16[1024,5120]{1,0:T(8,128)(2,1)} %get-tuple-element.17, ...), kind=kOutput, calls=%fused_computation.197 | convolution fusion | flops 13429635072 | bytes 34100224 | tf_op jit(solution)/shard_map/dot_general | solution.py:23
  324.5 7.7 fusion.68
  332.2 6.2 reshape.364
  338.4 23.8 %reshape.365 = bf16[1024,2,2560]{2,1,0:T(2,128)(2,1)} reshape(bf16[1024,5120]{1,0:T(8,128)(2,1)} %get-tuple-element.17) | data formatting | bytes 20971520 | tf_op jit(solution)/shard_map/reshape | solution.py:355
  362.2 8.1 constant_dynamic-slice_fusion.9
  370.3 5.4 convolution_convert_fusion.4
  376.2 23.3 %constant_dynamic-slice_fusion.5 = (bf16[1024,1,2560]{2,1,0:T(2,128)(2,1)}, bf16[1024,1,2560]{2,1,0:T(2,128)(2,1)}) fusion(bf16[1024,2,2560]{2,1,0:T(2,128)(2,1)S(1)} %bitcast.222, s32[]{:T(128)S(6)} %select_n.319, s32[]{:T(128)S(6)} %select_n.320), kind=kLoop, calls=%fused_computation.144 | loop fusion | bytes 20971528 | tf_op jit(solution)/shard_map/jit(dynamic_index_in_dim)/dynamic_slice | solution.py:246
  399.5 13.3 %convolution_convert_fusion = bf16[1280,2560]{1,0:T(8,128)(2,1)} fusion(bf16[1024,1280]{1,0:T(8,128)(2,1)S(1)} %copy-done.23, bf16[1024,1,2560]{2,1,0:T(2,128)(2,1)} %get-tuple-element.31), kind=kOutput, calls=%fused_computation.3 | convolution fusion | flops 6714163200 | bytes 14417920 | tf_op jit(solution)/shard_map/dot_general | solution.py:23
  412.8 4.7 fusion.14
  419.3 10.5 %convolution_convert_fusion.1 = bf16[5120,640]{1,0:T(8,128)(2,1)} fusion(bf16[1024,5120]{1,0:T(8,128)(2,1)S(1)} %bitcast.259, bf16[1024,2,640]{0,2,1:T(8,128)(2,1)S(1)} %copy-done.18, s32[]{:T(128)S(6)} %select_n.320), kind=kOutput, calls=%fused_computation.4 | convolution fusion | flops 6714163200 | bytes 18350084 | tf_op jit(solution)/shard_map/dot_general | solution.py:23
  430.3 8.2 collective-permute-done.16
  442.0 10.1 %convert_multiply_fusion = (f32[2048,640]{1,0:T(8,128)}, bf16[2048,640]{1,0:T(8,128)(2,1)}) fusion(bf16[2048,640]{1,0:T(8,128)(2,1)S(1)} %copy-done.19, bf16[2,640,1280]{2,1,0:T(8,128)(2,1)S(1)} %bitcast.214, s32[]{:T(128)S(6)} %select_n.334, bf16[1024,1280]{1,0:T(8,128)(2,1)} %collective-permute-done.6, bf16[1024,1280]{1,0:T(8,128)(2,1)} %get-tuple-element.28), kind=kOutput, calls=%fused_computation.26 | convolution fusion | flops 3371171840 | bytes 17367044 | tf_op jit(solution)/shard_map/dot_general | solution.py:23
  452.1 6.0 copy.116
  461.8 116.7 %attend_back.1 = (bf16[2048,640]{1,0:T(8,128)(2,1)}, bf16[2048,640]{1,0:T(8,128)(2,1)}, bf16[2048,640]{1,0:T(8,128)(2,1)}) custom-call(s32[2048,1]{1,0:T(8,128)} %bitcast.251, s32[1,2048]{1,0:T(1,128)} %bitcast.257, bf16[2048,1920]{1,0:T(8,128)(2,1)} %convolution_convert_fusion.3.q_ref.k_ref.v_ref, ...), custom_call_target="tpu_custom_call" | custom-call | flops 53687091200 | bytes 18350080 | tf_op jit(solution)/shard_map/attend_back/pallas_call | solution.py:129
  586.8 13.4 %convolution_convert_fusion.2 = bf16[1280,1920]{1,0:T(8,128)(2,1)S(1)} fusion(bf16[2048,1920]{1,0:T(8,128)(2,1)S(1)} %constant_dynamic-update-slice_fusion, bf16[1024,1280]{1,0:T(8,128)(2,1)} %collective-permute-done.2, bf16[1024,1280]{1,0:T(8,128)(2,1)} %multiply_convert_fusion.1), kind=kOutput, calls=%fused_computation.5 | convolution fusion | flops 10079272960 | bytes 18022400 | tf_op jit(solution)/shard_map/dot_general | solution.py:23
  608.8 20.9 %add_convert_fusion.3 = bf16[1024,1280]{1,0:T(8,128)(2,1)} fusion(f32[1024,1280]{1,0:T(8,128)S(1)} %bitcast.220, bf16[1024,5120]{1,0:T(8,128)(2,1)} %get-tuple-element.16, bf16[5120,1280]{1,0:T(8,128)(2,1)} %down_ref.1), kind=kOutput, calls=%fused_computation.29 | convolution fusion | flops 13424394240 | bytes 31457280 | tf_op jit(solution)/shard_map/dot_general | solution.py:23
  629.7 4.8 all-to-all-start.2
  634.5 26.6 %collective-permute-done.20 = bf16[80,640]{1,0:T(8,128)(2,1)S(1)} collective-permute-done((bf16[80,640]{1,0:T(8,128)(2,1)S(1)}, bf16[80,640]{1,0:T(8,128)(2,1)S(1)}, u32[]{:S(2)}, u32[]{:S(2)}) %collective-permute-start.20) | collective-permute-done | bytes 102432 | tf_op jit(solution)/shard_map/ppermute | solution.py:215
  664.2 10.6 %fusion.10 = f32[1024,1280]{1,0:T(8,128)} fusion(bf16[1280,1920]{0,1:T(8,128)(2,1)} %bitcast.239, bf16[2048,1920]{1,0:T(8,128)(2,1)} %copy-done.12), kind=kOutput, calls=%fused_computation.38 | convolution fusion | flops 5033164800 | bytes 14090240 | tf_op jit(solution)/shard_map/dot_general | solution.py:23
  678.3 20.7 %collective-permute-done.10 = bf16[2,2,80,1920]{3,2,0,1:T(8,128)(2,1)S(1)} collective-permute-done((bf16[2,2,80,1920]{3,2,0,1:T(8,128)(2,1)S(1)}, bf16[2,2,80,1920]{3,2,0,1:T(8,128)(2,1)S(1)}, u32[]{:S(2)}, u32[]{:S(2)}) %collective-permute-start.10) | collective-permute-done | bytes 1228832 | tf_op jit(solution)/shard_map/ppermute | solution.py:215
  700.3 6.4 collective-permute-start.11
  706.7 10.0 %add_convert_fusion.1 = bf16[1280,2560]{1,0:T(8,128)(2,1)S(1)} fusion(bf16[1280,2560]{1,0:T(8,128)(2,1)} %collective-permute-done.22, bf16[1024,1280]{1,0:T(8,128)(2,1)} %multiply_convert_fusion.n_ref, bf16[1024,1,2560]{2,1,0:T(2,128)(2,1)S(1)} %bitcast.229), kind=kOutput, calls=%fused_computation.2 | convolution fusion | flops 6720716800 | bytes 20971520 | tf_op jit(solution)/shard_map/dot_general | solution.py:23
  719.9 12.7 %add_convert_fusion = bf16[5120,640]{1,0:T(8,128)(2,1)S(1)} fusion(bf16[5120,640]{1,0:T(8,128)(2,1)} %collective-permute-done.29, bf16[1024,5120]{1,0:T(8,128)(2,1)} %get-tuple-element.16, bf16[1024,2,640]{0,2,1:T(8,128)(2,1)} %reshape_reshape.19, s32[]{:T(128)S(6)} %select_n.319), kind=kOutput, calls=%fused_computation.1 | convolution fusion | flops 6720716800 | bytes 24903684 | tf_op jit(solution)/shard_map/dot_general | solution.py:23
  738.4 10.3 %fusion.65 = (f32[1024]{0:T(1024)S(1)}, f32[1024]{0:T(1024)S(1)}, f32[1024,1280]{1,0:T(8,128)S(1)}) fusion(f32[1024]{0:T(1024)S(1)} %copy-done.31, f32[1024]{0:T(1024)S(1)} %copy-done.29, f32[8,128,1280]{2,1,0:T(8,128)S(1)} %bitcast.218, f32[1280]{0:T(1024)S(1)} %copy-done.35, f32[1024,1280]{1,0:T(8,128)} %fusion.10, ...), kind=kOutput, calls=%fused_computation.196 | convolution fusion | flops 5042337792 | bytes 24597504 | tf_op jit(solution)/shard_map/dot_general | solution.py:23
  749.7 43.7 %collective-permute-done.23 = bf16[2,2,2,80,2560]{4,3,0,1,2:T(8,128)(2,1)} collective-permute-done((bf16[2,2,2,80,2560]{4,3,0,1,2:T(8,128)(2,1)}, bf16[2,2,2,80,2560]{4,3,0,1,2:T(8,128)(2,1)}, u32[]{:S(2)}, u32[]{:S(2)}) %collective-permute-start.23) | collective-permute-done | bytes 3276832 | tf_op jit(solution)/shard_map/ppermute | solution.py:215
  800.9 4.7 all-to-all-start.3
  810.0 53.6 %collective-permute-done.30 = bf16[2,2,2,320,640]{4,3,0,1,2:T(8,128)(2,1)} collective-permute-done((bf16[2,2,2,320,640]{4,3,0,1,2:T(8,128)(2,1)}, bf16[2,2,2,320,640]{4,3,0,1,2:T(8,128)(2,1)}, u32[]{:S(2)}, u32[]{:S(2)}) %collective-permute-start.30) | collective-permute-done | bytes 3276832 | tf_op jit(solution)/shard_map/ppermute | solution.py:215
  886.8 16.8 %collective-permute-done.31 = bf16[2,2,320,640]{3,2,0,1:T(8,128)(2,1)} collective-permute-done((bf16[2,2,320,640]{3,2,0,1:T(8,128)(2,1)}, bf16[2,2,320,640]{3,2,0,1:T(8,128)(2,1)}, u32[]{:S(2)}, u32[]{:S(2)}) %collective-permute-start.31) | collective-permute-done | bytes 1638432 | tf_op jit(solution)/shard_map/ppermute | solution.py:215
  911.9 19.5 %collective-permute-done.32 = bf16[2,320,640]{2,1,0:T(8,128)(2,1)} collective-permute-done((bf16[2,320,640]{2,1,0:T(8,128)(2,1)S(1)}, bf16[2,320,640]{2,1,0:T(8,128)(2,1)}, u32[]{:S(2)}, u32[]{:S(2)}) %collective-permute-start.32) | collective-permute-done | bytes 819232 | tf_op jit(solution)/shard_map/ppermute | solution.py:215
  944.3 5.4 collective-permute-done.33
  955.5 6.0 collective-permute-done.34
  965.2 3.9 multiply_reduce_fusion.4
  (282 shorter events, 140.5 us)
Async XLA Ops:
  0.6 250.8 %copy-start = (bf16[1280,1280]{1,0:T(8,128)(2,1)S(1)}, bf16[1280,1280]{1,0:T(8,128)(2,1)}, u32[]{:S(2)}) copy-start(bf16[1280,1280]{1,0:T(8,128)(2,1)} %param.16) | copy-start | bytes 9830404
  6.6 3.5 collective-permute-start
  91.6 39.6 %collective-permute-start.2 = (bf16[1024,1280]{1,0:T(8,128)(2,1)}, bf16[1024,1280]{1,0:T(8,128)(2,1)}, u32[]{:S(2)}, u32[]{:S(2)}) collective-permute-start(bf16[1024,1280]{1,0:T(8,128)(2,1)} %multiply_convert_fusion.1), channel_id=1, source_target_pairs={{0,1},{1,0},{2,3},{3,2},{4,5},{5,4},{6,7},{7,6},{8,9},{9,8},{10,11... | collective-permute-start | bytes 7864328 | tf_op jit(solution)/shard_map/ppermute | solution.py:215
  91.7 29.0 %collective-permute-start.1 = (s32[4,2048]{1,0:T(4,128)S(1)}, s32[4,2048]{1,0:T(4,128)S(1)}, u32[]{:S(2)}, u32[]{:S(2)}) collective-permute-start(s32[4,2048]{1,0:T(4,128)S(1)} %fusion.47), channel_id=1, source_target_pairs={{0,1},{1,0},{2,3},{3,2},{4,5},{5,4},{6,7},{7,6},{8,9},{9,8},{10,11... | collective-permute-start | bytes 98312 | tf_op jit(solution)/shard_map/ppermute | solution.py:215
  96.3 26.5 %collective-permute-start.4 = (bf16[4,128,1280]{1,2,0:T(8,128)(2,1)}, bf16[4,128,1280]{1,2,0:T(8,128)(2,1)}, u32[]{:S(2)}, u32[]{:S(2)}) collective-permute-start(bf16[4,128,1280]{1,2,0:T(8,128)(2,1)} %bitcast.247), channel_id=1, source_target_pairs={{0,1},{1,0},{2,3},{3,2},{4,5},{5,4},{6,7},{7,6},{8,9},{9,8},{10,11... | collective-permute-start | bytes 3932168 | tf_op jit(solution)/shard_map/ppermute | solution.py:215
  126.6 106.0 %all-to-all-start.1 = ((bf16[8,128,1280]{1,2,0:T(8,128)(2,1)}), bf16[8,128,1280]{1,2,0:T(8,128)(2,1)}, u32[]{:S(2)}, u32[]{:S(2)}) async-start(bf16[8,128,1280]{1,2,0:T(8,128)(2,1)} %maximum_select_fusion.1), calls=%async_computation.1 | async-start | bytes 5242880 | tf_op jit(solution)/shard_map/all_to_all | solution.py:262
  232.1 23.1 %collective-permute-start.3 = (bf16[1024,640]{1,0:T(8,128)(2,1)}, bf16[1024,640]{1,0:T(8,128)(2,1)}, u32[]{:S(2)}, u32[]{:S(2)}) collective-permute-start(bf16[1024,640]{1,0:T(8,128)(2,1)} %get-tuple-element.43), channel_id=1, source_target_pairs={{0,1},{1,0},{2,3},{3,2},{4,5},{5,4},{6,7},{7,6},{8,9},{9,8},{10,11... | collective-permute-start | bytes 3932168 | tf_op jit(solution)/shard_map/ppermute | solution.py:215
  332.1 109.9 %collective-permute-start.6 = (bf16[1024,1280]{1,0:T(8,128)(2,1)}, bf16[1024,1280]{1,0:T(8,128)(2,1)}, u32[]{:S(2)}, u32[]{:S(2)}) collective-permute-start(bf16[1024,1280]{1,0:T(8,128)(2,1)} %get-tuple-element.28), channel_id=1, source_target_pairs={{0,1},{1,0},{2,3},{3,2},{4,5},{5,4},{6,7},{7,6},{8,9},{9,8},{10,11... | collective-permute-start | bytes 7864328 | tf_op jit(solution)/shard_map/ppermute | solution.py:215
  375.7 37.1 %collective-permute-start.15 = (bf16[1280,640]{1,0:T(8,128)(2,1)}, bf16[1280,640]{1,0:T(8,128)(2,1)}, u32[]{:S(2)}, u32[]{:S(2)}) collective-permute-start(bf16[1280,640]{1,0:T(8,128)(2,1)} %convolution_convert_fusion.4), channel_id=1, source_target_pairs={{0,1},{1,0},{2,3},{3,2},{4,5},{5,4},{6,7},{7,6},{8,9},{9,8},{10,11... | collective-permute-start | bytes 4915208 | tf_op jit(solution)/shard_map/ppermute | solution.py:215
  412.8 293.9 %collective-permute-start.22 = (bf16[1280,2560]{1,0:T(8,128)(2,1)}, bf16[1280,2560]{1,0:T(8,128)(2,1)}, u32[]{:S(2)}, u32[]{:S(2)}) collective-permute-start(bf16[1280,2560]{1,0:T(8,128)(2,1)} %convolution_convert_fusion), channel_id=1, source_target_pairs={{0,1},{1,0},{2,3},{3,2},{4,5},{5,4},{6,7},{7,6},{8,9},{9,8},{10,11... | collective-permute-start | bytes 19660808 | tf_op jit(solution)/shard_map/ppermute | solution.py:215
  417.8 20.7 %collective-permute-start.16 = (bf16[2,2,2,80,640]{4,3,0,1,2:T(8,128)(2,1)S(1)}, bf16[2,2,2,80,640]{4,3,0,1,2:T(8,128)(2,1)S(1)}, u32[]{:S(2)}, u32[]{:S(2)}) collective-permute-start(bf16[2,2,2,80,640]{4,3,0,1,2:T(8,128)(2,1)S(1)} %bitcast.252), channel_id=1, source_target_pairs={{0,2},{1,3},{2,0},{3,1},{4,6},{5,7},{6,4},{7,5},{8,10},{9,11},{10,... | collective-permute-start | bytes 2457608 | tf_op jit(solution)/shard_map/ppermute | solution.py:215
  429.9 290.0 %collective-permute-start.29 = (bf16[5120,640]{1,0:T(8,128)(2,1)}, bf16[5120,640]{1,0:T(8,128)(2,1)}, u32[]{:S(2)}, u32[]{:S(2)}) collective-permute-start(bf16[5120,640]{1,0:T(8,128)(2,1)} %convolution_convert_fusion.1), channel_id=1, source_target_pairs={{0,1},{1,0},{2,3},{3,2},{4,5},{5,4},{6,7},{7,6},{8,9},{9,8},{10,11... | collective-permute-start | bytes 19660808 | tf_op jit(solution)/shard_map/ppermute | solution.py:215
  440.3 142.6 %collective-permute-start.17 = (bf16[2,2,80,640]{3,2,0,1:T(8,128)(2,1)}, bf16[2,2,80,640]{3,2,0,1:T(8,128)(2,1)}, u32[]{:S(2)}, u32[]{:S(2)}) collective-permute-start(bf16[2,2,80,640]{3,2,0,1:T(8,128)(2,1)} %dynamic-slice_bitcast_fusion.12), channel_id=1, source_target_pairs={{0,4},{1,5},{2,6},{3,7},{4,0},{5,1},{6,2},{7,3},{8,12},{9,13},{10,... | collective-permute-start | bytes 1228808 | tf_op jit(solution)/shard_map/ppermute | solution.py:215
  582.5 26.3 %slice-start.4 = ((s8[5242880]{0:T(1024)(128)(4,1)}), s8[4194304]{0:T(1024)(128)(4,1)S(1)}, s32[]{:S(2)}) async-start(s8[5242880]{0:T(1024)(128)(4,1)} %bitcast.219), calls=%async_computation.8 | async-start | bytes 8388608
  585.3 15.0 %collective-permute-start.18 = (bf16[2,80,640]{2,1,0:T(8,128)(2,1)S(1)}, bf16[2,80,640]{2,1,0:T(8,128)(2,1)S(1)}, u32[]{:S(2)}, u32[]{:S(2)}) collective-permute-start(bf16[2,80,640]{2,1,0:T(8,128)(2,1)S(1)} %dynamic-slice_bitcast_fusion.14), channel_id=1, source_target_pairs={{0,8},{1,9},{2,10},{3,11},{4,12},{5,13},{6,14},{7,15},{8,0},{9,1},... | collective-permute-start | bytes 614408 | tf_op jit(solution)/shard_map/ppermute | solution.py:215
  600.4 6.8 collective-permute-start.19
  604.8 56.4 %collective-permute-start.9 = (bf16[2,2,2,80,1920]{4,3,0,1,2:T(8,128)(2,1)}, bf16[2,2,2,80,1920]{4,3,0,1,2:T(8,128)(2,1)}, u32[]{:S(2)}, u32[]{:S(2)}) collective-permute-start(bf16[2,2,2,80,1920]{4,3,0,1,2:T(8,128)(2,1)} %bitcast.210), channel_id=1, source_target_pairs={{0,2},{1,3},{2,0},{3,1},{4,6},{5,7},{6,4},{7,5},{8,10},{9,11},{10,... | collective-permute-start | bytes 7372808 | tf_op jit(solution)/shard_map/ppermute | solution.py:215
  607.2 53.8 %collective-permute-start.20 = (bf16[80,640]{1,0:T(8,128)(2,1)S(1)}, bf16[80,640]{1,0:T(8,128)(2,1)S(1)}, u32[]{:S(2)}, u32[]{:S(2)}) collective-permute-start(bf16[80,640]{1,0:T(8,128)(2,1)S(1)} %fusion.46), channel_id=1, source_target_pairs={{0,2},{1,3},{2,0},{3,1},{4,6},{5,7},{6,4},{7,5},{8,10},{9,11},{10,... | collective-permute-start | bytes 307208 | tf_op jit(solution)/shard_map/ppermute | solution.py:215
  629.7 171.2 %all-to-all-start.2 = ((bf16[8,128,1280]{2,1,0:T(8,128)(2,1)}), bf16[8,128,1280]{2,1,0:T(8,128)(2,1)}, u32[]{:S(2)}, u32[]{:S(2)}) async-start(bf16[8,128,1280]{2,1,0:T(8,128)(2,1)} %bitcast.241), calls=%async_computation.2 | async-start | bytes 5242880 | tf_op jit(solution)/shard_map/all_to_all | solution.py:265
  661.1 16.2 %collective-permute-start.21 = (bf16[160,640]{1,0:T(8,128)(2,1)S(1)}, bf16[160,640]{1,0:T(8,128)(2,1)S(1)}, u32[]{:S(2)}, u32[]{:S(2)}) collective-permute-start(bf16[160,640]{1,0:T(8,128)(2,1)S(1)} %maximum_select_fusion.15), channel_id=1, source_target_pairs={{0,1},{1,0},{2,3},{3,2},{4,5},{5,4},{6,7},{7,6},{8,9},{9,8},{10,11... | collective-permute-start | bytes 614408 | tf_op jit(solution)/shard_map/ppermute | solution.py:215
  663.5 43.2 %slice-start.11 = ((s8[10485760]{0:T(1024)(128)(4,1)}), s8[4194304]{0:T(1024)(128)(4,1)S(1)}, s32[]{:S(2)}) async-start(s8[10485760]{0:T(1024)(128)(4,1)} %bitcast.228), calls=%async_computation.15 | async-start | bytes 8388608
  663.6 43.1 %slice-start.12 = ((s8[10485760]{0:T(1024)(128)(4,1)}), s8[4194304]{0:T(1024)(128)(4,1)S(1)}, s32[]{:S(2)}) async-start(s8[10485760]{0:T(1024)(128)(4,1)} %bitcast.228), calls=%async_computation.16 | async-start | bytes 8388608
  663.6 43.1 %slice-start.13 = ((s8[10485760]{0:T(1024)(128)(4,1)}), s8[2097152]{0:T(1024)(128)(4,1)S(1)}, s32[]{:S(2)}) async-start(s8[10485760]{0:T(1024)(128)(4,1)} %bitcast.228), calls=%async_computation.17 | async-start | bytes 4194304
  663.6 35.4 %collective-permute-start.10 = (bf16[2,2,80,1920]{3,2,0,1:T(8,128)(2,1)S(1)}, bf16[2,2,80,1920]{3,2,0,1:T(8,128)(2,1)S(1)}, u32[]{:S(2)}, u32[]{:S(2)}) collective-permute-start(bf16[2,2,80,1920]{3,2,0,1:T(8,128)(2,1)S(1)} %dynamic-slice_bitcast_fusion.6), channel_id=1, source_target_pairs={{0,4},{1,5},{2,6},{3,7},{4,0},{5,1},{6,2},{7,3},{8,12},{9,13},{10,... | collective-permute-start | bytes 3686408 | tf_op jit(solution)/shard_map/ppermute | solution.py:215
  677.2 61.1 %collective-permute-start.7 = (bf16[1024,1920]{1,0:T(8,128)(2,1)}, bf16[1024,1920]{1,0:T(8,128)(2,1)}, u32[]{:S(2)}, u32[]{:S(2)}) collective-permute-start(bf16[1024,1920]{1,0:T(8,128)(2,1)} %slice.19), channel_id=1, source_target_pairs={{0,1},{1,0},{2,3},{3,2},{4,5},{5,4},{6,7},{7,6},{8,9},{9,8},{10,11... | collective-permute-start | bytes 11796488 | tf_op jit(solution)/shard_map/ppermute | solution.py:215
  700.3 48.5 %collective-permute-start.11 = (bf16[2,80,1920]{2,1,0:T(8,128)(2,1)}, bf16[2,80,1920]{2,1,0:T(8,128)(2,1)S(1)}, u32[]{:S(2)}, u32[]{:S(2)}) collective-permute-start(bf16[2,80,1920]{2,1,0:T(8,128)(2,1)} %dynamic-slice_bitcast_fusion.9), channel_id=1, source_target_pairs={{0,8},{1,9},{2,10},{3,11},{4,12},{5,13},{6,14},{7,15},{8,0},{9,1},... | collective-permute-start | bytes 1843208 | tf_op jit(solution)/shard_map/ppermute | solution.py:215
  719.3 74.1 %collective-permute-start.23 = (bf16[2,2,2,80,2560]{4,3,0,1,2:T(8,128)(2,1)}, bf16[2,2,2,80,2560]{4,3,0,1,2:T(8,128)(2,1)}, u32[]{:S(2)}, u32[]{:S(2)}) collective-permute-start(bf16[2,2,2,80,2560]{4,3,0,1,2:T(8,128)(2,1)} %bitcast.209), channel_id=1, source_target_pairs={{0,2},{1,3},{2,0},{3,1},{4,6},{5,7},{6,4},{7,5},{8,10},{9,11},{10,... | collective-permute-start | bytes 9830408 | tf_op jit(solution)/shard_map/ppermute | solution.py:215
  736.9 126.8 %collective-permute-start.30 = (bf16[2,2,2,320,640]{4,3,0,1,2:T(8,128)(2,1)}, bf16[2,2,2,320,640]{4,3,0,1,2:T(8,128)(2,1)}, u32[]{:S(2)}, u32[]{:S(2)}) collective-permute-start(bf16[2,2,2,320,640]{4,3,0,1,2:T(8,128)(2,1)} %bitcast.208), channel_id=1, source_target_pairs={{0,2},{1,3},{2,0},{3,1},{4,6},{5,7},{6,4},{7,5},{8,10},{9,11},{10,... | collective-permute-start | bytes 9830408 | tf_op jit(solution)/shard_map/ppermute | solution.py:215
  748.9 44.5 %copy-start.24 = (bf16[2,80,1920]{2,1,0:T(8,128)(2,1)}, bf16[2,80,1920]{2,1,0:T(8,128)(2,1)S(1)}, u32[]{:S(2)}) copy-start(bf16[2,80,1920]{2,1,0:T(8,128)(2,1)S(1)} %fusion.39) | copy-start | bytes 1843204
  749.7 57.9 %collective-permute-start.12 = (bf16[80,1920]{1,0:T(8,128)(2,1)}, bf16[80,1920]{1,0:T(8,128)(2,1)}, u32[]{:S(2)}, u32[]{:S(2)}) collective-permute-start(bf16[80,1920]{1,0:T(8,128)(2,1)} %dynamic-slice_bitcast_fusion.13), channel_id=1, source_target_pairs={{0,16},{1,17},{2,18},{3,19},{4,20},{5,21},{6,22},{7,23},{8,24},{9,... | collective-permute-start | bytes 921608 | tf_op jit(solution)/shard_map/ppermute | solution.py:215
  797.7 70.2 %collective-permute-start.24 = (bf16[2,2,80,2560]{3,2,0,1:T(8,128)(2,1)}, bf16[2,2,80,2560]{3,2,0,1:T(8,128)(2,1)}, u32[]{:S(2)}, u32[]{:S(2)}) collective-permute-start(bf16[2,2,80,2560]{3,2,0,1:T(8,128)(2,1)} %dynamic-slice_bitcast_fusion.1), channel_id=1, source_target_pairs={{0,4},{1,5},{2,6},{3,7},{4,0},{5,1},{6,2},{7,3},{8,12},{9,13},{10,... | collective-permute-start | bytes 4915208 | tf_op jit(solution)/shard_map/ppermute | solution.py:215
  800.9 107.5 %all-to-all-start.3 = ((bf16[8,128,1280]{2,1,0:T(8,128)(2,1)}), bf16[8,128,1280]{2,1,0:T(8,128)(2,1)}, u32[]{:S(2)}, u32[]{:S(2)}) async-start(bf16[8,128,1280]{2,1,0:T(8,128)(2,1)} %bitcast.230), calls=%async_computation.3 | async-start | bytes 5242880 | tf_op jit(solution)/shard_map/all_to_all | solution.py:265
  805.5 58.1 %copy-start.6 = (bf16[2,2,2,1,320,640]{5,4,3,2,1,0:T(8,128)(2,1)S(1)}, bf16[2,2,2,1,320,640]{5,4,3,2,1,0:T(8,128)(2,1)}, u32[]{:S(2)}) copy-start(bf16[2,2,2,1,320,640]{5,4,3,2,1,0:T(8,128)(2,1)} %get-tuple-element.34) | copy-start | bytes 9830404
  807.6 63.8 %collective-permute-start.5 = (bf16[4,128,1280]{2,1,0:T(8,128)(2,1)S(1)}, bf16[4,128,1280]{2,1,0:T(8,128)(2,1)S(1)}, u32[]{:S(2)}, u32[]{:S(2)}) collective-permute-start(bf16[4,128,1280]{2,1,0:T(8,128)(2,1)S(1)} %get-tuple-element.47), channel_id=1, source_target_pairs={{0,1},{1,0},{2,3},{3,2},{4,5},{5,4},{6,7},{7,6},{8,9},{9,8},{10,11... | collective-permute-start | bytes 3932168 | tf_op jit(solution)/shard_map/ppermute | solution.py:215
  809.5 67.2 %collective-permute-start.13 = (bf16[80,1920]{1,0:T(8,128)(2,1)}, bf16[80,1920]{1,0:T(8,128)(2,1)}, u32[]{:S(2)}, u32[]{:S(2)}) collective-permute-start(bf16[80,1920]{1,0:T(8,128)(2,1)} %fusion.43), channel_id=1, source_target_pairs={{0,2},{1,3},{2,0},{3,1},{4,6},{5,7},{6,4},{7,5},{8,10},{9,11},{10,... | collective-permute-start | bytes 921608 | tf_op jit(solution)/shard_map/ppermute | solution.py:215
  867.9 35.7 %collective-permute-start.31 = (bf16[2,2,320,640]{3,2,0,1:T(8,128)(2,1)}, bf16[2,2,320,640]{3,2,0,1:T(8,128)(2,1)}, u32[]{:S(2)}, u32[]{:S(2)}) collective-permute-start(bf16[2,2,320,640]{3,2,0,1:T(8,128)(2,1)} %dynamic-slice_bitcast_fusion), channel_id=1, source_target_pairs={{0,4},{1,5},{2,6},{3,7},{4,0},{5,1},{6,2},{7,3},{8,12},{9,13},{10,... | collective-permute-start | bytes 4915208 | tf_op jit(solution)/shard_map/ppermute | solution.py:215
  871.4 34.8 %collective-permute-start.25 = (bf16[2,80,2560]{2,1,0:T(8,128)(2,1)}, bf16[2,80,2560]{2,1,0:T(8,128)(2,1)}, u32[]{:S(2)}, u32[]{:S(2)}) collective-permute-start(bf16[2,80,2560]{2,1,0:T(8,128)(2,1)} %dynamic-slice_bitcast_fusion.8), channel_id=1, source_target_pairs={{0,8},{1,9},{2,10},{3,11},{4,12},{5,13},{6,14},{7,15},{8,0},{9,1},... | collective-permute-start | bytes 2457608 | tf_op jit(solution)/shard_map/ppermute | solution.py:215
  876.7 26.9 %copy-start.5 = (bf16[2,2,2,320,640]{4,3,0,1,2:T(8,128)(2,1)S(1)}, bf16[2,2,2,320,640]{4,3,0,1,2:T(8,128)(2,1)}, u32[]{:S(2)}) copy-start(bf16[2,2,2,320,640]{4,3,0,1,2:T(8,128)(2,1)} %copy-done.4) | copy-start | bytes 9830404
  881.8 54.2 %collective-permute-start.14 = (bf16[160,3,640]{2,0,1:T(8,128)(2,1)}, bf16[160,3,640]{2,0,1:T(8,128)(2,1)}, u32[]{:S(2)}, u32[]{:S(2)}) collective-permute-start(bf16[160,3,640]{2,0,1:T(8,128)(2,1)} %copy.124), channel_id=1, source_target_pairs={{0,1},{1,0},{2,3},{3,2},{4,5},{5,4},{6,7},{7,6},{8,9},{9,8},{10,11... | collective-permute-start | bytes 1843208 | tf_op jit(solution)/shard_map/ppermute | solution.py:215
  905.5 25.9 %collective-permute-start.32 = (bf16[2,320,640]{2,1,0:T(8,128)(2,1)S(1)}, bf16[2,320,640]{2,1,0:T(8,128)(2,1)}, u32[]{:S(2)}, u32[]{:S(2)}) collective-permute-start(bf16[2,320,640]{2,1,0:T(8,128)(2,1)S(1)} %dynamic-slice_bitcast_fusion.7), channel_id=1, source_target_pairs={{0,8},{1,9},{2,10},{3,11},{4,12},{5,13},{6,14},{7,15},{8,0},{9,1},... | collective-permute-start | bytes 2457608 | tf_op jit(solution)/shard_map/ppermute | solution.py:215
  908.4 25.3 %collective-permute-start.26 = (bf16[80,2560]{1,0:T(8,128)(2,1)}, bf16[80,2560]{1,0:T(8,128)(2,1)}, u32[]{:S(2)}, u32[]{:S(2)}) collective-permute-start(bf16[80,2560]{1,0:T(8,128)(2,1)} %dynamic-slice_bitcast_fusion.11), channel_id=1, source_target_pairs={{0,16},{1,17},{2,18},{3,19},{4,20},{5,21},{6,22},{7,23},{8,24},{9,... | collective-permute-start | bytes 1228808 | tf_op jit(solution)/shard_map/ppermute | solution.py:215
  911.9 24.2 %copy-start.26 = (bf16[160,3,1,640]{3,0,2,1:T(8,128)(2,1)S(1)}, bf16[160,3,1,640]{3,0,2,1:T(8,128)(2,1)}, u32[]{:S(2)}) copy-start(bf16[160,3,1,640]{3,0,2,1:T(8,128)(2,1)} %maximum_select_fusion.11) | copy-start | bytes 1843204
  911.9 50.0 %collective-permute-start.8 = (bf16[4,128,1280]{2,1,0:T(8,128)(2,1)}, bf16[4,128,1280]{2,1,0:T(8,128)(2,1)}, u32[]{:S(2)}, u32[]{:S(2)}) collective-permute-start(bf16[4,128,1280]{2,1,0:T(8,128)(2,1)} %get-tuple-element.45), channel_id=1, source_target_pairs={{0,1},{1,0},{2,3},{3,2},{4,5},{5,4},{6,7},{7,6},{8,9},{9,8},{10,11... | collective-permute-start | bytes 3932168 | tf_op jit(solution)/shard_map/ppermute | solution.py:215
  933.6 16.1 %collective-permute-start.33 = (bf16[320,640]{1,0:T(8,128)(2,1)}, bf16[320,640]{1,0:T(8,128)(2,1)}, u32[]{:S(2)}, u32[]{:S(2)}) collective-permute-start(bf16[320,640]{1,0:T(8,128)(2,1)} %dynamic-slice_bitcast_fusion.10), channel_id=1, source_target_pairs={{0,16},{1,17},{2,18},{3,19},{4,20},{5,21},{6,22},{7,23},{8,24},{9,... | collective-permute-start | bytes 1228808 | tf_op jit(solution)/shard_map/ppermute | solution.py:215
  935.5 16.0 %collective-permute-start.27 = (bf16[80,2560]{1,0:T(8,128)(2,1)}, bf16[80,2560]{1,0:T(8,128)(2,1)}, u32[]{:S(2)}, u32[]{:S(2)}) collective-permute-start(bf16[80,2560]{1,0:T(8,128)(2,1)} %fusion.41), channel_id=1, source_target_pairs={{0,2},{1,3},{2,0},{3,1},{4,6},{5,7},{6,4},{7,5},{8,10},{9,11},{10,... | collective-permute-start | bytes 1228808 | tf_op jit(solution)/shard_map/ppermute | solution.py:215
  950.9 10.7 %collective-permute-start.34 = (bf16[320,640]{1,0:T(8,128)(2,1)S(1)}, bf16[320,640]{1,0:T(8,128)(2,1)S(1)}, u32[]{:S(2)}, u32[]{:S(2)}) collective-permute-start(bf16[320,640]{1,0:T(8,128)(2,1)S(1)} %fusion.40), channel_id=1, source_target_pairs={{0,2},{1,3},{2,0},{3,1},{4,6},{5,7},{6,4},{7,5},{8,10},{9,11},{10,... | collective-permute-start | bytes 1228808 | tf_op jit(solution)/shard_map/ppermute | solution.py:215
  953.2 12.1 %collective-permute-start.28 = (bf16[160,2560]{1,0:T(8,128)(2,1)S(1)}, bf16[160,2560]{1,0:T(8,128)(2,1)S(1)}, u32[]{:S(2)}, u32[]{:S(2)}) collective-permute-start(bf16[160,2560]{1,0:T(8,128)(2,1)S(1)} %maximum_select_fusion.9), channel_id=1, source_target_pairs={{0,1},{1,0},{2,3},{3,2},{4,5},{5,4},{6,7},{7,6},{8,9},{9,8},{10,11... | collective-permute-start | bytes 2457608 | tf_op jit(solution)/shard_map/ppermute | solution.py:215
  961.8 8.6 collective-permute-start.35
  (48 other events, 405.1 us)

commit v2 on v1

v2 whole, which is shorter than its diff:
```python
import functools

import jax
import jax.numpy as jnp
from jax import lax
from jax.experimental import pallas as pl
from jax.experimental.pallas import tpu as pltpu
from jax.sharding import PartitionSpec as P

HDIM = 64
CORES = 2
epsilon = 1e-05
masked_score = -1e30
score_scale = HDIM ** (-0.5)
log2e = 1.4426950408889634
bf16 = jnp.bfloat16
f32 = jnp.float32
AXES = ("seq", "rows")
vmem_bytes = 60 * 2**20
feed_vmem_bytes = 62 * 2**20
feed_tile = 512
MESH = pl.DeviceIdType.MESH


def dot(a, b, ca, cb):
    return lax.dot_general(a, b, (((ca,), (cb,)), ((), ())), preferred_element_type=f32)


def attend_kernel(tile, key_tags, query_tags, q_ref, k_ref, v_ref, o_ref, lse_ref, v_turned):
    tokens = q_ref.shape[0]
    v_turned[...] = v_ref[...].T
    lane = lax.broadcasted_iota(jnp.int32, (tile, 2 * HDIM), 1)

    def body(step, _):
        part = pl.ds(pl.multiple_of(step * tile, tile), tile)
        q = q_ref[part, :]
        allowed = key_tags[...] == query_tags[:, part]
        pieces = []
        for head in range(2):
            own = jnp.where((lane // HDIM) == head, q, bf16(0))
            scores = dot(k_ref[...], own, 1, 1)
            scores = jnp.where(allowed, scores, masked_score)
            peak = jnp.max(scores, axis=0, keepdims=True)
            powers = jnp.exp2((scores - peak) * (score_scale * log2e))
            total = jnp.sum(powers, axis=0, keepdims=True)
            mixed = dot(v_turned[head * HDIM : (head + 1) * HDIM, :], powers.astype(bf16), 1, 0)
            pieces.append(mixed * (1.0 / total))
            lse_ref[head : head + 1, part] = peak * (score_scale * log2e) + jnp.log2(total)
        o_ref[part, :] = jnp.concatenate(pieces, axis=0).T.astype(bf16)
        return 0

    lax.fori_loop(0, tokens // tile, body, 0)


def attend(qkv, key_tags, query_tags):
    tokens, width = qkv.shape
    lanes = 2 * HDIM
    pairs = width // (3 * lanes)
    tile = min(512, tokens)

    def columns(place):
        return pl.BlockSpec((tokens, lanes), lambda i: (0, 3 * i + place))

    return pl.pallas_call(
        functools.partial(attend_kernel, tile),
        grid=(pairs,),
        in_specs=[
            pl.BlockSpec((tokens, 1), lambda i: (0, 0)),
            pl.BlockSpec((1, tokens), lambda i: (0, 0)),
            columns(0),
            columns(1),
            columns(2),
        ],
        out_specs=[
            pl.BlockSpec((tokens, lanes), lambda i: (0, i)),
            pl.BlockSpec((None, 2, tokens), lambda i: (i, 0, 0)),
        ],
        out_shape=[
            jax.ShapeDtypeStruct((tokens, pairs * lanes), bf16),
            jax.ShapeDtypeStruct((pairs, 2, tokens), f32),
        ],
        scratch_shapes=[pltpu.VMEM((lanes, tokens), bf16)],
        compiler_params=pltpu.CompilerParams(vmem_limit_bytes=vmem_bytes),
        cost_estimate=pl.CostEstimate(
            flops=32 * pairs * tokens * tokens * HDIM,
            bytes_accessed=8 * tokens * pairs * lanes,
            transcendentals=2 * pairs * tokens * tokens,
        ),
        name="attend",
    )(key_tags, query_tags, qkv, qkv, qkv)


def attend_back_kernel(
    tile, key_tags, query_tags, q_ref, k_ref, v_ref, o_ref, do_ref, lse_ref, grad_ref, k_turned, dq_turned, delta
):
    tokens = q_ref.shape[0]
    lanes = 2 * HDIM
    k_turned[...] = k_ref[...].T
    dq_turned[...] = (o_ref[...].astype(f32) * do_ref[...].astype(f32)).T
    for head in range(2):
        rows = dq_turned[head * HDIM : (head + 1) * HDIM, :]
        delta[head : head + 1, :] = jnp.sum(rows, axis=0, keepdims=True)
    dq_turned[...] = jnp.zeros_like(dq_turned)
    first = lax.broadcasted_iota(jnp.int32, (tile, lanes), 1) < HDIM

    def body(step, _):
        part = pl.ds(pl.multiple_of(step * tile, tile), tile)
        k, v = k_ref[part, :], v_ref[part, :]
        q, do = q_ref[...], do_ref[...]
        allowed = key_tags[part, :] == query_tags[...]
        dk, dv = [], []
        for head in range(2):
            own = first if head == 0 else jnp.logical_not(first)
            own_rows = slice(head * HDIM, (head + 1) * HDIM)
            scores = dot(jnp.where(own, k, bf16(0)), q, 1, 1)
            scores = jnp.where(allowed, scores, masked_score)
            chances = jnp.exp2(scores * (score_scale * log2e) - lse_ref[head : head + 1, :])
            weight_grad = dot(jnp.where(own, v, bf16(0)), do, 1, 1)
            score_grad = (chances * (weight_grad - delta[head : head + 1, :])).astype(bf16)
            dv.append(dot(chances.astype(bf16), do, 1, 0))
            dk.append(dot(score_grad, q, 1, 0))
            dq_turned[own_rows, :] += dot(k_turned[own_rows, part], score_grad, 1, 0)
        grad_ref[part, lanes : 2 * lanes] = (jnp.where(first, dk[0], dk[1]) * score_scale).astype(bf16)
        grad_ref[part, 2 * lanes :] = jnp.where(first, dv[0], dv[1]).astype(bf16)
        return 0

    lax.fori_loop(0, tokens // tile, body, 0)
    grad_ref[:, :lanes] = (dq_turned[...] * score_scale).T.astype(bf16)


def attend_back(qkv, mixed, d_mixed, lse, key_tags, query_tags, start, count):
    tokens = qkv.shape[0]
    tile = min(512, tokens)
    lanes = 2 * HDIM

    def columns(place):
        return pl.BlockSpec((tokens, lanes), lambda i: (0, 3 * (start + i) + place))

    pair = pl.BlockSpec((tokens, lanes), lambda i: (0, start + i))
    return pl.pallas_call(
        functools.partial(attend_back_kernel, tile),
        grid=(count,),
        in_specs=[
            pl.BlockSpec((tokens, 1), lambda i: (0, 0)),
            pl.BlockSpec((1, tokens), lambda i: (0, 0)),
            columns(0),
            columns(1),
            columns(2),
            pair,
            pair,
            pl.BlockSpec((None, 2, tokens), lambda i: (start + i, 0, 0)),
        ],
        out_specs=pl.BlockSpec((tokens, 3 * lanes), lambda i: (0, i)),
        out_shape=jax.ShapeDtypeStruct((tokens, 3 * count * lanes), bf16),
        scratch_shapes=[
            pltpu.VMEM((lanes, tokens), bf16),
            pltpu.VMEM((lanes, tokens), f32),
            pltpu.VMEM((2, tokens), f32),
        ],
        compiler_params=pltpu.CompilerParams(vmem_limit_bytes=vmem_bytes),
        cost_estimate=pl.CostEstimate(
            flops=80 * count * tokens * tokens * HDIM,
            bytes_accessed=16 * tokens * count * lanes,
            transcendentals=2 * count * tokens * tokens,
        ),
        name="attend_back",
    )(key_tags, query_tags, qkv, qkv, qkv, mixed, d_mixed, lse)


def copy_kernel(core_ref, from_ref, to_ref):
    to_ref[...] = from_ref[...]


def gather_pairs(core, qkv_weight):
    width, lanes = qkv_weight.shape[0], 2 * HDIM
    pairs = width // (CORES * lanes)
    return pl.pallas_call(
        copy_kernel,
        grid_spec=pltpu.PrefetchScalarGridSpec(
            num_scalar_prefetch=1,
            grid=(pairs, 3),
            in_specs=[
                pl.BlockSpec((width, lanes), lambda i, j, core: (0, (j * CORES + core[0]) * pairs + i))
            ],
            out_specs=pl.BlockSpec((width, lanes), lambda i, j, core: (0, 3 * i + j)),
        ),
        out_shape=jax.ShapeDtypeStruct((width, 3 * pairs * lanes), qkv_weight.dtype),
        cost_estimate=pl.CostEstimate(flops=0, bytes_accessed=12 * width * pairs * lanes, transcendentals=0),
        name="gather_pairs",
    )(core, qkv_weight)


def norm_parts(values):
    center = values - jnp.mean(values, axis=-1, keepdims=True)
    spread = jnp.mean(center * center, axis=-1, keepdims=True)
    scale = lax.rsqrt(spread + epsilon)
    return center * scale, scale


def norm_back(grad, gain, unit, scale):
    e = grad * gain
    return scale * (
        e - jnp.mean(e, axis=-1, keepdims=True) - unit * jnp.mean(e * unit, axis=-1, keepdims=True)
    )


def feed_kernel(rows, core_ref, middle_ref, cot_ref, gain_ref, up_ref, down_ref,
    out_ref, d_middle_ref, d_attn_ref, down_sent, down_kept, up_sent, up_kept, n2, n2_turned, total, d_n2):
    step, last = pl.program_id(0), pl.num_programs(0) - 1
    tokens, width = n2.shape
    half = width // 2

    @pl.when(step == 0)
    def _():
        def body(i, _):
            part = pl.ds(pl.multiple_of(i * rows, rows), rows)
            unit, _s = norm_parts(middle_ref[part, :])
            n2[part, :] = (unit * gain_ref[...]).astype(bf16)
            return 0
        lax.fori_loop(0, tokens // rows, body, 0)
        n2_turned[...] = n2[...].T

    up_w, down_w = up_ref[...], down_ref[...]
    up = dot(n2[...], up_w, 1, 0)
    d_act = dot(cot_ref[...], down_w, 1, 1)
    share = 0.5 + 0.5 * lax.erf(up * (0.5**0.5))
    density = jnp.exp(-0.5 * up * up) * 0.3989422804014327
    act = (up * share).astype(bf16)
    d_up = (d_act * (share + up * density)).astype(bf16)
    y = dot(act, down_w, 1, 0)
    d = dot(d_up, up_w, 1, 1)

    @pl.when(step == 0)
    def _():
        total[...] = middle_ref[...] + y
        d_n2[...] = d

    @pl.when(step > 0)
    def _():
        total[...] += y
        d_n2[...] += d

    up_grad = dot(n2_turned[...], d_up, 1, 0).astype(bf16)

    @pl.when(step <= last // 2)
    def _():
        up_sent[...] = up_grad

    @pl.when(step > last // 2)
    def _():
        up_kept[...] = up_grad

    down_grad = dot(act, cot_ref[...], 0, 0).astype(bf16)

    @pl.when(core_ref[0] == 0)
    def _():
        down_kept[...] = down_grad[:, :half]
        down_sent[...] = down_grad[:, half:]

    @pl.when(core_ref[0] != 0)
    def _():
        down_kept[...] = down_grad[:, half:]
        down_sent[...] = down_grad[:, :half]

    @pl.when(step == last)
    def _():
        def body(i, _):
            part = pl.ds(pl.multiple_of(i * rows, rows), rows)
            out_ref[part, :] = total[part, :].astype(bf16)
            unit, scale = norm_parts(middle_ref[part, :])
            grad = cot_ref[part, :].astype(f32) + norm_back(d_n2[part, :], gain_ref[...], unit, scale)
            d_middle_ref[part, :] = grad
            d_attn_ref[part, :] = grad.astype(bf16)
            return 0
        lax.fori_loop(0, tokens // rows, body, 0)


def feed(core, middle, cot, gain, up_weight, down_weight, tile=512):
    tokens, width = middle.shape
    wide = up_weight.shape[1]
    steps = wide // tile
    halves = steps // 2
    place = lambda i, core: (i + (1 - core[0]) * halves) % steps
    whole = lambda dtype: jax.ShapeDtypeStruct((tokens, width), dtype)
    fixed = lambda shape: pl.BlockSpec(shape, lambda i, core: (0, 0), pipeline_mode=pl.Buffered(1))
    return pl.pallas_call(
        functools.partial(feed_kernel, 128),
        grid_spec=pltpu.PrefetchScalarGridSpec(
            num_scalar_prefetch=1,
            grid=(steps,),
            in_specs=[
                fixed((tokens, width)),
                fixed((tokens, width)),
                fixed((1, width)),
                pl.BlockSpec((width, tile), lambda i, core: (0, place(i, core))),
                pl.BlockSpec((tile, width), lambda i, core: (place(i, core), 0)),
            ],
            out_specs=[
                fixed((tokens, width)),
                fixed((tokens, width)),
                fixed((tokens, width)),
                pl.BlockSpec((tile, width // 2), lambda i, core: (place(i, core), 0)),
                pl.BlockSpec((tile, width // 2), lambda i, core: (place(i, core), 0)),
                pl.BlockSpec((width, tile), lambda i, core: (0, jnp.minimum(i, halves - 1))),
                pl.BlockSpec((width, tile), lambda i, core: (0, jnp.maximum(i - halves, 0))),
            ],
            scratch_shapes=[
                pltpu.VMEM((tokens, width), bf16),
                pltpu.VMEM((width, tokens), bf16),
                pltpu.VMEM((tokens, width), f32),
                pltpu.VMEM((tokens, width), f32),
            ],
        ),
        out_shape=[
            whole(bf16), whole(f32), whole(bf16),
            jax.ShapeDtypeStruct((wide, width // 2), bf16),
            jax.ShapeDtypeStruct((wide, width // 2), bf16),
            jax.ShapeDtypeStruct((width, wide // 2), bf16),
            jax.ShapeDtypeStruct((width, wide // 2), bf16),
        ],
        compiler_params=pltpu.CompilerParams(vmem_limit_bytes=vmem_bytes),
        name="feed",
    )(core, middle, cot, gain.reshape(1, width), up_weight, down_weight)


def feed_kernel(rows, core_ref, middle_ref, cot_ref, gain_ref, up_ref, down_ref,
    out_ref, d_middle_ref, d_attn_ref, down_sent, down_kept, up_sent, up_kept, n2, n2_turned, total, d_n2):
    step, last = pl.program_id(0), pl.num_programs(0) - 1
    tokens, width = n2.shape
    half = width // 2

    @pl.when(step == 0)
    def _():
        def body(i, _):
            part = pl.ds(pl.multiple_of(i * rows, rows), rows)
            unit, _s = norm_parts(middle_ref[part, :])
            n2[part, :] = (unit * gain_ref[...]).astype(bf16)
            return 0
        lax.fori_loop(0, tokens // rows, body, 0)
        n2_turned[...] = n2[...].T

    up_w, down_w = up_ref[...], down_ref[...]
    up = dot(n2[...], up_w, 1, 0)
    d_act = dot(cot_ref[...], down_w, 1, 1)
    share = 0.5 + 0.5 * lax.erf(up * (0.5**0.5))
    density = jnp.exp(-0.5 * up * up) * 0.3989422804014327
    act = (up * share).astype(bf16)
    d_up = (d_act * (share + up * density)).astype(bf16)
    y = dot(act, down_w, 1, 0)
    d = dot(d_up, up_w, 1, 1)

    @pl.when(step == 0)
    def _():
        total[...] = middle_ref[...] + y
        d_n2[...] = d

    @pl.when(step > 0)
    def _():
        total[...] += y
        d_n2[...] += d

    up_grad = dot(n2_turned[...], d_up, 1, 0).astype(bf16)

    @pl.when(step <= last // 2)
    def _():
        up_sent[...] = up_grad

    @pl.when(step > last // 2)
    def _():
        up_kept[...] = up_grad

    down_grad = dot(act, cot_ref[...], 0, 0).astype(bf16)

    @pl.when(core_ref[0] == 0)
    def _():
        down_kept[...] = down_grad[:, :half]
        down_sent[...] = down_grad[:, half:]

    @pl.when(core_ref[0] != 0)
    def _():
        down_kept[...] = down_grad[:, half:]
        down_sent[...] = down_grad[:, :half]

    @pl.when(step == last)
    def _():
        def body(i, _):
            part = pl.ds(pl.multiple_of(i * rows, rows), rows)
            out_ref[part, :] = total[part, :].astype(bf16)
            unit, scale = norm_parts(middle_ref[part, :])
            grad = cot_ref[part, :].astype(f32) + norm_back(d_n2[part, :], gain_ref[...], unit, scale)
            d_middle_ref[part, :] = grad
            d_attn_ref[part, :] = grad.astype(bf16)
            return 0
        lax.fori_loop(0, tokens // rows, body, 0)


def feed(core, middle, cot, gain, up_weight, down_weight, tile=512):
    tokens, width = middle.shape
    wide = up_weight.shape[1]
    steps = wide // tile
    halves = steps // 2
    place = lambda i, core: (i + (1 - core[0]) * halves) % steps
    whole = lambda dtype: jax.ShapeDtypeStruct((tokens, width), dtype)
    fixed = lambda shape: pl.BlockSpec(shape, lambda i, core: (0, 0), pipeline_mode=pl.Buffered(1))
    return pl.pallas_call(
        functools.partial(feed_kernel, 128),
        grid_spec=pltpu.PrefetchScalarGridSpec(
            num_scalar_prefetch=1,
            grid=(steps,),
            in_specs=[
                fixed((tokens, width)),
                fixed((tokens, width)),
                fixed((1, width)),
                pl.BlockSpec((width, tile), lambda i, core: (0, place(i, core))),
                pl.BlockSpec((tile, width), lambda i, core: (place(i, core), 0)),
            ],
            out_specs=[
                fixed((tokens, width)),
                fixed((tokens, width)),
                fixed((tokens, width)),
                pl.BlockSpec((tile, width // 2), lambda i, core: (place(i, core), 0)),
                pl.BlockSpec((tile, width // 2), lambda i, core: (place(i, core), 0)),
                pl.BlockSpec((width, tile), lambda i, core: (0, jnp.minimum(i, halves - 1))),
                pl.BlockSpec((width, tile), lambda i, core: (0, jnp.maximum(i - halves, 0))),
            ],
            scratch_shapes=[
                pltpu.VMEM((tokens, width), bf16),
                pltpu.VMEM((width, tokens), bf16),
                pltpu.VMEM((tokens, width), f32),
                pltpu.VMEM((tokens, width), f32),
            ],
        ),
        out_shape=[
            whole(bf16), whole(f32), whole(bf16),
            jax.ShapeDtypeStruct((wide, width // 2), bf16),
            jax.ShapeDtypeStruct((wide, width // 2), bf16),
            jax.ShapeDtypeStruct((width, wide // 2), bf16),
            jax.ShapeDtypeStruct((width, wide // 2), bf16),
        ],
        compiler_params=pltpu.CompilerParams(vmem_limit_bytes=vmem_bytes),
        name="feed",
    )(core, middle, cot, gain.reshape(1, width), up_weight, down_weight)


def add_split_kernel(has_two, bit_ref, *refs):
    ins, outs = refs[: 2 if has_two else 1], refs[2 if has_two else 1 :]
    value = ins[0][...]
    if has_two:
        value = (value.astype(f32) + ins[1][...].astype(f32)).astype(bf16)
    if len(outs) == 1:
        outs[0][...] = value
    else:
        sends = pl.program_id(0) == 0

        @pl.when(sends)
        def _():
            outs[0][...] = value

        @pl.when(jnp.logical_not(sends))
        def _():
            outs[1][...] = value


def add_split(kept, received, inner, bit):
    rows, columns = kept.shape
    values = [kept] if received is None else [kept, received.reshape(rows, columns)]
    if bit is None:
        if received is None:
            return None, kept
        count = 4 if rows % 64 == 0 else 1
        block = pl.BlockSpec((rows // count, columns), lambda i, bit: (i, 0))
        grid, ins, outs = (count,), [block] * 2, block
        shapes = jax.ShapeDtypeStruct((rows, columns), bf16)
        bit = jnp.zeros((), jnp.int32)
    else:
        outer = rows // (2 * inner)
        cut = 1
        while inner // cut * columns > 2**19 and inner % (32 * cut) == 0:
            cut *= 2
        values = [value.reshape(outer, 2, inner, columns) for value in values]
        ins = [
            pl.BlockSpec(
                (None, None, inner // cut, columns),
                lambda w, i, j, bit: (i, jnp.where(w == 0, 1 - bit[0], bit[0]), j, 0),
            )
        ] * len(values)
        outs = [
            pl.BlockSpec(
                (None, inner // cut, columns),
                lambda w, i, j, bit: (jnp.where(w == 0, i, outer - 1), jnp.where(w == 0, j, cut - 1), 0),
            ),
            pl.BlockSpec(
                (None, inner // cut, columns),
                lambda w, i, j, bit: (jnp.where(w == 0, 0, i), jnp.where(w == 0, 0, j), 0),
            ),
        ]
        grid = (2, outer, cut)
        shapes = [jax.ShapeDtypeStruct((outer, inner, columns), bf16)] * 2
    done = pl.pallas_call(
        functools.partial(add_split_kernel, len(values) == 2),
        grid_spec=pltpu.PrefetchScalarGridSpec(
            num_scalar_prefetch=1, grid=grid, in_specs=ins, out_specs=outs
        ),
        out_shape=shapes,
        cost_estimate=pl.CostEstimate(flops=rows * columns, bytes_accessed=6 * rows * columns, transcendentals=0),
        name="add_split",
    )(bit.reshape(1), *values)
    if not isinstance(done, (list, tuple)):
        return None, done
    return done[0].reshape(rows // 2, columns), done[1].reshape(rows // 2, columns)


piece_rows = 32


def feed_kernel(
    tiles,
    rows,
    middle_ref,
    cot_ref,
    gain_ref,
    up_ref,
    down_ref,
    out_ref,
    d_middle_ref,
    d_attn_ref,
    down_part,
    up_part,
    n2,
    n2_turned,
    total,
    down_keep,
    down_send,
    down_recv,
    up_keep,
    up_send,
    up_recv,
    down_far_keep,
    down_far_send,
    down_far_recv,
    up_far_keep,
    up_far_send,
    up_far_recv,
    core_send_sem,
    core_recv_sem,
    far_send_sem,
    far_recv_sem,
    core_free,
    far_free,
):
    step = pl.program_id(0)
    tokens, width = n2.shape
    half = width // 2
    seq_at, rows_at = lax.axis_index("seq"), lax.axis_index("rows")
    core, high, low = rows_at % 2, (rows_at // 2) % 2, seq_at % 2
    core_peer = (seq_at, rows_at + 1 - 2 * core)
    far_peers = ((seq_at, rows_at + 2 - 4 * high), (seq_at + 1 - 2 * low, rows_at))

    def copies(slot, far):
        if far:
            refs = ((down_far_send, down_far_recv), (up_far_send, up_far_recv))
            sems, peers = (far_send_sem, far_recv_sem), far_peers
        else:
            refs = ((down_send, down_recv), (up_send, up_recv))
            sems, peers = (core_send_sem, core_recv_sem), (core_peer, core_peer)
        return [
            pltpu.make_async_remote_copy(
                src_ref=refs[kind][0].at[slot],
                dst_ref=refs[kind][1].at[slot],
                send_sem=sems[0].at[kind, slot],
                recv_sem=sems[1].at[kind, slot],
                device_id=peers[kind],
                device_id_type=MESH,
            )
            for kind in range(2)
        ]

    def signal(sem, peer):
        pl.semaphore_signal(sem, inc=1, device_id=peer, device_id_type=MESH)

    @pl.when(step == 0)
    def _():
        barrier = pltpu.get_barrier_semaphore()
        for peer in (core_peer,) + far_peers:
            signal(barrier, peer)
        pl.semaphore_wait(barrier, 3)

        def body(i, _):
            part = pl.ds(pl.multiple_of(i * rows, rows), rows)
            unit, _s = norm_parts(middle_ref[part, :])
            n2[part, :] = (unit * gain_ref[...]).astype(bf16)
            return 0

        lax.fori_loop(0, tokens // rows, body, 0)
        n2_turned[...] = n2[...].T
        total[...] = middle_ref[...]
        d_middle_ref[...] = jnp.zeros_like(d_middle_ref)

    @pl.when(step < tiles)
    def _():
        up_w, down_w = up_ref[...], down_ref[...]
        up = dot(n2[...], up_w, 1, 0)
        d_act = dot(cot_ref[...], down_w, 1, 1)
        share = 0.5 + 0.5 * lax.erf(up * (0.5**0.5))
        density = jnp.exp(-0.5 * up * up) * 0.3989422804014327
        act = (up * share).astype(bf16)
        d_up = (d_act * (share + up * density)).astype(bf16)
        total[...] += dot(act, down_w, 1, 0)
        d_middle_ref[...] += dot(d_up, up_w, 1, 1)
        slot = step % 2

        @pl.when(step >= 2)
        def _():
            for copy in copies(slot, False):
                copy.wait_send()

        up_grad = dot(n2_turned[...], d_up, 1, 0).astype(bf16)
        cut = up_grad.shape[1] // 2

        @pl.when(core == 0)
        def _():
            up_keep[slot] = up_grad[:, :cut].reshape(up_keep.shape[1:])
            up_send[slot] = up_grad[:, cut:].reshape(up_keep.shape[1:])

        @pl.when(core != 0)
        def _():
            up_keep[slot] = up_grad[:, cut:].reshape(up_keep.shape[1:])
            up_send[slot] = up_grad[:, :cut].reshape(up_keep.shape[1:])

        down_grad = dot(act, cot_ref[...], 0, 0).astype(bf16)

        @pl.when(core == 0)
        def _():
            down_keep[slot] = down_grad[:, :half].reshape(down_keep.shape[1:])
            down_send[slot] = down_grad[:, half:].reshape(down_keep.shape[1:])

        @pl.when(core != 0)
        def _():
            down_keep[slot] = down_grad[:, half:].reshape(down_keep.shape[1:])
            down_send[slot] = down_grad[:, :half].reshape(down_keep.shape[1:])

    def add(a, b):
        return (a.astype(f32) + b.astype(f32)).astype(bf16)

    def last_add():
        slot = step % 2
        for copy in copies(slot, True):
            copy.wait_recv()
        down_part[...] = add(down_far_keep[slot], down_far_recv[slot]).reshape(down_part.shape)
        up_part[...] = add(up_far_keep[slot], up_far_recv[slot]).reshape(up_part.shape)

        @pl.when(step < tiles)
        def _():
            signal(far_free.at[0], far_peers[0])
            signal(far_free.at[1], far_peers[1])

    def pass_on():
        slot = (step + 1) % 2
        for copy in copies(slot, False):
            copy.wait_recv()

        @pl.when(step >= 3)
        def _():
            for copy in copies(slot, True):
                copy.wait_send()
            pl.semaphore_wait(far_free.at[0], 1)
            pl.semaphore_wait(far_free.at[1], 1)

        down_far_send[slot] = add(down_keep[slot, :, 1 - high], down_recv[slot, :, 1 - high])
        down_far_keep[slot] = add(down_keep[slot, :, high], down_recv[slot, :, high])
        up_far_send[slot] = add(up_keep[slot, :, 1 - low], up_recv[slot, :, 1 - low])
        up_far_keep[slot] = add(up_keep[slot, :, low], up_recv[slot, :, low])
        for copy in copies(slot, True):
            copy.start()

        @pl.when(step < tiles - 1)
        def _():
            signal(core_free, core_peer)

    @pl.when((step >= 2) & (step <= tiles))
    def _():
        last_add()

    @pl.when((step >= 1) & (step <= tiles))
    def _():
        pass_on()

    @pl.when(step < tiles)
    def _():
        @pl.when(step >= 2)
        def _():
            pl.semaphore_wait(core_free, 1)

        for copy in copies(step % 2, False):
            copy.start()

    @pl.when(step == tiles)
    def _():
        def body(i, _):
            part = pl.ds(pl.multiple_of(i * rows, rows), rows)
            out_ref[part, :] = total[part, :].astype(bf16)
            unit, scale = norm_parts(middle_ref[part, :])
            grad = cot_ref[part, :].astype(f32) + norm_back(d_middle_ref[part, :], gain_ref[...], unit, scale)
            d_middle_ref[part, :] = grad
            d_attn_ref[part, :] = grad.astype(bf16)
            return 0

        lax.fori_loop(0, tokens // rows, body, 0)

    @pl.when(step == tiles + 1)
    def _():
        last_add()
        for slot in range(2):
            for far in (False, True):
                for copy in copies(slot, far):
                    copy.wait_send()


def feed(middle, cot, gain, up_weight, down_weight, n_seq):
    tokens, width = middle.shape
    wide = up_weight.shape[1]
    tile = feed_tile
    tiles = wide // tile
    half, shard = width // 2, width // n_seq
    whole = lambda dtype: jax.ShapeDtypeStruct((tokens, width), dtype)
    fixed = lambda shape: pl.BlockSpec(shape, lambda i: (0, 0), pipeline_mode=pl.Buffered(1))
    at = lambda i: jnp.minimum(i, tiles - 1)
    done = lambda i: jnp.maximum(i - 2, 0)
    down_shape = (2, tile // (2 * piece_rows), 2, piece_rows, half)
    up_shape = (2, n_seq // 2, 2, shard, tile // 2)
    near = [pltpu.VMEM(down_shape, bf16)] * 3 + [pltpu.VMEM(up_shape, bf16)] * 3
    far = [pltpu.VMEM(down_shape[:2] + down_shape[3:], bf16)] * 3 + [pltpu.VMEM(up_shape[:2] + up_shape[3:], bf16)] * 3
    return pl.pallas_call(
        functools.partial(feed_kernel, tiles, 128),
        grid=(tiles + 2,),
        in_specs=[
            fixed((tokens, width)),
            fixed((tokens, width)),
            fixed((1, width)),
            pl.BlockSpec((width, tile), lambda i: (0, at(i))),
            pl.BlockSpec((tile, width), lambda i: (at(i), 0)),
        ],
        out_specs=[
            fixed((tokens, width)),
            fixed((tokens, width)),
            fixed((tokens, width)),
            pl.BlockSpec((tile // 2, half), lambda i: (done(i), 0)),
            pl.BlockSpec((width // 2, tile // 2), lambda i: (0, done(i))),
        ],
        scratch_shapes=[
            pltpu.VMEM((tokens, width), bf16),
            pltpu.VMEM((width, tokens), bf16),
            pltpu.VMEM((tokens, width), f32),
        ]
        + near
        + far
        + [pltpu.SemaphoreType.DMA((2, 2))] * 4
        + [pltpu.SemaphoreType.REGULAR, pltpu.SemaphoreType.REGULAR((2,))],
        out_shape=[
            whole(bf16),
            whole(f32),
            whole(bf16),
            jax.ShapeDtypeStruct((wide // 2, half), bf16),
            jax.ShapeDtypeStruct((width // 2, wide // 2), bf16),
        ],
        compiler_params=pltpu.CompilerParams(
            vmem_limit_bytes=feed_vmem_bytes, collective_id=1, has_side_effects=True
        ),
        cost_estimate=pl.CostEstimate(
            flops=12 * tokens * width * wide,
            bytes_accessed=16 * tokens * width + 6 * width * wide,
            transcendentals=2 * tokens * wide,
        ),
        name="feed",
    )(middle, cot, gain.reshape(1, width), up_weight, down_weight)


def add_split_kernel(has_two, bit_ref, *refs):
    ins, outs = refs[: 2 if has_two else 1], refs[2 if has_two else 1 :]
    value = ins[0][...]
    if has_two:
        value = (value.astype(f32) + ins[1][...].astype(f32)).astype(bf16)
    if len(outs) == 1:
        outs[0][...] = value
    else:
        sends = pl.program_id(0) == 0

        @pl.when(sends)
        def _():
            outs[0][...] = value

        @pl.when(jnp.logical_not(sends))
        def _():
            outs[1][...] = value


def add_split(kept, received, inner, bit):
    rows, columns = kept.shape
    values = [kept] if received is None else [kept, received.reshape(rows, columns)]
    if bit is None:
        if received is None:
            return None, kept
        count = 4 if rows % 64 == 0 else 1
        block = pl.BlockSpec((rows // count, columns), lambda i, bit: (i, 0))
        grid, ins, outs = (count,), [block] * 2, block
        shapes = jax.ShapeDtypeStruct((rows, columns), bf16)
        bit = jnp.zeros((), jnp.int32)
    else:
        outer = rows // (2 * inner)
        cut = 1
        while inner // cut * columns > 2**19 and inner % (32 * cut) == 0:
            cut *= 2
        values = [value.reshape(outer, 2, inner, columns) for value in values]
        ins = [
            pl.BlockSpec(
                (None, None, inner // cut, columns),
                lambda w, i, j, bit: (i, jnp.where(w == 0, 1 - bit[0], bit[0]), j, 0),
            )
        ] * len(values)
        outs = [
            pl.BlockSpec(
                (None, inner // cut, columns),
                lambda w, i, j, bit: (jnp.where(w == 0, i, outer - 1), jnp.where(w == 0, j, cut - 1), 0),
            ),
            pl.BlockSpec(
                (None, inner // cut, columns),
                lambda w, i, j, bit: (jnp.where(w == 0, 0, i), jnp.where(w == 0, 0, j), 0),
            ),
        ]
        grid = (2, outer, cut)
        shapes = [jax.ShapeDtypeStruct((outer, inner, columns), bf16)] * 2
    done = pl.pallas_call(
        functools.partial(add_split_kernel, len(values) == 2),
        grid_spec=pltpu.PrefetchScalarGridSpec(
            num_scalar_prefetch=1, grid=grid, in_specs=ins, out_specs=outs
        ),
        out_shape=shapes,
        cost_estimate=pl.CostEstimate(flops=rows * columns, bytes_accessed=6 * rows * columns, transcendentals=0),
        name="add_split",
    )(bit.reshape(1), *values)
    if not isinstance(done, (list, tuple)):
        return None, done
    return done[0].reshape(rows // 2, columns), done[1].reshape(rows // 2, columns)


def tie(*values):
    return lax.optimization_barrier(values)


def build(n_seq, n_rows):
    highs = n_rows // CORES
    seq_bits = n_seq.bit_length() - 1
    high_bits = highs.bit_length() - 1
    bits = seq_bits + high_bits

    def permute(value, target):
        pairs = []
        for s in range(n_seq):
            for r in range(n_rows):
                to_s, to_r = target(s, r)
                pairs.append((s * n_rows + r, to_s * n_rows + to_r))
        return lax.ppermute(value, AXES, pairs)

    def other_core(value):
        return permute(value, lambda s, r: (s, r ^ 1))

    def pick(value, place, axis):
        return lax.dynamic_index_in_dim(value, place, axis, keepdims=False)

    def bit_of(step):
        name, bit = step
        return (lax.axis_index(name) >> bit) & 1

    def across(value, step):
        name, bit = step
        if name == "rows":
            return permute(value, lambda s, r: (s, r ^ (1 << bit)))
        return permute(value, lambda s, r: (s ^ (1 << bit), r))

    high_steps = [("rows", bit + 1) for bit in reversed(range(high_bits))]
    seq_steps = [("seq", bit) for bit in range(seq_bits)]

    class Sum:
        def __init__(self, kept, received, order):
            self.rows, self.columns = kept.shape
            self.kept, self.received = kept, received
            self.left = [step for step in seq_steps[::-1] + high_steps if step in order]
            self.order = list(order)

        def finish(self):
            step = self.order[0] if self.order else None
            inner = self.rows
            if step is not None:
                axis = self.left.index(step)
                inner = self.rows >> (axis + 1)
            self.sent, self.kept = add_split(self.kept, self.received, inner, step and bit_of(step))
            self.received = None

        def begin(self):
            step = self.order.pop(0)
            self.left.remove(step)
            self.rows //= 2
            self.received = across(self.sent, step)

        def finished(self):
            while self.order:
                self.finish()
                self.begin()
            self.finish()
            return self.kept

    rows_first = high_steps + seq_steps[1:2] + seq_steps[:1] + seq_steps[2:]
    down_order = [step for step in seq_steps + high_steps if step != ("rows", 1)]
    up_order = [step for step in high_steps + seq_steps if step != ("seq", 0)]

    def gather_high(value, pieces=0):
        for step in high_steps[::-1]:
            if pieces and step == ("rows", 1):
                continue
            received = across(value, step)
            value = jnp.where(
                bit_of(step) == 0,
                jnp.concatenate([value, received], 0),
                jnp.concatenate([received, value], 0),
            )
        if pieces:
            value = value.reshape(-1, 1, pieces, value.shape[1])
            received = across(value, ("rows", 1))
            value = jnp.where(
                bit_of(("rows", 1)) == 0,
                jnp.concatenate([value, received], 1),
                jnp.concatenate([received, value], 1),
            )
            value = value.reshape(-1, value.shape[-1])
        return value

    def per_device(
        inputs, cell_ids, valid_counts, cotangent, attention_gain, qkv_weight, out_weight, feed_gain, up_weight, down_weight
    ):
        row_count, block, width = inputs.shape
        seq_len = cell_ids.shape[1]
        heads = width // HDIM
        lanes = 2 * HDIM
        seq_at, rows_at = lax.axis_index("seq"), lax.axis_index("rows")
        core = rows_at % CORES
        chips = n_seq // (CORES * row_count)
        group = chips * CORES
        sub = block // group
        tokens = n_seq * sub
        member = (seq_at % chips) * CORES + core
        group_heads = heads // group
        pairs = -(-group_heads // 2)
        group_width = group_heads * HDIM
        padded = pairs * lanes - group_width

        def to_member(value, hop):
            def target(s, r):
                place = ((s % chips) * CORES + r % CORES + hop) % group
                return (s // chips * chips + place // CORES, r // CORES * CORES + place % CORES)

            return permute(value, target)

        def ordered(own, received, axis):
            return jnp.where(
                core == 0,
                jnp.concatenate([own, received], axis),
                jnp.concatenate([received, own], axis),
            )

        def to_rows(value):
            halves = value.reshape(row_count, CORES, block // CORES, width)
            received = other_core(pick(halves, 1 - core, 1))
            both = ordered(pick(halves, core, 1), received, 0).reshape(n_seq, sub, width)
            return lax.all_to_all(both, "seq", 0, 0, tiled=True).reshape(tokens, width)

        def from_rows(value):
            both = lax.all_to_all(value.reshape(n_seq, sub, width), "seq", 0, 0, tiled=True)
            both = both.reshape(CORES, row_count, block // CORES, width)
            received = other_core(pick(both, 1 - core, 0))
            own = pick(both, core, 0)
            return ordered(own[:, None], received[:, None], 1).reshape(row_count, block, width)

        places = jnp.arange(seq_len, dtype=jnp.int32)
        tags = jnp.where(places[None, :] < valid_counts[:, None], cell_ids, -1 - places[None, :])
        tags = ordered(tags, other_core(tags), 0)
        tags = pick(tags, seq_at // chips, 0).reshape(n_seq, CORES, chips, sub)
        tags = tags.transpose(2, 1, 0, 3).reshape(group, tokens)
        order = (member - jnp.arange(group, dtype=jnp.int32)) % group
        tags = jnp.take(tags, order, axis=0).reshape(1, seq_len)
        query_tags, key_tags = tags, tags.reshape(seq_len, 1)

        def pad_heads(value, axis):
            if not padded:
                return value
            fill = [(0, 0)] * value.ndim
            fill[axis] = (0, padded)
            return jnp.pad(value, fill)

        def qkv_of(hop):
            if group == CORES:
                return gather_pairs(((core + hop) % CORES).reshape(1), qkv_weight)
            piece = pick(qkv_weight.reshape(width, 3, group, group_width), (member + hop) % group, 2)
            piece = pad_heads(piece, 2).reshape(width, 3, pairs, lanes)
            return piece.transpose(0, 2, 1, 3).reshape(width, 3 * pairs * lanes)

        def out_of(hop):
            at = (member + hop) % group * group_width
            return pad_heads(lax.dynamic_slice_in_dim(out_weight, at, group_width, 0), 0)

        start = to_rows(inputs)
        qkv_parts = [qkv_of(hop) for hop in range(group)]
        out_parts = [out_of(hop) for hop in range(group)]
        start = start.astype(f32)
        unit1, scale1 = norm_parts(start)
        n1 = (unit1 * attention_gain).astype(bf16)
        n1_all = jnp.concatenate([n1] + [to_member(n1, hop) for hop in range(1, group)], 0)
        cotangent, _ = tie(cotangent, start[:1])
        cot = to_rows(cotangent)
        qkv = dot(n1_all, qkv_parts[0], 1, 0).astype(bf16)
        mixed, lse = attend(qkv, key_tags, query_tags)
        mixed_parts = [mixed[:tokens]] + [
            to_member(mixed[hop * tokens : (hop + 1) * tokens], group - hop) for hop in range(1, group)
        ]
        middle = start
        for part, weight in zip(mixed_parts, out_parts):
            middle = middle + dot(part, weight, 1, 0)
        outputs, d_middle, d_attn, down_part, up_part = feed(middle, cot, feed_gain, up_weight, down_weight, n_seq)

        d_attn_all = jnp.concatenate([d_attn] + [to_member(d_attn, hop) for hop in range(1, group)], 0)

        out_low = from_rows(outputs)

        half = width // CORES
        if group == CORES:
            mixed_own = ordered(mixed_parts[0], mixed_parts[1], 1)
        else:
            slots = jnp.stack([part[:, :group_width] for part in mixed_parts])
            back = (jnp.arange(group, dtype=jnp.int32) - member) % group
            mixed_own = jnp.take(slots, back, axis=0).transpose(1, 0, 2).reshape(tokens, width)
        out_sent = dot(mixed_own, lax.dynamic_slice_in_dim(d_attn, (1 - core) * half, half, 1), 0, 0)
        out_kept = dot(mixed_own, lax.dynamic_slice_in_dim(d_attn, core * half, half, 1), 0, 0)
        out_received = other_core(out_sent.astype(bf16))
        d_mixed = dot(d_attn_all, out_parts[0], 1, 1).astype(bf16)

        down = Sum(down_part, None, down_order)
        up = Sum(up_part, None, up_order)
        out = Sum(out_kept.astype(bf16), out_received, rows_first)

        def before_next(*sums):
            nonlocal d_mixed
            for each in sums:
                each.finish()
            values = tie(d_mixed, *[v for each in sums for v in (each.sent, each.kept)])
            d_mixed = values[0]
            for at, each in enumerate(sums):
                each.sent, each.kept = values[1 + 2 * at : 3 + 2 * at]
                each.begin()

        def back(at):
            return attend_back(qkv, mixed, d_mixed, lse, key_tags, query_tags, at, 1)

        cut = max(1, 3 * pairs // 5)
        before_next(down, up)
        d_qkv, qkv_sums, d_parts = [], [], [[] for _ in range(group)]

        def take_piece(pieces):
            piece = jnp.concatenate(pieces, axis=1)
            d_parts[0].append(piece[:tokens])
            for hop in range(1, group):
                d_parts[hop].append(to_member(piece[hop * tokens : (hop + 1) * tokens], group - hop))
            return dot(n1_all, piece, 0, 0)

        grads = []
        for at in range(pairs):
            d_qkv.append(back(at))
            d_mixed, d_qkv[at] = tie(d_mixed, d_qkv[at])
            if at + 1 == cut:
                grads.append(take_piece(d_qkv))
            if at == min(0, pairs - 1):
                before_next(out)
            if at == min(1, pairs - 1):
                before_next(down, up)
            if at == min(3, pairs - 1):
                before_next(down, up, out)
        if pairs > cut:
            grads.append(take_piece(d_qkv[cut:]))
        if group == CORES:
            qkv_sums = [Sum(grad.astype(bf16), None, rows_first) for grad in grads]
        else:
            grad = jnp.concatenate(grads, 1)
            grad = grad.reshape(width, pairs, 3, lanes).transpose(0, 2, 1, 3)
            grad = grad.reshape(width, 3, 1, pairs * lanes)[..., :group_width]
            grad = lax.dynamic_update_slice_in_dim(
                jnp.zeros((width, 3, group, group_width), f32), grad, member, 2
            ).reshape(width, 3, CORES, half)
            kept = pick(grad, core, 2).astype(bf16).reshape(width, 3 * half)
            sent = pick(grad, 1 - core, 2).astype(bf16).reshape(width, 3 * half)
            qkv_sums = [Sum(kept, other_core(sent), rows_first)]

        d_n1 = jnp.zeros((tokens, width), f32)
        for part, weight in zip(d_parts, qkv_parts):
            d_n1 = d_n1 + dot(jnp.concatenate(part, 1), weight, 1, 1)
        input_grad = d_middle + norm_back(d_n1, attention_gain, unit1, scale1)
        input_grad = from_rows(input_grad.astype(bf16))

        down_total = gather_high(down.finished(), piece_rows)
        down_total = ordered(down_total, other_core(down_total), 1).astype(f32)
        tile = feed_tile // CORES
        up_total = gather_high(up.finished()).reshape(width // n_seq, -1, 1, tile)
        up_total = ordered(up_total, other_core(up_total), 2).reshape(width // n_seq, -1).astype(f32)
        out_total = gather_high(out.finished())
        out_total = ordered(out_total, other_core(out_total), 1).astype(f32)
        qkv_part = gather_high(jnp.concatenate([each.finished() for each in qkv_sums], 1))
        if group == CORES:
            qkv_part = qkv_part.reshape(-1, pairs, 3, lanes).transpose(0, 2, 1, 3)
        qkv_part = qkv_part.reshape(-1, 3, half)
        qkv_total = ordered(qkv_part[:, :, None], other_core(qkv_part)[:, :, None], 2)
        qkv_total = qkv_total.reshape(-1, 3 * width).astype(f32)

        shard = width // n_seq

        def gain_total(weight, total, gain):
            rows = lax.dynamic_slice_in_dim(weight, seq_at * shard, shard, 0).astype(f32)
            return jnp.sum(rows * total, axis=1) / lax.dynamic_slice_in_dim(gain, seq_at * shard, shard, 0)

        return (
            out_low,
            input_grad,
            gain_total(qkv_weight, qkv_total, attention_gain),
            qkv_total,
            out_total,
            gain_total(up_weight, up_total, feed_gain),
            up_total,
            down_total,
        )

    return per_device


def solution(mesh):
    placed = (
        P("rows", "seq", None),
        P("rows", None),
        P("rows"),
        P("rows", "seq", None),
        P(),
        P(),
        P(),
        P(),
        P(),
        P(),
    )
    return jax.shard_map(
        build(mesh.shape["seq"], mesh.shape["rows"]),
        mesh=mesh,
        in_specs=placed,
        out_specs=(
            P("rows", "seq", None),
            P("rows", "seq", None),
            P("seq"),
            P("seq", None),
            P("seq", None),
            P("seq"),
            P("seq", None),
            P("seq", None),
        ),
        check_vma=False,
    )
```

time: 981 us -> 872 us (0.89)
  Pallas kernels: 238 us -> 463 us
  local copies, waits for them, and re-layouts: 182 us -> 65.1 us
  waiting for transfers between devices: 202 us -> 95.4 us
  matrix products: 168 us -> 87.2 us
  other arithmetic: 75.4 us -> 38.3 us
    pallas_call x1 -> x26, Pallas kernels: 40 us -> 247 us  [the longest x1 132 us: feed(): pl.pallas_call(functools.partial(feed_kernel, tiles, 128), grid=(tiles +...]
    ppermute x36 -> x37, waiting for transfers between devices: 202 us -> 95.4 us  [permute(): return lax.ppermute(value, AXES, pairs)]
    dot_general x15 -> x10, matrix products: 168 us -> 87.2 us  [dot(): lax.dot_general(a, b, (((ca,), (cb,)), ((), ())), preferred_element_type=...]
    dynamic_slice x13 -> x0, local copies, waits for them, and re-layouts: 53.8 us -> none  [pick(): return lax.dynamic_index_in_dim(value, place, axis, keepdims=False)]
    convert_element_type x20 -> x3, other arithmetic: 35.5 us -> 6.39 us  [the longest x1 3.96 us: per_device(): down_total = ordered(down_total, other_core(down_total), 1).astype(f32)]
    reshape x3 -> x2, local copies, waits for them, and re-layouts: 30.7 us -> 3.28 us  [the longest x1 2.68 us: per_device(): qkv_part = qkv_part.reshape(-1, 3, half)]
    unnamed x123 -> x75, local copies, waits for them, and re-layouts: 31.3 us -> 12.3 us
    pallas_call x1 -> x5, Pallas kernels: 117 us -> 135 us  [attend_back(): pl.pallas_call(functools.partial(attend_back_kernel, tile), grid=(count,)...]
  transfers between devices with their start and end apart: 39 -> 40, of which waited for: 11 -> 13; matrix products, arithmetic and copies ran while one was open for 37% -> 20% of each run, Pallas kernels for 20% -> 38%
where the time goes in v2:
time: 872 us; the launch traced here: 864 us
  Pallas kernels  463 us (53%)
  waiting for transfers between devices  95.4 us (11%)
  matrix products  87.2 us (10%)
  blocking collectives  66.7 us (8%)
  local copies, waits for them, and re-layouts  65.1 us (7%)
  starting transfers between devices  47.1 us (5%)
  other arithmetic  38.3 us (4%)
    pallas_call x5, Pallas kernels, attend_back(): pl.pallas_call(functools.partial(attend_back_kernel, tile), grid=(count,)...  135 us
    pallas_call x1, Pallas kernels, feed(): pl.pallas_call(functools.partial(feed_kernel, tiles, 128), grid=(tiles +...  132 us
    ppermute x37, waiting for transfers between devices, permute(): return lax.ppermute(value, AXES, pairs)  95.4 us
    pallas_call x23, Pallas kernels, add_split(): pl.pallas_call(functools.partial(add_split_kernel, len(values) == 2), gri...  94.2 us
    dot_general x10, matrix products, dot(): lax.dot_general(a, b, (((ca,), (cb,)), ((), ())), preferred_element_type=...  87.2 us
    pallas_call x1, Pallas kernels, attend(): pl.pallas_call(functools.partial(attend_kernel, tile), grid=(pairs,), in_...  81.4 us
    all_to_all x1, blocking collectives, to_rows(): return lax.all_to_all(both, 'seq', 0, 0, tiled=True).reshape(tokens, width)  66.7 us
    ppermute x37, starting transfers between devices, permute(): return lax.ppermute(value, AXES, pairs)  31.9 us
  transfers between devices with their start and end apart: 40, of which 13 were waited for; matrix products, arithmetic and copies ran while one was open for 20% of the time, Pallas kernels for 38%

profile of v2, /device:TPU:0, one launch (start us, length us, event | category | flops | bytes accessed | tf_op | source)
XLA Modules:
  0.0 864.4 jit_solution(13725923375446773746)
XLA Ops:
  7.4 66.7 %all_to_all.20 = bf16[8,128,1280]{2,1,0:T(8,128)(2,1)S(1)} all-to-all(bf16[8,128,1280]{2,1,0:T(8,128)(2,1)S(1)} %maximum_select_fusion), channel_id=1, replica_groups=mesh['seq'=8,'rows'=4] {'seq'}, dimensions={0} | all-to-all | bytes 5242880 | tf_op jit(solution)/shard_map/all_to_all | solution.py:974
  80.2 10.3 %gather_pairs.2 = bf16[1280,1920]{1,0:T(8,128)(2,1)} custom-call(s32[1]{0:T(128)} %bitcast.10.core_ref, bf16[1280,3840]{1,0:T(8,128)(2,1)} %from_ref.3), custom_call_target="tpu_custom_call" | custom-call | bytes 9830400 | tf_op jit(solution)/shard_map/gather_pairs/pallas_call | solution.py:177
  92.5 3.9 maximum_select_fusion.1
  96.4 4.7 all-to-all-start.1
  101.1 16.5 %convolution_convert_fusion.q_ref.k_ref.v_ref = bf16[2048,1920]{1,0:T(8,128)(2,1)} fusion(bf16[1280,1920]{1,0:T(8,128)(2,1)} %gather_pairs.2, bf16[1024,1280]{1,0:T(8,128)(2,1)} %collective-permute-done.2, bf16[1024,1280]{1,0:T(8,128)(2,1)} %fusion.10), kind=kOutput, calls=%fused_computation.1 | convolution fusion | flops 10080747520 | bytes 18022400 | tf_op jit(solution)/shard_map/dot_general | solution.py:26
  117.6 81.4 %attend.1 = (bf16[2048,640]{1,0:T(8,128)(2,1)}, f32[5,2,2048]{2,1,0:T(2,128)}) custom-call(s32[2048,1]{1,0:T(8,128)} %bitcast.175, s32[1,2048]{1,0:T(1,128)} %bitcast.200, bf16[2048,1920]{1,0:T(8,128)(2,1)} %convolution_convert_fusion.q_ref.k_ref.v_ref, bf16[2048,1920]{1,0:T(8,128)(2,1)} %convolution_convert_fusion.q_ref.k_ref.v_ref, ...), custom_call_target="tpu_custom_call" | custom-call | flops 42949672960 | bytes 10485760 | tf_op jit(solution)/shard_map/attend/pallas_call | solution.py:64
  203.5 4.2 fusion.31
  207.7 5.8 fusion.16.middle_ref
  213.6 131.9 %feed.1 = (bf16[1024,1280]{1,0:T(8,128)(2,1)}, f32[1024,1280]{1,0:T(8,128)}, bf16[1024,1280]{1,0:T(8,128)(2,1)}, bf16[2560,640]{1,0:T(8,128)(2,1)}, bf16[640,2560]{1,0:T(8,128)(2,1)}) custom-call(f32[1024,1280]{1,0:T(8,128)} %fusion.16.middle_ref, bf16[1024,1280]{1,0:T(8,128)(2,1)} %bitcast.14.cot_ref, f32[1,1280]{1,0:T(1,128)} %reshape.492.gain_ref, ...), custom_call_target="tpu_custom_call" | custom-call | flops 80530636800 | bytes 60293120 | tf_op jit(solution)/shard_map/feed/pallas_call | solution.py:733
  345.6 5.7 convolution_convert_fusion.3
  351.7 5.7 all-to-all-start.2
  357.4 6.5 add_split.23
  363.9 6.4 add_split.24
  370.3 5.6 convolution_convert_fusion.4
  377.1 9.9 %add_split.25 = (bf16[8,80,640]{2,1,0:T(8,128)(2,1)}, bf16[8,80,640]{2,1,0:T(8,128)(2,1)}) custom-call(s32[1]{0:T(128)} %bitcast.25.bit_ref, bf16[8,2,80,640]{3,2,1,0:T(8,128)(2,1)} %bitcast.173, bf16[8,2,80,640]{3,2,1,0:T(8,128)(2,1)} %bitcast.170), custom_call_target="tpu_custom_call" | custom-call | flops 819200 | bytes 4915200 | tf_op jit(solution)/shard_map/add_split/pallas_call | solution.py:832
  387.0 8.8 %fusion.24.do_ref = bf16[2048,640]{1,0:T(8,128)(2,1)} fusion(bf16[1024,1280]{1,0:T(8,128)(2,1)} %collective-permute-done.6, bf16[1024,1280]{1,0:T(8,128)(2,1)} %get-tuple-element.83, bf16[1280,1280]{1,0:T(8,128)(2,1)} %param.16, s32[]{:T(128)S(6)} %select_n.266), kind=kOutput, calls=%fused_computation.37 | convolution fusion | flops 3367239680 | bytes 9502724 | tf_op jit(solution)/shard_map/dot_general | solution.py:26
  395.8 27.0 %attend_back.5 = bf16[2048,384]{1,0:T(8,128)(2,1)} custom-call(s32[2048,1]{1,0:T(8,128)} %bitcast.176, s32[1,2048]{1,0:T(1,128)} %bitcast.201, bf16[2048,1920]{1,0:T(8,128)(2,1)} %convolution_convert_fusion.q_ref.k_ref.v_ref, bf16[2048,1920]{1,0:T(8,128)(2,1)} %convolution_convert_fusion.q_ref.k_ref.v_ref, ...), custom_call_target="tpu_custom_call" | custom-call | flops 21474836480 | bytes 4194304 | tf_op jit(solution)/shard_map/attend_back/pallas_call | solution.py:140
  426.8 26.9 %attend_back.6 = bf16[2048,384]{1,0:T(8,128)(2,1)} custom-call(s32[2048,1]{1,0:T(8,128)} %bitcast.177, s32[1,2048]{1,0:T(1,128)} %bitcast.202, bf16[2048,1920]{1,0:T(8,128)(2,1)} %convolution_convert_fusion.q_ref.k_ref.v_ref, bf16[2048,1920]{1,0:T(8,128)(2,1)} %convolution_convert_fusion.q_ref.k_ref.v_ref, ...), custom_call_target="tpu_custom_call" | custom-call | flops 21474836480 | bytes 4194304 | tf_op jit(solution)/shard_map/attend_back/pallas_call | solution.py:140
  457.9 21.9 %collective-permute-done.12 = bf16[640,640]{1,0:T(8,128)(2,1)} collective-permute-done((bf16[640,640]{1,0:T(8,128)(2,1)}, bf16[640,640]{1,0:T(8,128)(2,1)}, u32[]{:S(2)}, u32[]{:S(2)}) %collective-permute-start.12) | collective-permute-done | bytes 819232 | tf_op jit(solution)/shard_map/ppermute | solution.py:862
  479.8 3.7 add_split.30
  484.7 4.4 add_split.26
  490.3 4.4 add_split.27
  494.6 27.3 %attend_back.7 = bf16[2048,384]{1,0:T(8,128)(2,1)} custom-call(s32[2048,1]{1,0:T(8,128)} %bitcast.178, s32[1,2048]{1,0:T(1,128)} %bitcast.203, bf16[2048,1920]{1,0:T(8,128)(2,1)} %convolution_convert_fusion.q_ref.k_ref.v_ref, bf16[2048,1920]{1,0:T(8,128)(2,1)} %convolution_convert_fusion.q_ref.k_ref.v_ref, ...), custom_call_target="tpu_custom_call" | custom-call | flops 21474836480 | bytes 4194304 | tf_op jit(solution)/shard_map/attend_back/pallas_call | solution.py:140
  521.9 27.1 %attend_back.8 = bf16[2048,384]{1,0:T(8,128)(2,1)} custom-call(s32[2048,1]{1,0:T(8,128)} %bitcast.179, s32[1,2048]{1,0:T(1,128)} %bitcast.204, bf16[2048,1920]{1,0:T(8,128)(2,1)} %convolution_convert_fusion.q_ref.k_ref.v_ref, bf16[2048,1920]{1,0:T(8,128)(2,1)} %convolution_convert_fusion.q_ref.k_ref.v_ref, ...), custom_call_target="tpu_custom_call" | custom-call | flops 21474836480 | bytes 4194304 | tf_op jit(solution)/shard_map/attend_back/pallas_call | solution.py:140
  552.4 5.0 fusion.60
  557.6 12.9 %collective-permute-done.10 = bf16[640,640]{1,0:T(8,128)(2,1)} collective-permute-done((bf16[640,640]{1,0:T(8,128)(2,1)}, bf16[640,640]{1,0:T(8,128)(2,1)}, u32[]{:S(2)}, u32[]{:S(2)}) %collective-permute-start.10) | collective-permute-done | bytes 819232 | tf_op jit(solution)/shard_map/ppermute | solution.py:862
  573.0 12.5 %collective-permute-done.11 = bf16[160,2560]{1,0:T(8,128)(2,1)} collective-permute-done((bf16[160,2560]{1,0:T(8,128)(2,1)}, bf16[160,2560]{1,0:T(8,128)(2,1)}, u32[]{:S(2)}, u32[]{:S(2)}) %collective-permute-start.11) | collective-permute-done | bytes 819232 | tf_op jit(solution)/shard_map/ppermute | solution.py:862
  588.1 26.8 %attend_back.9 = bf16[2048,384]{1,0:T(8,128)(2,1)} custom-call(s32[2048,1]{1,0:T(8,128)} %bitcast.180, s32[1,2048]{1,0:T(1,128)} %bitcast.205, bf16[2048,1920]{1,0:T(8,128)(2,1)} %convolution_convert_fusion.q_ref.k_ref.v_ref, bf16[2048,1920]{1,0:T(8,128)(2,1)} %convolution_convert_fusion.q_ref.k_ref.v_ref, ...), custom_call_target="tpu_custom_call" | custom-call | flops 21474836480 | bytes 4194304 | tf_op jit(solution)/shard_map/attend_back/pallas_call | solution.py:140
  618.5 10.2 %gather_pairs.3 = bf16[1280,1920]{1,0:T(8,128)(2,1)} custom-call(s32[1]{0:T(128)} %bitcast.55.core_ref, bf16[1280,3840]{1,0:T(8,128)(2,1)} %from_ref.3), custom_call_target="tpu_custom_call" | custom-call | bytes 9830400 | tf_op jit(solution)/shard_map/gather_pairs/pallas_call | solution.py:177
  628.7 10.4 %fusion.17 = f32[1024,1280]{1,0:T(8,128)} fusion(bf16[1280,1920]{1,0:T(8,128)(2,1)} %gather_pairs.2, bf16[1024,768]{1,0:T(8,128)(2,1)} %get-tuple-element.157, bf16[1024,1152]{1,0:T(8,128)(2,1)} %get-tuple-element.155), kind=kOutput, calls=%fused_computation.26 | convolution fusion | flops 5041029120 | bytes 14090240 | tf_op jit(solution)/shard_map/dot_general | solution.py:26
  639.2 10.5 %fusion.59 = (f32[1024]{0:T(1024)S(1)}, f32[1024]{0:T(1024)S(1)}, f32[1024,1280]{1,0:T(8,128)S(1)}) fusion(f32[1024]{0:T(1024)S(1)} %copy-done.26, f32[1024]{0:T(1024)S(1)} %copy-done.24, bf16[8,128,1280]{2,1,0:T(8,128)(2,1)S(1)} %copy-done.1, f32[1280]{0:T(1024)S(1)} %copy-done.30, f32[1024,1280]{1,0:T(8,128)} %fusion.17, ...), kind=kOutput, calls=%fused_computation.122 | convolution fusion | flops 5051512832 | bytes 21976064 | tf_op jit(solution)/shard_map/dot_general | solution.py:26
  652.6 4.8 all-to-all-start.3
  657.4 11.5 %convolution_convert_fusion.1 = bf16[1280,1152]{1,0:T(8,128)(2,1)} fusion(bf16[2048,1152]{1,0:T(8,128)(2,1)} %constant_dynamic-update-slice_fusion, bf16[1024,1280]{1,0:T(8,128)(2,1)} %collective-permute-done.2, bf16[1024,1280]{1,0:T(8,128)(2,1)} %fusion.10), kind=kOutput, calls=%fused_computation.2 | convolution fusion | flops 6051758080 | bytes 12910592 | tf_op jit(solution)/shard_map/dot_general | solution.py:26
  668.9 9.9 %add_split.31 = (bf16[8,80,1152]{2,1,0:T(8,128)(2,1)}, bf16[8,80,1152]{2,1,0:T(8,128)(2,1)}) custom-call(s32[1]{0:T(128)} %bitcast.25.bit_ref, bf16[8,2,80,1152]{3,2,1,0:T(8,128)(2,1)} %bitcast.160), custom_call_target="tpu_custom_call" | custom-call | flops 1474560 | bytes 8847360 | tf_op jit(solution)/shard_map/add_split/pallas_call | solution.py:832
  679.4 8.1 convolution_convert_fusion.2
  687.5 9.5 %add_split.36 = (bf16[8,80,768]{2,1,0:T(8,128)(2,1)}, bf16[8,80,768]{2,1,0:T(8,128)(2,1)}) custom-call(s32[1]{0:T(128)} %bitcast.25.bit_ref, bf16[8,2,80,768]{3,2,1,0:T(8,128)(2,1)} %bitcast.165), custom_call_target="tpu_custom_call" | custom-call | flops 983040 | bytes 5898240 | tf_op jit(solution)/shard_map/add_split/pallas_call | solution.py:832
  703.3 10.8 %collective-permute-done.16 = bf16[640,1152]{1,0:T(8,128)(2,1)} collective-permute-done((bf16[640,1152]{1,0:T(8,128)(2,1)}, bf16[640,1152]{1,0:T(8,128)(2,1)}, u32[]{:S(2)}, u32[]{:S(2)}) %collective-permute-start.16) | collective-permute-done | bytes 1474592 | tf_op jit(solution)/shard_map/ppermute | solution.py:862
  714.2 4.2 add_split.32
  722.8 10.0 %collective-permute-done.26 = bf16[320,640]{1,0:T(8,128)(2,1)} collective-permute-done((bf16[320,640]{1,0:T(8,128)(2,1)}, bf16[320,640]{1,0:T(8,128)(2,1)}, u32[]{:S(2)}, u32[]{:S(2)}) %collective-permute-start.26) | collective-permute-done | bytes 409632 | tf_op jit(solution)/shard_map/ppermute | solution.py:862
  739.7 3.9 add_split.37
  754.2 6.0 collective-permute-done.34.refs_1_
  771.2 3.7 add_split.33
  779.7 3.8 add_split.38
  787.0 5.2 collective-permute-done.22
  802.5 5.6 collective-permute-done.23.refs_1_
  819.1 4.2 copy.74
  823.3 4.2 reshape.560
  844.8 4.0 fusion.28
  (207 shorter events, 148.5 us)
Async XLA Ops:
  3.6 3.3 collective-permute-start
  74.1 133.6 %copy-start = (bf16[8,128,1280]{2,1,0:T(8,128)(2,1)}, bf16[8,128,1280]{2,1,0:T(8,128)(2,1)S(1)}, u32[]{:S(2)}) copy-start(bf16[8,128,1280]{2,1,0:T(8,128)(2,1)S(1)} %all_to_all.20) | copy-start | bytes 7864324
  77.8 23.4 %collective-permute-start.2 = (bf16[1024,1280]{1,0:T(8,128)(2,1)}, bf16[1024,1280]{1,0:T(8,128)(2,1)}, u32[]{:S(2)}, u32[]{:S(2)}) collective-permute-start(bf16[1024,1280]{1,0:T(8,128)(2,1)} %fusion.10), channel_id=1, source_target_pairs={{0,1},{1,0},{2,3},{3,2},{4,5},{5,4},{6,7},{7,6},{8,9},{9,8},{10,11... | collective-permute-start | bytes 7864328 | tf_op jit(solution)/shard_map/ppermute | solution.py:862
  79.5 13.1 %collective-permute-start.4 = (bf16[4,128,1280]{2,1,0:T(8,128)(2,1)}, bf16[4,128,1280]{2,1,0:T(8,128)(2,1)}, u32[]{:S(2)}, u32[]{:S(2)}) collective-permute-start(bf16[4,128,1280]{2,1,0:T(8,128)(2,1)} %get-tuple-element.165), channel_id=1, source_target_pairs={{0,1},{1,0},{2,3},{3,2},{4,5},{5,4},{6,7},{7,6},{8,9},{9,8},{10,11... | collective-permute-start | bytes 3932168 | tf_op jit(solution)/shard_map/ppermute | solution.py:862
  80.0 10.4 %collective-permute-start.1 = (s32[4,2048]{1,0:T(4,128)S(1)}, s32[4,2048]{1,0:T(4,128)S(1)}, u32[]{:S(2)}, u32[]{:S(2)}) collective-permute-start(s32[4,2048]{1,0:T(4,128)S(1)} %fusion.38), channel_id=1, source_target_pairs={{0,1},{1,0},{2,3},{3,2},{4,5},{5,4},{6,7},{7,6},{8,9},{9,8},{10,11... | collective-permute-start | bytes 98312 | tf_op jit(solution)/shard_map/ppermute | solution.py:862
  96.4 117.1 %all-to-all-start.1 = ((bf16[8,128,1280]{2,1,0:T(8,128)(2,1)}), bf16[8,128,1280]{2,1,0:T(8,128)(2,1)}, u32[]{:S(2)}, u32[]{:S(2)}) async-start(bf16[8,128,1280]{2,1,0:T(8,128)(2,1)} %maximum_select_fusion.1), calls=%async_computation.1 | async-start | bytes 5242880 | tf_op jit(solution)/shard_map/all_to_all | solution.py:974
  202.5 5.3 collective-permute-start.3
  213.6 132.0 %copy-start.14 = (bf16[1024,640]{1,0:T(8,128)(2,1)S(1)}, bf16[1024,640]{1,0:T(8,128)(2,1)}, u32[]{:S(2)}) copy-start(bf16[1024,640]{1,0:T(8,128)(2,1)} %get-tuple-element.160) | copy-start | bytes 3932164
  345.5 41.5 %collective-permute-start.6 = (bf16[1024,1280]{1,0:T(8,128)(2,1)}, bf16[1024,1280]{1,0:T(8,128)(2,1)}, u32[]{:S(2)}, u32[]{:S(2)}) collective-permute-start(bf16[1024,1280]{1,0:T(8,128)(2,1)} %get-tuple-element.83), channel_id=1, source_target_pairs={{0,1},{1,0},{2,3},{3,2},{4,5},{5,4},{6,7},{7,6},{8,9},{9,8},{10,11... | collective-permute-start | bytes 7864328 | tf_op jit(solution)/shard_map/ppermute | solution.py:862
  351.3 24.7 %collective-permute-start.7 = (bf16[1280,640]{1,0:T(8,128)(2,1)}, bf16[1280,640]{1,0:T(8,128)(2,1)S(1)}, u32[]{:S(2)}, u32[]{:S(2)}) collective-permute-start(bf16[1280,640]{1,0:T(8,128)(2,1)} %convolution_convert_fusion.3), channel_id=1, source_target_pairs={{0,1},{1,0},{2,3},{3,2},{4,5},{5,4},{6,7},{7,6},{8,9},{9,8},{10,11... | collective-permute-start | bytes 4915208 | tf_op jit(solution)/shard_map/ppermute | solution.py:862
  351.7 300.9 %all-to-all-start.2 = ((bf16[8,128,1280]{2,1,0:T(8,128)(2,1)}), bf16[8,128,1280]{2,1,0:T(8,128)(2,1)}, u32[]{:S(2)}, u32[]{:S(2)}) async-start(bf16[8,128,1280]{2,1,0:T(8,128)(2,1)} %bitcast.15), calls=%async_computation.2 | async-start | bytes 5242880 | tf_op jit(solution)/shard_map/all_to_all | solution.py:977
  422.8 60.7 %collective-permute-start.8 = (bf16[1280,640]{1,0:T(8,128)(2,1)}, bf16[1280,640]{1,0:T(8,128)(2,1)S(1)}, u32[]{:S(2)}, u32[]{:S(2)}) collective-permute-start(bf16[1280,640]{1,0:T(8,128)(2,1)} %bitcast.23), channel_id=1, source_target_pairs={{0,4},{1,5},{2,6},{3,7},{4,0},{5,1},{6,2},{7,3},{8,12},{9,13},{10,... | collective-permute-start | bytes 4915208 | tf_op jit(solution)/shard_map/ppermute | solution.py:862
  424.8 64.3 %collective-permute-start.9 = (bf16[320,2560]{1,0:T(8,128)(2,1)}, bf16[320,2560]{1,0:T(8,128)(2,1)S(1)}, u32[]{:S(2)}, u32[]{:S(2)}) collective-permute-start(bf16[320,2560]{1,0:T(8,128)(2,1)} %bitcast.206), channel_id=1, source_target_pairs={{0,2},{1,3},{2,0},{3,1},{4,6},{5,7},{6,4},{7,5},{8,10},{9,11},{10,... | collective-permute-start | bytes 4915208 | tf_op jit(solution)/shard_map/ppermute | solution.py:862
  425.4 54.4 %collective-permute-start.12 = (bf16[640,640]{1,0:T(8,128)(2,1)}, bf16[640,640]{1,0:T(8,128)(2,1)}, u32[]{:S(2)}, u32[]{:S(2)}) collective-permute-start(bf16[640,640]{1,0:T(8,128)(2,1)} %bitcast.209), channel_id=1, source_target_pairs={{0,2},{1,3},{2,0},{3,1},{4,6},{5,7},{6,4},{7,5},{8,10},{9,11},{10,... | collective-permute-start | bytes 2457608 | tf_op jit(solution)/shard_map/ppermute | solution.py:862
  521.9 29.2 %copy-start.12 = (bf16[2048,384]{1,0:T(8,128)(2,1)S(1)}, bf16[2048,384]{1,0:T(8,128)(2,1)}, u32[]{:S(2)}) copy-start(bf16[2048,384]{1,0:T(8,128)(2,1)} %attend_back.7) | copy-start | bytes 4718596
  549.1 21.5 %collective-permute-start.10 = (bf16[640,640]{1,0:T(8,128)(2,1)}, bf16[640,640]{1,0:T(8,128)(2,1)}, u32[]{:S(2)}, u32[]{:S(2)}) collective-permute-start(bf16[640,640]{1,0:T(8,128)(2,1)} %bitcast.36), channel_id=1, source_target_pairs={{0,8},{1,9},{2,10},{3,11},{4,12},{5,13},{6,14},{7,15},{8,0},{9,1},... | collective-permute-start | bytes 2457608 | tf_op jit(solution)/shard_map/ppermute | solution.py:862
  550.5 35.0 %collective-permute-start.11 = (bf16[160,2560]{1,0:T(8,128)(2,1)}, bf16[160,2560]{1,0:T(8,128)(2,1)}, u32[]{:S(2)}, u32[]{:S(2)}) collective-permute-start(bf16[160,2560]{1,0:T(8,128)(2,1)} %bitcast.40), channel_id=1, source_target_pairs={{0,8},{1,9},{2,10},{3,11},{4,12},{5,13},{6,14},{7,15},{8,0},{9,1},... | collective-permute-start | bytes 2457608 | tf_op jit(solution)/shard_map/ppermute | solution.py:862
  557.5 81.7 %collective-permute-start.13 = (bf16[1024,1152]{1,0:T(8,128)(2,1)}, bf16[1024,1152]{1,0:T(8,128)(2,1)}, u32[]{:S(2)}, u32[]{:S(2)}) collective-permute-start(bf16[1024,1152]{1,0:T(8,128)(2,1)} %get-tuple-element.154), channel_id=1, source_target_pairs={{0,1},{1,0},{2,3},{3,2},{4,5},{5,4},{6,7},{7,6},{8,9},{9,8},{10,11... | collective-permute-start | bytes 7077896 | tf_op jit(solution)/shard_map/ppermute | solution.py:862
  618.5 20.6 %collective-permute-start.14 = (bf16[1024,768]{1,0:T(8,128)(2,1)}, bf16[1024,768]{1,0:T(8,128)(2,1)}, u32[]{:S(2)}, u32[]{:S(2)}) collective-permute-start(bf16[1024,768]{1,0:T(8,128)(2,1)} %get-tuple-element.156), channel_id=1, source_target_pairs={{0,1},{1,0},{2,3},{3,2},{4,5},{5,4},{6,7},{7,6},{8,9},{9,8},{10,11... | collective-permute-start | bytes 4718600 | tf_op jit(solution)/shard_map/ppermute | solution.py:862
  628.7 10.5 %copy-start.26 = (f32[1024]{0:T(1024)S(1)}, f32[1024]{0:T(1024)}, u32[]{:S(2)}) copy-start(f32[1024]{0:T(1024)} %copy-done.25) | copy-start | bytes 12292
  628.7 10.5 %copy-start.30 = (f32[1280]{0:T(1024)S(1)}, f32[1280]{0:T(1024)}, u32[]{:S(2)}) copy-start(f32[1280]{0:T(1024)} %param.14) | copy-start | bytes 15364
  628.7 21.0 %slice-start = ((s8[5242880]{0:T(1024)(128)(4,1)}), s8[4194304]{0:T(1024)(128)(4,1)S(1)}, s32[]{:S(2)}) async-start(s8[5242880]{0:T(1024)(128)(4,1)} %bitcast.156), calls=%async_computation.4 | async-start | bytes 8388608
  639.1 10.6 %slice-start.1 = ((s8[5242880]{0:T(1024)(128)(4,1)}), s8[1048576]{0:T(1024)(128)(4,1)S(1)}, s32[]{:S(2)}) async-start(s8[5242880]{0:T(1024)(128)(4,1)} %bitcast.156), calls=%async_computation.5 | async-start | bytes 2097152
  652.6 185.0 %all-to-all-start.3 = ((bf16[8,128,1280]{2,1,0:T(8,128)(2,1)}), bf16[8,128,1280]{2,1,0:T(8,128)(2,1)}, u32[]{:S(2)}, u32[]{:S(2)}) async-start(bf16[8,128,1280]{2,1,0:T(8,128)(2,1)} %bitcast.56), calls=%async_computation.3 | async-start | bytes 5242880 | tf_op jit(solution)/shard_map/all_to_all | solution.py:977
  678.8 35.4 %collective-permute-start.16 = (bf16[640,1152]{1,0:T(8,128)(2,1)}, bf16[640,1152]{1,0:T(8,128)(2,1)}, u32[]{:S(2)}, u32[]{:S(2)}) collective-permute-start(bf16[640,1152]{1,0:T(8,128)(2,1)} %bitcast.207), channel_id=1, source_target_pairs={{0,2},{1,3},{2,0},{3,1},{4,6},{5,7},{6,4},{7,5},{8,10},{9,11},{10,... | collective-permute-start | bytes 4423688 | tf_op jit(solution)/shard_map/ppermute | solution.py:862
  697.0 41.8 %collective-permute-start.20 = (bf16[640,768]{1,0:T(8,128)(2,1)}, bf16[640,768]{1,0:T(8,128)(2,1)S(1)}, u32[]{:S(2)}, u32[]{:S(2)}) collective-permute-start(bf16[640,768]{1,0:T(8,128)(2,1)} %bitcast.208), channel_id=1, source_target_pairs={{0,2},{1,3},{2,0},{3,1},{4,6},{5,7},{6,4},{7,5},{8,10},{9,11},{10,... | collective-permute-start | bytes 2949128 | tf_op jit(solution)/shard_map/ppermute | solution.py:862
  698.4 34.4 %collective-permute-start.26 = (bf16[320,640]{1,0:T(8,128)(2,1)}, bf16[320,640]{1,0:T(8,128)(2,1)}, u32[]{:S(2)}, u32[]{:S(2)}) collective-permute-start(bf16[320,640]{1,0:T(8,128)(2,1)} %bitcast.213), channel_id=1, source_target_pairs={{0,8},{1,9},{2,10},{3,11},{4,12},{5,13},{6,14},{7,15},{8,0},{9,1},... | collective-permute-start | bytes 1228808 | tf_op jit(solution)/shard_map/ppermute | solution.py:862
  703.3 95.8 %collective-permute-start.5 = (bf16[4,128,1280]{2,1,0:T(8,128)(2,1)}, bf16[4,128,1280]{2,1,0:T(8,128)(2,1)}, u32[]{:S(2)}, u32[]{:S(2)}) collective-permute-start(bf16[4,128,1280]{2,1,0:T(8,128)(2,1)} %get-tuple-element.163), channel_id=1, source_target_pairs={{0,1},{1,0},{2,3},{3,2},{4,5},{5,4},{6,7},{7,6},{8,9},{9,8},{10,11... | collective-permute-start | bytes 3932168 | tf_op jit(solution)/shard_map/ppermute | solution.py:862
  718.4 50.0 %collective-permute-start.17 = (bf16[320,1152]{1,0:T(8,128)(2,1)}, bf16[320,1152]{1,0:T(8,128)(2,1)S(1)}, u32[]{:S(2)}, u32[]{:S(2)}) collective-permute-start(bf16[320,1152]{1,0:T(8,128)(2,1)} %bitcast.210), channel_id=1, source_target_pairs={{0,8},{1,9},{2,10},{3,11},{4,12},{5,13},{6,14},{7,15},{8,0},{9,1},... | collective-permute-start | bytes 2211848 | tf_op jit(solution)/shard_map/ppermute | solution.py:862
  720.4 26.1 %collective-permute-start.31 = (bf16[80,2560]{1,0:T(8,128)(2,1)}, bf16[80,2560]{1,0:T(8,128)(2,1)}, u32[]{:S(2)}, u32[]{:S(2)}) collective-permute-start(bf16[80,2560]{1,0:T(8,128)(2,1)} %bitcast.49), channel_id=1, source_target_pairs={{0,16},{1,17},{2,18},{3,19},{4,20},{5,21},{6,22},{7,23},{8,24},{9,... | collective-permute-start | bytes 1228808 | tf_op jit(solution)/shard_map/ppermute | solution.py:862
  732.8 27.4 %collective-permute-start.34 = (bf16[320,640]{1,0:T(8,128)(2,1)}, bf16[320,640]{1,0:T(8,128)(2,1)S(1)}, u32[]{:S(2)}, u32[]{:S(2)}) collective-permute-start(bf16[320,640]{1,0:T(8,128)(2,1)} %bitcast.212), channel_id=1, source_target_pairs={{0,16},{1,17},{2,18},{3,19},{4,20},{5,21},{6,22},{7,23},{8,24},{9,... | collective-permute-start | bytes 1228808 | tf_op jit(solution)/shard_map/ppermute | solution.py:862
  738.8 13.1 %collective-permute-start.27 = (bf16[160,640]{1,0:T(8,128)(2,1)}, bf16[160,640]{1,0:T(8,128)(2,1)}, u32[]{:S(2)}, u32[]{:S(2)}) collective-permute-start(bf16[160,640]{1,0:T(8,128)(2,1)} %bitcast.216), channel_id=1, source_target_pairs={{0,4},{1,5},{2,6},{3,7},{4,0},{5,1},{6,2},{7,3},{8,12},{9,13},{10,... | collective-permute-start | bytes 614408 | tf_op jit(solution)/shard_map/ppermute | solution.py:862
  746.5 33.2 %collective-permute-start.21 = (bf16[320,768]{1,0:T(8,128)(2,1)}, bf16[320,768]{1,0:T(8,128)(2,1)}, u32[]{:S(2)}, u32[]{:S(2)}) collective-permute-start(bf16[320,768]{1,0:T(8,128)(2,1)} %bitcast.211), channel_id=1, source_target_pairs={{0,8},{1,9},{2,10},{3,11},{4,12},{5,13},{6,14},{7,15},{8,0},{9,1},... | collective-permute-start | bytes 1474568 | tf_op jit(solution)/shard_map/ppermute | solution.py:862
  751.9 26.4 %collective-permute-start.32 = (bf16[80,2560]{1,0:T(8,128)(2,1)}, bf16[80,2560]{1,0:T(8,128)(2,1)}, u32[]{:S(2)}, u32[]{:S(2)}) collective-permute-start(bf16[80,2560]{1,0:T(8,128)(2,1)} %add_split.44), channel_id=1, source_target_pairs={{0,2},{1,3},{2,0},{3,1},{4,6},{5,7},{6,4},{7,5},{8,10},{9,11},{10,... | collective-permute-start | bytes 1228808 | tf_op jit(solution)/shard_map/ppermute | solution.py:862
  760.2 6.0 collective-permute-start.28
  766.2 18.3 %collective-permute-start.35 = (bf16[10,1,32,640]{3,2,0,1:T(8,128)(2,1)}, bf16[10,1,32,640]{3,2,0,1:T(8,128)(2,1)}, u32[]{:S(2)}, u32[]{:S(2)}) collective-permute-start(bf16[10,1,32,640]{3,2,0,1:T(8,128)(2,1)} %bitcast.166), channel_id=1, source_target_pairs={{0,2},{1,3},{2,0},{3,1},{4,6},{5,7},{6,4},{7,5},{8,10},{9,11},{10,... | collective-permute-start | bytes 1228808 | tf_op jit(solution)/shard_map/ppermute | solution.py:862
  768.4 7.7 collective-permute-start.29
  776.1 18.0 %collective-permute-start.18 = (bf16[160,1152]{1,0:T(8,128)(2,1)}, bf16[160,1152]{1,0:T(8,128)(2,1)}, u32[]{:S(2)}, u32[]{:S(2)}) collective-permute-start(bf16[160,1152]{1,0:T(8,128)(2,1)} %bitcast.214), channel_id=1, source_target_pairs={{0,4},{1,5},{2,6},{3,7},{4,0},{5,1},{6,2},{7,3},{8,12},{9,13},{10,... | collective-permute-start | bytes 1105928 | tf_op jit(solution)/shard_map/ppermute | solution.py:862
  778.3 38.3 %collective-permute-start.30 = (bf16[160,640]{1,0:T(8,128)(2,1)}, bf16[160,640]{1,0:T(8,128)(2,1)}, u32[]{:S(2)}, u32[]{:S(2)}) collective-permute-start(bf16[160,640]{1,0:T(8,128)(2,1)} %maximum_select_fusion.14), channel_id=1, source_target_pairs={{0,1},{1,0},{2,3},{3,2},{4,5},{5,4},{6,7},{7,6},{8,9},{9,8},{10,11... | collective-permute-start | bytes 614408 | tf_op jit(solution)/shard_map/ppermute | solution.py:862
  783.5 8.7 %collective-permute-start.22 = (bf16[160,768]{1,0:T(8,128)(2,1)}, bf16[160,768]{1,0:T(8,128)(2,1)}, u32[]{:S(2)}, u32[]{:S(2)}) collective-permute-start(bf16[160,768]{1,0:T(8,128)(2,1)} %bitcast.215), channel_id=1, source_target_pairs={{0,4},{1,5},{2,6},{3,7},{4,0},{5,1},{6,2},{7,3},{8,12},{9,13},{10,... | collective-permute-start | bytes 737288 | tf_op jit(solution)/shard_map/ppermute | solution.py:862
  784.5 34.4 %collective-permute-start.33 = (bf16[160,10,1,256]{3,0,2,1:T(8,128)(2,1)S(1)}, bf16[160,10,1,256]{3,0,2,1:T(8,128)(2,1)S(1)}, u32[]{:S(2)}, u32[]{:S(2)}) collective-permute-start(bf16[160,10,1,256]{3,0,2,1:T(8,128)(2,1)S(1)} %maximum_select_fusion.9), channel_id=1, source_target_pairs={{0,1},{1,0},{2,3},{3,2},{4,5},{5,4},{6,7},{7,6},{8,9},{9,8},{10,11... | collective-permute-start | bytes 2457608 | tf_op jit(solution)/shard_map/ppermute | solution.py:862
  792.3 52.5 %collective-permute-start.36 = (bf16[640,640]{1,0:T(8,128)(2,1)}, bf16[640,640]{1,0:T(8,128)(2,1)}, u32[]{:S(2)}, u32[]{:S(2)}) collective-permute-start(bf16[640,640]{1,0:T(8,128)(2,1)} %bitcast.98), channel_id=1, source_target_pairs={{0,1},{1,0},{2,3},{3,2},{4,5},{5,4},{6,7},{7,6},{8,9},{9,8},{10,11... | collective-permute-start | bytes 2457608 | tf_op jit(solution)/shard_map/ppermute | solution.py:862
  794.1 14.0 %collective-permute-start.23 = (bf16[80,768]{1,0:T(8,128)(2,1)}, bf16[80,768]{1,0:T(8,128)(2,1)S(1)}, u32[]{:S(2)}, u32[]{:S(2)}) collective-permute-start(bf16[80,768]{1,0:T(8,128)(2,1)} %bitcast.218), channel_id=1, source_target_pairs={{0,16},{1,17},{2,18},{3,19},{4,20},{5,21},{6,22},{7,23},{8,24},{9,... | collective-permute-start | bytes 368648 | tf_op jit(solution)/shard_map/ppermute | solution.py:862
  799.1 12.7 %collective-permute-start.19 = (bf16[80,1152]{1,0:T(8,128)(2,1)}, bf16[80,1152]{1,0:T(8,128)(2,1)S(1)}, u32[]{:S(2)}, u32[]{:S(2)}) collective-permute-start(bf16[80,1152]{1,0:T(8,128)(2,1)} %bitcast.217), channel_id=1, source_target_pairs={{0,16},{1,17},{2,18},{3,19},{4,20},{5,21},{6,22},{7,23},{8,24},{9,... | collective-permute-start | bytes 552968 | tf_op jit(solution)/shard_map/ppermute | solution.py:862
  816.0 13.6 %collective-permute-start.24 = (bf16[80,1920]{1,0:T(8,128)(2,1)}, bf16[80,1920]{1,0:T(8,128)(2,1)}, u32[]{:S(2)}, u32[]{:S(2)}) collective-permute-start(bf16[80,1920]{1,0:T(8,128)(2,1)} %pad_maximum_fusion.4), channel_id=1, source_target_pairs={{0,2},{1,3},{2,0},{3,1},{4,6},{5,7},{6,4},{7,5},{8,10},{9,11},{10,... | collective-permute-start | bytes 921608 | tf_op jit(solution)/shard_map/ppermute | solution.py:862
  827.5 14.0 %copy-start.2 = (f32[160,5120]{1,0:T(8,128)}, f32[160,5120]{1,0:T(8,128)S(1)}, u32[]{:S(2)}) copy-start(f32[160,5120]{1,0:T(8,128)S(1)} %reshape.560) | copy-start | bytes 9830404
  837.5 12.0 %collective-permute-start.25 = (bf16[160,3,640]{2,0,1:T(8,128)(2,1)}, bf16[160,3,640]{2,0,1:T(8,128)(2,1)}, u32[]{:S(2)}, u32[]{:S(2)}) collective-permute-start(bf16[160,3,640]{2,0,1:T(8,128)(2,1)} %reshape.550), channel_id=1, source_target_pairs={{0,1},{1,0},{2,3},{3,2},{4,5},{5,4},{6,7},{7,6},{8,9},{9,8},{10,11... | collective-permute-start | bytes 1843208 | tf_op jit(solution)/shard_map/ppermute | solution.py:862
  841.0 19.8 %collective-permute-start.15 = (bf16[4,128,1280]{2,1,0:T(8,128)(2,1)}, bf16[4,128,1280]{2,1,0:T(8,128)(2,1)}, u32[]{:S(2)}, u32[]{:S(2)}) collective-permute-start(bf16[4,128,1280]{2,1,0:T(8,128)(2,1)} %get-tuple-element.159), channel_id=1, source_target_pairs={{0,1},{1,0},{2,3},{3,2},{4,5},{5,4},{6,7},{7,6},{8,9},{9,8},{10,11... | collective-permute-start | bytes 3932168 | tf_op jit(solution)/shard_map/ppermute | solution.py:862
  (27 other events, 98.7 us)

commit v3 on v2

--- a/solution.py
+++ b/solution.py
@@ -202,312 +202,6 @@
     return scale * (
         e - jnp.mean(e, axis=-1, keepdims=True) - unit * jnp.mean(e * unit, axis=-1, keepdims=True)
     )
-
-
-def feed_kernel(rows, core_ref, middle_ref, cot_ref, gain_ref, up_ref, down_ref,
-    out_ref, d_middle_ref, d_attn_ref, down_sent, down_kept, up_sent, up_kept, n2, n2_turned, total, d_n2):
-    step, last = pl.program_id(0), pl.num_programs(0) - 1
-    tokens, width = n2.shape
-    half = width // 2
-
-    @pl.when(step == 0)
-    def _():
-        def body(i, _):
-            part = pl.ds(pl.multiple_of(i * rows, rows), rows)
-            unit, _s = norm_parts(middle_ref[part, :])
-            n2[part, :] = (unit * gain_ref[...]).astype(bf16)
-            return 0
-        lax.fori_loop(0, tokens // rows, body, 0)
-        n2_turned[...] = n2[...].T
-
-    up_w, down_w = up_ref[...], down_ref[...]
-    up = dot(n2[...], up_w, 1, 0)
-    d_act = dot(cot_ref[...], down_w, 1, 1)
-    share = 0.5 + 0.5 * lax.erf(up * (0.5**0.5))
-    density = jnp.exp(-0.5 * up * up) * 0.3989422804014327
-    act = (up * share).astype(bf16)
-    d_up = (d_act * (share + up * density)).astype(bf16)
-    y = dot(act, down_w, 1, 0)
-    d = dot(d_up, up_w, 1, 1)
-
-    @pl.when(step == 0)
-    def _():
-        total[...] = middle_ref[...] + y
-        d_n2[...] = d
-
-    @pl.when(step > 0)
-    def _():
-        total[...] += y
-        d_n2[...] += d
-
-    up_grad = dot(n2_turned[...], d_up, 1, 0).astype(bf16)
-
-    @pl.when(step <= last // 2)
-    def _():
-        up_sent[...] = up_grad
-
-    @pl.when(step > last // 2)
-    def _():
-        up_kept[...] = up_grad
-
-    down_grad = dot(act, cot_ref[...], 0, 0).astype(bf16)
-
-    @pl.when(core_ref[0] == 0)
-    def _():
-        down_kept[...] = down_grad[:, :half]
-        down_sent[...] = down_grad[:, half:]
-
-    @pl.when(core_ref[0] != 0)
-    def _():
-        down_kept[...] = down_grad[:, half:]
-        down_sent[...] = down_grad[:, :half]
-
-    @pl.when(step == last)
-    def _():
-        def body(i, _):
-            part = pl.ds(pl.multiple_of(i * rows, rows), rows)
-            out_ref[part, :] = total[part, :].astype(bf16)
-            unit, scale = norm_parts(middle_ref[part, :])
-            grad = cot_ref[part, :].astype(f32) + norm_back(d_n2[part, :], gain_ref[...], unit, scale)
-            d_middle_ref[part, :] = grad
-            d_attn_ref[part, :] = grad.astype(bf16)
-            return 0
-        lax.fori_loop(0, tokens // rows, body, 0)
-
-
-def feed(core, middle, cot, gain, up_weight, down_weight, tile=512):
-    tokens, width = middle.shape
-    wide = up_weight.shape[1]
-    steps = wide // tile
-    halves = steps // 2
-    place = lambda i, core: (i + (1 - core[0]) * halves) % steps
-    whole = lambda dtype: jax.ShapeDtypeStruct((tokens, width), dtype)
-    fixed = lambda shape: pl.BlockSpec(shape, lambda i, core: (0, 0), pipeline_mode=pl.Buffered(1))
-    return pl.pallas_call(
-        functools.partial(feed_kernel, 128),
-        grid_spec=pltpu.PrefetchScalarGridSpec(
-            num_scalar_prefetch=1,
-            grid=(steps,),
-            in_specs=[
-                fixed((tokens, width)),
-                fixed((tokens, width)),
-                fixed((1, width)),
-                pl.BlockSpec((width, tile), lambda i, core: (0, place(i, core))),
-                pl.BlockSpec((tile, width), lambda i, core: (place(i, core), 0)),
-            ],
-            out_specs=[
-                fixed((tokens, width)),
-                fixed((tokens, width)),
-                fixed((tokens, width)),
-                pl.BlockSpec((tile, width // 2), lambda i, core: (place(i, core), 0)),
-                pl.BlockSpec((tile, width // 2), lambda i, core: (place(i, core), 0)),
-                pl.BlockSpec((width, tile), lambda i, core: (0, jnp.minimum(i, halves - 1))),
-                pl.BlockSpec((width, tile), lambda i, core: (0, jnp.maximum(i - halves, 0))),
-            ],
-            scratch_shapes=[
-                pltpu.VMEM((tokens, width), bf16),
-                pltpu.VMEM((width, tokens), bf16),
-                pltpu.VMEM((tokens, width), f32),
-                pltpu.VMEM((tokens, width), f32),
-            ],
-        ),
-        out_shape=[
-            whole(bf16), whole(f32), whole(bf16),
-            jax.ShapeDtypeStruct((wide, width // 2), bf16),
-            jax.ShapeDtypeStruct((wide, width // 2), bf16),
-            jax.ShapeDtypeStruct((width, wide // 2), bf16),
-            jax.ShapeDtypeStruct((width, wide // 2), bf16),
-        ],
-        compiler_params=pltpu.CompilerParams(vmem_limit_bytes=vmem_bytes),
-        name="feed",
-    )(core, middle, cot, gain.reshape(1, width), up_weight, down_weight)
-
-
-def feed_kernel(rows, core_ref, middle_ref, cot_ref, gain_ref, up_ref, down_ref,
-    out_ref, d_middle_ref, d_attn_ref, down_sent, down_kept, up_sent, up_kept, n2, n2_turned, total, d_n2):
-    step, last = pl.program_id(0), pl.num_programs(0) - 1
-    tokens, width = n2.shape
-    half = width // 2
-
-    @pl.when(step == 0)
-    def _():
-        def body(i, _):
-            part = pl.ds(pl.multiple_of(i * rows, rows), rows)
-            unit, _s = norm_parts(middle_ref[part, :])
-            n2[part, :] = (unit * gain_ref[...]).astype(bf16)
-            return 0
-        lax.fori_loop(0, tokens // rows, body, 0)
-        n2_turned[...] = n2[...].T
-
-    up_w, down_w = up_ref[...], down_ref[...]
-    up = dot(n2[...], up_w, 1, 0)
-    d_act = dot(cot_ref[...], down_w, 1, 1)
-    share = 0.5 + 0.5 * lax.erf(up * (0.5**0.5))
-    density = jnp.exp(-0.5 * up * up) * 0.3989422804014327
-    act = (up * share).astype(bf16)
-    d_up = (d_act * (share + up * density)).astype(bf16)
-    y = dot(act, down_w, 1, 0)
-    d = dot(d_up, up_w, 1, 1)
-
-    @pl.when(step == 0)
-    def _():
-        total[...] = middle_ref[...] + y
-        d_n2[...] = d
-
-    @pl.when(step > 0)
-    def _():
-        total[...] += y
-        d_n2[...] += d
-
-    up_grad = dot(n2_turned[...], d_up, 1, 0).astype(bf16)
-
-    @pl.when(step <= last // 2)
-    def _():
-        up_sent[...] = up_grad
-
-    @pl.when(step > last // 2)
-    def _():
-        up_kept[...] = up_grad
-
-    down_grad = dot(act, cot_ref[...], 0, 0).astype(bf16)
-
-    @pl.when(core_ref[0] == 0)
-    def _():
-        down_kept[...] = down_grad[:, :half]
-        down_sent[...] = down_grad[:, half:]
-
-    @pl.when(core_ref[0] != 0)
-    def _():
-        down_kept[...] = down_grad[:, half:]
-        down_sent[...] = down_grad[:, :half]
-
-    @pl.when(step == last)
-    def _():
-        def body(i, _):
-            part = pl.ds(pl.multiple_of(i * rows, rows), rows)
-            out_ref[part, :] = total[part, :].astype(bf16)
-            unit, scale = norm_parts(middle_ref[part, :])
-            grad = cot_ref[part, :].astype(f32) + norm_back(d_n2[part, :], gain_ref[...], unit, scale)
-            d_middle_ref[part, :] = grad
-            d_attn_ref[part, :] = grad.astype(bf16)
-            return 0
-        lax.fori_loop(0, tokens // rows, body, 0)
-
-
-def feed(core, middle, cot, gain, up_weight, down_weight, tile=512):
-    tokens, width = middle.shape
-    wide = up_weight.shape[1]
-    steps = wide // tile
-    halves = steps // 2
-    place = lambda i, core: (i + (1 - core[0]) * halves) % steps
-    whole = lambda dtype: jax.ShapeDtypeStruct((tokens, width), dtype)
-    fixed = lambda shape: pl.BlockSpec(shape, lambda i, core: (0, 0), pipeline_mode=pl.Buffered(1))
-    return pl.pallas_call(
-        functools.partial(feed_kernel, 128),
-        grid_spec=pltpu.PrefetchScalarGridSpec(
-            num_scalar_prefetch=1,
-            grid=(steps,),
-            in_specs=[
-                fixed((tokens, width)),
-                fixed((tokens, width)),
-                fixed((1, width)),
-                pl.BlockSpec((width, tile), lambda i, core: (0, place(i, core))),
-                pl.BlockSpec((tile, width), lambda i, core: (place(i, core), 0)),
-            ],
-            out_specs=[
-                fixed((tokens, width)),
-                fixed((tokens, width)),
-                fixed((tokens, width)),
-                pl.BlockSpec((tile, width // 2), lambda i, core: (place(i, core), 0)),
-                pl.BlockSpec((tile, width // 2), lambda i, core: (place(i, core), 0)),
-                pl.BlockSpec((width, tile), lambda i, core: (0, jnp.minimum(i, halves - 1))),
-                pl.BlockSpec((width, tile), lambda i, core: (0, jnp.maximum(i - halves, 0))),
-            ],
-            scratch_shapes=[
-                pltpu.VMEM((tokens, width), bf16),
-                pltpu.VMEM((width, tokens), bf16),
-                pltpu.VMEM((tokens, width), f32),
-                pltpu.VMEM((tokens, width), f32),
-            ],
-        ),
-        out_shape=[
-            whole(bf16), whole(f32), whole(bf16),
-            jax.ShapeDtypeStruct((wide, width // 2), bf16),
-            jax.ShapeDtypeStruct((wide, width // 2), bf16),
-            jax.ShapeDtypeStruct((width, wide // 2), bf16),
-            jax.ShapeDtypeStruct((width, wide // 2), bf16),
-        ],
-        compiler_params=pltpu.CompilerParams(vmem_limit_bytes=vmem_bytes),
-        name="feed",
-    )(core, middle, cot, gain.reshape(1, width), up_weight, down_weight)
-
-
-def add_split_kernel(has_two, bit_ref, *refs):
-    ins, outs = refs[: 2 if has_two else 1], refs[2 if has_two else 1 :]
-    value = ins[0][...]
-    if has_two:
-        value = (value.astype(f32) + ins[1][...].astype(f32)).astype(bf16)
-    if len(outs) == 1:
-        outs[0][...] = value
-    else:
-        sends = pl.program_id(0) == 0
-
-        @pl.when(sends)
-        def _():
-            outs[0][...] = value
-
-        @pl.when(jnp.logical_not(sends))
-        def _():
-            outs[1][...] = value
-
-
-def add_split(kept, received, inner, bit):
-    rows, columns = kept.shape
-    values = [kept] if received is None else [kept, received.reshape(rows, columns)]
-    if bit is None:
-        if received is None:
-            return None, kept
-        count = 4 if rows % 64 == 0 else 1
-        block = pl.BlockSpec((rows // count, columns), lambda i, bit: (i, 0))
-        grid, ins, outs = (count,), [block] * 2, block
-        shapes = jax.ShapeDtypeStruct((rows, columns), bf16)
-        bit = jnp.zeros((), jnp.int32)
-    else:
-        outer = rows // (2 * inner)
-        cut = 1
-        while inner // cut * columns > 2**19 and inner % (32 * cut) == 0:
-            cut *= 2
-        values = [value.reshape(outer, 2, inner, columns) for value in values]
-        ins = [
-            pl.BlockSpec(
-                (None, None, inner // cut, columns),
-                lambda w, i, j, bit: (i, jnp.where(w == 0, 1 - bit[0], bit[0]), j, 0),
-            )
-        ] * len(values)
-        outs = [
-            pl.BlockSpec(
-                (None, inner // cut, columns),
-                lambda w, i, j, bit: (jnp.where(w == 0, i, outer - 1), jnp.where(w == 0, j, cut - 1), 0),
-            ),
-            pl.BlockSpec(
-                (None, inner // cut, columns),
-                lambda w, i, j, bit: (jnp.where(w == 0, 0, i), jnp.where(w == 0, 0, j), 0),
-            ),
-        ]
-        grid = (2, outer, cut)
-        shapes = [jax.ShapeDtypeStruct((outer, inner, columns), bf16)] * 2
-    done = pl.pallas_call(
-        functools.partial(add_split_kernel, len(values) == 2),
-        grid_spec=pltpu.PrefetchScalarGridSpec(
-            num_scalar_prefetch=1, grid=grid, in_specs=ins, out_specs=outs
-        ),
-        out_shape=shapes,
-        cost_estimate=pl.CostEstimate(flops=rows * columns, bytes_accessed=6 * rows * columns, transcendentals=0),
-        name="add_split",
-    )(bit.reshape(1), *values)
-    if not isinstance(done, (list, tuple)):
-        return None, done
-    return done[0].reshape(rows // 2, columns), done[1].reshape(rows // 2, columns)
 
 
 piece_rows = 32
@@ -775,6 +469,521 @@
     )(middle, cot, gain.reshape(1, width), up_weight, down_weight)
 
 
+class Stream:
+    def __init__(self, levels, rows, columns):
+        self.levels, self.rows, self.columns = levels, rows, columns
+
+    def shape(self, level):
+        outer = 2 ** (len(self.levels) - 1 - level)
+        return (max(outer // 2, 1), min(outer, 2), self.rows, self.columns)
+
+    def scratch(self):
+        shapes = []
+        for level in range(len(self.levels)):
+            shape = self.shape(level)
+            shapes += [pltpu.VMEM(shape, bf16), pltpu.VMEM(shape, bf16), pltpu.VMEM((2,) + shape, bf16)]
+        return shapes
+
+
+def streams_of(block_rows, width, pairs):
+    lanes = 2 * HDIM
+    return (
+        Stream(("x", "y", "z1", "z2"), width // 16, 4 * lanes),
+        Stream(("y", "z1", "z2"), block_rows // 2, lanes),
+        Stream(("x", "z1", "z2"), width // 16, block_rows * 8 // CORES // pairs),
+    )
+
+
+def back_kernel(pairs, tile, streams, row_count, *refs):
+    (
+        key_tags, query_tags, q_ref, k_ref, v_ref, o_ref, do_ref, lse_ref, turned_ref, own_weight, other_weight,
+        gain_ref, out_kept, out_came, down_ref, up_ref, start_ref, d_middle_ref, outputs_ref,
+    ) = refs[:19]
+    grad_out, outputs_out, *gathered = refs[19:24]
+    rest = list(refs[24:])
+    take = lambda count: [rest.pop(0) for _ in range(count)]
+    k_turned, dq_turned, delta, d_pair, d_came, d_n1, staged, start_part, middle_part = take(9)
+    levels = []
+    for stream in streams:
+        levels.append([take(3) for _ in stream.levels])
+    joined = take(len(streams))
+    (
+        send_sems, recv_sems, join_send, join_recv, core_send, core_recv, local_sems,
+        pair_send, pair_recv, home_send, home_recv, home_local, part_sems, result_send, result_recv, result_local,
+    ) = rest
+
+    step = pl.program_id(0)
+    tokens, lanes = q_ref.shape
+    own_tokens = tokens // CORES
+    seq_at, rows_at = lax.axis_index("seq"), lax.axis_index("rows")
+    core, high = rows_at % 2, (rows_at // 2) % 2
+    places = {"x": high, "y": seq_at % 2, "z1": (seq_at // 2) % 2, "z2": seq_at // 4}
+    peers = {
+        "x": (seq_at, rows_at + 2 - 4 * high),
+        "y": (seq_at + 1 - 2 * places["y"], rows_at),
+        "z1": (seq_at + 2 - 4 * places["z1"], rows_at),
+        "z2": (seq_at + 4 - 8 * places["z2"], rows_at),
+        "core": (seq_at, rows_at + 1 - 2 * core),
+    }
+    n_seq = 2 * row_count
+    sub = start_part.shape[1]
+
+    def remote(source, target, send, recv, peer):
+        return pltpu.make_async_remote_copy(
+            src_ref=source, dst_ref=target, send_sem=send, recv_sem=recv, device_id=peer, device_id_type=MESH
+        )
+
+    def add(a, b):
+        return (a.astype(f32) + b.astype(f32)).astype(bf16)
+
+    def level_copy(at, level, item):
+        send, _, came = levels[at][level]
+        slot = item % 2
+        return remote(
+            send, came.at[slot], send_sems.at[at, level], recv_sems.at[at, level, slot], peers[streams[at].levels[level]]
+        )
+
+    def join_copy(at, item):
+        part = joined[at].at[item, high]
+        return remote(part, part, join_send.at[at], join_recv.at[at, item % 2], peers["x"])
+
+    def core_copy(at, item):
+        return remote(
+            joined[at].at[item],
+            gathered[at].at[item, core],
+            core_send.at[at],
+            core_recv.at[at, item % 2],
+            peers["core"],
+        )
+
+    def local_copy(at, item):
+        return pltpu.make_async_copy(joined[at].at[item], gathered[at].at[item, core], local_sems.at[at])
+
+    def pair_copy(item):
+        slot = item % 2
+        return remote(
+            d_pair.at[slot, pl.ds(own_tokens, own_tokens)],
+            d_came.at[slot],
+            pair_send.at[slot],
+            pair_recv.at[slot],
+            peers["core"],
+        )
+
+    home = seq_at // row_count
+
+    def to_home(block, own, result):
+        if result:
+            source, target = outputs_ref.at[pl.ds(block * sub, sub)], outputs_out
+            sems = result_send, result_recv, result_local
+        else:
+            source, target = staged.at[block], grad_out
+            sems = home_send, home_recv, home_local
+        row = seq_at % row_count
+        if own:
+            return pltpu.make_async_copy(source, target.at[row, core], sems[2])
+        return remote(source, target.at[row, core], sems[0].at[block], sems[1].at[row, core], (block, rows_at - core + home))
+
+    def start_home(block, result):
+        @pl.when(is_own(block))
+        def _():
+            to_home(block, True, result).start()
+
+        @pl.when(jnp.logical_not(is_own(block)))
+        def _():
+            to_home(block, False, result).start()
+
+    def wait_home(result):
+        for block in range(n_seq):
+            @pl.when(is_own(block))
+            def _():
+                to_home(block, True, result).wait()
+
+            @pl.when(jnp.logical_not(is_own(block)))
+            def _():
+                to_home(block, False, result).wait_send()
+        source, target = (outputs_ref.at[pl.ds(0, sub)], outputs_out) if result else (staged.at[0], grad_out)
+        sems = (result_send, result_recv) if result else (home_send, home_recv)
+        for row in range(row_count):
+            for c in range(CORES):
+                @pl.when(jnp.logical_not((seq_at == core * row_count + row) & (core == c)))
+                def _():
+                    remote(source, target.at[row, c], sems[0].at[0], sems[1].at[row, c], peers["core"]).wait_recv()
+
+    def is_own(block):
+        return (seq_at == block) & (home == core)
+
+    @pl.when(step == 0)
+    def _():
+        barrier = pltpu.get_barrier_semaphore()
+        for s in range(n_seq):
+            for c in range(CORES):
+                @pl.when(jnp.logical_not((seq_at == s) & (core == c)))
+                def _():
+                    pl.semaphore_signal(barrier, inc=1, device_id=(s, rows_at - core + c), device_id_type=MESH)
+        pl.semaphore_signal(barrier, inc=1, device_id=peers["x"], device_id_type=MESH)
+        pl.semaphore_wait(barrier, n_seq * CORES)
+        d_n1[...] = jnp.zeros_like(d_n1)
+        for block in range(n_seq):
+            start_home(block, True)
+
+    @pl.when(step < pairs)
+    def _():
+        slot = step % 2
+        k_turned[...] = k_ref[...].T
+        dq_turned[...] = (o_ref[...].astype(f32) * do_ref[...].astype(f32)).T
+        for head in range(2):
+            own_rows = dq_turned[head * HDIM : (head + 1) * HDIM, :]
+            delta[head : head + 1, :] = jnp.sum(own_rows, axis=0, keepdims=True)
+        dq_turned[...] = jnp.zeros_like(dq_turned)
+        first = lax.broadcasted_iota(jnp.int32, (tile, lanes), 1) < HDIM
+
+        def body(i, _):
+            part = pl.ds(pl.multiple_of(i * tile, tile), tile)
+            k, v = k_ref[part, :], v_ref[part, :]
+            q, do = q_ref[...], do_ref[...]
+            allowed = key_tags[part, :] == query_tags[...]
+            dk, dv = [], []
+            for head in range(2):
+                own = first if head == 0 else jnp.logical_not(first)
+                own_rows = slice(head * HDIM, (head + 1) * HDIM)
+                scores = dot(jnp.where(own, k, bf16(0)), q, 1, 1)
+                scores = jnp.where(allowed, scores, masked_score)
+                chances = jnp.exp2(scores * (score_scale * log2e) - lse_ref[head : head + 1, :])
+                weight_grad = dot(jnp.where(own, v, bf16(0)), do, 1, 1)
+                score_grad = (chances * (weight_grad - delta[head : head + 1, :])).astype(bf16)
+                dv.append(dot(chances.astype(bf16), do, 1, 0))
+                dk.append(dot(score_grad, q, 1, 0))
+                dq_turned[own_rows, :] += dot(k_turned[own_rows, part], score_grad, 1, 0)
+            d_pair[slot, part, lanes : 2 * lanes] = (jnp.where(first, dk[0], dk[1]) * score_scale).astype(bf16)
+            d_pair[slot, part, 2 * lanes :] = jnp.where(first, dv[0], dv[1]).astype(bf16)
+            return 0
+
+        lax.fori_loop(0, tokens // tile, body, 0)
+        d_pair[slot, :, :lanes] = (dq_turned[...] * score_scale).T.astype(bf16)
+
+    def add_pair():
+        item = step - 1
+        slot = item % 2
+        pair_copy(item).wait()
+        d_n1[...] += dot(d_pair[slot, :own_tokens, :], own_weight[...], 1, 1) + dot(
+            d_came[slot], other_weight[...], 1, 1
+        )
+
+    @pl.when((step >= 1) & (step <= pairs))
+    def _():
+        add_pair()
+
+    @pl.when(step < pairs)
+    def _():
+        pair_copy(step).start()
+
+    def part_copies(block):
+        rows = pl.ds(block * start_part.shape[1], start_part.shape[1])
+        slot = block % 2
+        return (
+            pltpu.make_async_copy(start_ref.at[rows], start_part.at[slot], part_sems.at[0, slot]),
+            pltpu.make_async_copy(d_middle_ref.at[rows], middle_part.at[slot], part_sems.at[1, slot]),
+        )
+
+    @pl.when(step == pairs)
+    def _():
+        for copy in part_copies(0):
+            copy.start()
+        for block in range(n_seq):
+            if block + 1 < n_seq:
+                for copy in part_copies(block + 1):
+                    copy.start()
+            for copy in part_copies(block):
+                copy.wait()
+            unit, scale = norm_parts(start_part[block % 2].astype(f32))
+            grad = norm_back(d_n1[block * sub : (block + 1) * sub, :], gain_ref[...], unit, scale)
+            staged[block] = (middle_part[block % 2] + grad).astype(bf16)
+            start_home(block, False)
+
+    for at, stream in enumerate(streams):
+        depth = len(stream.levels)
+
+        def item_at(lag):
+            return step - lag, (step >= lag) & (step - lag < pairs)
+
+        item, here = item_at(depth + 2)
+
+        @pl.when(here)
+        def _(at=at, item=item):
+            core_copy(at, item).wait()
+            local_copy(at, item).wait()
+
+        item, here = item_at(depth + 1)
+
+        @pl.when(here)
+        def _(at=at, item=item):
+            join_copy(at, item).wait()
+            core_copy(at, item).start()
+            local_copy(at, item).start()
+
+        for level in reversed(range(depth)):
+            item, here = item_at(level + 1)
+
+            @pl.when(here)
+            def _(at=at, item=item, level=level, stream=stream, depth=depth):
+                _, keep, came = levels[at][level]
+                slot = item % 2
+                level_copy(at, level, item).wait_recv()
+                if level == depth - 1:
+                    joined[at][item, high] = add(keep[0, 0], came[slot, 0, 0])
+                    join_copy(at, item).start()
+                    return
+
+                @pl.when(item > 0)
+                def _():
+                    level_copy(at, level + 1, item - 1).wait_send()
+
+                next_send, next_keep, _ = levels[at][level + 1]
+                place = places[stream.levels[level + 1]]
+                next_send[...] = add(keep[:, 1 - place], came[slot, :, 1 - place]).reshape(next_send.shape)
+                next_keep[...] = add(keep[:, place], came[slot, :, place]).reshape(next_keep.shape)
+                level_copy(at, level + 1, item).start()
+
+    @pl.when(step < pairs)
+    def _():
+        @pl.when(step > 0)
+        def _():
+            for at in range(len(streams)):
+                level_copy(at, 0, step - 1).wait_send()
+
+        send, keep, _ = levels[0][0]
+        grad = dot(turned_ref[...], d_pair[step % 2], 1, 0).astype(bf16)
+        grad = grad.reshape(n_seq, 2, send.shape[2], 3 * lanes)
+        shape = send.shape[:3] + (3 * lanes,)
+
+        @pl.when(high == 0)
+        def _():
+            send[:, :, :, : 3 * lanes] = grad[:, 1].reshape(shape)
+            keep[:, :, :, : 3 * lanes] = grad[:, 0].reshape(shape)
+
+        @pl.when(high != 0)
+        def _():
+            send[:, :, :, : 3 * lanes] = grad[:, 0].reshape(shape)
+            keep[:, :, :, : 3 * lanes] = grad[:, 1].reshape(shape)
+
+        shape = send.shape[:3] + (lanes,)
+        send[:, :, :, 3 * lanes :] = add(out_kept[:, 1 - high], out_came[:, 1 - high]).reshape(shape)
+        keep[:, :, :, 3 * lanes :] = add(out_kept[:, high], out_came[:, high]).reshape(shape)
+        for at, (ref, place) in enumerate(((down_ref, places["y"]), (up_ref, high)), 1):
+            send, keep, _ = levels[at][0]
+            send[...] = ref[:, 1 - place].reshape(send.shape)
+            keep[...] = ref[:, place].reshape(keep.shape)
+        for at in range(len(streams)):
+            level_copy(at, 0, step).start()
+
+    @pl.when(step == pl.num_programs(0) - 1)
+    def _():
+        for at, stream in enumerate(streams):
+            for level in range(len(stream.levels)):
+                level_copy(at, level, pairs - 1).wait_send()
+        wait_home(False)
+        wait_home(True)
+
+
+def back(
+    qkv, mixed, d_mixed, lse, key_tags, query_tags, n1_turned, weights, gain, out_kept, out_came, down_part, up_part,
+    start, d_middle, outputs, row_count,
+):
+    tokens = qkv.shape[0]
+    width = n1_turned.shape[0]
+    own_tokens = tokens // CORES
+    lanes = 2 * HDIM
+    pairs = qkv.shape[1] // (3 * lanes)
+    n_seq = 2 * row_count
+    tile = 256
+    sub = own_tokens // n_seq
+    streams = streams_of(down_part.shape[0] * 2 // n_seq, width, pairs)
+    last = pairs - 1
+    now = lambda i: jnp.minimum(i, last)
+    before = lambda i: jnp.clip(i - 1, 0, last)
+    fixed = lambda shape: pl.BlockSpec(shape, lambda i: (0,) * len(shape), pipeline_mode=pl.Buffered(1))
+
+    def columns(place):
+        return pl.BlockSpec((tokens, lanes), lambda i: (0, 3 * now(i) + place))
+
+    pair = pl.BlockSpec((tokens, lanes), lambda i: (0, now(i)))
+    weight = pl.BlockSpec((width, 3 * lanes), lambda i: (0, before(i)))
+    hbm = pl.BlockSpec(memory_space=pl.ANY)
+
+    def piece(value, place):
+        parts = (value.shape[0] // (2 * place), 2, place, value.shape[1] // pairs)
+        whole = value.reshape(parts[:3] + value.shape[1:])
+        return whole, pl.BlockSpec(parts, lambda i: (0, 0, 0, now(i)))
+
+    outs = [piece(value, width // 16) for value in (out_kept, out_came)]
+    down = piece(down_part, streams[1].rows)
+    up = piece(up_part, streams[2].rows)
+    count = len(streams)
+    deepest = max(len(stream.levels) for stream in streams)
+    return pl.pallas_call(
+        functools.partial(back_kernel, pairs, tile, streams, row_count),
+        grid=(pairs + deepest + 2,),
+        in_specs=[
+            fixed((tokens, 1)),
+            fixed((1, tokens)),
+            columns(0),
+            columns(1),
+            columns(2),
+            pair,
+            pair,
+            pl.BlockSpec((None, 2, tokens), lambda i: (now(i), 0, 0)),
+            fixed((width, tokens)),
+            weight,
+            weight,
+            fixed((1, width)),
+            outs[0][1],
+            outs[1][1],
+            down[1],
+            up[1],
+            hbm,
+            hbm,
+            hbm,
+        ],
+        out_specs=[hbm] * 5,
+        out_shape=[jax.ShapeDtypeStruct((row_count, CORES, sub, width), bf16)] * 2
+        + [jax.ShapeDtypeStruct((pairs, CORES, 2, stream.rows, stream.columns), bf16) for stream in streams],
+        scratch_shapes=[
+            pltpu.VMEM((lanes, tokens), bf16),
+            pltpu.VMEM((lanes, tokens), f32),
+            pltpu.VMEM((2, tokens), f32),
+            pltpu.VMEM((2, tokens, 3 * lanes), bf16),
+            pltpu.VMEM((2, own_tokens, 3 * lanes), bf16),
+            pltpu.VMEM((own_tokens, width), f32),
+            pltpu.VMEM((n_seq, sub, width), bf16),
+            pltpu.VMEM((2, sub, width), bf16),
+            pltpu.VMEM((2, sub, width), f32),
+        ]
+        + [shape for stream in streams for shape in stream.scratch()]
+        + [pltpu.VMEM((pairs, 2, stream.rows, stream.columns), bf16) for stream in streams]
+        + [
+            pltpu.SemaphoreType.DMA((count, deepest)),
+            pltpu.SemaphoreType.DMA((count, deepest, 2)),
+            pltpu.SemaphoreType.DMA((count,)),
+            pltpu.SemaphoreType.DMA((count, 2)),
+            pltpu.SemaphoreType.DMA((count,)),
+            pltpu.SemaphoreType.DMA((count, 2)),
+            pltpu.SemaphoreType.DMA((count,)),
+            pltpu.SemaphoreType.DMA((2,)),
+            pltpu.SemaphoreType.DMA((2,)),
+            pltpu.SemaphoreType.DMA((n_seq,)),
+            pltpu.SemaphoreType.DMA((row_count, CORES)),
+            pltpu.SemaphoreType.DMA,
+            pltpu.SemaphoreType.DMA((2, 2)),
+            pltpu.SemaphoreType.DMA((n_seq,)),
+            pltpu.SemaphoreType.DMA((row_count, CORES)),
+            pltpu.SemaphoreType.DMA,
+        ],
+        compiler_params=pltpu.CompilerParams(
+            vmem_limit_bytes=feed_vmem_bytes, collective_id=2, has_side_effects=True
+        ),
+        cost_estimate=pl.CostEstimate(
+            flops=80 * pairs * tokens * tokens * HDIM,
+            bytes_accessed=16 * tokens * pairs * lanes,
+            transcendentals=2 * pairs * tokens * tokens,
+        ),
+        name="back",
+    )(
+        key_tags, query_tags, qkv, qkv, qkv, mixed, d_mixed, lse, n1_turned, weights[0], weights[1],
+        gain.reshape(1, width), outs[0][0], outs[1][0], down[0], up[0], start, d_middle, outputs,
+    )
+
+
+def collect_kernel(pairs, seq_ref, *refs):
+    qkv_parts, down_parts, up_parts = refs[:3]
+    qkv_weights, up_weight, first_gain, second_gain = refs[3:9], refs[9], refs[10], refs[11]
+    qkv_out, out_out, down_out, up_out, first_out, second_out = refs[12:]
+    item = pl.program_id(0)
+    lanes = 2 * HDIM
+    rows = qkv_parts.shape[2]
+    width = out_out.shape[1]
+    half = width // CORES
+    tile = feed_tile // CORES
+
+    @pl.when(item == 0)
+    def _():
+        first_out[...] = jnp.zeros_like(first_out)
+        second_out[...] = jnp.zeros_like(second_out)
+
+    for core in range(CORES):
+        place = pl.multiple_of(core * half + item * lanes, lanes)
+        for high in range(2):
+            own = slice(high * rows, (high + 1) * rows)
+            part = qkv_parts[core, high].astype(f32)
+            for kind in range(3):
+                value = part[:, kind * lanes : (kind + 1) * lanes]
+                qkv_out[own, pl.ds(kind * width + place, lanes)] = value
+                weight = qkv_weights[kind * CORES + core][own, :].astype(f32)
+                first_out[own, :] += jnp.sum(value * weight, axis=1, keepdims=True)
+            out_out[own, pl.ds(place, lanes)] = part[:, 3 * lanes :]
+            part = up_parts[core, high].astype(f32)
+            for at in range(part.shape[1] // tile):
+                value = part[:, at * tile : (at + 1) * tile]
+                columns = slice(at * feed_tile + core * tile, at * feed_tile + (core + 1) * tile)
+                up_out[own, columns] = value
+                second_out[own, :] += jnp.sum(value * up_weight[own, columns].astype(f32), axis=1, keepdims=True)
+            part = down_parts[core, high].astype(f32)
+            for at in range(part.shape[0] // piece_rows):
+                start = (2 * at + high) * piece_rows
+                down_out[start : start + piece_rows, pl.ds(place, lanes)] = part[at * piece_rows : (at + 1) * piece_rows]
+
+    @pl.when(item == pairs - 1)
+    def _():
+        first_out[...] = first_out[...] / first_gain[...]
+        second_out[...] = second_out[...] / second_gain[...]
+
+
+def collect(seq_at, qkv_parts, down_parts, up_parts, qkv_weight, up_weight, first_gain, second_gain):
+    pairs, _, _, rows, _ = qkv_parts.shape
+    width, lanes = qkv_weight.shape[0], 2 * HDIM
+    shard, wide = 2 * rows, up_weight.shape[1]
+    down_rows = 2 * down_parts.shape[3]
+
+    def parts(value):
+        return pl.BlockSpec((None,) + value.shape[1:], lambda i, seq: (i, 0, 0, 0, 0))
+
+    def weight(kind, core):
+        return pl.BlockSpec((shard, lanes), lambda i, seq: (seq[0], (kind * CORES + core) * pairs + i))
+
+    gain = pl.BlockSpec((shard, 1), lambda i, seq: (seq[0], 0))
+    whole = lambda shape: pl.BlockSpec(shape, lambda i, seq: (0, 0))
+    return pl.pallas_call(
+        functools.partial(collect_kernel, pairs),
+        grid_spec=pltpu.PrefetchScalarGridSpec(
+            num_scalar_prefetch=1,
+            grid=(pairs,),
+            in_specs=[parts(qkv_parts), parts(down_parts), parts(up_parts)]
+            + [weight(kind, core) for kind in range(3) for core in range(CORES)]
+            + [pl.BlockSpec((shard, wide // pairs), lambda i, seq: (seq[0], i)), gain, gain],
+            out_specs=[
+                whole((shard, 3 * width)),
+                whole((shard, width)),
+                whole((down_rows, width)),
+                pl.BlockSpec((shard, wide // pairs), lambda i, seq: (0, i)),
+                whole((shard, 1)),
+                whole((shard, 1)),
+            ],
+        ),
+        out_shape=[
+            jax.ShapeDtypeStruct((shard, 3 * width), f32),
+            jax.ShapeDtypeStruct((shard, width), f32),
+            jax.ShapeDtypeStruct((down_rows, width), f32),
+            jax.ShapeDtypeStruct((shard, wide), f32),
+            jax.ShapeDtypeStruct((shard, 1), f32),
+            jax.ShapeDtypeStruct((shard, 1), f32),
+        ],
+        compiler_params=pltpu.CompilerParams(vmem_limit_bytes=vmem_bytes),
+        name="collect",
+    )(
+        seq_at.reshape(1), qkv_parts, down_parts, up_parts, *[qkv_weight] * 6, up_weight,
+        first_gain.reshape(width, 1), second_gain.reshape(width, 1),
+    )
+
+
 def add_split_kernel(has_two, bit_ref, *refs):
     ins, outs = refs[: 2 if has_two else 1], refs[2 if has_two else 1 :]
     value = ins[0][...]
@@ -934,117 +1143,16 @@
             value = value.reshape(-1, value.shape[-1])
         return value
 
-    def per_device(
-        inputs, cell_ids, valid_counts, cotangent, attention_gain, qkv_weight, out_weight, feed_gain, up_weight, down_weight
+    def back_by_steps(
+        qkv, mixed, d_mixed, lse, key_tags, query_tags, n1_all, qkv_parts, attention_gain,
+        out_kept, out_received, down_part, up_part, start, d_middle, to_member, ordered, from_rows, sizes,
     ):
-        row_count, block, width = inputs.shape
-        seq_len = cell_ids.shape[1]
-        heads = width // HDIM
-        lanes = 2 * HDIM
-        seq_at, rows_at = lax.axis_index("seq"), lax.axis_index("rows")
-        core = rows_at % CORES
-        chips = n_seq // (CORES * row_count)
-        group = chips * CORES
-        sub = block // group
-        tokens = n_seq * sub
-        member = (seq_at % chips) * CORES + core
-        group_heads = heads // group
-        pairs = -(-group_heads // 2)
-        group_width = group_heads * HDIM
-        padded = pairs * lanes - group_width
-
-        def to_member(value, hop):
-            def target(s, r):
-                place = ((s % chips) * CORES + r % CORES + hop) % group
-                return (s // chips * chips + place // CORES, r // CORES * CORES + place % CORES)
-
-            return permute(value, target)
-
-        def ordered(own, received, axis):
-            return jnp.where(
-                core == 0,
-                jnp.concatenate([own, received], axis),
-                jnp.concatenate([received, own], axis),
-            )
-
-        def to_rows(value):
-            halves = value.reshape(row_count, CORES, block // CORES, width)
-            received = other_core(pick(halves, 1 - core, 1))
-            both = ordered(pick(halves, core, 1), received, 0).reshape(n_seq, sub, width)
-            return lax.all_to_all(both, "seq", 0, 0, tiled=True).reshape(tokens, width)
-
-        def from_rows(value):
-            both = lax.all_to_all(value.reshape(n_seq, sub, width), "seq", 0, 0, tiled=True)
-            both = both.reshape(CORES, row_count, block // CORES, width)
-            received = other_core(pick(both, 1 - core, 0))
-            own = pick(both, core, 0)
-            return ordered(own[:, None], received[:, None], 1).reshape(row_count, block, width)
-
-        places = jnp.arange(seq_len, dtype=jnp.int32)
-        tags = jnp.where(places[None, :] < valid_counts[:, None], cell_ids, -1 - places[None, :])
-        tags = ordered(tags, other_core(tags), 0)
-        tags = pick(tags, seq_at // chips, 0).reshape(n_seq, CORES, chips, sub)
-        tags = tags.transpose(2, 1, 0, 3).reshape(group, tokens)
-        order = (member - jnp.arange(group, dtype=jnp.int32)) % group
-        tags = jnp.take(tags, order, axis=0).reshape(1, seq_len)
-        query_tags, key_tags = tags, tags.reshape(seq_len, 1)
-
-        def pad_heads(value, axis):
-            if not padded:
-                return value
-            fill = [(0, 0)] * value.ndim
-            fill[axis] = (0, padded)
-            return jnp.pad(value, fill)
-
-        def qkv_of(hop):
-            if group == CORES:
-                return gather_pairs(((core + hop) % CORES).reshape(1), qkv_weight)
-            piece = pick(qkv_weight.reshape(width, 3, group, group_width), (member + hop) % group, 2)
-            piece = pad_heads(piece, 2).reshape(width, 3, pairs, lanes)
-            return piece.transpose(0, 2, 1, 3).reshape(width, 3 * pairs * lanes)
-
-        def out_of(hop):
-            at = (member + hop) % group * group_width
-            return pad_heads(lax.dynamic_slice_in_dim(out_weight, at, group_width, 0), 0)
-
-        start = to_rows(inputs)
-        qkv_parts = [qkv_of(hop) for hop in range(group)]
-        out_parts = [out_of(hop) for hop in range(group)]
-        start = start.astype(f32)
+        group, member, core, pairs, group_width, tokens, width = sizes
+        lanes, half = 2 * HDIM, width // CORES
         unit1, scale1 = norm_parts(start)
-        n1 = (unit1 * attention_gain).astype(bf16)
-        n1_all = jnp.concatenate([n1] + [to_member(n1, hop) for hop in range(1, group)], 0)
-        cotangent, _ = tie(cotangent, start[:1])
-        cot = to_rows(cotangent)
-        qkv = dot(n1_all, qkv_parts[0], 1, 0).astype(bf16)
-        mixed, lse = attend(qkv, key_tags, query_tags)
-        mixed_parts = [mixed[:tokens]] + [
-            to_member(mixed[hop * tokens : (hop + 1) * tokens], group - hop) for hop in range(1, group)
-        ]
-        middle = start
-        for part, weight in zip(mixed_parts, out_parts):
-            middle = middle + dot(part, weight, 1, 0)
-        outputs, d_middle, d_attn, down_part, up_part = feed(middle, cot, feed_gain, up_weight, down_weight, n_seq)
-
-        d_attn_all = jnp.concatenate([d_attn] + [to_member(d_attn, hop) for hop in range(1, group)], 0)
-
-        out_low = from_rows(outputs)
-
-        half = width // CORES
-        if group == CORES:
-            mixed_own = ordered(mixed_parts[0], mixed_parts[1], 1)
-        else:
-            slots = jnp.stack([part[:, :group_width] for part in mixed_parts])
-            back = (jnp.arange(group, dtype=jnp.int32) - member) % group
-            mixed_own = jnp.take(slots, back, axis=0).transpose(1, 0, 2).reshape(tokens, width)
-        out_sent = dot(mixed_own, lax.dynamic_slice_in_dim(d_attn, (1 - core) * half, half, 1), 0, 0)
-        out_kept = dot(mixed_own, lax.dynamic_slice_in_dim(d_attn, core * half, half, 1), 0, 0)
-        out_received = other_core(out_sent.astype(bf16))
-        d_mixed = dot(d_attn_all, out_parts[0], 1, 1).astype(bf16)
-
         down = Sum(down_part, None, down_order)
         up = Sum(up_part, None, up_order)
-        out = Sum(out_kept.astype(bf16), out_received, rows_first)
+        out = Sum(out_kept, out_received, rows_first)
 
         def before_next(*sums):
             nonlocal d_mixed
@@ -1056,7 +1164,7 @@
                 each.sent, each.kept = values[1 + 2 * at : 3 + 2 * at]
                 each.begin()
 
-        def back(at):
+        def back_at(at):
             return attend_back(qkv, mixed, d_mixed, lse, key_tags, query_tags, at, 1)
 
         cut = max(1, 3 * pairs // 5)
@@ -1072,7 +1180,7 @@
 
         grads = []
         for at in range(pairs):
-            d_qkv.append(back(at))
+            d_qkv.append(back_at(at))
             d_mixed, d_qkv[at] = tie(d_mixed, d_qkv[at])
             if at + 1 == cut:
                 grads.append(take_piece(d_qkv))
@@ -1116,6 +1224,141 @@
         qkv_part = qkv_part.reshape(-1, 3, half)
         qkv_total = ordered(qkv_part[:, :, None], other_core(qkv_part)[:, :, None], 2)
         qkv_total = qkv_total.reshape(-1, 3 * width).astype(f32)
+
+        return input_grad, qkv_total, out_total, down_total, up_total
+
+    def per_device(
+        inputs, cell_ids, valid_counts, cotangent, attention_gain, qkv_weight, out_weight, feed_gain, up_weight, down_weight
+    ):
+        row_count, block, width = inputs.shape
+        seq_len = cell_ids.shape[1]
+        heads = width // HDIM
+        lanes = 2 * HDIM
+        seq_at, rows_at = lax.axis_index("seq"), lax.axis_index("rows")
+        core = rows_at % CORES
+        chips = n_seq // (CORES * row_count)
+        group = chips * CORES
+        sub = block // group
+        tokens = n_seq * sub
+        member = (seq_at % chips) * CORES + core
+        group_heads = heads // group
+        pairs = -(-group_heads // 2)
+        group_width = group_heads * HDIM
+        padded = pairs * lanes - group_width
+
+        def to_member(value, hop):
+            def target(s, r):
+                place = ((s % chips) * CORES + r % CORES + hop) % group
+                return (s // chips * chips + place // CORES, r // CORES * CORES + place % CORES)
+
+            return permute(value, target)
+
+        def ordered(own, received, axis):
+            return jnp.where(
+                core == 0,
+                jnp.concatenate([own, received], axis),
+                jnp.concatenate([received, own], axis),
+            )
+
+        def to_rows(value):
+            halves = value.reshape(row_count, CORES, block // CORES, width)
+            received = other_core(pick(halves, 1 - core, 1))
+            both = ordered(pick(halves, core, 1), received, 0).reshape(n_seq, sub, width)
+            return lax.all_to_all(both, "seq", 0, 0, tiled=True).reshape(tokens, width)
+
+        def from_rows(value):
+            both = lax.all_to_all(value.reshape(n_seq, sub, width), "seq", 0, 0, tiled=True)
+            both = both.reshape(CORES, row_count, block // CORES, width)
+            received = other_core(pick(both, 1 - core, 0))
+            own = pick(both, core, 0)
+            return ordered(own[:, None], received[:, None], 1).reshape(row_count, block, width)
+
+        places = jnp.arange(seq_len, dtype=jnp.int32)
+        tags = jnp.where(places[None, :] < valid_counts[:, None], cell_ids, -1 - places[None, :])
+        tags = ordered(tags, other_core(tags), 0)
+        tags = pick(tags, seq_at // chips, 0).reshape(n_seq, CORES, chips, sub)
+        tags = tags.transpose(2, 1, 0, 3).reshape(group, tokens)
+        order = (member - jnp.arange(group, dtype=jnp.int32)) % group
+        tags = jnp.take(tags, order, axis=0).reshape(1, seq_len)
+        query_tags, key_tags = tags, tags.reshape(seq_len, 1)
+
+        def pad_heads(value, axis):
+            if not padded:
+                return value
+            fill = [(0, 0)] * value.ndim
+            fill[axis] = (0, padded)
+            return jnp.pad(value, fill)
+
+        def qkv_of(hop):
+            if group == CORES:
+                return gather_pairs(((core + hop) % CORES).reshape(1), qkv_weight)
+            piece = pick(qkv_weight.reshape(width, 3, group, group_width), (member + hop) % group, 2)
+            piece = pad_heads(piece, 2).reshape(width, 3, pairs, lanes)
+            return piece.transpose(0, 2, 1, 3).reshape(width, 3 * pairs * lanes)
+
+        def out_of(hop):
+            at = (member + hop) % group * group_width
+            return pad_heads(lax.dynamic_slice_in_dim(out_weight, at, group_width, 0), 0)
+
+        start = to_rows(inputs)
+        qkv_parts = [qkv_of(hop) for hop in range(group)]
+        out_parts = [out_of(hop) for hop in range(group)]
+        start_low = start
+        start = start.astype(f32)
+        unit1, scale1 = norm_parts(start)
+        n1 = (unit1 * attention_gain).astype(bf16)
+        n1_all = jnp.concatenate([n1] + [to_member(n1, hop) for hop in range(1, group)], 0)
+        cotangent, _ = tie(cotangent, start[:1])
+        cot = to_rows(cotangent)
+        qkv = dot(n1_all, qkv_parts[0], 1, 0).astype(bf16)
+        mixed, lse = attend(qkv, key_tags, query_tags)
+        mixed_parts = [mixed[:tokens]] + [
+            to_member(mixed[hop * tokens : (hop + 1) * tokens], group - hop) for hop in range(1, group)
+        ]
+        middle = start
+        for part, weight in zip(mixed_parts, out_parts):
+            middle = middle + dot(part, weight, 1, 0)
+        outputs, d_middle, d_attn, down_part, up_part = feed(middle, cot, feed_gain, up_weight, down_weight, n_seq)
+
+        d_attn_all = jnp.concatenate([d_attn] + [to_member(d_attn, hop) for hop in range(1, group)], 0)
+
+
+        half = width // CORES
+        if group == CORES:
+            mixed_own = ordered(mixed_parts[0], mixed_parts[1], 1)
+        else:
+            slots = jnp.stack([part[:, :group_width] for part in mixed_parts])
+            turn = (jnp.arange(group, dtype=jnp.int32) - member) % group
+            mixed_own = jnp.take(slots, turn, axis=0).transpose(1, 0, 2).reshape(tokens, width)
+        out_grad = dot(mixed_own, d_attn, 0, 0).astype(bf16)
+        out_kept = lax.dynamic_slice_in_dim(out_grad, core * half, half, 1)
+        out_received = other_core(lax.dynamic_slice_in_dim(out_grad, (1 - core) * half, half, 1))
+        d_mixed = dot(d_attn_all, out_parts[0], 1, 1).astype(bf16)
+
+        if chips == 1 and highs == 2:
+            input_grad, out_low, qkv_out, down_all, up_all = back(
+                qkv, mixed, d_mixed, lse, key_tags, query_tags, n1_all.T, qkv_parts, attention_gain,
+                out_kept, out_received, down_part, up_part, start_low, d_middle, outputs, row_count,
+            )
+            qkv_total, out_total, down_total, up_total, first, second = collect(
+                seq_at, qkv_out, down_all, up_all, qkv_weight, up_weight, attention_gain, feed_gain
+            )
+            return (
+                out_low.reshape(inputs.shape),
+                input_grad.reshape(inputs.shape),
+                first.reshape(-1),
+                qkv_total,
+                out_total,
+                second.reshape(-1),
+                up_total,
+                down_total,
+            )
+        out_low = from_rows(outputs)
+        input_grad, qkv_total, out_total, down_total, up_total = back_by_steps(
+            qkv, mixed, d_mixed, lse, key_tags, query_tags, n1_all, qkv_parts, attention_gain,
+            out_kept, out_received, down_part, up_part, start, d_middle, to_member, ordered, from_rows,
+            (group, member, core, pairs, group_width, tokens, width),
+        )
 
         shard = width // n_seq
 

time: 872 us -> 677 us (0.78)
  waiting for transfers between devices: 95.4 us -> 2.89 us
  Pallas kernels: 463 us -> 510 us
  matrix products: 87.2 us -> 41.5 us
  starting transfers between devices: 47.1 us -> 6.46 us
  local copies, waits for them, and re-layouts: 65.1 us -> 27.2 us
  other arithmetic: 38.3 us -> 16.6 us
    ppermute x37 -> x7, waiting for transfers between devices: 95.4 us -> 2.89 us  [permute(): return lax.ppermute(value, AXES, pairs)]
    pallas_call x28 -> x2, Pallas kernels: 229 us -> 276 us  [the longest x1 266 us: back(): pl.pallas_call(functools.partial(back_kernel, pairs, tile, streams, row_c...]
    dot_general x10 -> x5, matrix products: 87.2 us -> 41.5 us  [dot(): lax.dot_general(a, b, (((ca,), (cb,)), ((), ())), preferred_element_type=...]
    ppermute x37 -> x7, starting transfers between devices: 31.9 us -> 1.84 us  [permute(): return lax.ppermute(value, AXES, pairs)]
    convert_element_type x4 -> x0, local copies, waits for them, and re-layouts: 15.1 us -> none  [the longest x2 8.44 us: per_device(): ordered(up_total, other_core(up_total), 2).reshape(width // n_seq, -1)]
    convert_element_type x5 -> x0, other arithmetic: 10.7 us -> none  [the longest x1 3.96 us: per_device(): down_total = ordered(down_total, other_core(down_total), 1).astype(f32)]
    all_to_all x2 -> x0, starting transfers between devices: 10.5 us -> none  [from_rows(): lax.all_to_all(value.reshape(n_seq, sub, width), 'seq', 0, 0, tiled=True)]
    concatenate x8 -> x0, local copies, waits for them, and re-layouts: 9.64 us -> none  [the longest x6 6.56 us: gather_high(): jnp.concatenate([value, received], 0)]
  transfers between devices with their start and end apart: 40 -> 8, of which waited for: 13 -> 1; matrix products, arithmetic and copies ran while one was open for 20% -> 11% of each run, Pallas kernels for 38% -> 15%
where the time goes in v3:
time: 677 us; the launch traced here: 672 us
  Pallas kernels  510 us (75%)
  blocking collectives  66.7 us (10%)
  matrix products  41.5 us (6%)
  local copies, waits for them, and re-layouts  27.2 us (4%)
  other arithmetic  16.6 us (2%)
    pallas_call x1, Pallas kernels, back(): pl.pallas_call(functools.partial(back_kernel, pairs, tile, streams, row_c...  266 us
    pallas_call x1, Pallas kernels, feed(): pl.pallas_call(functools.partial(feed_kernel, tiles, 128), grid=(tiles +...  132 us
    pallas_call x1, Pallas kernels, attend(): pl.pallas_call(functools.partial(attend_kernel, tile), grid=(pairs,), in_...  81 us
    all_to_all x1, blocking collectives, to_rows(): return lax.all_to_all(both, 'seq', 0, 0, tiled=True).reshape(tokens, width)  66.7 us
    dot_general x5, matrix products, dot(): lax.dot_general(a, b, (((ca,), (cb,)), ((), ())), preferred_element_type=...  41.5 us
    pallas_call x2, Pallas kernels, gather_pairs(): pl.pallas_call(copy_kernel, grid_spec=pltpu.PrefetchScalarGridSpec(num_sc...  20.5 us
  transfers between devices with their start and end apart: 8, of which 1 were waited for; matrix products, arithmetic and copies ran while one was open for 11% of the time, Pallas kernels for 15%

profile of v3, /device:TPU:0, one launch (start us, length us, event | category | flops | bytes accessed | tf_op | source)
XLA Modules:
  0.0 672.3 jit_solution(1333472659943760064)
XLA Ops:
  0.7 3.0 dynamic-slice_bitcast_fusion.3
  3.6 0.5 collective-permute-start.1
  4.1 2.9 collective-permute-done.1
  6.9 0.4 maximum_select_fusion
  7.4 66.7 %all_to_all.10 = bf16[8,128,1280]{2,1,0:T(8,128)(2,1)S(1)} all-to-all(bf16[8,128,1280]{2,1,0:T(8,128)(2,1)S(1)} %maximum_select_fusion), channel_id=1, replica_groups=mesh['seq'=8,'rows'=4] {'seq'}, dimensions={0} | all-to-all | bytes 5242880 | tf_op jit(solution)/shard_map/all_to_all | solution.py:1267
  74.1 0.4 convert_reduce_fusion
  74.5 0.8 fusion.5
  75.4 0.0 copy-start.3
  75.4 2.3 fusion.2
  77.8 1.7 dynamic-slice_bitcast_fusion.1
  79.4 0.5 collective-permute-start.4
  79.9 0.1 fusion.24
  80.0 0.0 collective-permute-start
  80.1 10.3 %gather_pairs.2.refs_9_ = bf16[1280,1920]{1,0:T(8,128)(2,1)} custom-call(s32[1]{0:T(128)} %bitcast.10.core_ref, bf16[1280,3840]{1,0:T(8,128)(2,1)} %refs_8_.1), custom_call_target="tpu_custom_call" | custom-call | bytes 9830400 | tf_op jit(solution)/shard_map/gather_pairs/pallas_call | solution.py:177
  90.4 0.1 broadcast_select_fusion
  90.5 0.6 gather_fusion
  91.0 0.1 select_bitcast_fusion
  91.1 1.4 copy.25
  92.5 3.9 maximum_select_fusion.1
  96.4 4.6 all-to-all-start.1
  101.1 16.5 %convolution_convert_fusion.1.q_ref.k_ref.v_ref.refs_2_.refs_3_.refs_4_ = bf16[2048,1920]{1,0:T(8,128)(2,1)} fusion(bf16[1280,1920]{1,0:T(8,128)(2,1)} %gather_pairs.2.refs_9_, bf16[1024,1280]{1,0:T(8,128)(2,1)} %collective-permute-done.2, bf16[1024,1280]{1,0:T(8,128)(2,1)} %fusion.2), kind=kOutput, calls=%fused_computation.2 | convolution fusion | flops 10080747520 | bytes 18022400 | tf_op jit(solution)/shard_map/dot_general | solution.py:26
  117.6 81.0 %attend.1 = (bf16[2048,640]{1,0:T(8,128)(2,1)}, f32[5,2,2048]{2,1,0:T(2,128)}) custom-call(s32[2048,1]{1,0:T(8,128)} %bitcast.53, s32[1,2048]{1,0:T(1,128)} %bitcast.57, bf16[2048,1920]{1,0:T(8,128)(2,1)} %convolution_convert_fusion.1.q_ref.k_ref.v_ref.refs_2_.refs_3_.refs_4_, ...), custom_call_target="tpu_custom_call" | custom-call | flops 42949672960 | bytes 10485760 | tf_op jit(solution)/shard_map/attend/pallas_call | solution.py:64
  198.6 0.0 copy-start.10
  198.7 3.5 fusion.38
  202.1 0.5 collective-permute-start.3
  202.6 0.6 reshape.221.gain_ref
  203.2 4.2 fusion.22
  207.4 5.8 fusion.3.middle_ref
  213.2 132.3 %feed.1 = (bf16[1024,1280]{1,0:T(8,128)(2,1)}, f32[1024,1280]{1,0:T(8,128)}, bf16[1024,1280]{1,0:T(8,128)(2,1)}, bf16[2560,640]{1,0:T(8,128)(2,1)}, bf16[640,2560]{1,0:T(8,128)(2,1)}) custom-call(f32[1024,1280]{1,0:T(8,128)} %fusion.3.middle_ref, bf16[1024,1280]{1,0:T(8,128)(2,1)} %bitcast.14.cot_ref, f32[1,1280]{1,0:T(1,128)} %reshape.221.gain_ref, ...), custom_call_target="tpu_custom_call" | custom-call | flops 80530636800 | bytes 60293120 | tf_op jit(solution)/shard_map/feed/pallas_call | solution.py:427
  345.6 0.1 collective-permute-start.5
  345.7 6.2 convolution_convert_fusion
  351.8 0.0 copy-start.7
  351.8 1.6 constant_dynamic-slice_fusion
  353.5 0.3 collective-permute-start.6
  353.8 0.6 broadcast_in_dim.29.refs_11_
  354.4 1.1 reshape.242.refs_10_
  355.4 1.1 reshape.243.refs_11_
  356.5 10.2 %gather_pairs.3.refs_10_ = bf16[1280,1920]{1,0:T(8,128)(2,1)} custom-call(s32[1]{0:T(128)} %bitcast.16.core_ref, bf16[1280,3840]{1,0:T(8,128)(2,1)} %refs_8_.1), custom_call_target="tpu_custom_call" | custom-call | bytes 9830400 | tf_op jit(solution)/shard_map/gather_pairs/pallas_call | solution.py:177
  366.7 5.2 fusion.10
  372.0 8.0 %copy.21.refs_8_ = bf16[1280,2048]{1,0:T(8,128)(2,1)} copy(bf16[1280,2048]{0,1:T(8,128)(2,1)} %fusion.10) | data formatting | bytes 10485760 | tf_op jit(solution)/shard_map/transpose | solution.py:1340
  379.9 8.8 %fusion.11.refs_6_ = bf16[2048,640]{1,0:T(8,128)(2,1)} fusion(bf16[1024,1280]{1,0:T(8,128)(2,1)} %collective-permute-done.5, bf16[1024,1280]{1,0:T(8,128)(2,1)} %get-tuple-element.27, bf16[1280,1280]{1,0:T(8,128)(2,1)} %param.16, s32[]{:T(128)S(6)} %select_n.154), kind=kOutput, calls=%fused_computation.19 | convolution fusion | flops 3367239680 | bytes 9502724 | tf_op jit(solution)/shard_map/dot_general | solution.py:26
  388.7 266.5 %back.1 = (bf16[4,2,128,1280]{3,2,1,0:T(8,128)(2,1)}, bf16[4,2,128,1280]{3,2,1,0:T(8,128)(2,1)}, bf16[5,2,2,80,512]{4,3,2,1,0:T(8,128)(2,1)}, bf16[5,2,2,320,128...) custom-call(s32[2048,1]{1,0:T(8,128)} %bitcast.54, s32[1,2048]{1,0:T(1,128)} %bitcast.58, ...), custom_call_target="tpu_custom_call" | custom-call | flops 107374182400 | bytes 20971520 | tf_op jit(solution)/shard_map/back/pallas_call | solution.py:823
  655.2 9.6 %collect.1 = (f32[160,3840]{1,0:T(8,128)}, f32[160,1280]{1,0:T(8,128)}, f32[640,1280]{1,0:T(8,128)}, f32[160,5120]{1,0:T(8,128)}, f32[160,1]{1,0:T(8,128)}, /*index=5*/f32[160,1]{1,0:T(8,128)}) custom-call(s32[1]{0:T(128)} %bitcast.23.seq_ref, bf16[5,2,2,80,512]{4,3,2,1,0:T(8,128)(2,1)} %get-tuple-element.35.refs_0_, ...), custom_call_target="tpu_custom_call" | custom-call | tf_op jit(solution)/shard_map/collect/pallas_call | solution.py:954
  664.8 1.6 reduce.2
  666.3 1.6 reduce.3
  667.9 1.5 copy.29
  669.4 1.2 copy-done.1
  670.6 1.5 copy.30
  (35 shorter events, 0.1 us)
Async XLA Ops:
  3.6 3.3 collective-permute-start.1
  74.1 133.3 %copy-start = (bf16[8,128,1280]{2,1,0:T(8,128)(2,1)}, bf16[8,128,1280]{2,1,0:T(8,128)(2,1)S(1)}, u32[]{:S(2)}) copy-start(bf16[8,128,1280]{2,1,0:T(8,128)(2,1)S(1)} %all_to_all.10) | copy-start | bytes 7864324
  74.1 1.3 copy-start.6
  75.4 2.4 copy-start.3
  77.7 23.3 %collective-permute-start.2 = (bf16[1024,1280]{1,0:T(8,128)(2,1)}, bf16[1024,1280]{1,0:T(8,128)(2,1)}, u32[]{:S(2)}, u32[]{:S(2)}) collective-permute-start(bf16[1024,1280]{1,0:T(8,128)(2,1)} %fusion.2), channel_id=1, source_target_pairs={{0,1},{1,0},{2,3},{3,2},{4,5},{5,4},{6,7},{7,6},{8,9},{9,8},{10,11... | collective-permute-start | bytes 7864328 | tf_op jit(solution)/shard_map/ppermute | solution.py:1071
  77.7 2.2 copy-start.9
  77.8 2.2 copy-start.11
  79.4 13.1 %collective-permute-start.4 = (bf16[4,128,1280]{2,1,0:T(8,128)(2,1)}, bf16[4,128,1280]{2,1,0:T(8,128)(2,1)}, u32[]{:S(2)}, u32[]{:S(2)}) collective-permute-start(bf16[4,128,1280]{2,1,0:T(8,128)(2,1)} %get-tuple-element.49), channel_id=1, source_target_pairs={{0,1},{1,0},{2,3},{3,2},{4,5},{5,4},{6,7},{7,6},{8,9},{9,8},{10,11... | collective-permute-start | bytes 3932168 | tf_op jit(solution)/shard_map/ppermute | solution.py:1071
  80.0 10.4 %collective-permute-start = (s32[4,2048]{1,0:T(4,128)S(1)}, s32[4,2048]{1,0:T(4,128)S(1)}, u32[]{:S(2)}, u32[]{:S(2)}) collective-permute-start(s32[4,2048]{1,0:T(4,128)S(1)} %fusion.24), channel_id=1, source_target_pairs={{0,1},{1,0},{2,3},{3,2},{4,5},{5,4},{6,7},{7,6},{8,9},{9,8},{10,11... | collective-permute-start | bytes 98312 | tf_op jit(solution)/shard_map/ppermute | solution.py:1071
  91.1 5.3 copy-start.8
  96.4 116.8 %all-to-all-start.1 = ((bf16[8,128,1280]{2,1,0:T(8,128)(2,1)}), bf16[8,128,1280]{2,1,0:T(8,128)(2,1)}, u32[]{:S(2)}, u32[]{:S(2)}) async-start(bf16[8,128,1280]{2,1,0:T(8,128)(2,1)} %maximum_select_fusion.1), calls=%async_computation.1 | async-start | bytes 5242880 | tf_op jit(solution)/shard_map/all_to_all | solution.py:1267
  198.6 4.0 copy-start.10
  202.1 5.3 collective-permute-start.3
  203.2 4.2 copy-start.5
  213.2 132.4 %copy-start.4 = (bf16[1024,640]{1,0:T(8,128)(2,1)S(1)}, bf16[1024,640]{1,0:T(8,128)(2,1)}, u32[]{:S(2)}) copy-start(bf16[1024,640]{1,0:T(8,128)(2,1)} %get-tuple-element.46) | copy-start | bytes 3932164
  345.6 34.4 %collective-permute-start.5 = (bf16[1024,1280]{1,0:T(8,128)(2,1)}, bf16[1024,1280]{1,0:T(8,128)(2,1)}, u32[]{:S(2)}, u32[]{:S(2)}) collective-permute-start(bf16[1024,1280]{1,0:T(8,128)(2,1)} %get-tuple-element.27), channel_id=1, source_target_pairs={{0,1},{1,0},{2,3},{3,2},{4,5},{5,4},{6,7},{7,6},{8,9},{9,8},{10,11... | collective-permute-start | bytes 7864328 | tf_op jit(solution)/shard_map/ppermute | solution.py:1071
  351.8 1.9 copy-start.7
  353.5 35.2 %collective-permute-start.6 = (bf16[1280,640]{1,0:T(8,128)(2,1)S(1)}, bf16[1280,640]{1,0:T(8,128)(2,1)}, u32[]{:S(2)}, u32[]{:S(2)}) collective-permute-start(bf16[1280,640]{1,0:T(8,128)(2,1)S(1)} %get-tuple-element.44), channel_id=1, source_target_pairs={{0,1},{1,0},{2,3},{3,2},{4,5},{5,4},{6,7},{7,6},{8,9},{9,8},{10,11... | collective-permute-start | bytes 4915208 | tf_op jit(solution)/shard_map/ppermute | solution.py:1071
  655.2 12.7 %copy-start.2 = (bf16[4,2,128,1280]{3,2,1,0:T(8,128)(2,1)S(1)}, bf16[4,2,128,1280]{3,2,1,0:T(8,128)(2,1)}, u32[]{:S(2)}) copy-start(bf16[4,2,128,1280]{3,2,1,0:T(8,128)(2,1)} %get-tuple-element.33) | copy-start | bytes 7864324
  667.9 2.7 copy-start.1

commit v4 on v3

--- a/solution.py
+++ b/solution.py
@@ -19,6 +19,7 @@
 vmem_bytes = 60 * 2**20
 feed_vmem_bytes = 62 * 2**20
 feed_tile = 512
+max_cells = 7
 MESH = pl.DeviceIdType.MESH
 
 
@@ -204,7 +205,404 @@
     )
 
 
-piece_rows = 32
+def all_signal(n_seq, seq_at, rows_at, extra=()):
+    core = rows_at % CORES
+    barrier = pltpu.get_barrier_semaphore()
+    for s in range(n_seq):
+        for c in range(CORES):
+            @pl.when(jnp.logical_not((seq_at == s) & (core == c)))
+            def _():
+                pl.semaphore_signal(barrier, inc=1, device_id=(s, rows_at - core + c), device_id_type=MESH)
+    for peer in extra:
+        pl.semaphore_signal(barrier, inc=1, device_id=peer, device_id_type=MESH)
+    pl.semaphore_wait(barrier, n_seq * CORES - 1 + len(extra))
+
+
+class ToRows:
+    def __init__(self, source, target, send, recv, local, row_count, seq_at, rows_at):
+        self.source, self.target, self.send, self.recv, self.local = source, target, send, recv, local
+        self.row_count, self.seq_at, self.rows_at = row_count, seq_at, rows_at
+        self.core = rows_at % CORES
+
+    def copy(self, row, c):
+        chip = self.core * self.row_count + row
+        return pltpu.make_async_remote_copy(
+            src_ref=self.source.at[row, c],
+            dst_ref=self.target.at[self.seq_at],
+            send_sem=self.send.at[row, c],
+            recv_sem=self.recv.at[self.seq_at],
+            device_id=(chip, self.rows_at - self.core + c),
+            device_id_type=MESH,
+        )
+
+    def own(self, row, c):
+        return pltpu.make_async_copy(self.source.at[row, c], self.target.at[self.seq_at], self.local)
+
+    def each(self, own, other):
+        for row_turn in range(self.row_count):
+            for core_turn in range(CORES):
+                row = (row_turn + self.seq_at) % self.row_count
+                c = (core_turn + self.seq_at // self.row_count) % CORES
+                here = (self.core * self.row_count + row == self.seq_at) & (self.core == c)
+
+                @pl.when(here)
+                def _():
+                    own(row, c)
+
+                @pl.when(jnp.logical_not(here))
+                def _():
+                    other(row, c)
+
+    def start(self):
+        self.each(lambda row, c: self.own(row, c).start(), lambda row, c: self.copy(row, c).start())
+
+    def wait_block(self, s):
+        here = (s == self.seq_at) & (self.seq_at // self.row_count == self.core)
+
+        @pl.when(here)
+        def _():
+            self.own(0, 0).wait()
+
+        @pl.when(jnp.logical_not(here))
+        def _():
+            pltpu.make_async_remote_copy(
+                src_ref=self.source.at[0, 0],
+                dst_ref=self.target.at[s],
+                send_sem=self.send.at[0, 0],
+                recv_sem=self.recv.at[s],
+                device_id=(self.seq_at, self.rows_at + 1 - 2 * self.core),
+                device_id_type=MESH,
+            ).wait_recv()
+
+    def wait_sends(self):
+        self.each(lambda row, c: None, lambda row, c: self.copy(row, c).wait_send())
+
+
+def begin_kernel(
+    row_count, pairs, x_ref, weight_ref, gain_ref, x_out, n1_out, qkv_out, own_out, other_out,
+    x_part, n1, qkv, weight, other_weight,
+    x_send, x_recv, x_local, n1_send, n1_recv, weight_sems, out_sems, x_sems, qkv_sems, n1_sems,
+):
+    seq_at, rows_at = lax.axis_index("seq"), lax.axis_index("rows")
+    core = rows_at % CORES
+    n_seq, sub, width = x_part.shape
+    lanes = 2 * HDIM
+    tokens = n_seq * sub
+    moves = ToRows(x_ref, x_part, x_send, x_recv, x_local, row_count, seq_at, rows_at)
+
+    def weight_copies(item, which):
+        pair, kind = item // 3, item % 3
+        to = pl.ds(pl.multiple_of(item * lanes, lanes), lanes)
+
+        def columns(c):
+            return pl.ds(pl.multiple_of((kind * CORES + c) * pairs * lanes + pair * lanes, lanes), lanes)
+
+        source = weight_ref.at[:, columns(1 - core if which else core)]
+        return pltpu.make_async_copy(source, (weight, other_weight)[which].at[:, to], weight_sems.at[which, item])
+
+    def each_weight(act, which):
+        def body(item, _):
+            act(weight_copies(item, which))
+            return 0
+
+        lax.fori_loop(0, 3 * pairs, body, 0)
+
+    each_weight(lambda copy: copy.start(), 0)
+    all_signal(n_seq, seq_at, rows_at)
+    moves.start()
+    each_weight(lambda copy: copy.start(), 1)
+    each_weight(lambda copy: copy.wait(), 0)
+    weights_out = (
+        pltpu.make_async_copy(weight, own_out, out_sems.at[0]),
+        pltpu.make_async_copy(other_weight, other_out, out_sems.at[1]),
+    )
+    weights_out[0].start()
+    each_weight(lambda copy: copy.wait(), 1)
+    weights_out[1].start()
+
+    def block_of(place):
+        near = (place % 2) * ((place + 1) // 2) + (1 - place % 2) * ((n_seq - place // 2) % n_seq)
+        return (seq_at + near) % n_seq
+
+    def rows_of(s, other):
+        return pl.ds(pl.multiple_of(s * sub + other * tokens, sub), sub)
+
+    def n1_copy(s):
+        return pltpu.make_async_remote_copy(
+            src_ref=n1.at[rows_of(s, 0)],
+            dst_ref=n1.at[rows_of(s, 1)],
+            send_sem=n1_send.at[s],
+            recv_sem=n1_recv.at[s],
+            device_id=(seq_at, rows_at + 1 - 2 * core),
+            device_id_type=MESH,
+        )
+
+    def x_copy(s):
+        return pltpu.make_async_copy(x_part.at[s], x_out.at[s], x_sems.at[s])
+
+    def out_copies(s, other):
+        rows = rows_of(s, other)
+        return (
+            pltpu.make_async_copy(qkv.at[rows], qkv_out.at[rows], qkv_sems.at[other, s]),
+            pltpu.make_async_copy(n1.at[rows], n1_out.at[rows], n1_sems.at[other, s]),
+        )
+
+    def product(first, second, other):
+        both = jnp.concatenate([n1[rows_of(first, other), :], n1[rows_of(second, other), :]], 0)
+        found = dot(both, weight[...], 1, 0).astype(bf16)
+        for at, s in enumerate((first, second)):
+            qkv[rows_of(s, other), :] = found[at * sub : (at + 1) * sub]
+            for copy in out_copies(s, other):
+                copy.start()
+
+    def body(group, _):
+        @pl.when(group < n_seq // 2)
+        def _():
+            places = block_of(2 * group), block_of(2 * group + 1)
+            for s in places:
+                moves.wait_block(s)
+                x_copy(s).start()
+                unit, _s = norm_parts(x_part[s].astype(f32))
+                n1[rows_of(s, 0), :] = (unit * gain_ref[...]).astype(bf16)
+                n1_copy(s).start()
+            product(*places, 0)
+
+        @pl.when(group > 0)
+        def _():
+            places = block_of(2 * group - 2), block_of(2 * group - 1)
+            for s in places:
+                n1_copy(s).wait()
+            product(*places, 1)
+
+        return 0
+
+    lax.fori_loop(0, n_seq // 2 + 1, body, 0)
+
+    def finish(s, _):
+        x_copy(s).wait()
+        for other in range(2):
+            for copy in out_copies(s, other):
+                copy.wait()
+        return 0
+
+    lax.fori_loop(0, n_seq, finish, 0)
+    moves.wait_sends()
+    for copy in weights_out:
+        copy.wait()
+
+
+def begin(inputs, qkv_weight, gain):
+    row_count, block, width = inputs.shape
+    n_seq = CORES * row_count
+    lanes = 2 * HDIM
+    pairs = width // (CORES * lanes)
+    sub = block // CORES
+    tokens = n_seq * sub
+    hbm = pl.BlockSpec(memory_space=pl.ANY)
+    return pl.pallas_call(
+        functools.partial(begin_kernel, row_count, pairs),
+        in_specs=[hbm, hbm, pl.BlockSpec(memory_space=pltpu.VMEM)],
+        out_specs=[hbm] * 5,
+        out_shape=[
+            jax.ShapeDtypeStruct((n_seq, sub, width), bf16),
+            jax.ShapeDtypeStruct((CORES * tokens, width), bf16),
+            jax.ShapeDtypeStruct((CORES * tokens, 3 * pairs * lanes), bf16),
+            jax.ShapeDtypeStruct((width, 3 * pairs * lanes), bf16),
+            jax.ShapeDtypeStruct((width, 3 * pairs * lanes), bf16),
+        ],
+        scratch_shapes=[
+            pltpu.VMEM((n_seq, sub, width), bf16),
+            pltpu.VMEM((CORES * tokens, width), bf16),
+            pltpu.VMEM((CORES * tokens, 3 * pairs * lanes), bf16),
+            pltpu.VMEM((width, 3 * pairs * lanes), bf16),
+            pltpu.VMEM((width, 3 * pairs * lanes), bf16),
+            pltpu.SemaphoreType.DMA((row_count, CORES)),
+            pltpu.SemaphoreType.DMA((n_seq,)),
+            pltpu.SemaphoreType.DMA,
+            pltpu.SemaphoreType.DMA((n_seq,)),
+            pltpu.SemaphoreType.DMA((n_seq,)),
+            pltpu.SemaphoreType.DMA((2, 3 * pairs)),
+            pltpu.SemaphoreType.DMA((2,)),
+            pltpu.SemaphoreType.DMA((n_seq,)),
+            pltpu.SemaphoreType.DMA((CORES, n_seq)),
+            pltpu.SemaphoreType.DMA((CORES, n_seq)),
+        ],
+        compiler_params=pltpu.CompilerParams(
+            vmem_limit_bytes=vmem_bytes, collective_id=3, has_side_effects=True
+        ),
+        name="begin",
+    )(inputs.reshape(row_count, CORES, sub, width), qkv_weight, gain.reshape(1, width))
+
+
+def with_cells(value, tags, head, is_key):
+    lane = lax.broadcasted_iota(jnp.int32, value.shape, 1)
+    cell = lane - (1 - head) * HDIM
+    if is_key:
+        marks = jnp.where((cell == tags) | (cell >= max_cells), 0.0, -1.0)
+    else:
+        marks = jnp.where(cell == tags, -masked_score, 0.0)
+    return jnp.where((lane // HDIM) == head, value, marks.astype(bf16))
+
+
+def attend_row_kernel(
+    tile, row_count, tags, row_tags, q_ref, k_ref, v_ref, cot_ref, o_ref, lse_ref, cot_out, own_out,
+    v_turned, keys, scores_ref, mixed_ref, parts,
+    cot_send, cot_recv, cot_local, part_send, part_recv, part_local,
+):
+    item, last = pl.program_id(0), pl.num_programs(0) - 1
+    seq_at, rows_at = lax.axis_index("seq"), lax.axis_index("rows")
+    core = rows_at % CORES
+    tokens, lanes = q_ref.shape
+    own_tokens = tokens // CORES
+    n_seq = cot_out.shape[0]
+    moves = ToRows(cot_ref, cot_out, cot_send, cot_recv, cot_local, row_count, seq_at, rows_at)
+
+    def part_copies(at):
+        slot = at % 2
+        half = pl.num_programs(0) * lanes
+        columns = pl.ds(pl.multiple_of(core * half + at * lanes, lanes), lanes)
+        return (
+            pltpu.make_async_remote_copy(
+                src_ref=parts.at[slot, pl.ds(own_tokens, own_tokens)],
+                dst_ref=own_out.at[:, columns],
+                send_sem=part_send.at[slot],
+                recv_sem=part_recv.at[at],
+                device_id=(seq_at, rows_at + 1 - 2 * core),
+                device_id_type=MESH,
+            ),
+            pltpu.make_async_copy(parts.at[slot, pl.ds(0, own_tokens)], own_out.at[:, columns], part_local.at[slot]),
+        )
+
+    def part_came(at):
+        half = pl.num_programs(0) * lanes
+        columns = pl.ds(pl.multiple_of((1 - core) * half + at * lanes, lanes), lanes)
+        return pltpu.make_async_remote_copy(
+            src_ref=parts.at[0, pl.ds(own_tokens, own_tokens)],
+            dst_ref=own_out.at[:, columns],
+            send_sem=part_send.at[0],
+            recv_sem=part_recv.at[at],
+            device_id=(seq_at, rows_at + 1 - 2 * core),
+            device_id_type=MESH,
+        )
+
+    @pl.when(item == 0)
+    def _():
+        all_signal(n_seq, seq_at, rows_at)
+        moves.start()
+
+    for head in range(2):
+        keys[head] = with_cells(k_ref[...], tags[...], head, True)
+        v_turned[head, :HDIM, :] = v_ref[...].T[head * HDIM : (head + 1) * HDIM, :]
+        v_turned[head, HDIM:, :] = jnp.ones((16, tokens), bf16)
+
+    def begin_scores(step, head):
+        part = pl.ds(pl.multiple_of(step * tile, tile), tile)
+        scores_ref[head] = dot(keys[head], with_cells(q_ref[part, :], tags[part, :], head, False), 1, 1)
+
+    def finish(step, head):
+        part = pl.ds(pl.multiple_of(step * tile, tile), tile)
+        scores = scores_ref[head]
+        peak = jnp.max(scores, axis=0, keepdims=True)
+        powers = jnp.exp2((scores - peak) * (score_scale * log2e))
+        mixed = dot(v_turned[head], powers.astype(bf16), 1, 0)
+        total = mixed[HDIM : HDIM + 1, :]
+        mixed_ref[head * HDIM : (head + 1) * HDIM, part] = mixed[:HDIM, :] * (1.0 / total)
+        lse = peak * (score_scale * log2e) + jnp.log2(total)
+        lse_ref[head : head + 1, part] = jnp.where(row_tags[:, part] < 0, -masked_score, lse)
+
+    steps = tokens // tile
+    begin_scores(0, 0)
+
+    def body(step, _):
+        begin_scores(step, 1)
+        finish(step, 0)
+        begin_scores(jnp.minimum(step + 1, steps - 1), 0)
+        finish(step, 1)
+        return 0
+
+    lax.fori_loop(0, steps, body, 0)
+    found = jnp.where(tags[...] < 0, v_ref[...], mixed_ref[...].T.astype(bf16))
+    o_ref[...] = found
+
+    @pl.when(item >= 2)
+    def _():
+        remote, local = part_copies(item - 2)
+        remote.wait_send()
+        local.wait()
+
+    parts[item % 2] = found
+    for copy in part_copies(item):
+        copy.start()
+
+    @pl.when(item == last)
+    def _():
+        for at in range(2):
+            remote, local = part_copies(last - at)
+            remote.wait_send()
+            local.wait()
+        for at in range(part_recv.shape[0]):
+            part_came(at).wait_recv()
+        for s in range(n_seq):
+            moves.wait_block(s)
+        moves.wait_sends()
+
+
+def attend_row(qkv, tags, row_tags, cotangent):
+    tokens, width = qkv.shape
+    row_count, block, model = cotangent.shape
+    lanes = 2 * HDIM
+    pairs = width // (3 * lanes)
+    tile = 512
+    n_seq, sub = CORES * row_count, block // CORES
+    hbm = pl.BlockSpec(memory_space=pl.ANY)
+
+    def columns(place):
+        return pl.BlockSpec((tokens, lanes), lambda i: (0, 3 * i + place))
+
+    return pl.pallas_call(
+        functools.partial(attend_row_kernel, tile, row_count),
+        grid=(pairs,),
+        in_specs=[
+            pl.BlockSpec((tokens, 1), lambda i: (0, 0)),
+            pl.BlockSpec((1, tokens), lambda i: (0, 0)),
+            columns(0),
+            columns(1),
+            columns(2),
+            hbm,
+        ],
+        out_specs=[
+            pl.BlockSpec((tokens, lanes), lambda i: (0, i)),
+            pl.BlockSpec((None, 2, tokens), lambda i: (i, 0, 0)),
+            hbm,
+            hbm,
+        ],
+        out_shape=[
+            jax.ShapeDtypeStruct((tokens, pairs * lanes), bf16),
+            jax.ShapeDtypeStruct((pairs, 2, tokens), f32),
+            jax.ShapeDtypeStruct((n_seq, sub, model), bf16),
+            jax.ShapeDtypeStruct((tokens // CORES, model), bf16),
+        ],
+        scratch_shapes=[
+            pltpu.VMEM((2, HDIM + 16, tokens), bf16),
+            pltpu.VMEM((2, tokens, lanes), bf16),
+            pltpu.VMEM((2, tokens, tile), f32),
+            pltpu.VMEM((lanes, tokens), f32),
+            pltpu.VMEM((2, tokens, lanes), bf16),
+            pltpu.SemaphoreType.DMA((row_count, CORES)),
+            pltpu.SemaphoreType.DMA((n_seq,)),
+            pltpu.SemaphoreType.DMA,
+            pltpu.SemaphoreType.DMA((2,)),
+            pltpu.SemaphoreType.DMA((pairs,)),
+            pltpu.SemaphoreType.DMA((2,)),
+        ],
+        compiler_params=pltpu.CompilerParams(
+            vmem_limit_bytes=vmem_bytes, collective_id=4, has_side_effects=True
+        ),
+        name="attend_row",
+    )(tags, row_tags, qkv, qkv, qkv, cotangent.reshape(row_count, CORES, sub, model))
+
+
+piece_rows = 16
 
 
 def feed_kernel(
@@ -217,12 +615,13 @@
     down_ref,
     out_ref,
     d_middle_ref,
-    d_attn_ref,
+    d_attn_out,
     down_part,
     up_part,
     n2,
     n2_turned,
     total,
+    d_attn,
     down_keep,
     down_send,
     down_recv,
@@ -241,6 +640,7 @@
     far_recv_sem,
     core_free,
     far_free,
+    d_attn_sems,
 ):
     step = pl.program_id(0)
     tokens, width = n2.shape
@@ -396,14 +796,33 @@
             unit, scale = norm_parts(middle_ref[part, :])
             grad = cot_ref[part, :].astype(f32) + norm_back(d_middle_ref[part, :], gain_ref[...], unit, scale)
             d_middle_ref[part, :] = grad
-            d_attn_ref[part, :] = grad.astype(bf16)
+            d_attn[part, :] = grad.astype(bf16)
             return 0
 
         lax.fori_loop(0, tokens // rows, body, 0)
 
+    d_attn_copies = lambda: (
+        pltpu.make_async_copy(d_attn, d_attn_out.at[0], d_attn_sems.at[0]),
+        pltpu.make_async_remote_copy(
+            src_ref=d_attn,
+            dst_ref=d_attn_out.at[1],
+            send_sem=d_attn_sems.at[1],
+            recv_sem=d_attn_sems.at[2],
+            device_id=core_peer,
+            device_id_type=MESH,
+        ),
+    )
+
+    @pl.when(step == tiles)
+    def _():
+        for copy in d_attn_copies():
+            copy.start()
+
     @pl.when(step == tiles + 1)
     def _():
         last_add()
+        for copy in d_attn_copies():
+            copy.wait()
         for slot in range(2):
             for far in (False, True):
                 for copy in copies(slot, far):
@@ -419,7 +838,7 @@
     whole = lambda dtype: jax.ShapeDtypeStruct((tokens, width), dtype)
     fixed = lambda shape: pl.BlockSpec(shape, lambda i: (0, 0), pipeline_mode=pl.Buffered(1))
     at = lambda i: jnp.minimum(i, tiles - 1)
-    done = lambda i: jnp.maximum(i - 2, 0)
+    late = lambda i: jnp.maximum(i - 2, 0)
     down_shape = (2, tile // (2 * piece_rows), 2, piece_rows, half)
     up_shape = (2, n_seq // 2, 2, shard, tile // 2)
     near = [pltpu.VMEM(down_shape, bf16)] * 3 + [pltpu.VMEM(up_shape, bf16)] * 3
@@ -437,23 +856,24 @@
         out_specs=[
             fixed((tokens, width)),
             fixed((tokens, width)),
-            fixed((tokens, width)),
-            pl.BlockSpec((tile // 2, half), lambda i: (done(i), 0)),
-            pl.BlockSpec((width // 2, tile // 2), lambda i: (0, done(i))),
+            pl.BlockSpec(memory_space=pl.ANY),
+            pl.BlockSpec((tile // 2, half), lambda i: (late(i), 0)),
+            pl.BlockSpec((width // 2, tile // 2), lambda i: (0, late(i))),
         ],
         scratch_shapes=[
             pltpu.VMEM((tokens, width), bf16),
             pltpu.VMEM((width, tokens), bf16),
             pltpu.VMEM((tokens, width), f32),
+            pltpu.VMEM((tokens, width), bf16),
         ]
         + near
         + far
         + [pltpu.SemaphoreType.DMA((2, 2))] * 4
-        + [pltpu.SemaphoreType.REGULAR, pltpu.SemaphoreType.REGULAR((2,))],
+        + [pltpu.SemaphoreType.REGULAR, pltpu.SemaphoreType.REGULAR((2,)), pltpu.SemaphoreType.DMA((3,))],
         out_shape=[
             whole(bf16),
             whole(f32),
-            whole(bf16),
+            jax.ShapeDtypeStruct((2, tokens, width), bf16),
             jax.ShapeDtypeStruct((wide // 2, half), bf16),
             jax.ShapeDtypeStruct((width // 2, wide // 2), bf16),
         ],
@@ -470,8 +890,8 @@
 
 
 class Stream:
-    def __init__(self, levels, rows, columns):
-        self.levels, self.rows, self.columns = levels, rows, columns
+    def __init__(self, levels, rows, columns, first, count):
+        self.levels, self.rows, self.columns, self.first, self.count = levels, rows, columns, first, count
 
     def shape(self, level):
         outer = 2 ** (len(self.levels) - 1 - level)
@@ -485,18 +905,22 @@
         return shapes
 
 
-def streams_of(block_rows, width, pairs):
+down_pieces = 4
+
+
+def streams_of(width, wide, n_seq, pairs):
     lanes = 2 * HDIM
+    rows = width // (2 * n_seq)
     return (
-        Stream(("x", "y", "z1", "z2"), width // 16, 4 * lanes),
-        Stream(("y", "z1", "z2"), block_rows // 2, lanes),
-        Stream(("x", "z1", "z2"), width // 16, block_rows * 8 // CORES // pairs),
+        Stream(("x", "y", "z1", "z2"), rows, 4 * lanes, 1, pairs),
+        Stream(("y", "z1", "z2"), wide // (2 * n_seq * down_pieces), width // CORES, 0, down_pieces),
+        Stream(("x", "z1", "z2"), rows, wide // CORES // down_pieces, 0, down_pieces),
     )
 
 
 def back_kernel(pairs, tile, streams, row_count, *refs):
     (
-        key_tags, query_tags, q_ref, k_ref, v_ref, o_ref, do_ref, lse_ref, turned_ref, own_weight, other_weight,
+        key_tags, query_tags, q_ref, k_ref, v_ref, o_ref, do_ref, lse_ref, n1_ref, own_weight, other_weight,
         gain_ref, out_kept, out_came, down_ref, up_ref, start_ref, d_middle_ref, outputs_ref,
     ) = refs[:19]
     grad_out, outputs_out, *gathered = refs[19:24]
@@ -626,22 +1050,29 @@
         for block in range(n_seq):
             start_home(block, True)
 
-    @pl.when(step < pairs)
-    def _():
-        slot = step % 2
+    working, second = step < 2 * pairs, step % 2
+
+    @pl.when(working & (second == 0))
+    def _():
         k_turned[...] = k_ref[...].T
         dq_turned[...] = (o_ref[...].astype(f32) * do_ref[...].astype(f32)).T
         for head in range(2):
             own_rows = dq_turned[head * HDIM : (head + 1) * HDIM, :]
             delta[head : head + 1, :] = jnp.sum(own_rows, axis=0, keepdims=True)
         dq_turned[...] = jnp.zeros_like(dq_turned)
+
+    @pl.when(working)
+    def _():
+        slot = step // 2 % 2
+        half_steps = tokens // tile // 2
         first = lax.broadcasted_iota(jnp.int32, (tile, lanes), 1) < HDIM
 
         def body(i, _):
-            part = pl.ds(pl.multiple_of(i * tile, tile), tile)
+            part = pl.ds(pl.multiple_of((i + second * half_steps) * tile, tile), tile)
             k, v = k_ref[part, :], v_ref[part, :]
             q, do = q_ref[...], do_ref[...]
-            allowed = key_tags[part, :] == query_tags[...]
+            tag = key_tags[part, :]
+            allowed = tag == query_tags[...]
             dk, dv = [], []
             for head in range(2):
                 own = first if head == 0 else jnp.logical_not(first)
@@ -655,27 +1086,31 @@
                 dk.append(dot(score_grad, q, 1, 0))
                 dq_turned[own_rows, :] += dot(k_turned[own_rows, part], score_grad, 1, 0)
             d_pair[slot, part, lanes : 2 * lanes] = (jnp.where(first, dk[0], dk[1]) * score_scale).astype(bf16)
-            d_pair[slot, part, 2 * lanes :] = jnp.where(first, dv[0], dv[1]).astype(bf16)
+            d_v = jnp.where(first, dv[0], dv[1]).astype(bf16)
+            d_pair[slot, part, 2 * lanes :] = jnp.where(tag < 0, do_ref[part, :], d_v)
             return 0
 
-        lax.fori_loop(0, tokens // tile, body, 0)
-        d_pair[slot, :, :lanes] = (dq_turned[...] * score_scale).T.astype(bf16)
+        lax.fori_loop(0, half_steps, body, 0)
+
+    @pl.when(working & (second == 1))
+    def _():
+        d_pair[step // 2 % 2, :, :lanes] = (dq_turned[...] * score_scale).T.astype(bf16)
 
     def add_pair():
-        item = step - 1
+        item = step // 2 - 1
         slot = item % 2
         pair_copy(item).wait()
         d_n1[...] += dot(d_pair[slot, :own_tokens, :], own_weight[...], 1, 1) + dot(
             d_came[slot], other_weight[...], 1, 1
         )
 
-    @pl.when((step >= 1) & (step <= pairs))
+    @pl.when((step >= 2) & (step <= 2 * pairs) & (second == 0))
     def _():
         add_pair()
 
-    @pl.when(step < pairs)
-    def _():
-        pair_copy(step).start()
+    @pl.when(working & (second == 1))
+    def _():
+        pair_copy(step // 2).start()
 
     def part_copies(block):
         rows = pl.ds(block * start_part.shape[1], start_part.shape[1])
@@ -685,7 +1120,7 @@
             pltpu.make_async_copy(d_middle_ref.at[rows], middle_part.at[slot], part_sems.at[1, slot]),
         )
 
-    @pl.when(step == pairs)
+    @pl.when(step == 2 * pairs)
     def _():
         for copy in part_copies(0):
             copy.start()
@@ -703,8 +1138,9 @@
     for at, stream in enumerate(streams):
         depth = len(stream.levels)
 
-        def item_at(lag):
-            return step - lag, (step >= lag) & (step - lag < pairs)
+        def item_at(lag, stream=stream):
+            since = step - stream.first - lag
+            return since // 2, (since >= 0) & (since % 2 == 0) & (since < 2 * stream.count)
 
         item, here = item_at(depth + 2)
 
@@ -744,15 +1180,22 @@
                 next_keep[...] = add(keep[:, place], came[slot, :, place]).reshape(next_keep.shape)
                 level_copy(at, level + 1, item).start()
 
-    @pl.when(step < pairs)
-    def _():
-        @pl.when(step > 0)
-        def _():
-            for at in range(len(streams)):
-                level_copy(at, 0, step - 1).wait_send()
-
-        send, keep, _ = levels[0][0]
-        grad = dot(turned_ref[...], d_pair[step % 2], 1, 0).astype(bf16)
+    def begin_piece(fills):
+        for at, fill in fills.items():
+            stream = streams[at]
+            item = (step - stream.first) // 2
+
+            @pl.when((step % 2 == stream.first) & (item < stream.count))
+            def _(at=at, fill=fill, item=item):
+                @pl.when(item > 0)
+                def _():
+                    level_copy(at, 0, item - 1).wait_send()
+
+                fill(*levels[at][0][:2])
+                level_copy(at, 0, item).start()
+
+    def fill_pair(send, keep):
+        grad = dot(n1_ref[...], d_pair[step // 2 % 2], 0, 0).astype(bf16)
         grad = grad.reshape(n_seq, 2, send.shape[2], 3 * lanes)
         shape = send.shape[:3] + (3 * lanes,)
 
@@ -769,38 +1212,42 @@
         shape = send.shape[:3] + (lanes,)
         send[:, :, :, 3 * lanes :] = add(out_kept[:, 1 - high], out_came[:, 1 - high]).reshape(shape)
         keep[:, :, :, 3 * lanes :] = add(out_kept[:, high], out_came[:, high]).reshape(shape)
-        for at, (ref, place) in enumerate(((down_ref, places["y"]), (up_ref, high)), 1):
-            send, keep, _ = levels[at][0]
+
+    def fill_from(ref, place):
+        def fill(send, keep):
             send[...] = ref[:, 1 - place].reshape(send.shape)
             keep[...] = ref[:, place].reshape(keep.shape)
-        for at in range(len(streams)):
-            level_copy(at, 0, step).start()
+
+        return fill
+
+    begin_piece({0: fill_pair, 1: fill_from(down_ref, places["y"]), 2: fill_from(up_ref, high)})
 
     @pl.when(step == pl.num_programs(0) - 1)
     def _():
         for at, stream in enumerate(streams):
             for level in range(len(stream.levels)):
-                level_copy(at, level, pairs - 1).wait_send()
+                level_copy(at, level, stream.count - 1).wait_send()
         wait_home(False)
         wait_home(True)
 
 
 def back(
-    qkv, mixed, d_mixed, lse, key_tags, query_tags, n1_turned, weights, gain, out_kept, out_came, down_part, up_part,
+    qkv, mixed, d_mixed, lse, key_tags, query_tags, n1, weights, gain, out_kept, out_came, down_part, up_part,
     start, d_middle, outputs, row_count,
 ):
     tokens = qkv.shape[0]
-    width = n1_turned.shape[0]
+    width = n1.shape[1]
     own_tokens = tokens // CORES
     lanes = 2 * HDIM
     pairs = qkv.shape[1] // (3 * lanes)
     n_seq = 2 * row_count
     tile = 256
     sub = own_tokens // n_seq
-    streams = streams_of(down_part.shape[0] * 2 // n_seq, width, pairs)
+    streams = streams_of(width, down_part.shape[0] * 2, n_seq, pairs)
     last = pairs - 1
-    now = lambda i: jnp.minimum(i, last)
-    before = lambda i: jnp.clip(i - 1, 0, last)
+    now = lambda i: jnp.minimum(i // 2, last)
+    before = lambda i: jnp.clip(i // 2 - 1, 0, last)
+    early = lambda i: jnp.minimum(i // 2, down_pieces - 1)
     fixed = lambda shape: pl.BlockSpec(shape, lambda i: (0,) * len(shape), pipeline_mode=pl.Buffered(1))
 
     def columns(place):
@@ -810,19 +1257,22 @@
     weight = pl.BlockSpec((width, 3 * lanes), lambda i: (0, before(i)))
     hbm = pl.BlockSpec(memory_space=pl.ANY)
 
-    def piece(value, place):
-        parts = (value.shape[0] // (2 * place), 2, place, value.shape[1] // pairs)
-        whole = value.reshape(parts[:3] + value.shape[1:])
-        return whole, pl.BlockSpec(parts, lambda i: (0, 0, 0, now(i)))
-
-    outs = [piece(value, width // 16) for value in (out_kept, out_came)]
-    down = piece(down_part, streams[1].rows)
-    up = piece(up_part, streams[2].rows)
+    rows = streams[0].rows
+
+    def out_piece(value):
+        whole = value.reshape(n_seq, 2, rows, value.shape[1])
+        return whole, pl.BlockSpec((n_seq, 2, rows, lanes), lambda i: (0, 0, 0, now(i)))
+
+    outs = [out_piece(value) for value in (out_kept, out_came)]
+    down = down_part.reshape(n_seq // 2, 2, -1, width // CORES)
+    up = up_part.reshape(n_seq // 2, 2, rows, -1)
+    down_spec = pl.BlockSpec((n_seq // 2, 2, streams[1].rows, width // CORES), lambda i: (0, 0, early(i), 0))
+    up_spec = pl.BlockSpec((n_seq // 2, 2, rows, streams[2].columns), lambda i: (0, 0, 0, early(i)))
     count = len(streams)
     deepest = max(len(stream.levels) for stream in streams)
     return pl.pallas_call(
         functools.partial(back_kernel, pairs, tile, streams, row_count),
-        grid=(pairs + deepest + 2,),
+        grid=(2 * pairs + deepest + 2,),
         in_specs=[
             fixed((tokens, 1)),
             fixed((1, tokens)),
@@ -832,21 +1282,21 @@
             pair,
             pair,
             pl.BlockSpec((None, 2, tokens), lambda i: (now(i), 0, 0)),
-            fixed((width, tokens)),
+            fixed((tokens, width)),
             weight,
             weight,
             fixed((1, width)),
             outs[0][1],
             outs[1][1],
-            down[1],
-            up[1],
+            down_spec,
+            up_spec,
             hbm,
             hbm,
             hbm,
         ],
         out_specs=[hbm] * 5,
         out_shape=[jax.ShapeDtypeStruct((row_count, CORES, sub, width), bf16)] * 2
-        + [jax.ShapeDtypeStruct((pairs, CORES, 2, stream.rows, stream.columns), bf16) for stream in streams],
+        + [jax.ShapeDtypeStruct((stream.count, CORES, 2, stream.rows, stream.columns), bf16) for stream in streams],
         scratch_shapes=[
             pltpu.VMEM((lanes, tokens), bf16),
             pltpu.VMEM((lanes, tokens), f32),
@@ -859,7 +1309,7 @@
             pltpu.VMEM((2, sub, width), f32),
         ]
         + [shape for stream in streams for shape in stream.scratch()]
-        + [pltpu.VMEM((pairs, 2, stream.rows, stream.columns), bf16) for stream in streams]
+        + [pltpu.VMEM((stream.count, 2, stream.rows, stream.columns), bf16) for stream in streams]
         + [
             pltpu.SemaphoreType.DMA((count, deepest)),
             pltpu.SemaphoreType.DMA((count, deepest, 2)),
@@ -888,8 +1338,8 @@
         ),
         name="back",
     )(
-        key_tags, query_tags, qkv, qkv, qkv, mixed, d_mixed, lse, n1_turned, weights[0], weights[1],
-        gain.reshape(1, width), outs[0][0], outs[1][0], down[0], up[0], start, d_middle, outputs,
+        key_tags, query_tags, qkv, qkv, qkv, mixed, d_mixed, lse, n1, weights[0], weights[1],
+        gain.reshape(1, width), outs[0][0], outs[1][0], down, up, start, d_middle, outputs,
     )
 
 
@@ -920,16 +1370,24 @@
                 weight = qkv_weights[kind * CORES + core][own, :].astype(f32)
                 first_out[own, :] += jnp.sum(value * weight, axis=1, keepdims=True)
             out_out[own, pl.ds(place, lanes)] = part[:, 3 * lanes :]
-            part = up_parts[core, high].astype(f32)
-            for at in range(part.shape[1] // tile):
-                value = part[:, at * tile : (at + 1) * tile]
-                columns = slice(at * feed_tile + core * tile, at * feed_tile + (core + 1) * tile)
-                up_out[own, columns] = value
-                second_out[own, :] += jnp.sum(value * up_weight[own, columns].astype(f32), axis=1, keepdims=True)
-            part = down_parts[core, high].astype(f32)
-            for at in range(part.shape[0] // piece_rows):
-                start = (2 * at + high) * piece_rows
-                down_out[start : start + piece_rows, pl.ds(place, lanes)] = part[at * piece_rows : (at + 1) * piece_rows]
+
+    @pl.when(item < down_pieces)
+    def _():
+        for core in range(CORES):
+            for high in range(2):
+                own = slice(high * rows, (high + 1) * rows)
+                for at in range(up_parts.shape[3] // lanes):
+                    column = item * up_parts.shape[3] + at * lanes
+                    column = column // tile * feed_tile + core * tile + column % tile
+                    columns = pl.ds(pl.multiple_of(column, lanes), lanes)
+                    value = up_parts[core, high, :, at * lanes : (at + 1) * lanes].astype(f32)
+                    up_out[own, columns] = value
+                    second_out[own, :] += jnp.sum(value * up_weight[own, columns].astype(f32), axis=1, keepdims=True)
+                count = down_parts.shape[2] // piece_rows
+                for at in range(count):
+                    start = ((item * count + at) * 2 + high) * piece_rows
+                    value = down_parts[core, high, at * piece_rows : (at + 1) * piece_rows, :].astype(f32)
+                    down_out[pl.ds(pl.multiple_of(start, piece_rows), piece_rows), core * half : (core + 1) * half] = value
 
     @pl.when(item == pairs - 1)
     def _():
@@ -941,10 +1399,12 @@
     pairs, _, _, rows, _ = qkv_parts.shape
     width, lanes = qkv_weight.shape[0], 2 * HDIM
     shard, wide = 2 * rows, up_weight.shape[1]
-    down_rows = 2 * down_parts.shape[3]
+    down_rows = 2 * down_pieces * down_parts.shape[3]
 
     def parts(value):
-        return pl.BlockSpec((None,) + value.shape[1:], lambda i, seq: (i, 0, 0, 0, 0))
+        return pl.BlockSpec(
+            (None,) + value.shape[1:], lambda i, seq: (jnp.minimum(i, value.shape[0] - 1), 0, 0, 0, 0)
+        )
 
     def weight(kind, core):
         return pl.BlockSpec((shard, lanes), lambda i, seq: (seq[0], (kind * CORES + core) * pairs + i))
@@ -958,12 +1418,12 @@
             grid=(pairs,),
             in_specs=[parts(qkv_parts), parts(down_parts), parts(up_parts)]
             + [weight(kind, core) for kind in range(3) for core in range(CORES)]
-            + [pl.BlockSpec((shard, wide // pairs), lambda i, seq: (seq[0], i)), gain, gain],
+            + [pl.BlockSpec((shard, wide), lambda i, seq: (seq[0], 0)), gain, gain],
             out_specs=[
                 whole((shard, 3 * width)),
                 whole((shard, width)),
                 whole((down_rows, width)),
-                pl.BlockSpec((shard, wide // pairs), lambda i, seq: (0, i)),
+                whole((shard, wide)),
                 whole((shard, 1)),
                 whole((shard, 1)),
             ],
@@ -1300,10 +1760,41 @@
             at = (member + hop) % group * group_width
             return pad_heads(lax.dynamic_slice_in_dim(out_weight, at, group_width, 0), 0)
 
+        if chips == 1 and highs == 2:
+            half = width // CORES
+            x_row, n1, qkv, own_weight, other_weight = begin(inputs, qkv_weight, attention_gain)
+            start = x_row.reshape(tokens, width)
+            mixed, lse, cot, mixed_own = attend_row(qkv, key_tags, query_tags, cotangent)
+            middle = start.astype(f32) + dot(mixed_own, out_weight, 1, 0)
+            outputs, d_middle, d_attn, down_part, up_part = feed(
+                middle, cot.reshape(tokens, width), feed_gain, up_weight, down_weight, n_seq
+            )
+            out_grad = dot(mixed_own, d_attn[0], 0, 0).astype(bf16)
+            out_kept = lax.dynamic_slice_in_dim(out_grad, core * half, half, 1)
+            out_received = other_core(lax.dynamic_slice_in_dim(out_grad, (1 - core) * half, half, 1))
+            out_own = lax.dynamic_slice_in_dim(out_weight, core * half, half, 0)
+            d_mixed = dot(d_attn.reshape(seq_len, width), out_own, 1, 1).astype(bf16)
+            input_grad, out_low, qkv_out, down_all, up_all = back(
+                qkv, mixed, d_mixed, lse, key_tags, query_tags, n1, (own_weight, other_weight), attention_gain,
+                out_kept, out_received, down_part, up_part, start, d_middle, outputs, row_count,
+            )
+            qkv_total, out_total, down_total, up_total, first, second = collect(
+                seq_at, qkv_out, down_all, up_all, qkv_weight, up_weight, attention_gain, feed_gain
+            )
+            return (
+                out_low.reshape(inputs.shape),
+                input_grad.reshape(inputs.shape),
+                first.reshape(-1),
+                qkv_total,
+                out_total,
+                second.reshape(-1),
+                up_total,
+                down_total,
+            )
+
         start = to_rows(inputs)
         qkv_parts = [qkv_of(hop) for hop in range(group)]
         out_parts = [out_of(hop) for hop in range(group)]
-        start_low = start
         start = start.astype(f32)
         unit1, scale1 = norm_parts(start)
         n1 = (unit1 * attention_gain).astype(bf16)
@@ -1319,6 +1810,7 @@
         for part, weight in zip(mixed_parts, out_parts):
             middle = middle + dot(part, weight, 1, 0)
         outputs, d_middle, d_attn, down_part, up_part = feed(middle, cot, feed_gain, up_weight, down_weight, n_seq)
+        d_attn = d_attn[0]
 
         d_attn_all = jnp.concatenate([d_attn] + [to_member(d_attn, hop) for hop in range(1, group)], 0)
 
@@ -1335,24 +1827,6 @@
         out_received = other_core(lax.dynamic_slice_in_dim(out_grad, (1 - core) * half, half, 1))
         d_mixed = dot(d_attn_all, out_parts[0], 1, 1).astype(bf16)
 
-        if chips == 1 and highs == 2:
-            input_grad, out_low, qkv_out, down_all, up_all = back(
-                qkv, mixed, d_mixed, lse, key_tags, query_tags, n1_all.T, qkv_parts, attention_gain,
-                out_kept, out_received, down_part, up_part, start_low, d_middle, outputs, row_count,
-            )
-            qkv_total, out_total, down_total, up_total, first, second = collect(
-                seq_at, qkv_out, down_all, up_all, qkv_weight, up_weight, attention_gain, feed_gain
-            )
-            return (
-                out_low.reshape(inputs.shape),
-                input_grad.reshape(inputs.shape),
-                first.reshape(-1),
-                qkv_total,
-                out_total,
-                second.reshape(-1),
-                up_total,
-                down_total,
-            )
         out_low = from_rows(outputs)
         input_grad, qkv_total, out_total, down_total, up_total = back_by_steps(
             qkv, mixed, d_mixed, lse, key_tags, query_tags, n1_all, qkv_parts, attention_gain,

time: 677 us -> 627 us (0.926)
  Pallas kernels: 510 us -> 578 us
  blocking collectives: 66.7 us -> 0 us
  matrix products: 41.5 us -> 20.2 us
  local copies, waits for them, and re-layouts: 27.2 us -> 14.4 us
  other arithmetic: 16.6 us -> 4.3 us
    all_to_all x1 -> x0, blocking collectives: 66.7 us -> none  [to_rows(): return lax.all_to_all(both, 'seq', 0, 0, tiled=True).reshape(tokens, width)]
    pallas_call x3 -> x2, Pallas kernels: 102 us -> 146 us  [the longest x1 74.1 us: attend_row(): pl.pallas_call(functools.partial(attend_row_kernel, tile, row_count), gri...]
    pallas_call x1, Pallas kernels: 266 us -> 290 us  [back(): pl.pallas_call(functools.partial(back_kernel, pairs, tile, streams, row_c...]
    dot_general x5 -> x3, matrix products: 41.5 us -> 20.2 us  [dot(): lax.dot_general(a, b, (((ca,), (cb,)), ((), ())), preferred_element_type=...]
    transpose x1 -> x0, local copies, waits for them, and re-layouts: 7.96 us -> none  [per_device(): input_grad, out_low, qkv_out, down_all, up_all = back(qkv, mixed, d_mixed...]
  transfers between devices with their start and end apart: 8 -> 2, of which waited for: 1 -> 0; matrix products, arithmetic and copies ran while one was open for 11% -> 2% of each run, Pallas kernels for 15% -> 12%
where the time goes in v4:
time: 627 us; the launch traced here: 618 us
  Pallas kernels  578 us (92%)
  matrix products  20.2 us (3%)
  local copies, waits for them, and re-layouts  14.4 us (2%)
    pallas_call x1, Pallas kernels, back(): pl.pallas_call(functools.partial(back_kernel, pairs, tile, streams, row_c...  290 us
    pallas_call x1, Pallas kernels, feed(): pl.pallas_call(functools.partial(feed_kernel, tiles, 128), grid=(tiles +...  131 us
    pallas_call x1, Pallas kernels, attend_row(): pl.pallas_call(functools.partial(attend_row_kernel, tile, row_count), gri...  74.1 us
    pallas_call x1, Pallas kernels, begin(): pl.pallas_call(functools.partial(begin_kernel, row_count, pairs), in_spec...  72 us
    dot_general x3, matrix products, dot(): lax.dot_general(a, b, (((ca,), (cb,)), ((), ())), preferred_element_type=...  20.2 us
  transfers between devices with their start and end apart: 2, of which 0 were waited for; matrix products, arithmetic and copies ran while one was open for 2% of the time, Pallas kernels for 12%

profile of v4, /device:TPU:0, one launch (start us, length us, event | category | flops | bytes accessed | tf_op | source)
XLA Modules:
  0.0 618.3 jit_solution(15446411899458124781)
XLA Ops:
  0.6 0.8 fusion.3
  1.5 0.5 collective-permute-start
  2.0 1.3 reshape.184.gain_ref.refs_11_
  3.3 1.3 reshape.188.gain_ref
  4.6 72.0 %begin.1 = (bf16[8,128,1280]{2,1,0:T(8,128)(2,1)}, bf16[2048,1280]{1,0:T(8,128)(2,1)}, bf16[2048,1920]{1,0:T(8,128)(2,1)}, bf16[1280,1920]{1,0:T(8,128)(2,1)}, bf16[1280,1920]{1,0:T(8,128)(2,1)}) custom-call(bf16[4,2,128,1280]{3,2,1,0:T(8,128)(2,1)} %bitcast.39, bf16[1280,3840]{1,0:T(8,128)(2,1)} %refs_8_.1, f32[1,1280]{1,0:T(1,128)} %reshape.184.gain_ref.refs_11_), custom_call_target="tpu_custom_call" | custom-call | tf_op jit(solution)/shard_map/begin/pallas_call | solution.py:402
  76.6 0.0 collective-permute-done
  76.6 0.1 broadcast_select_fusion
  76.7 0.6 gather_fusion
  77.3 0.1 select_bitcast_fusion
  77.3 0.0 copy-start.1
  77.4 1.3 copy.23
  78.7 0.0 copy-done.1
  78.7 0.0 copy-start.4
  78.7 74.1 %attend_row.1 = (bf16[2048,640]{1,0:T(8,128)(2,1)}, f32[5,2,2048]{2,1,0:T(2,128)}, bf16[8,128,1280]{2,1,0:T(8,128)(2,1)}, bf16[1024,1280]{1,0:T(8,128)(2,1)}) custom-call(s32[2048,1]{1,0:T(8,128)} %bitcast.34, s32[1,2048]{1,0:T(1,128)} %bitcast.43, bf16[2048,1920]{1,0:T(8,128)(2,1)} %get-tuple-element.33.q_ref.k_ref.v_ref.refs_2_.refs_3_.refs_4_, ...), custom_call_target="tpu_custom_call" | custom-call | tf_op jit(solution)/shard_map/attend_row/pallas_call | solution.py:562
  152.8 0.0 copy-done.4
  152.8 8.4 %convert_add_fusion.middle_ref = f32[1024,1280]{1,0:T(8,128)} fusion(bf16[1024,1280]{1,0:T(8,128)(2,1)} %bitcast.45, bf16[1024,1280]{1,0:T(8,128)(2,1)} %get-tuple-element.36, bf16[1280,1280]{1,0:T(8,128)(2,1)S(1)} %copy-done.4), kind=kOutput, calls=%fused_computation.2 | convolution fusion | flops 3358064640 | bytes 13762560 | tf_op jit(solution)/shard_map/dot_general | solution.py:27
  161.3 131.2 %feed.1 = (bf16[1024,1280]{1,0:T(8,128)(2,1)}, f32[1024,1280]{1,0:T(8,128)}, bf16[2,1024,1280]{2,1,0:T(8,128)(2,1)}, bf16[2560,640]{1,0:T(8,128)(2,1)}, bf16[640,2560]{1,0:T(8,128)(2,1)}) custom-call(f32[1024,1280]{1,0:T(8,128)} %convert_add_fusion.middle_ref, bf16[1024,1280]{1,0:T(8,128)(2,1)} %bitcast.47, f32[1,1280]{1,0:T(1,128)} %reshape.188.gain_ref, ...), custom_call_target="tpu_custom_call" | custom-call | flops 80530636800 | bytes 60293120 | tf_op jit(solution)/shard_map/feed/pallas_call | solution.py:846
  292.5 0.0 copy-start.7
  292.5 6.3 %convolution_convert_fusion = bf16[1280,1280]{1,0:T(8,128)(2,1)S(1)} fusion(bf16[1024,1280]{1,0:T(8,128)(2,1)} %get-tuple-element.36, bf16[2,1024,1280]{2,1,0:T(8,128)(2,1)} %get-tuple-element.38), kind=kOutput, calls=%fused_computation.1 | convolution fusion | flops 3357081600 | bytes 8519680 | tf_op jit(solution)/shard_map/dot_general | solution.py:27
  298.8 0.0 copy-start.2
  298.8 0.0 copy-start.3
  298.8 0.0 copy-start.5
  298.9 1.6 constant_dynamic-slice_fusion
  300.5 0.0 collective-permute-start.1
  300.5 0.0 copy-done.2
  300.5 1.1 reshape.209.refs_10_
  301.6 0.0 copy-done.3
  301.6 1.1 reshape.210.refs_11_
  302.7 0.0 copy-done.7
  302.7 0.0 copy-done.5
  302.7 5.5 convolution_convert_fusion.1.refs_6_
  308.2 0.0 collective-permute-done.1
  308.2 0.0 copy-start.6
  308.2 1.2 copy-done.6
  309.4 290.4 %back.1 = (bf16[4,2,128,1280]{3,2,1,0:T(8,128)(2,1)}, bf16[4,2,128,1280]{3,2,1,0:T(8,128)(2,1)}, bf16[5,2,2,80,512]{4,3,2,1,0:T(8,128)(2,1)}, bf16[4,2,2,80,640]...) custom-call(s32[2048,1]{1,0:T(8,128)} %bitcast.35, s32[1,2048]{1,0:T(1,128)} %bitcast.44, ...), custom_call_target="tpu_custom_call" | custom-call | flops 107374182400 | bytes 20971520 | tf_op jit(solution)/shard_map/back/pallas_call | solution.py:1273
  599.8 10.1 %collect.1 = (f32[160,3840]{1,0:T(8,128)}, f32[160,1280]{1,0:T(8,128)}, f32[640,1280]{1,0:T(8,128)}, f32[160,5120]{1,0:T(8,128)}, f32[160,1]{1,0:T(8,128)}, /*index=5*/f32[160,1]{1,0:T(8,128)}) custom-call(s32[1]{0:T(128)} %bitcast.16.seq_ref, bf16[5,2,2,80,512]{4,3,2,1,0:T(8,128)(2,1)} %get-tuple-element.49.refs_0_, ...), custom_call_target="tpu_custom_call" | custom-call | tf_op jit(solution)/shard_map/collect/pallas_call | solution.py:1414
  609.9 0.0 copy-start
  609.9 1.7 reduce
  611.7 1.6 reduce.1
  613.2 3.4 copy.27
  616.6 0.0 copy-done
  616.6 1.5 copy.28
  (5 shorter events, 0.1 us)
Async XLA Ops:
  1.5 75.1 %collective-permute-start = (s32[4,2048]{1,0:T(4,128)S(1)}, s32[4,2048]{1,0:T(4,128)S(1)}, u32[]{:S(2)}, u32[]{:S(2)}) collective-permute-start(s32[4,2048]{1,0:T(4,128)S(1)} %fusion.3), channel_id=1, source_target_pairs={{0,1},{1,0},{2,3},{3,2},{4,5},{5,4},{6,7},{7,6},{8,9},{9,8},{10,11... | collective-permute-start | bytes 98312 | tf_op jit(solution)/shard_map/ppermute | solution.py:1531
  77.3 1.4 copy-start.1
  78.7 74.1 %copy-start.4 = (bf16[1280,1280]{1,0:T(8,128)(2,1)S(1)}, bf16[1280,1280]{1,0:T(8,128)(2,1)}, u32[]{:S(2)}) copy-start(bf16[1280,1280]{1,0:T(8,128)(2,1)} %param.16) | copy-start | bytes 9830404
  292.5 10.2 %copy-start.7 = (bf16[2,1024,1280]{2,1,0:T(8,128)(2,1)S(1)}, bf16[2,1024,1280]{2,1,0:T(8,128)(2,1)}, u32[]{:S(2)}) copy-start(bf16[2,1024,1280]{2,1,0:T(8,128)(2,1)} %get-tuple-element.38) | copy-start | bytes 15728644
  298.8 1.7 copy-start.2
  298.8 2.7 copy-start.3
  298.8 3.8 copy-start.5
  300.5 7.7 %collective-permute-start.1 = (bf16[1280,640]{1,0:T(8,128)(2,1)S(1)}, bf16[1280,640]{1,0:T(8,128)(2,1)S(1)}, u32[]{:S(2)}, u32[]{:S(2)}) collective-permute-start(bf16[1280,640]{1,0:T(8,128)(2,1)S(1)} %get-tuple-element.58), channel_id=1, source_target_pairs={{0,1},{1,0},{2,3},{3,2},{4,5},{5,4},{6,7},{7,6},{8,9},{9,8},{10,11... | collective-permute-start | bytes 4915208 | tf_op jit(solution)/shard_map/ppermute | solution.py:1531
  308.2 1.2 copy-start.6
  609.9 6.7 %copy-start = (bf16[4,2,128,1280]{3,2,1,0:T(8,128)(2,1)S(1)}, bf16[4,2,128,1280]{3,2,1,0:T(8,128)(2,1)}, u32[]{:S(2)}) copy-start(bf16[4,2,128,1280]{3,2,1,0:T(8,128)(2,1)} %get-tuple-element.48) | copy-start | bytes 7864324

commit v5 on v4

--- a/solution.py
+++ b/solution.py
@@ -613,15 +613,24 @@
     gain_ref,
     up_ref,
     down_ref,
+    mixed_ref,
+    out_weight_ref,
     out_ref,
     d_middle_ref,
     d_attn_out,
+    d_mixed_out,
+    out_kept,
+    out_came,
     down_part,
     up_part,
     n2,
-    n2_turned,
     total,
     d_attn,
+    d_attn_other,
+    out_weight,
+    out_keep,
+    out_send,
+    d_mixed,
     down_keep,
     down_send,
     down_recv,
@@ -634,6 +643,9 @@
     up_far_keep,
     up_far_send,
     up_far_recv,
+    up_last_keep,
+    up_last_send,
+    up_last_recv,
     core_send_sem,
     core_recv_sem,
     far_send_sem,
@@ -641,14 +653,18 @@
     core_free,
     far_free,
     d_attn_sems,
+    last_send_sem,
+    last_recv_sem,
+    out_sems,
 ):
     step = pl.program_id(0)
     tokens, width = n2.shape
     half = width // 2
     seq_at, rows_at = lax.axis_index("seq"), lax.axis_index("rows")
-    core, high, low = rows_at % 2, (rows_at // 2) % 2, seq_at % 2
+    core, high, low, mid = rows_at % 2, (rows_at // 2) % 2, seq_at % 2, (seq_at // 2) % 2
     core_peer = (seq_at, rows_at + 1 - 2 * core)
     far_peers = ((seq_at, rows_at + 2 - 4 * high), (seq_at + 1 - 2 * low, rows_at))
+    last_peer = (seq_at + 2 - 4 * mid, rows_at)
 
     def copies(slot, far):
         if far:
@@ -675,9 +691,9 @@
     @pl.when(step == 0)
     def _():
         barrier = pltpu.get_barrier_semaphore()
-        for peer in (core_peer,) + far_peers:
+        for peer in (core_peer,) + far_peers + (last_peer,):
             signal(barrier, peer)
-        pl.semaphore_wait(barrier, 3)
+        pl.semaphore_wait(barrier, 4)
 
         def body(i, _):
             part = pl.ds(pl.multiple_of(i * rows, rows), rows)
@@ -686,7 +702,6 @@
             return 0
 
         lax.fori_loop(0, tokens // rows, body, 0)
-        n2_turned[...] = n2[...].T
         total[...] = middle_ref[...]
         d_middle_ref[...] = jnp.zeros_like(d_middle_ref)
 
@@ -708,7 +723,7 @@
             for copy in copies(slot, False):
                 copy.wait_send()
 
-        up_grad = dot(n2_turned[...], d_up, 1, 0).astype(bf16)
+        up_grad = dot(n2[...], d_up, 0, 0).astype(bf16)
         cut = up_grad.shape[1] // 2
 
         @pl.when(core == 0)
@@ -736,12 +751,34 @@
     def add(a, b):
         return (a.astype(f32) + b.astype(f32)).astype(bf16)
 
+    def last_copy(slot):
+        return pltpu.make_async_remote_copy(
+            src_ref=up_last_send.at[slot],
+            dst_ref=up_last_recv.at[slot],
+            send_sem=last_send_sem.at[slot],
+            recv_sem=last_recv_sem.at[slot],
+            device_id=last_peer,
+            device_id_type=MESH,
+        )
+
     def last_add():
+        slot = (step + 1) % 2
+        last_copy(slot).wait_recv()
+        up_part[...] = add(up_last_keep[slot], up_last_recv[slot]).reshape(up_part.shape)
+
+    def far_add():
         slot = step % 2
         for copy in copies(slot, True):
             copy.wait_recv()
         down_part[...] = add(down_far_keep[slot], down_far_recv[slot]).reshape(down_part.shape)
-        up_part[...] = add(up_far_keep[slot], up_far_recv[slot]).reshape(up_part.shape)
+
+        @pl.when(step >= 4)
+        def _():
+            last_copy(slot).wait_send()
+
+        up_last_send[slot] = add(up_far_keep[slot, :, 1 - mid], up_far_recv[slot, :, 1 - mid])
+        up_last_keep[slot] = add(up_far_keep[slot, :, mid], up_far_recv[slot, :, mid])
+        last_copy(slot).start()
 
         @pl.when(step < tiles)
         def _():
@@ -762,8 +799,9 @@
 
         down_far_send[slot] = add(down_keep[slot, :, 1 - high], down_recv[slot, :, 1 - high])
         down_far_keep[slot] = add(down_keep[slot, :, high], down_recv[slot, :, high])
-        up_far_send[slot] = add(up_keep[slot, :, 1 - low], up_recv[slot, :, 1 - low])
-        up_far_keep[slot] = add(up_keep[slot, :, low], up_recv[slot, :, low])
+        shape = up_far_send.shape[1:]
+        up_far_send[slot] = add(up_keep[slot, :, 1 - low], up_recv[slot, :, 1 - low]).reshape(shape)
+        up_far_keep[slot] = add(up_keep[slot, :, low], up_recv[slot, :, low]).reshape(shape)
         for copy in copies(slot, True):
             copy.start()
 
@@ -771,9 +809,13 @@
         def _():
             signal(core_free, core_peer)
 
+    @pl.when((step >= 3) & (step <= tiles + 1))
+    def _():
+        last_add()
+
     @pl.when((step >= 2) & (step <= tiles))
     def _():
-        last_add()
+        far_add()
 
     @pl.when((step >= 1) & (step <= tiles))
     def _():
@@ -801,35 +843,71 @@
 
         lax.fori_loop(0, tokens // rows, body, 0)
 
-    d_attn_copies = lambda: (
-        pltpu.make_async_copy(d_attn, d_attn_out.at[0], d_attn_sems.at[0]),
-        pltpu.make_async_remote_copy(
-            src_ref=d_attn,
-            dst_ref=d_attn_out.at[1],
-            send_sem=d_attn_sems.at[1],
-            recv_sem=d_attn_sems.at[2],
+    def to_core(source, target, at):
+        return pltpu.make_async_remote_copy(
+            src_ref=source,
+            dst_ref=target,
+            send_sem=d_attn_sems.at[at],
+            recv_sem=d_attn_sems.at[at + 1],
             device_id=core_peer,
             device_id_type=MESH,
-        ),
+        )
+
+    d_attn_copy = lambda: to_core(d_attn, d_attn_other, 0)
+    out_copy = lambda: to_core(out_send, out_came, 2)
+    mixed_copy = lambda: pltpu.make_async_copy(mixed_ref, n2, out_sems.at[0])
+    weight_copy = lambda: pltpu.make_async_copy(
+        out_weight_ref.at[pl.ds(pl.multiple_of(core * half, half), half)], out_weight, out_sems.at[1]
     )
+    d_attn_save = lambda: pltpu.make_async_copy(d_attn, d_attn_out, out_sems.at[2])
+    out_save = lambda: pltpu.make_async_copy(out_keep, out_kept, out_sems.at[3])
+    d_mixed_save = lambda: pltpu.make_async_copy(d_mixed, d_mixed_out, out_sems.at[4])
 
     @pl.when(step == tiles)
     def _():
-        for copy in d_attn_copies():
-            copy.start()
+        d_attn_copy().start()
+        d_attn_save().start()
+        mixed_copy().start()
+        weight_copy().start()
 
     @pl.when(step == tiles + 1)
     def _():
+        mixed_copy().wait()
+        grad = dot(n2[...], d_attn[...], 0, 0).astype(bf16)
+
+        @pl.when(core == 0)
+        def _():
+            out_keep[...] = grad[:, :half]
+            out_send[...] = grad[:, half:]
+
+        @pl.when(core != 0)
+        def _():
+            out_keep[...] = grad[:, half:]
+            out_send[...] = grad[:, :half]
+
+        out_copy().start()
+        out_save().start()
+        far_add()
+
+    @pl.when(step == tiles + 2)
+    def _():
+        weight_copy().wait()
+        d_attn_copy().wait()
+        d_mixed[:tokens, :] = dot(d_attn[...], out_weight[...], 1, 1).astype(bf16)
+        d_mixed[tokens:, :] = dot(d_attn_other[...], out_weight[...], 1, 1).astype(bf16)
+        d_mixed_save().start()
         last_add()
-        for copy in d_attn_copies():
+        out_copy().wait()
+        for copy in (d_attn_save(), out_save(), d_mixed_save()):
             copy.wait()
         for slot in range(2):
+            last_copy(slot).wait_send()
             for far in (False, True):
                 for copy in copies(slot, far):
                     copy.wait_send()
 
 
-def feed(middle, cot, gain, up_weight, down_weight, n_seq):
+def feed(middle, cot, gain, up_weight, down_weight, mixed_own, out_weight, n_seq):
     tokens, width = middle.shape
     wide = up_weight.shape[1]
     tile = feed_tile
@@ -838,44 +916,61 @@
     whole = lambda dtype: jax.ShapeDtypeStruct((tokens, width), dtype)
     fixed = lambda shape: pl.BlockSpec(shape, lambda i: (0, 0), pipeline_mode=pl.Buffered(1))
     at = lambda i: jnp.minimum(i, tiles - 1)
-    late = lambda i: jnp.maximum(i - 2, 0)
+    hbm = pl.BlockSpec(memory_space=pl.ANY)
+    late = lambda i: jnp.clip(i - 2, 0, tiles - 1)
     down_shape = (2, tile // (2 * piece_rows), 2, piece_rows, half)
     up_shape = (2, n_seq // 2, 2, shard, tile // 2)
     near = [pltpu.VMEM(down_shape, bf16)] * 3 + [pltpu.VMEM(up_shape, bf16)] * 3
-    far = [pltpu.VMEM(down_shape[:2] + down_shape[3:], bf16)] * 3 + [pltpu.VMEM(up_shape[:2] + up_shape[3:], bf16)] * 3
+    up_far = (2, n_seq // 4, 2, shard, tile // 2)
+    far = [pltpu.VMEM(down_shape[:2] + down_shape[3:], bf16)] * 3 + [pltpu.VMEM(up_far, bf16)] * 3
+    far += [pltpu.VMEM(up_far[:2] + up_far[3:], bf16)] * 3
     return pl.pallas_call(
         functools.partial(feed_kernel, tiles, 128),
-        grid=(tiles + 2,),
+        grid=(tiles + 3,),
         in_specs=[
             fixed((tokens, width)),
             fixed((tokens, width)),
             fixed((1, width)),
             pl.BlockSpec((width, tile), lambda i: (0, at(i))),
             pl.BlockSpec((tile, width), lambda i: (at(i), 0)),
+            hbm,
+            hbm,
         ],
         out_specs=[
             fixed((tokens, width)),
             fixed((tokens, width)),
-            pl.BlockSpec(memory_space=pl.ANY),
+            hbm,
+            hbm,
+            hbm,
+            hbm,
             pl.BlockSpec((tile // 2, half), lambda i: (late(i), 0)),
-            pl.BlockSpec((width // 2, tile // 2), lambda i: (0, late(i))),
+            pl.BlockSpec((width // 4, tile // 2), lambda i: (0, jnp.maximum(i - 3, 0))),
         ],
         scratch_shapes=[
             pltpu.VMEM((tokens, width), bf16),
-            pltpu.VMEM((width, tokens), bf16),
             pltpu.VMEM((tokens, width), f32),
             pltpu.VMEM((tokens, width), bf16),
+            pltpu.VMEM((tokens, width), bf16),
+            pltpu.VMEM((half, width), bf16),
+            pltpu.VMEM((width, half), bf16),
+            pltpu.VMEM((width, half), bf16),
+            pltpu.VMEM((2 * tokens, half), bf16),
         ]
         + near
         + far
         + [pltpu.SemaphoreType.DMA((2, 2))] * 4
-        + [pltpu.SemaphoreType.REGULAR, pltpu.SemaphoreType.REGULAR((2,)), pltpu.SemaphoreType.DMA((3,))],
+        + [pltpu.SemaphoreType.REGULAR, pltpu.SemaphoreType.REGULAR((2,)), pltpu.SemaphoreType.DMA((4,))]
+        + [pltpu.SemaphoreType.DMA((2,))] * 2
+        + [pltpu.SemaphoreType.DMA((5,))],
         out_shape=[
             whole(bf16),
             whole(f32),
-            jax.ShapeDtypeStruct((2, tokens, width), bf16),
+            whole(bf16),
+            jax.ShapeDtypeStruct((2 * tokens, half), bf16),
+            jax.ShapeDtypeStruct((width, half), bf16),
+            jax.ShapeDtypeStruct((width, half), bf16),
             jax.ShapeDtypeStruct((wide // 2, half), bf16),
-            jax.ShapeDtypeStruct((width // 2, wide // 2), bf16),
+            jax.ShapeDtypeStruct((width // 4, wide // 2), bf16),
         ],
         compiler_params=pltpu.CompilerParams(
             vmem_limit_bytes=feed_vmem_bytes, collective_id=1, has_side_effects=True
@@ -886,12 +981,13 @@
             transcendentals=2 * tokens * wide,
         ),
         name="feed",
-    )(middle, cot, gain.reshape(1, width), up_weight, down_weight)
+    )(middle, cot, gain.reshape(1, width), up_weight, down_weight, mixed_own, out_weight)
 
 
 class Stream:
-    def __init__(self, levels, rows, columns, first, count):
+    def __init__(self, levels, rows, columns, first, count, lag):
         self.levels, self.rows, self.columns, self.first, self.count = levels, rows, columns, first, count
+        self.lag = lag
 
     def shape(self, level):
         outer = 2 ** (len(self.levels) - 1 - level)
@@ -912,9 +1008,9 @@
     lanes = 2 * HDIM
     rows = width // (2 * n_seq)
     return (
-        Stream(("x", "y", "z1", "z2"), rows, 4 * lanes, 1, pairs),
-        Stream(("y", "z1", "z2"), wide // (2 * n_seq * down_pieces), width // CORES, 0, down_pieces),
-        Stream(("x", "z1", "z2"), rows, wide // CORES // down_pieces, 0, down_pieces),
+        Stream(("x", "y", "z1", "z2"), rows, 4 * lanes, 1, pairs, 2),
+        Stream(("y", "z1", "z2"), wide // (2 * n_seq * down_pieces), width // CORES, 2, down_pieces, 1),
+        Stream(("x", "z2"), rows, wide // CORES // down_pieces, 2, down_pieces, 1),
     )
 
 
@@ -997,7 +1093,7 @@
 
     def to_home(block, own, result):
         if result:
-            source, target = outputs_ref.at[pl.ds(block * sub, sub)], outputs_out
+            source, target = outputs_ref.at[pl.ds(pl.multiple_of(block * sub, sub), sub)], outputs_out
             sems = result_send, result_recv, result_local
         else:
             source, target = staged.at[block], grad_out
@@ -1047,8 +1143,10 @@
         pl.semaphore_signal(barrier, inc=1, device_id=peers["x"], device_id_type=MESH)
         pl.semaphore_wait(barrier, n_seq * CORES)
         d_n1[...] = jnp.zeros_like(d_n1)
-        for block in range(n_seq):
-            start_home(block, True)
+
+    @pl.when(step < n_seq)
+    def _():
+        start_home((seq_at + step) % n_seq, True)
 
     working, second = step < 2 * pairs, step % 2
 
@@ -1112,9 +1210,9 @@
     def _():
         pair_copy(step // 2).start()
 
-    def part_copies(block):
-        rows = pl.ds(block * start_part.shape[1], start_part.shape[1])
-        slot = block % 2
+    def part_copies(turn):
+        rows = pl.ds(pl.multiple_of((seq_at + turn) % n_seq * sub, sub), sub)
+        slot = turn % 2
         return (
             pltpu.make_async_copy(start_ref.at[rows], start_part.at[slot], part_sems.at[0, slot]),
             pltpu.make_async_copy(d_middle_ref.at[rows], middle_part.at[slot], part_sems.at[1, slot]),
@@ -1124,16 +1222,25 @@
     def _():
         for copy in part_copies(0):
             copy.start()
-        for block in range(n_seq):
-            if block + 1 < n_seq:
-                for copy in part_copies(block + 1):
+
+        def body(turn, _):
+            block = (seq_at + turn) % n_seq
+
+            @pl.when(turn + 1 < n_seq)
+            def _():
+                for copy in part_copies(turn + 1):
                     copy.start()
-            for copy in part_copies(block):
+
+            for copy in part_copies(turn):
                 copy.wait()
-            unit, scale = norm_parts(start_part[block % 2].astype(f32))
-            grad = norm_back(d_n1[block * sub : (block + 1) * sub, :], gain_ref[...], unit, scale)
-            staged[block] = (middle_part[block % 2] + grad).astype(bf16)
+            unit, scale = norm_parts(start_part[turn % 2].astype(f32))
+            rows = pl.ds(pl.multiple_of(block * sub, sub), sub)
+            grad = norm_back(d_n1[rows, :], gain_ref[...], unit, scale)
+            staged[block] = (middle_part[turn % 2] + grad).astype(bf16)
             start_home(block, False)
+            return 0
+
+        lax.fori_loop(0, n_seq, body, 0)
 
     for at, stream in enumerate(streams):
         depth = len(stream.levels)
@@ -1142,14 +1249,14 @@
             since = step - stream.first - lag
             return since // 2, (since >= 0) & (since % 2 == 0) & (since < 2 * stream.count)
 
-        item, here = item_at(depth + 2)
+        item, here = item_at(depth + 1 + stream.lag)
 
         @pl.when(here)
         def _(at=at, item=item):
             core_copy(at, item).wait()
             local_copy(at, item).wait()
 
-        item, here = item_at(depth + 1)
+        item, here = item_at(depth + stream.lag)
 
         @pl.when(here)
         def _(at=at, item=item):
@@ -1158,7 +1265,7 @@
             local_copy(at, item).start()
 
         for level in reversed(range(depth)):
-            item, here = item_at(level + 1)
+            item, here = item_at(level + stream.lag)
 
             @pl.when(here)
             def _(at=at, item=item, level=level, stream=stream, depth=depth):
@@ -1185,7 +1292,7 @@
             stream = streams[at]
             item = (step - stream.first) // 2
 
-            @pl.when((step % 2 == stream.first) & (item < stream.count))
+            @pl.when((step % 2 == stream.first % 2) & (step >= stream.first) & (item < stream.count))
             def _(at=at, fill=fill, item=item):
                 @pl.when(item > 0)
                 def _():
@@ -1241,13 +1348,13 @@
     lanes = 2 * HDIM
     pairs = qkv.shape[1] // (3 * lanes)
     n_seq = 2 * row_count
-    tile = 256
+    tile = 512
     sub = own_tokens // n_seq
     streams = streams_of(width, down_part.shape[0] * 2, n_seq, pairs)
     last = pairs - 1
     now = lambda i: jnp.minimum(i // 2, last)
     before = lambda i: jnp.clip(i // 2 - 1, 0, last)
-    early = lambda i: jnp.minimum(i // 2, down_pieces - 1)
+    early = lambda i: jnp.clip(i // 2 - 1, 0, down_pieces - 1)
     fixed = lambda shape: pl.BlockSpec(shape, lambda i: (0,) * len(shape), pipeline_mode=pl.Buffered(1))
 
     def columns(place):
@@ -1265,14 +1372,14 @@
 
     outs = [out_piece(value) for value in (out_kept, out_came)]
     down = down_part.reshape(n_seq // 2, 2, -1, width // CORES)
-    up = up_part.reshape(n_seq // 2, 2, rows, -1)
+    up = up_part.reshape(n_seq // 4, 2, rows, -1)
     down_spec = pl.BlockSpec((n_seq // 2, 2, streams[1].rows, width // CORES), lambda i: (0, 0, early(i), 0))
-    up_spec = pl.BlockSpec((n_seq // 2, 2, rows, streams[2].columns), lambda i: (0, 0, 0, early(i)))
+    up_spec = pl.BlockSpec((n_seq // 4, 2, rows, streams[2].columns), lambda i: (0, 0, 0, early(i)))
     count = len(streams)
     deepest = max(len(stream.levels) for stream in streams)
     return pl.pallas_call(
         functools.partial(back_kernel, pairs, tile, streams, row_count),
-        grid=(2 * pairs + deepest + 2,),
+        grid=(2 * pairs + deepest + 1 + streams[0].lag,),
         in_specs=[
             fixed((tokens, 1)),
             fixed((1, tokens)),
@@ -1580,7 +1687,7 @@
 
     rows_first = high_steps + seq_steps[1:2] + seq_steps[:1] + seq_steps[2:]
     down_order = [step for step in seq_steps + high_steps if step != ("rows", 1)]
-    up_order = [step for step in high_steps + seq_steps if step != ("seq", 0)]
+    up_order = [step for step in high_steps + seq_steps if step not in (("seq", 0), ("seq", 1))]
 
     def gather_high(value, pieces=0):
         for step in high_steps[::-1]:
@@ -1766,14 +1873,9 @@
             start = x_row.reshape(tokens, width)
             mixed, lse, cot, mixed_own = attend_row(qkv, key_tags, query_tags, cotangent)
             middle = start.astype(f32) + dot(mixed_own, out_weight, 1, 0)
-            outputs, d_middle, d_attn, down_part, up_part = feed(
-                middle, cot.reshape(tokens, width), feed_gain, up_weight, down_weight, n_seq
+            outputs, d_middle, _, d_mixed, out_kept, out_received, down_part, up_part = feed(
+                middle, cot.reshape(tokens, width), feed_gain, up_weight, down_weight, mixed_own, out_weight, n_seq
             )
-            out_grad = dot(mixed_own, d_attn[0], 0, 0).astype(bf16)
-            out_kept = lax.dynamic_slice_in_dim(out_grad, core * half, half, 1)
-            out_received = other_core(lax.dynamic_slice_in_dim(out_grad, (1 - core) * half, half, 1))
-            out_own = lax.dynamic_slice_in_dim(out_weight, core * half, half, 0)
-            d_mixed = dot(d_attn.reshape(seq_len, width), out_own, 1, 1).astype(bf16)
             input_grad, out_low, qkv_out, down_all, up_all = back(
                 qkv, mixed, d_mixed, lse, key_tags, query_tags, n1, (own_weight, other_weight), attention_gain,
                 out_kept, out_received, down_part, up_part, start, d_middle, outputs, row_count,
@@ -1809,19 +1911,20 @@
         middle = start
         for part, weight in zip(mixed_parts, out_parts):
             middle = middle + dot(part, weight, 1, 0)
-        outputs, d_middle, d_attn, down_part, up_part = feed(middle, cot, feed_gain, up_weight, down_weight, n_seq)
-        d_attn = d_attn[0]
-
-        d_attn_all = jnp.concatenate([d_attn] + [to_member(d_attn, hop) for hop in range(1, group)], 0)
-
-
-        half = width // CORES
         if group == CORES:
             mixed_own = ordered(mixed_parts[0], mixed_parts[1], 1)
         else:
             slots = jnp.stack([part[:, :group_width] for part in mixed_parts])
             turn = (jnp.arange(group, dtype=jnp.int32) - member) % group
             mixed_own = jnp.take(slots, turn, axis=0).transpose(1, 0, 2).reshape(tokens, width)
+        outputs, d_middle, d_attn, _, _, _, down_part, up_part = feed(
+            middle, cot, feed_gain, up_weight, down_weight, mixed_own, out_weight, n_seq
+        )
+
+        d_attn_all = jnp.concatenate([d_attn] + [to_member(d_attn, hop) for hop in range(1, group)], 0)
+
+
+        half = width // CORES
         out_grad = dot(mixed_own, d_attn, 0, 0).astype(bf16)
         out_kept = lax.dynamic_slice_in_dim(out_grad, core * half, half, 1)
         out_received = other_core(lax.dynamic_slice_in_dim(out_grad, (1 - core) * half, half, 1))

time: 627 us -> 601 us (0.959)
  Pallas kernels: 578 us -> 565 us
  matrix products: 20.2 us -> 8.43 us
    pallas_call x1, Pallas kernels: 290 us -> 259 us  [back(): pl.pallas_call(functools.partial(back_kernel, pairs, tile, streams, row_c...]
    pallas_call x1, Pallas kernels: 131 us -> 149 us  [feed(): pl.pallas_call(functools.partial(feed_kernel, tiles, 128), grid=(tiles +...]
    dot_general x3 -> x1, matrix products: 20.2 us -> 8.43 us  [dot(): lax.dot_general(a, b, (((ca,), (cb,)), ((), ())), preferred_element_type=...]
  transfers between devices with their start and end apart: 2 -> 1, of which waited for: 0 -> 0; matrix products, arithmetic and copies ran while one was open for 2% -> 1% of each run, Pallas kernels for 12% -> 12%
where the time goes in v5:
time: 601 us; the launch traced here: 591 us
  Pallas kernels  565 us (94%)
  local copies, waits for them, and re-layouts  12.2 us (2%)
  matrix products  8.43 us (1%)
    pallas_call x1, Pallas kernels, back(): pl.pallas_call(functools.partial(back_kernel, pairs, tile, streams, row_c...  259 us
    pallas_call x1, Pallas kernels, feed(): pl.pallas_call(functools.partial(feed_kernel, tiles, 128), grid=(tiles +...  149 us
    pallas_call x1, Pallas kernels, attend_row(): pl.pallas_call(functools.partial(attend_row_kernel, tile, row_count), gri...  74.2 us
    pallas_call x1, Pallas kernels, begin(): pl.pallas_call(functools.partial(begin_kernel, row_count, pairs), in_spec...  72 us
  transfers between devices with their start and end apart: 1, of which 0 were waited for; matrix products, arithmetic and copies ran while one was open for 1% of the time, Pallas kernels for 12%

profile of v5, /device:TPU:0, one launch (start us, length us, event | category | flops | bytes accessed | tf_op | source)
XLA Modules:
  0.0 590.9 jit_solution(471020042358216681)
XLA Ops:
  0.6 0.8 fusion
  1.5 0.5 collective-permute-start
  2.0 1.3 reshape.181.gain_ref.refs_11_
  3.3 1.8 reshape.205.refs_10_
  5.1 1.3 reshape.185.gain_ref
  6.3 1.8 reshape.206.refs_11_
  8.1 72.0 %begin.1 = (bf16[8,128,1280]{2,1,0:T(8,128)(2,1)}, bf16[2048,1280]{1,0:T(8,128)(2,1)}, bf16[2048,1920]{1,0:T(8,128)(2,1)}, bf16[1280,1920]{1,0:T(8,128)(2,1)}, bf16[1280,1920]{1,0:T(8,128)(2,1)}) custom-call(bf16[4,2,128,1280]{3,2,1,0:T(8,128)(2,1)} %bitcast.33, bf16[1280,3840]{1,0:T(8,128)(2,1)} %refs_8_.1, f32[1,1280]{1,0:T(1,128)} %reshape.181.gain_ref.refs_11_), custom_call_target="tpu_custom_call" | custom-call | tf_op jit(solution)/shard_map/begin/pallas_call | solution.py:402
  80.1 0.0 collective-permute-done
  80.1 0.1 broadcast_select_fusion
  80.2 0.6 gather_fusion
  80.8 0.1 select_bitcast_fusion
  80.8 0.0 copy-start.2
  80.9 1.3 copy.23
  82.2 0.0 copy-done.2
  82.2 0.0 copy-start.3
  82.2 74.2 %attend_row.1 = (bf16[2048,640]{1,0:T(8,128)(2,1)}, f32[5,2,2048]{2,1,0:T(2,128)}, bf16[8,128,1280]{2,1,0:T(8,128)(2,1)}, bf16[1024,1280]{1,0:T(8,128)(2,1)}) custom-call(s32[2048,1]{1,0:T(8,128)} %bitcast.28, s32[1,2048]{1,0:T(1,128)} %bitcast.36, bf16[2048,1920]{1,0:T(8,128)(2,1)} %get-tuple-element.35.q_ref.k_ref.v_ref.refs_2_.refs_3_.refs_4_, ...), custom_call_target="tpu_custom_call" | custom-call | tf_op jit(solution)/shard_map/attend_row/pallas_call | solution.py:562
  156.4 0.0 copy-done.3
  156.4 8.4 %convert_add_fusion.middle_ref = f32[1024,1280]{1,0:T(8,128)} fusion(bf16[1024,1280]{1,0:T(8,128)(2,1)} %bitcast.38, bf16[1024,1280]{1,0:T(8,128)(2,1)} %get-tuple-element.38.mixed_ref, bf16[1280,1280]{1,0:T(8,128)(2,1)S(1)} %copy-done.3), kind=kOutput, calls=%fused_computation.1 | convolution fusion | flops 3358064640 | bytes 13762560 | tf_op jit(solution)/shard_map/dot_general | solution.py:27
  164.8 148.9 %feed.1 = (bf16[1024,1280]{1,0:T(8,128)(2,1)}, f32[1024,1280]{1,0:T(8,128)}, bf16[1024,1280]{1,0:T(8,128)(2,1)}, bf16[2048,640]{1,0:T(8,128)(2,1)}, bf16[1280,64...) custom-call(f32[1024,1280]{1,0:T(8,128)} %convert_add_fusion.middle_ref, ...), custom_call_target="tpu_custom_call" | custom-call | flops 80530636800 | bytes 60293120 | tf_op jit(solution)/shard_map/feed/pallas_call | solution.py:927
  313.7 259.4 %back.1 = (bf16[4,2,128,1280]{3,2,1,0:T(8,128)(2,1)}, bf16[4,2,128,1280]{3,2,1,0:T(8,128)(2,1)}, bf16[5,2,2,80,512]{4,3,2,1,0:T(8,128)(2,1)}, bf16[4,2,2,80,640]...) custom-call(s32[2048,1]{1,0:T(8,128)} %bitcast.29, s32[1,2048]{1,0:T(1,128)} %bitcast.37, ...), custom_call_target="tpu_custom_call" | custom-call | flops 107374182400 | bytes 20971520 | tf_op jit(solution)/shard_map/back/pallas_call | solution.py:1380
  573.2 0.0 copy-start.1
  573.2 10.2 %collect.1 = (f32[160,3840]{1,0:T(8,128)}, f32[160,1280]{1,0:T(8,128)}, f32[640,1280]{1,0:T(8,128)}, f32[160,5120]{1,0:T(8,128)}, f32[160,1]{1,0:T(8,128)}, /*index=5*/f32[160,1]{1,0:T(8,128)}) custom-call(s32[1]{0:T(128)} %bitcast.14.seq_ref, bf16[5,2,2,80,512]{4,3,2,1,0:T(8,128)(2,1)} %get-tuple-element.53.refs_0_, ...), custom_call_target="tpu_custom_call" | custom-call | tf_op jit(solution)/shard_map/collect/pallas_call | solution.py:1521
  583.4 1.6 reduce
  585.0 1.6 reduce.1
  586.5 0.0 copy-done.1
  586.5 0.0 copy-start
  586.5 1.5 copy.27
  588.0 1.2 copy-done
  589.2 1.5 copy.28
  (5 shorter events, 0.1 us)
Async XLA Ops:
  1.5 78.6 %collective-permute-start = (s32[4,2048]{1,0:T(4,128)S(1)}, s32[4,2048]{1,0:T(4,128)S(1)}, u32[]{:S(2)}, u32[]{:S(2)}) collective-permute-start(s32[4,2048]{1,0:T(4,128)S(1)} %fusion), channel_id=1, source_target_pairs={{0,1},{1,0},{2,3},{3,2},{4,5},{5,4},{6,7},{7,6},{8,9},{9,8},{10,11... | collective-permute-start | bytes 98312 | tf_op jit(solution)/shard_map/ppermute | solution.py:1638
  80.8 1.4 copy-start.2
  82.2 74.2 %copy-start.3 = (bf16[1280,1280]{1,0:T(8,128)(2,1)S(1)}, bf16[1280,1280]{1,0:T(8,128)(2,1)}, u32[]{:S(2)}) copy-start(bf16[1280,1280]{1,0:T(8,128)(2,1)} %out_weight_ref.1) | copy-start | bytes 9830404
  573.2 13.4 %copy-start.1 = (bf16[4,2,128,1280]{3,2,1,0:T(8,128)(2,1)S(1)}, bf16[4,2,128,1280]{3,2,1,0:T(8,128)(2,1)}, u32[]{:S(2)}) copy-start(bf16[4,2,128,1280]{3,2,1,0:T(8,128)(2,1)} %get-tuple-element.51) | copy-start | bytes 7864324
  586.5 2.7 copy-start

commit v6 on v5

--- a/solution.py
+++ b/solution.py
@@ -17,7 +17,7 @@
 f32 = jnp.float32
 AXES = ("seq", "rows")
 vmem_bytes = 60 * 2**20
-feed_vmem_bytes = 62 * 2**20
+feed_vmem_bytes = 63 * 2**20
 feed_tile = 512
 max_cells = 7
 MESH = pl.DeviceIdType.MESH
@@ -626,16 +626,16 @@
     n2,
     total,
     d_attn,
-    d_attn_other,
     out_weight,
     out_keep,
     out_send,
-    d_mixed,
-    down_keep,
-    down_send,
+    acts,
+    d_ups,
+    up_before,
+    down_before,
+    down_halves,
     down_recv,
-    up_keep,
-    up_send,
+    up_halves,
     up_recv,
     down_far_keep,
     down_far_send,
@@ -657,9 +657,10 @@
     last_recv_sem,
     out_sems,
 ):
-    step = pl.program_id(0)
+    ahead = pl.program_id(0)
+    step = ahead - 1
     tokens, width = n2.shape
-    half = width // 2
+    half, tile = width // 2, up_ref.shape[1]
     seq_at, rows_at = lax.axis_index("seq"), lax.axis_index("rows")
     core, high, low, mid = rows_at % 2, (rows_at // 2) % 2, seq_at % 2, (seq_at // 2) % 2
     core_peer = (seq_at, rows_at + 1 - 2 * core)
@@ -671,7 +672,7 @@
             refs = ((down_far_send, down_far_recv), (up_far_send, up_far_recv))
             sems, peers = (far_send_sem, far_recv_sem), far_peers
         else:
-            refs = ((down_send, down_recv), (up_send, up_recv))
+            refs = ((down_halves.at[:, 1 - core], down_recv), (up_halves.at[:, 1 - core], up_recv))
             sems, peers = (core_send_sem, core_recv_sem), (core_peer, core_peer)
         return [
             pltpu.make_async_remote_copy(
@@ -688,7 +689,7 @@
     def signal(sem, peer):
         pl.semaphore_signal(sem, inc=1, device_id=peer, device_id_type=MESH)
 
-    @pl.when(step == 0)
+    @pl.when(ahead == 0)
     def _():
         barrier = pltpu.get_barrier_semaphore()
         for peer in (core_peer,) + far_peers + (last_peer,):
@@ -705,48 +706,49 @@
         total[...] = middle_ref[...]
         d_middle_ref[...] = jnp.zeros_like(d_middle_ref)
 
-    @pl.when(step < tiles)
-    def _():
-        up_w, down_w = up_ref[...], down_ref[...]
-        up = dot(n2[...], up_w, 1, 0)
-        d_act = dot(cot_ref[...], down_w, 1, 1)
+    def activate():
+        up = dot(n2[...], up_ref[...], 1, 0)
+        d_act = dot(cot_ref[...], down_ref[...], 1, 1)
         share = 0.5 + 0.5 * lax.erf(up * (0.5**0.5))
         density = jnp.exp(-0.5 * up * up) * 0.3989422804014327
-        act = (up * share).astype(bf16)
-        d_up = (d_act * (share + up * density)).astype(bf16)
-        total[...] += dot(act, down_w, 1, 0)
-        d_middle_ref[...] += dot(d_up, up_w, 1, 1)
+        acts[ahead % 2] = (up * share).astype(bf16)
+        d_ups[ahead % 2] = (d_act * (share + up * density)).astype(bf16)
+
+    def use():
         slot = step % 2
-
-        @pl.when(step >= 2)
-        def _():
-            for copy in copies(slot, False):
-                copy.wait_send()
-
+        act, d_up = acts[slot], d_ups[slot]
+        total[...] += dot(act, down_before[...], 1, 0)
+        d_middle_ref[...] += dot(d_up, up_before[...], 1, 1)
         up_grad = dot(n2[...], d_up, 0, 0).astype(bf16)
         cut = up_grad.shape[1] // 2
-
-        @pl.when(core == 0)
-        def _():
-            up_keep[slot] = up_grad[:, :cut].reshape(up_keep.shape[1:])
-            up_send[slot] = up_grad[:, cut:].reshape(up_keep.shape[1:])
-
-        @pl.when(core != 0)
-        def _():
-            up_keep[slot] = up_grad[:, cut:].reshape(up_keep.shape[1:])
-            up_send[slot] = up_grad[:, :cut].reshape(up_keep.shape[1:])
-
+        up_halves[slot, 0] = up_grad[:, :cut].reshape(up_halves.shape[2:])
+        up_halves[slot, 1] = up_grad[:, cut:].reshape(up_halves.shape[2:])
         down_grad = dot(act, cot_ref[...], 0, 0).astype(bf16)
-
-        @pl.when(core == 0)
-        def _():
-            down_keep[slot] = down_grad[:, :half].reshape(down_keep.shape[1:])
-            down_send[slot] = down_grad[:, half:].reshape(down_keep.shape[1:])
-
-        @pl.when(core != 0)
-        def _():
-            down_keep[slot] = down_grad[:, half:].reshape(down_keep.shape[1:])
-            down_send[slot] = down_grad[:, :half].reshape(down_keep.shape[1:])
+        down_halves[slot, 0] = down_grad[:, :half].reshape(down_halves.shape[2:])
+        down_halves[slot, 1] = down_grad[:, half:].reshape(down_halves.shape[2:])
+
+    @pl.when((step >= 2) & (step < tiles))
+    def _():
+        for copy in copies(step % 2, False):
+            copy.wait_send()
+
+    @pl.when(ahead == 0)
+    def _():
+        activate()
+
+    @pl.when((ahead > 0) & (ahead < tiles))
+    def _():
+        activate()
+        use()
+
+    @pl.when(ahead == tiles)
+    def _():
+        use()
+
+    @pl.when(ahead < tiles)
+    def _():
+        up_before[...] = up_ref[...]
+        down_before[...] = down_ref[...]
 
     def add(a, b):
         return (a.astype(f32) + b.astype(f32)).astype(bf16)
@@ -797,11 +799,11 @@
             pl.semaphore_wait(far_free.at[0], 1)
             pl.semaphore_wait(far_free.at[1], 1)
 
-        down_far_send[slot] = add(down_keep[slot, :, 1 - high], down_recv[slot, :, 1 - high])
-        down_far_keep[slot] = add(down_keep[slot, :, high], down_recv[slot, :, high])
+        down_far_send[slot] = add(down_halves[slot, core, :, 1 - high], down_recv[slot, :, 1 - high])
+        down_far_keep[slot] = add(down_halves[slot, core, :, high], down_recv[slot, :, high])
         shape = up_far_send.shape[1:]
-        up_far_send[slot] = add(up_keep[slot, :, 1 - low], up_recv[slot, :, 1 - low]).reshape(shape)
-        up_far_keep[slot] = add(up_keep[slot, :, low], up_recv[slot, :, low]).reshape(shape)
+        up_far_send[slot] = add(up_halves[slot, core, :, 1 - low], up_recv[slot, :, 1 - low]).reshape(shape)
+        up_far_keep[slot] = add(up_halves[slot, core, :, low], up_recv[slot, :, low]).reshape(shape)
         for copy in copies(slot, True):
             copy.start()
 
@@ -821,7 +823,7 @@
     def _():
         pass_on()
 
-    @pl.when(step < tiles)
+    @pl.when((step >= 0) & (step < tiles))
     def _():
         @pl.when(step >= 2)
         def _():
@@ -834,7 +836,10 @@
     def _():
         def body(i, _):
             part = pl.ds(pl.multiple_of(i * rows, rows), rows)
-            out_ref[part, :] = total[part, :].astype(bf16)
+            low_total = total[part, :].astype(bf16)
+            for at in range(2):
+                acts[at, part, :] = low_total[:, at * tile : (at + 1) * tile]
+            d_ups[0, part, : width - 2 * tile] = low_total[:, 2 * tile :]
             unit, scale = norm_parts(middle_ref[part, :])
             grad = cot_ref[part, :].astype(f32) + norm_back(d_middle_ref[part, :], gain_ref[...], unit, scale)
             d_middle_ref[part, :] = grad
@@ -853,18 +858,37 @@
             device_id_type=MESH,
         )
 
-    d_attn_copy = lambda: to_core(d_attn, d_attn_other, 0)
+    d_attn_copy = lambda: to_core(d_attn, d_attn_out.at[1], 0)
     out_copy = lambda: to_core(out_send, out_came, 2)
     mixed_copy = lambda: pltpu.make_async_copy(mixed_ref, n2, out_sems.at[0])
     weight_copy = lambda: pltpu.make_async_copy(
         out_weight_ref.at[pl.ds(pl.multiple_of(core * half, half), half)], out_weight, out_sems.at[1]
     )
-    d_attn_save = lambda: pltpu.make_async_copy(d_attn, d_attn_out, out_sems.at[2])
+    d_attn_save = lambda: pltpu.make_async_copy(d_attn, d_attn_out.at[0], out_sems.at[2])
     out_save = lambda: pltpu.make_async_copy(out_keep, out_kept, out_sems.at[3])
-    d_mixed_save = lambda: pltpu.make_async_copy(d_mixed, d_mixed_out, out_sems.at[4])
+    d_mixed_save = lambda: pltpu.make_async_copy(down_halves, d_mixed_out, out_sems.at[4])
+
+    def in_slots():
+        wide = [(acts.at[at], pl.ds(at * tile, tile)) for at in range(2)]
+        wide.append((d_ups.at[0, :, pl.ds(0, width - 2 * tile)], pl.ds(2 * tile, width - 2 * tile)))
+        return list(enumerate(wide))
+
+    def total_saves():
+        return [
+            pltpu.make_async_copy(source, out_ref.at[:, columns], out_sems.at[5 + at])
+            for at, (source, columns) in in_slots()
+        ]
+
+    def d_attn_loads():
+        return [
+            pltpu.make_async_copy(d_attn_out.at[1, :, columns], target, out_sems.at[8 + at])
+            for at, (target, columns) in in_slots()
+        ]
 
     @pl.when(step == tiles)
     def _():
+        for copy in total_saves():
+            copy.start()
         d_attn_copy().start()
         d_attn_save().start()
         mixed_copy().start()
@@ -891,10 +915,25 @@
 
     @pl.when(step == tiles + 2)
     def _():
+        for copy in total_saves():
+            copy.wait()
+        d_attn_copy().wait()
+        for copy in d_attn_loads():
+            copy.start()
         weight_copy().wait()
-        d_attn_copy().wait()
-        d_mixed[:tokens, :] = dot(d_attn[...], out_weight[...], 1, 1).astype(bf16)
-        d_mixed[tokens:, :] = dot(d_attn_other[...], out_weight[...], 1, 1).astype(bf16)
+        for slot in range(2):
+            for copy in copies(slot, False):
+                copy.wait_send()
+
+        def keep_d_mixed(at, found):
+            found = found.astype(bf16).reshape((-1,) + down_halves.shape[2:])
+            down_halves[at, : found.shape[0]] = found
+
+        keep_d_mixed(0, dot(d_attn[...], out_weight[...], 1, 1))
+        for copy in d_attn_loads():
+            copy.wait()
+        other = jnp.concatenate([acts[0], acts[1], d_ups[0, :, : width - 2 * tile]], 1)
+        keep_d_mixed(1, dot(other, out_weight[...], 1, 1))
         d_mixed_save().start()
         last_add()
         out_copy().wait()
@@ -902,9 +941,8 @@
             copy.wait()
         for slot in range(2):
             last_copy(slot).wait_send()
-            for far in (False, True):
-                for copy in copies(slot, far):
-                    copy.wait_send()
+            for copy in copies(slot, True):
+                copy.wait_send()
 
 
 def feed(middle, cot, gain, up_weight, down_weight, mixed_own, out_weight, n_seq):
@@ -917,16 +955,19 @@
     fixed = lambda shape: pl.BlockSpec(shape, lambda i: (0, 0), pipeline_mode=pl.Buffered(1))
     at = lambda i: jnp.minimum(i, tiles - 1)
     hbm = pl.BlockSpec(memory_space=pl.ANY)
-    late = lambda i: jnp.clip(i - 2, 0, tiles - 1)
+    late = lambda i: jnp.clip(i - 3, 0, tiles - 1)
     down_shape = (2, tile // (2 * piece_rows), 2, piece_rows, half)
     up_shape = (2, n_seq // 2, 2, shard, tile // 2)
-    near = [pltpu.VMEM(down_shape, bf16)] * 3 + [pltpu.VMEM(up_shape, bf16)] * 3
+    near = [pltpu.VMEM((2, tokens, tile), bf16)] * 2
+    near += [pltpu.VMEM((width, tile), bf16), pltpu.VMEM((tile, width), bf16)]
+    for shape in (down_shape, up_shape):
+        near += [pltpu.VMEM(shape[:1] + (CORES,) + shape[1:], bf16), pltpu.VMEM(shape, bf16)]
     up_far = (2, n_seq // 4, 2, shard, tile // 2)
     far = [pltpu.VMEM(down_shape[:2] + down_shape[3:], bf16)] * 3 + [pltpu.VMEM(up_far, bf16)] * 3
     far += [pltpu.VMEM(up_far[:2] + up_far[3:], bf16)] * 3
     return pl.pallas_call(
         functools.partial(feed_kernel, tiles, 128),
-        grid=(tiles + 3,),
+        grid=(tiles + 4,),
         in_specs=[
             fixed((tokens, width)),
             fixed((tokens, width)),
@@ -937,36 +978,34 @@
             hbm,
         ],
         out_specs=[
-            fixed((tokens, width)),
+            hbm,
             fixed((tokens, width)),
             hbm,
             hbm,
             hbm,
             hbm,
             pl.BlockSpec((tile // 2, half), lambda i: (late(i), 0)),
-            pl.BlockSpec((width // 4, tile // 2), lambda i: (0, jnp.maximum(i - 3, 0))),
+            pl.BlockSpec((width // 4, tile // 2), lambda i: (0, jnp.clip(i - 4, 0, tiles - 1))),
         ],
         scratch_shapes=[
             pltpu.VMEM((tokens, width), bf16),
             pltpu.VMEM((tokens, width), f32),
             pltpu.VMEM((tokens, width), bf16),
-            pltpu.VMEM((tokens, width), bf16),
             pltpu.VMEM((half, width), bf16),
             pltpu.VMEM((width, half), bf16),
             pltpu.VMEM((width, half), bf16),
-            pltpu.VMEM((2 * tokens, half), bf16),
         ]
         + near
         + far
         + [pltpu.SemaphoreType.DMA((2, 2))] * 4
         + [pltpu.SemaphoreType.REGULAR, pltpu.SemaphoreType.REGULAR((2,)), pltpu.SemaphoreType.DMA((4,))]
         + [pltpu.SemaphoreType.DMA((2,))] * 2
-        + [pltpu.SemaphoreType.DMA((5,))],
+        + [pltpu.SemaphoreType.DMA((11,))],
         out_shape=[
             whole(bf16),
             whole(f32),
-            whole(bf16),
-            jax.ShapeDtypeStruct((2 * tokens, half), bf16),
+            jax.ShapeDtypeStruct((2, tokens, width), bf16),
+            jax.ShapeDtypeStruct(down_shape[:1] + (CORES,) + down_shape[1:], bf16),
             jax.ShapeDtypeStruct((width, half), bf16),
             jax.ShapeDtypeStruct((width, half), bf16),
             jax.ShapeDtypeStruct((wide // 2, half), bf16),
@@ -1452,8 +1491,8 @@
 
 def collect_kernel(pairs, seq_ref, *refs):
     qkv_parts, down_parts, up_parts = refs[:3]
-    qkv_weights, up_weight, first_gain, second_gain = refs[3:9], refs[9], refs[10], refs[11]
-    qkv_out, out_out, down_out, up_out, first_out, second_out = refs[12:]
+    qkv_weights, up_weight = refs[3:9], refs[9]
+    qkv_out, out_out, down_out, up_out, first_out, second_out, first_sum, second_sum = refs[10:]
     item = pl.program_id(0)
     lanes = 2 * HDIM
     rows = qkv_parts.shape[2]
@@ -1463,8 +1502,8 @@
 
     @pl.when(item == 0)
     def _():
-        first_out[...] = jnp.zeros_like(first_out)
-        second_out[...] = jnp.zeros_like(second_out)
+        first_sum[...] = jnp.zeros_like(first_sum)
+        second_sum[...] = jnp.zeros_like(second_sum)
 
     for core in range(CORES):
         place = pl.multiple_of(core * half + item * lanes, lanes)
@@ -1475,7 +1514,7 @@
                 value = part[:, kind * lanes : (kind + 1) * lanes]
                 qkv_out[own, pl.ds(kind * width + place, lanes)] = value
                 weight = qkv_weights[kind * CORES + core][own, :].astype(f32)
-                first_out[own, :] += jnp.sum(value * weight, axis=1, keepdims=True)
+                first_sum[own, :] += value * weight
             out_out[own, pl.ds(place, lanes)] = part[:, 3 * lanes :]
 
     @pl.when(item < down_pieces)
@@ -1489,7 +1528,7 @@
                     columns = pl.ds(pl.multiple_of(column, lanes), lanes)
                     value = up_parts[core, high, :, at * lanes : (at + 1) * lanes].astype(f32)
                     up_out[own, columns] = value
-                    second_out[own, :] += jnp.sum(value * up_weight[own, columns].astype(f32), axis=1, keepdims=True)
+                    second_sum[own, :] += value * up_weight[own, columns].astype(f32)
                 count = down_parts.shape[2] // piece_rows
                 for at in range(count):
                     start = ((item * count + at) * 2 + high) * piece_rows
@@ -1498,11 +1537,11 @@
 
     @pl.when(item == pairs - 1)
     def _():
-        first_out[...] = first_out[...] / first_gain[...]
-        second_out[...] = second_out[...] / second_gain[...]
-
-
-def collect(seq_at, qkv_parts, down_parts, up_parts, qkv_weight, up_weight, first_gain, second_gain):
+        first_out[...] = jnp.sum(first_sum[...].T, axis=0, keepdims=True)
+        second_out[...] = jnp.sum(second_sum[...].T, axis=0, keepdims=True)
+
+
+def collect(seq_at, qkv_parts, down_parts, up_parts, qkv_weight, up_weight):
     pairs, _, _, rows, _ = qkv_parts.shape
     width, lanes = qkv_weight.shape[0], 2 * HDIM
     shard, wide = 2 * rows, up_weight.shape[1]
@@ -1516,7 +1555,6 @@
     def weight(kind, core):
         return pl.BlockSpec((shard, lanes), lambda i, seq: (seq[0], (kind * CORES + core) * pairs + i))
 
-    gain = pl.BlockSpec((shard, 1), lambda i, seq: (seq[0], 0))
     whole = lambda shape: pl.BlockSpec(shape, lambda i, seq: (0, 0))
     return pl.pallas_call(
         functools.partial(collect_kernel, pairs),
@@ -1525,29 +1563,29 @@
             grid=(pairs,),
             in_specs=[parts(qkv_parts), parts(down_parts), parts(up_parts)]
             + [weight(kind, core) for kind in range(3) for core in range(CORES)]
-            + [pl.BlockSpec((shard, wide), lambda i, seq: (seq[0], 0)), gain, gain],
+            + [pl.BlockSpec((shard, wide), lambda i, seq: (seq[0], 0))],
             out_specs=[
                 whole((shard, 3 * width)),
                 whole((shard, width)),
                 whole((down_rows, width)),
                 whole((shard, wide)),
-                whole((shard, 1)),
-                whole((shard, 1)),
+                whole((1, shard)),
+                whole((1, shard)),
             ],
+            scratch_shapes=[pltpu.VMEM((shard, lanes), f32)] * 2,
         ),
         out_shape=[
             jax.ShapeDtypeStruct((shard, 3 * width), f32),
             jax.ShapeDtypeStruct((shard, width), f32),
             jax.ShapeDtypeStruct((down_rows, width), f32),
             jax.ShapeDtypeStruct((shard, wide), f32),
-            jax.ShapeDtypeStruct((shard, 1), f32),
-            jax.ShapeDtypeStruct((shard, 1), f32),
+            jax.ShapeDtypeStruct((1, shard), f32),
+            jax.ShapeDtypeStruct((1, shard), f32),
         ],
         compiler_params=pltpu.CompilerParams(vmem_limit_bytes=vmem_bytes),
         name="collect",
     )(
         seq_at.reshape(1), qkv_parts, down_parts, up_parts, *[qkv_weight] * 6, up_weight,
-        first_gain.reshape(width, 1), second_gain.reshape(width, 1),
     )
 
 
@@ -1877,19 +1915,24 @@
                 middle, cot.reshape(tokens, width), feed_gain, up_weight, down_weight, mixed_own, out_weight, n_seq
             )
             input_grad, out_low, qkv_out, down_all, up_all = back(
-                qkv, mixed, d_mixed, lse, key_tags, query_tags, n1, (own_weight, other_weight), attention_gain,
+                qkv, mixed, d_mixed.reshape(seq_len, half), lse, key_tags, query_tags, n1, (own_weight, other_weight), attention_gain,
                 out_kept, out_received, down_part, up_part, start, d_middle, outputs, row_count,
             )
             qkv_total, out_total, down_total, up_total, first, second = collect(
-                seq_at, qkv_out, down_all, up_all, qkv_weight, up_weight, attention_gain, feed_gain
+                seq_at, qkv_out, down_all, up_all, qkv_weight, up_weight
             )
+            shard = width // n_seq
+
+            def gain_grad(sums, gain):
+                return sums.reshape(shard) / lax.dynamic_slice_in_dim(gain, seq_at * shard, shard, 0)
+
             return (
                 out_low.reshape(inputs.shape),
                 input_grad.reshape(inputs.shape),
-                first.reshape(-1),
+                gain_grad(first, attention_gain),
                 qkv_total,
                 out_total,
-                second.reshape(-1),
+                gain_grad(second, feed_gain),
                 up_total,
                 down_total,
             )
@@ -1920,6 +1963,7 @@
         outputs, d_middle, d_attn, _, _, _, down_part, up_part = feed(
             middle, cot, feed_gain, up_weight, down_weight, mixed_own, out_weight, n_seq
         )
+        d_attn = d_attn[0]
 
         d_attn_all = jnp.concatenate([d_attn] + [to_member(d_attn, hop) for hop in range(1, group)], 0)
 

time: 601 us -> 596 us (level)
  transfers between devices with their start and end apart: 1 -> 1, of which waited for: 0 -> 0; matrix products, arithmetic and copies ran while one was open for 1% -> 0% of each run, Pallas kernels for 12% -> 12%
where the time goes in v6:
time: 596 us; the launch traced here: 587 us
  Pallas kernels  566 us (95%)
  local copies, waits for them, and re-layouts  8.7 us (1%)
  matrix products  8.45 us (1%)
    pallas_call x1, Pallas kernels, back(): pl.pallas_call(functools.partial(back_kernel, pairs, tile, streams, row_c...  259 us
    pallas_call x1, Pallas kernels, feed(): pl.pallas_call(functools.partial(feed_kernel, tiles, 128), grid=(tiles +...  151 us
    pallas_call x1, Pallas kernels, attend_row(): pl.pallas_call(functools.partial(attend_row_kernel, tile, row_count), gri...  74.1 us
    pallas_call x1, Pallas kernels, begin(): pl.pallas_call(functools.partial(begin_kernel, row_count, pairs), in_spec...  72 us
  transfers between devices with their start and end apart: 1, of which 0 were waited for; matrix products, arithmetic and copies ran while one was open for 0% of the time, Pallas kernels for 12%

profile of v6, /device:TPU:0, one launch (start us, length us, event | category | flops | bytes accessed | tf_op | source)
XLA Modules:
  0.0 587.0 jit_solution(12703894370613357968)
XLA Ops:
  0.6 0.8 fusion
  1.5 0.5 collective-permute-start
  2.0 1.3 reshape.178.gain_ref.refs_11_
  3.3 1.3 reshape.182.gain_ref
  4.6 72.0 %begin.1 = (bf16[8,128,1280]{2,1,0:T(8,128)(2,1)}, bf16[2048,1280]{1,0:T(8,128)(2,1)}, bf16[2048,1920]{1,0:T(8,128)(2,1)}, bf16[1280,1920]{1,0:T(8,128)(2,1)}, bf16[1280,1920]{1,0:T(8,128)(2,1)}) custom-call(bf16[4,2,128,1280]{3,2,1,0:T(8,128)(2,1)} %bitcast.36, bf16[1280,3840]{1,0:T(8,128)(2,1)} %refs_8_.1, f32[1,1280]{1,0:T(1,128)} %reshape.178.gain_ref.refs_11_), custom_call_target="tpu_custom_call" | custom-call | tf_op jit(solution)/shard_map/begin/pallas_call | solution.py:402
  76.6 0.0 collective-permute-done
  76.6 0.1 broadcast_select_fusion
  76.7 0.6 gather_fusion
  77.3 0.1 select_bitcast_fusion
  77.3 0.0 copy-start.2
  77.4 1.3 copy.21
  78.7 0.0 copy-done.2
  78.7 0.0 copy-start.3
  78.7 74.1 %attend_row.1 = (bf16[2048,640]{1,0:T(8,128)(2,1)}, f32[5,2,2048]{2,1,0:T(2,128)}, bf16[8,128,1280]{2,1,0:T(8,128)(2,1)}, bf16[1024,1280]{1,0:T(8,128)(2,1)}) custom-call(s32[2048,1]{1,0:T(8,128)} %bitcast.31, s32[1,2048]{1,0:T(1,128)} %bitcast.39, bf16[2048,1920]{1,0:T(8,128)(2,1)} %get-tuple-element.35.q_ref.k_ref.v_ref.refs_2_.refs_3_.refs_4_, ...), custom_call_target="tpu_custom_call" | custom-call | tf_op jit(solution)/shard_map/attend_row/pallas_call | solution.py:562
  152.8 0.0 copy-done.3
  152.8 8.4 %convert_add_fusion.middle_ref = f32[1024,1280]{1,0:T(8,128)} fusion(bf16[1024,1280]{1,0:T(8,128)(2,1)} %bitcast.43, bf16[1024,1280]{1,0:T(8,128)(2,1)} %get-tuple-element.38.mixed_ref, bf16[1280,1280]{1,0:T(8,128)(2,1)S(1)} %copy-done.3), kind=kOutput, calls=%fused_computation.1 | convolution fusion | flops 3358064640 | bytes 13762560 | tf_op jit(solution)/shard_map/dot_general | solution.py:27
  161.2 151.3 %feed.1 = (bf16[1024,1280]{1,0:T(8,128)(2,1)}, f32[1024,1280]{1,0:T(8,128)}, bf16[2,1024,1280]{2,1,0:T(8,128)(2,1)}, bf16[2,2,16,2,16,640]{5,4,3,2,1,0:T(8,128)(...) custom-call(f32[1024,1280]{1,0:T(8,128)} %convert_add_fusion.middle_, ...), custom_call_target="tpu_custom_call" | custom-call | flops 80530636800 | bytes 60293120 | tf_op jit(solution)/shard_map/feed/pallas_call | solution.py:968
  312.5 259.2 %back.1 = (bf16[4,2,128,1280]{3,2,1,0:T(8,128)(2,1)}, bf16[4,2,128,1280]{3,2,1,0:T(8,128)(2,1)}, bf16[5,2,2,80,512]{4,3,2,1,0:T(8,128)(2,1)}, bf16[4,2,2,80,640]...) custom-call(s32[2048,1]{1,0:T(8,128)} %bitcast.32, s32[1,2048]{1,0:T(1,128)} %bitcast.40, ...), custom_call_target="tpu_custom_call" | custom-call | flops 107374182400 | bytes 20971520 | tf_op jit(solution)/shard_map/back/pallas_call | solution.py:1419
  571.7 0.0 copy-start.1
  571.7 9.5 %collect.1 = (f32[160,3840]{1,0:T(8,128)}, f32[160,1280]{1,0:T(8,128)}, f32[640,1280]{1,0:T(8,128)}, f32[160,5120]{1,0:T(8,128)}, f32[1,160]{1,0:T(1,128)}, /*index=5*/f32[1,160]{1,0:T(1,128)}) custom-call(s32[1]{0:T(128)} %bitcast.15.seq_ref, bf16[5,2,2,80,512]{4,3,2,1,0:T(8,128)(2,1)} %get-tuple-element.53.refs_0_, ...), custom_call_target="tpu_custom_call" | custom-call | tf_op jit(solution)/shard_map/collect/pallas_call | solution.py:1559
  581.2 1.4 dynamic-slice_divide_fusion
  582.6 0.0 copy-done.1
  582.6 0.0 copy-start
  582.6 1.5 copy.25
  584.1 1.2 copy-done
  585.3 1.5 copy.26
  (5 shorter events, 0.1 us)
Async XLA Ops:
  1.5 75.1 %collective-permute-start = (s32[4,2048]{1,0:T(4,128)S(1)}, s32[4,2048]{1,0:T(4,128)S(1)}, u32[]{:S(2)}, u32[]{:S(2)}) collective-permute-start(s32[4,2048]{1,0:T(4,128)S(1)} %fusion), channel_id=1, source_target_pairs={{0,1},{1,0},{2,3},{3,2},{4,5},{5,4},{6,7},{7,6},{8,9},{9,8},{10,11... | collective-permute-start | bytes 98312 | tf_op jit(solution)/shard_map/ppermute | solution.py:1676
  77.3 1.4 copy-start.2
  78.7 74.1 %copy-start.3 = (bf16[1280,1280]{1,0:T(8,128)(2,1)S(1)}, bf16[1280,1280]{1,0:T(8,128)(2,1)}, u32[]{:S(2)}) copy-start(bf16[1280,1280]{1,0:T(8,128)(2,1)} %out_weight_ref.1) | copy-start | bytes 9830404
  571.7 10.9 %copy-start.1 = (bf16[4,2,128,1280]{3,2,1,0:T(8,128)(2,1)S(1)}, bf16[4,2,128,1280]{3,2,1,0:T(8,128)(2,1)}, u32[]{:S(2)}) copy-start(bf16[4,2,128,1280]{3,2,1,0:T(8,128)(2,1)} %get-tuple-element.51) | copy-start | bytes 7864324
  582.6 2.7 copy-start

commit v7 on v6

--- a/solution.py
+++ b/solution.py
@@ -445,16 +445,16 @@
 
 
 def attend_row_kernel(
-    tile, row_count, tags, row_tags, q_ref, k_ref, v_ref, cot_ref, o_ref, lse_ref, cot_out, own_out,
-    v_turned, keys, scores_ref, mixed_ref, parts,
-    cot_send, cot_recv, cot_local, part_send, part_recv, part_local,
+    tile, row_count, tags, row_tags, q_ref, k_ref, v_ref, cot_ref, x_ref, weight_ref, o_ref, lse_ref, cot_out, own_out,
+    middle_out, v_turned, keys, scores_ref, mixed_ref, parts, x_part, weight, own, middle,
+    cot_send, cot_recv, cot_local, part_send, part_recv, part_local, in_sems, out_sems,
 ):
     item, last = pl.program_id(0), pl.num_programs(0) - 1
     seq_at, rows_at = lax.axis_index("seq"), lax.axis_index("rows")
     core = rows_at % CORES
     tokens, lanes = q_ref.shape
     own_tokens = tokens // CORES
-    n_seq = cot_out.shape[0]
+    n_seq, sub, _w = cot_out.shape
     moves = ToRows(cot_ref, cot_out, cot_send, cot_recv, cot_local, row_count, seq_at, rows_at)
 
     def part_copies(at):
@@ -485,10 +485,25 @@
             device_id_type=MESH,
         )
 
+    def in_copies():
+        return [
+            pltpu.make_async_copy(x_ref, x_part, in_sems.at[0]),
+            pltpu.make_async_copy(weight_ref, weight, in_sems.at[1]),
+        ]
+
+    def own_copy():
+        return pltpu.make_async_copy(own_out, own, in_sems.at[2])
+
+    def middle_copy(at):
+        rows = pl.ds(at * sub, sub)
+        return pltpu.make_async_copy(middle.at[rows], middle_out.at[rows], out_sems.at[at])
+
     @pl.when(item == 0)
     def _():
         all_signal(n_seq, seq_at, rows_at)
         moves.start()
+        for copy in in_copies():
+            copy.start()
 
     for head in range(2):
         keys[head] = with_cells(k_ref[...], tags[...], head, True)
@@ -542,12 +557,22 @@
             local.wait()
         for at in range(part_recv.shape[0]):
             part_came(at).wait_recv()
+        own_copy().start()
+        for copy in in_copies() + [own_copy()]:
+            copy.wait()
+        for at in range(n_seq // 2):
+            rows = slice(2 * at * sub, 2 * (at + 1) * sub)
+            middle[rows, :] = x_part[rows, :].astype(f32) + dot(own[rows, :], weight[...], 1, 0)
+            middle_copy(2 * at).start()
+            middle_copy(2 * at + 1).start()
         for s in range(n_seq):
             moves.wait_block(s)
         moves.wait_sends()
-
-
-def attend_row(qkv, tags, row_tags, cotangent):
+        for at in range(n_seq):
+            middle_copy(at).wait()
+
+
+def attend_row(qkv, tags, row_tags, cotangent, start, out_weight):
     tokens, width = qkv.shape
     row_count, block, model = cotangent.shape
     lanes = 2 * HDIM
@@ -569,10 +594,13 @@
             columns(1),
             columns(2),
             hbm,
+            hbm,
+            hbm,
         ],
         out_specs=[
             pl.BlockSpec((tokens, lanes), lambda i: (0, i)),
             pl.BlockSpec((None, 2, tokens), lambda i: (i, 0, 0)),
+            hbm,
             hbm,
             hbm,
         ],
@@ -581,6 +609,7 @@
             jax.ShapeDtypeStruct((pairs, 2, tokens), f32),
             jax.ShapeDtypeStruct((n_seq, sub, model), bf16),
             jax.ShapeDtypeStruct((tokens // CORES, model), bf16),
+            jax.ShapeDtypeStruct((tokens // CORES, model), f32),
         ],
         scratch_shapes=[
             pltpu.VMEM((2, HDIM + 16, tokens), bf16),
@@ -588,18 +617,24 @@
             pltpu.VMEM((2, tokens, tile), f32),
             pltpu.VMEM((lanes, tokens), f32),
             pltpu.VMEM((2, tokens, lanes), bf16),
+            pltpu.VMEM((tokens // CORES, model), bf16),
+            pltpu.VMEM((model, model), bf16),
+            pltpu.VMEM((tokens // CORES, model), bf16),
+            pltpu.VMEM((tokens // CORES, model), f32),
             pltpu.SemaphoreType.DMA((row_count, CORES)),
             pltpu.SemaphoreType.DMA((n_seq,)),
             pltpu.SemaphoreType.DMA,
             pltpu.SemaphoreType.DMA((2,)),
             pltpu.SemaphoreType.DMA((pairs,)),
             pltpu.SemaphoreType.DMA((2,)),
+            pltpu.SemaphoreType.DMA((3,)),
+            pltpu.SemaphoreType.DMA((n_seq,)),
         ],
         compiler_params=pltpu.CompilerParams(
             vmem_limit_bytes=vmem_bytes, collective_id=4, has_side_effects=True
         ),
         name="attend_row",
-    )(tags, row_tags, qkv, qkv, qkv, cotangent.reshape(row_count, CORES, sub, model))
+    )(tags, row_tags, qkv, qkv, qkv, cotangent.reshape(row_count, CORES, sub, model), start, out_weight)
 
 
 piece_rows = 16
@@ -1909,8 +1944,7 @@
             half = width // CORES
             x_row, n1, qkv, own_weight, other_weight = begin(inputs, qkv_weight, attention_gain)
             start = x_row.reshape(tokens, width)
-            mixed, lse, cot, mixed_own = attend_row(qkv, key_tags, query_tags, cotangent)
-            middle = start.astype(f32) + dot(mixed_own, out_weight, 1, 0)
+            mixed, lse, cot, mixed_own, middle = attend_row(qkv, key_tags, query_tags, cotangent, start, out_weight)
             outputs, d_middle, _, d_mixed, out_kept, out_received, down_part, up_part = feed(
                 middle, cot.reshape(tokens, width), feed_gain, up_weight, down_weight, mixed_own, out_weight, n_seq
             )

time: 596 us -> 595 us (level)
  matrix products: 8.45 us -> 0 us
  Pallas kernels: 566 us -> 572 us
    dot_general x1 -> x0, matrix products: 8.45 us -> none  [dot(): lax.dot_general(a, b, (((ca,), (cb,)), ((), ())), preferred_element_type=...]
    pallas_call x1, Pallas kernels: 74.1 us -> 80.4 us  [attend_row(): pl.pallas_call(functools.partial(attend_row_kernel, tile, row_count), gri...]
where the time goes in v7:
time: 595 us; the launch traced here: 585 us
  Pallas kernels  572 us (96%)
  local copies, waits for them, and re-layouts  8.7 us (1%)
    pallas_call x1, Pallas kernels, back(): pl.pallas_call(functools.partial(back_kernel, pairs, tile, streams, row_c...  259 us
    pallas_call x1, Pallas kernels, feed(): pl.pallas_call(functools.partial(feed_kernel, tiles, 128), grid=(tiles +...  151 us
    pallas_call x1, Pallas kernels, attend_row(): pl.pallas_call(functools.partial(attend_row_kernel, tile, row_count), gri...  80.4 us
    pallas_call x1, Pallas kernels, begin(): pl.pallas_call(functools.partial(begin_kernel, row_count, pairs), in_spec...  72 us
  transfers between devices with their start and end apart: 1, of which 0 were waited for; matrix products, arithmetic and copies ran while one was open for 0% of the time, Pallas kernels for 12%

profile of v7, /device:TPU:0, one launch (start us, length us, event | category | flops | bytes accessed | tf_op | source)
XLA Modules:
  0.0 584.7 jit_solution(10456827354451347026)
XLA Ops:
  0.6 0.8 fusion
  1.5 0.5 collective-permute-start
  2.0 1.3 reshape.178.gain_ref.refs_11_
  3.3 1.3 reshape.182.gain_ref
  4.6 72.0 %begin.1 = (bf16[8,128,1280]{2,1,0:T(8,128)(2,1)}, bf16[2048,1280]{1,0:T(8,128)(2,1)}, bf16[2048,1920]{1,0:T(8,128)(2,1)}, bf16[1280,1920]{1,0:T(8,128)(2,1)}, bf16[1280,1920]{1,0:T(8,128)(2,1)}) custom-call(bf16[4,2,128,1280]{3,2,1,0:T(8,128)(2,1)} %bitcast.36, bf16[1280,3840]{1,0:T(8,128)(2,1)} %refs_8_.1, f32[1,1280]{1,0:T(1,128)} %reshape.178.gain_ref.refs_11_), custom_call_target="tpu_custom_call" | custom-call | tf_op jit(solution)/shard_map/begin/pallas_call | solution.py:402
  76.6 0.0 collective-permute-done
  76.6 0.1 broadcast_select_fusion
  76.7 0.6 gather_fusion
  77.2 0.1 select_bitcast_fusion
  77.3 0.0 copy-start.2
  77.3 1.3 copy.21
  78.7 0.0 copy-done.2
  78.7 80.4 %attend_row.1 = (bf16[2048,640]{1,0:T(8,128)(2,1)}, f32[5,2,2048]{2,1,0:T(2,128)}, bf16[8,128,1280]{2,1,0:T(8,128)(2,1)}, bf16[1024,1280]{1,0:T(8,128)(2,1)}, f32[1024,1280]{1,0:T(8,128)}) custom-call(s32[2048,1]{1,0:T(8,128)} %bitcast.29, s32[1,2048]{1,0:T(1,128)} %bitcast.39, ...), custom_call_target="tpu_custom_call" | custom-call | tf_op jit(solution)/shard_map/attend_row/pallas_call | solution.py:587
  159.1 151.4 %feed.1 = (bf16[1024,1280]{1,0:T(8,128)(2,1)}, f32[1024,1280]{1,0:T(8,128)}, bf16[2,1024,1280]{2,1,0:T(8,128)(2,1)}, bf16[2,2,16,2,16,640]{5,4,3,2,1,0:T(8,128)(...) custom-call(f32[1024,1280]{1,0:T(8,128)} %get-tuple-element.39.middl, ...), custom_call_target="tpu_custom_call" | custom-call | flops 80530636800 | bytes 60293120 | tf_op jit(solution)/shard_map/feed/pallas_call | solution.py:1003
  310.5 258.9 %back.1 = (bf16[4,2,128,1280]{3,2,1,0:T(8,128)(2,1)}, bf16[4,2,128,1280]{3,2,1,0:T(8,128)(2,1)}, bf16[5,2,2,80,512]{4,3,2,1,0:T(8,128)(2,1)}, bf16[4,2,2,80,640]...) custom-call(s32[2048,1]{1,0:T(8,128)} %bitcast.30, s32[1,2048]{1,0:T(1,128)} %bitcast.40, ...), custom_call_target="tpu_custom_call" | custom-call | flops 107374182400 | bytes 20971520 | tf_op jit(solution)/shard_map/back/pallas_call | solution.py:1454
  569.4 0.0 copy-start.1
  569.4 9.5 %collect.1 = (f32[160,3840]{1,0:T(8,128)}, f32[160,1280]{1,0:T(8,128)}, f32[640,1280]{1,0:T(8,128)}, f32[160,5120]{1,0:T(8,128)}, f32[1,160]{1,0:T(1,128)}, /*index=5*/f32[1,160]{1,0:T(1,128)}) custom-call(s32[1]{0:T(128)} %bitcast.15.seq_ref, bf16[5,2,2,80,512]{4,3,2,1,0:T(8,128)(2,1)} %get-tuple-element.55.refs_0_, ...), custom_call_target="tpu_custom_call" | custom-call | tf_op jit(solution)/shard_map/collect/pallas_call | solution.py:1594
  578.9 1.4 dynamic-slice_divide_fusion
  580.3 0.0 copy-done.1
  580.3 0.0 copy-start
  580.3 1.5 copy.25
  581.8 1.2 copy-done
  583.0 1.5 copy.26
  (5 shorter events, 0.1 us)
Async XLA Ops:
  1.5 75.1 %collective-permute-start = (s32[4,2048]{1,0:T(4,128)S(1)}, s32[4,2048]{1,0:T(4,128)S(1)}, u32[]{:S(2)}, u32[]{:S(2)}) collective-permute-start(s32[4,2048]{1,0:T(4,128)S(1)} %fusion), channel_id=1, source_target_pairs={{0,1},{1,0},{2,3},{3,2},{4,5},{5,4},{6,7},{7,6},{8,9},{9,8},{10,11... | collective-permute-start | bytes 98312 | tf_op jit(solution)/shard_map/ppermute | solution.py:1711
  77.3 1.4 copy-start.2
  569.4 10.9 %copy-start.1 = (bf16[4,2,128,1280]{3,2,1,0:T(8,128)(2,1)S(1)}, bf16[4,2,128,1280]{3,2,1,0:T(8,128)(2,1)}, u32[]{:S(2)}) copy-start(bf16[4,2,128,1280]{3,2,1,0:T(8,128)(2,1)} %get-tuple-element.53) | copy-start | bytes 7864324
  580.3 2.7 copy-start

commit v8 on v7

--- a/solution.py
+++ b/solution.py
@@ -1083,7 +1083,7 @@
     rows = width // (2 * n_seq)
     return (
         Stream(("x", "y", "z1", "z2"), rows, 4 * lanes, 1, pairs, 2),
-        Stream(("y", "z1", "z2"), wide // (2 * n_seq * down_pieces), width // CORES, 2, down_pieces, 1),
+        Stream(("y", "z1", "z2"), wide // (2 * n_seq * down_pieces), width // CORES, 2, down_pieces, 2),
         Stream(("x", "z2"), rows, wide // CORES // down_pieces, 2, down_pieces, 1),
     )
 
@@ -1218,9 +1218,10 @@
         pl.semaphore_wait(barrier, n_seq * CORES)
         d_n1[...] = jnp.zeros_like(d_n1)
 
-    @pl.when(step < n_seq)
-    def _():
-        start_home((seq_at + step) % n_seq, True)
+    @pl.when(step < n_seq // 2)
+    def _():
+        for turn in range(2):
+            start_home((seq_at + 2 * step + turn) % n_seq, True)
 
     working, second = step < 2 * pairs, step % 2
 

time: 595 us -> 586 us (0.985)
  Pallas kernels: 572 us -> 565 us
    pallas_call x1, Pallas kernels: 259 us -> 252 us  [back(): pl.pallas_call(functools.partial(back_kernel, pairs, tile, streams, row_c...]
where the time goes in v8:
time: 586 us; the launch traced here: 578 us
  Pallas kernels  565 us (96%)
  local copies, waits for them, and re-layouts  8.7 us (1%)
    pallas_call x1, Pallas kernels, back(): pl.pallas_call(functools.partial(back_kernel, pairs, tile, streams, row_c...  252 us
    pallas_call x1, Pallas kernels, feed(): pl.pallas_call(functools.partial(feed_kernel, tiles, 128), grid=(tiles +...  151 us
    pallas_call x1, Pallas kernels, attend_row(): pl.pallas_call(functools.partial(attend_row_kernel, tile, row_count), gri...  80.4 us
    pallas_call x1, Pallas kernels, begin(): pl.pallas_call(functools.partial(begin_kernel, row_count, pairs), in_spec...  72 us
  transfers between devices with their start and end apart: 1, of which 0 were waited for; matrix products, arithmetic and copies ran while one was open for 0% of the time, Pallas kernels for 12%

profile of v8, /device:TPU:0, one launch (start us, length us, event | category | flops | bytes accessed | tf_op | source)
XLA Modules:
  0.0 577.9 jit_solution(18375899870939411988)
XLA Ops:
  0.6 0.8 fusion
  1.5 0.5 collective-permute-start
  2.0 1.3 reshape.178.gain_ref.refs_11_
  3.3 1.3 reshape.182.gain_ref
  4.6 72.0 %begin.1 = (bf16[8,128,1280]{2,1,0:T(8,128)(2,1)}, bf16[2048,1280]{1,0:T(8,128)(2,1)}, bf16[2048,1920]{1,0:T(8,128)(2,1)}, bf16[1280,1920]{1,0:T(8,128)(2,1)}, bf16[1280,1920]{1,0:T(8,128)(2,1)}) custom-call(bf16[4,2,128,1280]{3,2,1,0:T(8,128)(2,1)} %bitcast.36, bf16[1280,3840]{1,0:T(8,128)(2,1)} %refs_8_.1, f32[1,1280]{1,0:T(1,128)} %reshape.178.gain_ref.refs_11_), custom_call_target="tpu_custom_call" | custom-call | tf_op jit(solution)/shard_map/begin/pallas_call | solution.py:402
  76.6 0.0 collective-permute-done
  76.6 0.1 broadcast_select_fusion
  76.7 0.6 gather_fusion
  77.2 0.1 select_bitcast_fusion
  77.3 0.0 copy-start.2
  77.3 1.3 copy.21
  78.7 0.0 copy-done.2
  78.7 80.4 %attend_row.1 = (bf16[2048,640]{1,0:T(8,128)(2,1)}, f32[5,2,2048]{2,1,0:T(2,128)}, bf16[8,128,1280]{2,1,0:T(8,128)(2,1)}, bf16[1024,1280]{1,0:T(8,128)(2,1)}, f32[1024,1280]{1,0:T(8,128)}) custom-call(s32[2048,1]{1,0:T(8,128)} %bitcast.29, s32[1,2048]{1,0:T(1,128)} %bitcast.39, ...), custom_call_target="tpu_custom_call" | custom-call | tf_op jit(solution)/shard_map/attend_row/pallas_call | solution.py:587
  159.1 151.4 %feed.1 = (bf16[1024,1280]{1,0:T(8,128)(2,1)}, f32[1024,1280]{1,0:T(8,128)}, bf16[2,1024,1280]{2,1,0:T(8,128)(2,1)}, bf16[2,2,16,2,16,640]{5,4,3,2,1,0:T(8,128)(...) custom-call(f32[1024,1280]{1,0:T(8,128)} %get-tuple-element.39.middl, ...), custom_call_target="tpu_custom_call" | custom-call | flops 80530636800 | bytes 60293120 | tf_op jit(solution)/shard_map/feed/pallas_call | solution.py:1003
  310.5 252.1 %back.1 = (bf16[4,2,128,1280]{3,2,1,0:T(8,128)(2,1)}, bf16[4,2,128,1280]{3,2,1,0:T(8,128)(2,1)}, bf16[5,2,2,80,512]{4,3,2,1,0:T(8,128)(2,1)}, bf16[4,2,2,80,640]...) custom-call(s32[2048,1]{1,0:T(8,128)} %bitcast.30, s32[1,2048]{1,0:T(1,128)} %bitcast.40, ...), custom_call_target="tpu_custom_call" | custom-call | flops 107374182400 | bytes 20971520 | tf_op jit(solution)/shard_map/back/pallas_call | solution.py:1455
  562.7 0.0 copy-start.1
  562.7 9.5 %collect.1 = (f32[160,3840]{1,0:T(8,128)}, f32[160,1280]{1,0:T(8,128)}, f32[640,1280]{1,0:T(8,128)}, f32[160,5120]{1,0:T(8,128)}, f32[1,160]{1,0:T(1,128)}, /*index=5*/f32[1,160]{1,0:T(1,128)}) custom-call(s32[1]{0:T(128)} %bitcast.15.seq_ref, bf16[5,2,2,80,512]{4,3,2,1,0:T(8,128)(2,1)} %get-tuple-element.55.refs_0_, ...), custom_call_target="tpu_custom_call" | custom-call | tf_op jit(solution)/shard_map/collect/pallas_call | solution.py:1595
  572.2 1.4 dynamic-slice_divide_fusion
  573.6 0.0 copy-done.1
  573.6 0.0 copy-start
  573.6 1.5 copy.25
  575.1 1.2 copy-done
  576.3 1.5 copy.26
  (5 shorter events, 0.1 us)
Async XLA Ops:
  1.5 75.1 %collective-permute-start = (s32[4,2048]{1,0:T(4,128)S(1)}, s32[4,2048]{1,0:T(4,128)S(1)}, u32[]{:S(2)}, u32[]{:S(2)}) collective-permute-start(s32[4,2048]{1,0:T(4,128)S(1)} %fusion), channel_id=1, source_target_pairs={{0,1},{1,0},{2,3},{3,2},{4,5},{5,4},{6,7},{7,6},{8,9},{9,8},{10,11... | collective-permute-start | bytes 98312 | tf_op jit(solution)/shard_map/ppermute | solution.py:1712
  77.3 1.4 copy-start.2
  562.7 10.9 %copy-start.1 = (bf16[4,2,128,1280]{3,2,1,0:T(8,128)(2,1)S(1)}, bf16[4,2,128,1280]{3,2,1,0:T(8,128)(2,1)}, u32[]{:S(2)}) copy-start(bf16[4,2,128,1280]{3,2,1,0:T(8,128)(2,1)} %get-tuple-element.53) | copy-start | bytes 7864324
  573.6 2.7 copy-start

commit v9 on v8

--- a/solution.py
+++ b/solution.py
@@ -431,7 +431,7 @@
             vmem_limit_bytes=vmem_bytes, collective_id=3, has_side_effects=True
         ),
         name="begin",
-    )(inputs.reshape(row_count, CORES, sub, width), qkv_weight, gain.reshape(1, width))
+    )(inputs.reshape(row_count, CORES, sub, width), qkv_weight, gain)
 
 
 def with_cells(value, tags, head, is_key):
@@ -1006,7 +1006,7 @@
         in_specs=[
             fixed((tokens, width)),
             fixed((tokens, width)),
-            fixed((1, width)),
+            pl.BlockSpec((width,), lambda i: (0,), pipeline_mode=pl.Buffered(1)),
             pl.BlockSpec((width, tile), lambda i: (0, at(i))),
             pl.BlockSpec((tile, width), lambda i: (at(i), 0)),
             hbm,
@@ -1055,7 +1055,7 @@
             transcendentals=2 * tokens * wide,
         ),
         name="feed",
-    )(middle, cot, gain.reshape(1, width), up_weight, down_weight, mixed_own, out_weight)
+    )(middle, cot, gain, up_weight, down_weight, mixed_own, out_weight)
 
 
 class Stream:
@@ -1467,7 +1467,7 @@
             fixed((tokens, width)),
             weight,
             weight,
-            fixed((1, width)),
+            pl.BlockSpec((width,), lambda i: (0,), pipeline_mode=pl.Buffered(1)),
             outs[0][1],
             outs[1][1],
             down_spec,
@@ -1521,7 +1521,7 @@
         name="back",
     )(
         key_tags, query_tags, qkv, qkv, qkv, mixed, d_mixed, lse, n1, weights[0], weights[1],
-        gain.reshape(1, width), outs[0][0], outs[1][0], down, up, start, d_middle, outputs,
+        gain, outs[0][0], outs[1][0], down, up, start, d_middle, outputs,
     )
 
 

time: 586 us -> 584 us (level)
  transfers between devices with their start and end apart: 1 -> 1, of which waited for: 0 -> 0; matrix products, arithmetic and copies ran while one was open for 0% -> 0% of each run, Pallas kernels for 12% -> 13%
where the time goes in v9:
time: 584 us; the launch traced here: 575 us
  Pallas kernels  566 us (97%)
  local copies, waits for them, and re-layouts  6.11 us (1%)
    pallas_call x1, Pallas kernels, back(): pl.pallas_call(functools.partial(back_kernel, pairs, tile, streams, row_c...  252 us
    pallas_call x1, Pallas kernels, feed(): pl.pallas_call(functools.partial(feed_kernel, tiles, 128), grid=(tiles +...  151 us
    pallas_call x1, Pallas kernels, attend_row(): pl.pallas_call(functools.partial(attend_row_kernel, tile, row_count), gri...  80.4 us
    pallas_call x1, Pallas kernels, begin(): pl.pallas_call(functools.partial(begin_kernel, row_count, pairs), in_spec...  72 us
  transfers between devices with their start and end apart: 1, of which 0 were waited for; matrix products, arithmetic and copies ran while one was open for 0% of the time, Pallas kernels for 13%

profile of v9, /device:TPU:0, one launch (start us, length us, event | category | flops | bytes accessed | tf_op | source)
XLA Modules:
  0.0 575.5 jit_solution(14305229063666727987)
XLA Ops:
  0.6 0.8 fusion
  1.5 0.5 collective-permute-start
  2.0 72.0 %begin.1 = (bf16[8,128,1280]{2,1,0:T(8,128)(2,1)}, bf16[2048,1280]{1,0:T(8,128)(2,1)}, bf16[2048,1920]{1,0:T(8,128)(2,1)}, bf16[1280,1920]{1,0:T(8,128)(2,1)}, bf16[1280,1920]{1,0:T(8,128)(2,1)}) custom-call(bf16[4,2,128,1280]{3,2,1,0:T(8,128)(2,1)} %bitcast.36, bf16[1280,3840]{1,0:T(8,128)(2,1)} %refs_8_.1, f32[1280]{0:T(1024)} %refs_11_.1), custom_call_target="tpu_custom_call" | custom-call | tf_op jit(solution)/shard_map/begin/pallas_call | solution.py:402
  74.0 0.0 collective-permute-done
  74.0 0.1 broadcast_select_fusion
  74.1 0.6 gather_fusion
  74.7 0.1 select_bitcast_fusion
  74.7 0.0 copy-start.2
  74.8 1.3 copy.21
  76.1 0.0 copy-done.2
  76.1 80.4 %attend_row.1 = (bf16[2048,640]{1,0:T(8,128)(2,1)}, f32[5,2,2048]{2,1,0:T(2,128)}, bf16[8,128,1280]{2,1,0:T(8,128)(2,1)}, bf16[1024,1280]{1,0:T(8,128)(2,1)}, f32[1024,1280]{1,0:T(8,128)}) custom-call(s32[2048,1]{1,0:T(8,128)} %bitcast.29, s32[1,2048]{1,0:T(1,128)} %bitcast.39, ...), custom_call_target="tpu_custom_call" | custom-call | tf_op jit(solution)/shard_map/attend_row/pallas_call | solution.py:587
  156.5 151.4 %feed.1 = (bf16[1024,1280]{1,0:T(8,128)(2,1)}, f32[1024,1280]{1,0:T(8,128)}, bf16[2,1024,1280]{2,1,0:T(8,128)(2,1)}, bf16[2,2,16,2,16,640]{5,4,3,2,1,0:T(8,128)(...) custom-call(f32[1024,1280]{1,0:T(8,128)} %get-tuple-element.39.middl, ...), custom_call_target="tpu_custom_call" | custom-call | flops 80530636800 | bytes 60293120 | tf_op jit(solution)/shard_map/feed/pallas_call | solution.py:1003
  307.9 252.2 %back.1 = (bf16[4,2,128,1280]{3,2,1,0:T(8,128)(2,1)}, bf16[4,2,128,1280]{3,2,1,0:T(8,128)(2,1)}, bf16[5,2,2,80,512]{4,3,2,1,0:T(8,128)(2,1)}, bf16[4,2,2,80,640]...) custom-call(s32[2048,1]{1,0:T(8,128)} %bitcast.30, s32[1,2048]{1,0:T(1,128)} %bitcast.40, ...), custom_call_target="tpu_custom_call" | custom-call | flops 107374182400 | bytes 20971520 | tf_op jit(solution)/shard_map/back/pallas_call | solution.py:1455
  560.2 0.0 copy-start.1
  560.2 9.5 %collect.1 = (f32[160,3840]{1,0:T(8,128)}, f32[160,1280]{1,0:T(8,128)}, f32[640,1280]{1,0:T(8,128)}, f32[160,5120]{1,0:T(8,128)}, f32[1,160]{1,0:T(1,128)}, /*index=5*/f32[1,160]{1,0:T(1,128)}) custom-call(s32[1]{0:T(128)} %bitcast.15.seq_ref, bf16[5,2,2,80,512]{4,3,2,1,0:T(8,128)(2,1)} %get-tuple-element.55.refs_0_, ...), custom_call_target="tpu_custom_call" | custom-call | tf_op jit(solution)/shard_map/collect/pallas_call | solution.py:1595
  569.7 1.4 dynamic-slice_divide_fusion
  571.1 0.0 copy-done.1
  571.1 0.0 copy-start
  571.1 1.5 copy.25
  572.6 1.2 copy-done
  573.8 1.5 copy.26
  (5 shorter events, 0.1 us)
Async XLA Ops:
  1.5 72.5 %collective-permute-start = (s32[4,2048]{1,0:T(4,128)S(1)}, s32[4,2048]{1,0:T(4,128)S(1)}, u32[]{:S(2)}, u32[]{:S(2)}) collective-permute-start(s32[4,2048]{1,0:T(4,128)S(1)} %fusion), channel_id=1, source_target_pairs={{0,1},{1,0},{2,3},{3,2},{4,5},{5,4},{6,7},{7,6},{8,9},{9,8},{10,11... | collective-permute-start | bytes 98312 | tf_op jit(solution)/shard_map/ppermute | solution.py:1712
  74.7 1.4 copy-start.2
  560.2 10.9 %copy-start.1 = (bf16[4,2,128,1280]{3,2,1,0:T(8,128)(2,1)S(1)}, bf16[4,2,128,1280]{3,2,1,0:T(8,128)(2,1)}, u32[]{:S(2)}) copy-start(bf16[4,2,128,1280]{3,2,1,0:T(8,128)(2,1)} %get-tuple-element.53) | copy-start | bytes 7864324
  571.1 2.7 copy-start
